TPU v7x, 32 devices: a whole 2x2x4 slice. The times are simulated.
32 devices in a mesh: ctx: 8 (over y, x, core), fsdp: 4 (over z).
Axes of the slice: x: 2, y: 2, z: 4, core: 2. Of those that a mesh axis runs over, the one named last changes fastest.
Arguments:
- tokens: bfloat16 [4, 6144, 960], P('fsdp', 'ctx'), may hold values from -6 to 6
- cotangent: bfloat16 [4, 6144, 960], P('fsdp', 'ctx'), may hold values from -6 to 6
- doc_lengths: int32 [4, 1, 4], P('fsdp'), may hold values from 1 to 3072, 6144 in all within a row
- deal: int32 [4, 48], P('fsdp'), may hold values from 0 to 47, each once within a row
- attn_gain: bfloat16 [960], P('fsdp'), may hold values from 0.25 to 1.75
- w_query: bfloat16 [960, 960], P('fsdp'), may hold values from -0.1875 to 0.1875
- w_key: bfloat16 [960, 320], P('fsdp'), may hold values from -0.1875 to 0.1875
- w_value: bfloat16 [960, 320], P('fsdp'), may hold values from -0.1875 to 0.1875
- w_out: bfloat16 [960, 960], P('fsdp'), may hold values from -1.5 to 1.5
- mlp_gain: bfloat16 [960], P('fsdp'), may hold values from 0.25 to 1.75
- w_gate: bfloat16 [960, 2560], P(None, 'fsdp'), may hold values from -0.1875 to 0.1875
- w_up: bfloat16 [960, 2560], P(None, 'fsdp'), may hold values from -0.1875 to 0.1875
- w_down: bfloat16 [2560, 960], P('fsdp'), may hold values from -0.125 to 0.125
Outputs:
- output: bfloat16 [4, 6144, 960], P('fsdp', 'ctx')
- input_grad: bfloat16 [4, 6144, 960], P('fsdp', 'ctx')
- attn_gain_grad: float32 [960], P('fsdp')
- query_grad: float32 [960, 960], P('fsdp')
- key_grad: float32 [960, 320], P('fsdp')
- value_grad: float32 [960, 320], P('fsdp')
- out_grad: float32 [960, 960], P('fsdp')
- mlp_gain_grad: float32 [960], P('fsdp')
- gate_grad: float32 [960, 2560], P(None, 'fsdp')
- up_grad: float32 [960, 2560], P(None, 'fsdp')
- down_grad: float32 [2560, 960], P('fsdp')
Inputs may be any that keep to these rules, and one draw needn't show every extreme that they name: `deal`: each row orders the 48 sequence-order blocks of 128 tokens of one group: entry i names the block at dealt position i, and device j of ctx holds the positions from j * 6 on. `doc_lengths`: row [f, s] lists the lengths of the 4 documents of sequence s of group f in order, summing to 6144.
All inputs are finite; a program needn't handle non-finite values.
Results may differ from a plain program's by a relative error of at most 0.022.
Values may be sent and summed in bfloat16 or wider, within the bound.
No kernel may reach another device: no remote copies, remote signals or barrier semaphores. Data moves between devices by JAX's collectives and lax.ppermute only.
A program may use at most 320 MiB of HBM per device.

v0:
```python
import jax
import jax.numpy as jnp
from jax import lax
from jax.sharding import PartitionSpec as P

HQ = 15
KVH = 5
HD = 64
BLK = 128
WIN = 1024
KVW = 320


NORM_EPS = 1e-05
ROPE_THETA = 100000.0
MASK_FILL = -1e30


def matmul(inputs, others):
    return jnp.dot(inputs, others, preferred_element_type=jnp.float32)


def dot_nt(inputs, others):
    return lax.dot_general(
        inputs, others, (((1,), (1,)), ((), ())), preferred_element_type=jnp.float32
    )


def dot_tn(inputs, others):
    return lax.dot_general(
        inputs, others, (((0,), (0,)), ((), ())), preferred_element_type=jnp.float32
    )


def rope_tables(positions):
    half_dim = HD // 2
    freqs = ROPE_THETA ** (-jnp.arange(half_dim, dtype=jnp.float32) * (2.0 / HD))
    angle = positions.astype(jnp.float32)[:, None] * freqs[None, :]
    return (jnp.cos(angle)[:, None, :], jnp.sin(angle)[:, None, :])


def rotate(values, cos_tab, sin_tab, direction):
    row_count = values.shape[0]
    half_dim = HD // 2
    shaped = values.reshape(row_count, -1, HD)
    first_half = shaped[..., :half_dim]
    second_half = shaped[..., half_dim:]
    turned = direction * sin_tab
    head_result = jnp.concatenate(
        [first_half * cos_tab - second_half * turned, second_half * cos_tab + first_half * turned],
        axis=-1,
    )
    return head_result.reshape(row_count, -1)


def norm_forward(values):
    factor = lax.rsqrt(jnp.mean(values * values, axis=-1, keepdims=True) + NORM_EPS)
    return (values * factor, factor)


def norm_backward(grad_in, normed, factor, gain_vec):
    scaled = grad_in * gain_vec
    grad_values = factor * (scaled - normed * jnp.mean(scaled * normed, axis=-1, keepdims=True))
    return (grad_values, jnp.sum(grad_in * normed, axis=0))


def head_scores(query_head_slice, key_head_slice, key_mask, score_scale):
    scores = (
        jnp.einsum(
            "efow,ejw->efoj", query_head_slice, key_head_slice, preferred_element_type=jnp.float32
        )
        * score_scale
    )
    return jnp.where(key_mask[:, None], scores, MASK_FILL)


def head_forward(query_head_slice, key_head_slice, value_head_slice, key_mask, score_scale):
    scores = head_scores(query_head_slice, key_head_slice, key_mask, score_scale)
    top_score = jnp.max(scores, axis=-1, keepdims=True)
    expo = jnp.exp(scores - top_score)
    denom = jnp.sum(expo, axis=-1, keepdims=True)
    probabilities_reduced = (expo / denom).astype(jnp.bfloat16)
    head_result = jnp.einsum(
        "pmxj,pjf->pmxf",
        probabilities_reduced,
        value_head_slice,
        preferred_element_type=jnp.float32,
    )
    return (head_result, top_score + jnp.log(denom))


def head_backward(
    query_head_slice,
    key_head_slice,
    value_head_slice,
    head_gradient,
    log_total,
    key_mask,
    score_scale,
):
    scores = head_scores(query_head_slice, key_head_slice, key_mask, score_scale)
    probabilities = jnp.exp(scores - log_total)
    probability_gradient = jnp.einsum(
        "efow,ejw->efoj", head_gradient, value_head_slice, preferred_element_type=jnp.float32
    )
    row_dot = jnp.sum(probabilities * probability_gradient, axis=-1, keepdims=True)
    score_gradient = (probabilities * (probability_gradient - row_dot)).astype(jnp.bfloat16)
    grad_q = (
        jnp.einsum(
            "pmxj,pjf->pmxf", score_gradient, key_head_slice, preferred_element_type=jnp.float32
        )
        * score_scale
    )
    grad_k = (
        jnp.einsum(
            "ucxo,ucxi->uoi", score_gradient, query_head_slice, preferred_element_type=jnp.float32
        )
        * score_scale
    )
    grad_v = jnp.einsum(
        "ucxo,ucxi->uoi",
        probabilities.astype(jnp.bfloat16),
        head_gradient,
        preferred_element_type=jnp.float32,
    )
    return (grad_q, grad_k, grad_v, row_dot)


def on_device(
    tokens,
    cotangent,
    doc_lengths,
    deal,
    attn_gain,
    w_query,
    w_key,
    w_value,
    w_out,
    mlp_gain,
    w_gate,
    w_up,
    w_down,
):
    my_index = lax.axis_index("ctx")
    tok_rows = tokens.shape[1]
    per_dev = tok_rows // BLK
    deal_row = deal[0]
    blocks = deal_row.shape[0]
    group_size = blocks * BLK
    doc_lens = doc_lengths[0]
    seq_count = doc_lens.shape[0]
    length = group_size // seq_count
    key_span = WIN + BLK
    head_group = HQ // KVH
    score_scale = HD ** (-0.5)
    block_ids = jnp.arange(blocks, dtype=jnp.int32)
    inverse = jnp.sum(
        jnp.where(deal_row[None, :] == block_ids[:, None], block_ids[None, :], 0), axis=1
    )
    mine = lax.dynamic_slice_in_dim(deal_row, my_index * per_dev, per_dev)
    doc_ends = (
        jnp.cumsum(doc_lens, axis=1) + (jnp.arange(seq_count, dtype=jnp.int32) * length)[:, None]
    ).reshape(-1)
    doc_starts = doc_ends - doc_lens.reshape(-1)
    doc_ids = jnp.arange(doc_ends.shape[0], dtype=jnp.int32)

    def locate(t_values):
        doc_num = jnp.sum((t_values[..., None] >= doc_ends).astype(jnp.int32), axis=-1)
        doc_begin = jnp.sum(jnp.where(doc_num[..., None] == doc_ids, doc_starts, 0), axis=-1)
        return (doc_num, t_values - doc_begin)

    q_time = mine[:, None] * BLK + jnp.arange(BLK, dtype=jnp.int32)[None, :]
    k_time = mine[:, None] * BLK - WIN + jnp.arange(key_span, dtype=jnp.int32)[None, :]
    q_docs, q_pos = locate(q_time)
    k_docs = locate(k_time)[0]
    key_mask = (
        (k_time[:, None, :] >= 0)
        & (k_time[:, None, :] <= q_time[:, :, None])
        & (q_time[:, :, None] - k_time[:, None, :] < WIN)
        & (q_docs[:, :, None] == k_docs[:, None, :])
    )
    cos_tab, sin_tab = rope_tables(q_pos.reshape(-1))
    (
        gain_one,
        query_full,
        key_full,
        value_full,
        out_full,
        gain_two,
        gate_full,
        up_full,
        down_full,
    ) = (
        lax.all_gather(attn_gain, "fsdp", axis=0, tiled=True),
        lax.all_gather(w_query, "fsdp", axis=0, tiled=True),
        lax.all_gather(w_key, "fsdp", axis=0, tiled=True),
        lax.all_gather(w_value, "fsdp", axis=0, tiled=True),
        lax.all_gather(w_out, "fsdp", axis=0, tiled=True),
        lax.all_gather(mlp_gain, "fsdp", axis=0, tiled=True),
        lax.all_gather(w_gate, "fsdp", axis=1, tiled=True),
        lax.all_gather(w_up, "fsdp", axis=1, tiled=True),
        lax.all_gather(w_down, "fsdp", axis=0, tiled=True),
    )
    gain_one_f = gain_one.astype(jnp.float32)
    gain_two_f = gain_two.astype(jnp.float32)
    inputs = tokens[0].astype(jnp.float32)
    normed_one, factor_one = norm_forward(inputs)
    attn_in = (normed_one * gain_one_f).astype(jnp.bfloat16)
    query_pre = matmul(attn_in, query_full)
    key_pre = matmul(attn_in, key_full)
    value_low = matmul(attn_in, value_full).astype(jnp.bfloat16)
    query_low = rotate(query_pre, cos_tab, sin_tab, 1.0).astype(jnp.bfloat16)
    key_low = rotate(key_pre, cos_tab, sin_tab, 1.0).astype(jnp.bfloat16)
    key_all, value_all = (
        lax.all_gather(key_low, "ctx", axis=0, tiled=True),
        lax.all_gather(value_low, "ctx", axis=0, tiled=True),
    )

    def windows(source):
        ordered = jnp.take(source.reshape(blocks, BLK, -1), inverse, axis=0).reshape(group_size, -1)
        padded = jnp.concatenate(
            [jnp.zeros((WIN, ordered.shape[1]), ordered.dtype), ordered], axis=0
        )
        return jax.vmap(lambda first_row: lax.dynamic_slice_in_dim(padded, first_row, key_span, 0))(
            mine * BLK
        )

    def split_queries(flat):
        return flat.reshape(per_dev, BLK, KVH, head_group, HD).transpose(2, 0, 3, 1, 4)

    def split_keys(window_rows):
        return window_rows.reshape(per_dev, key_span, KVH, HD).transpose(2, 0, 1, 3)

    def merge_queries(per_head):
        return per_head.transpose(1, 3, 0, 2, 4).reshape(tok_rows, HQ * HD)

    def merge_keys(per_head):
        return per_head.transpose(1, 2, 0, 3).reshape(per_dev, key_span, KVW)

    q_heads = split_queries(query_low)
    k_heads = split_keys(windows(key_all))
    v_heads = split_keys(windows(value_all))
    head_out, head_lse = lax.map(
        lambda packed: head_forward(packed[0], packed[1], packed[2], key_mask, score_scale),
        (q_heads, k_heads, v_heads),
    )
    attn_mid = merge_queries(head_out).astype(jnp.bfloat16)
    hidden_one = inputs + matmul(attn_mid, out_full)
    normed_two, factor_two = norm_forward(hidden_one)
    mlp_in = (normed_two * gain_two_f).astype(jnp.bfloat16)
    gate_pre = matmul(mlp_in, gate_full)
    up_pre = matmul(mlp_in, up_full)
    sigmoid_gate = jax.nn.sigmoid(gate_pre)
    swish = gate_pre * sigmoid_gate
    hidden_low = (swish * up_pre).astype(jnp.bfloat16)
    mlp_out = matmul(hidden_low, down_full)
    output = (hidden_one + mlp_out).astype(jnp.bfloat16)
    grad_low = cotangent[0]
    grad_top = grad_low.astype(jnp.float32)
    grad_hid = dot_nt(grad_low, down_full)
    grad_down = dot_tn(hidden_low, grad_low)
    grad_gate_low = (
        grad_hid * up_pre * sigmoid_gate * (1.0 + gate_pre * (1.0 - sigmoid_gate))
    ).astype(jnp.bfloat16)
    grad_up_low = (grad_hid * swish).astype(jnp.bfloat16)
    grad_gate = dot_tn(mlp_in, grad_gate_low)
    grad_up = dot_tn(mlp_in, grad_up_low)
    grad_mlp_in = dot_nt(grad_gate_low, gate_full) + dot_nt(grad_up_low, up_full)
    grad_norm_two, grad_gain_two = norm_backward(grad_mlp_in, normed_two, factor_two, gain_two_f)
    grad_hidden = grad_top + grad_norm_two
    res_low = grad_hidden.astype(jnp.bfloat16)
    grad_out_proj = dot_tn(attn_mid, res_low)
    grad_mid_low = dot_nt(res_low, out_full).astype(jnp.bfloat16)
    grad_heads = split_queries(grad_mid_low)
    grad_q_heads, grad_k_heads, grad_v_heads, head_dots = lax.map(
        lambda packed: head_backward(
            packed[0], packed[1], packed[2], packed[3], packed[4], key_mask, score_scale
        ),
        (q_heads, k_heads, v_heads, grad_heads, head_lse),
    )

    def spread(window_grads):

        def add_block(blk_index, running):
            first_row = mine[blk_index] * BLK
            current = lax.dynamic_slice_in_dim(running, first_row, key_span, 0)
            return lax.dynamic_update_slice_in_dim(
                running, current + window_grads[blk_index], first_row, 0
            )

        padded = lax.fori_loop(
            0, per_dev, add_block, jnp.zeros((WIN + group_size, KVW), jnp.float32)
        )
        ordered = padded[WIN:].reshape(blocks, BLK, KVW)
        return jnp.take(ordered, deal_row, axis=0).reshape(group_size, KVW)

    key_sum, value_sum = (
        lax.psum_scatter(
            spread(merge_keys(grad_k_heads)).astype(jnp.bfloat16),
            "ctx",
            scatter_dimension=0,
            tiled=True,
        ).astype(jnp.float32),
        lax.psum_scatter(
            spread(merge_keys(grad_v_heads)).astype(jnp.bfloat16),
            "ctx",
            scatter_dimension=0,
            tiled=True,
        ).astype(jnp.float32),
    )
    query_grad_low = rotate(merge_queries(grad_q_heads), cos_tab, sin_tab, -1.0).astype(
        jnp.bfloat16
    )
    key_grad_low = rotate(key_sum, cos_tab, sin_tab, -1.0).astype(jnp.bfloat16)
    value_grad_low = value_sum.astype(jnp.bfloat16)
    grad_query = dot_tn(attn_in, query_grad_low)
    grad_key = dot_tn(attn_in, key_grad_low)
    grad_value = dot_tn(attn_in, value_grad_low)
    grad_attn_in = (
        dot_nt(query_grad_low, query_full)
        + dot_nt(key_grad_low, key_full)
        + dot_nt(value_grad_low, value_full)
    )
    grad_norm_one, grad_gain_one = norm_backward(grad_attn_in, normed_one, factor_one, gain_one_f)
    input_grad = (grad_hidden + grad_norm_one).astype(jnp.bfloat16)
    (
        share_g1,
        share_query,
        share_key,
        share_value,
        share_out,
        share_g2,
        share_gate,
        share_up,
        share_down,
    ) = (
        lax.psum_scatter(
            grad_gain_one.astype(jnp.bfloat16), "fsdp", scatter_dimension=0, tiled=True
        ).astype(jnp.float32),
        lax.psum_scatter(
            grad_query.astype(jnp.bfloat16), "fsdp", scatter_dimension=0, tiled=True
        ).astype(jnp.float32),
        lax.psum_scatter(
            grad_key.astype(jnp.bfloat16), "fsdp", scatter_dimension=0, tiled=True
        ).astype(jnp.float32),
        lax.psum_scatter(
            grad_value.astype(jnp.bfloat16), "fsdp", scatter_dimension=0, tiled=True
        ).astype(jnp.float32),
        lax.psum_scatter(
            grad_out_proj.astype(jnp.bfloat16), "fsdp", scatter_dimension=0, tiled=True
        ).astype(jnp.float32),
        lax.psum_scatter(
            grad_gain_two.astype(jnp.bfloat16), "fsdp", scatter_dimension=0, tiled=True
        ).astype(jnp.float32),
        lax.psum_scatter(
            grad_gate.astype(jnp.bfloat16), "fsdp", scatter_dimension=1, tiled=True
        ).astype(jnp.float32),
        lax.psum_scatter(
            grad_up.astype(jnp.bfloat16), "fsdp", scatter_dimension=1, tiled=True
        ).astype(jnp.float32),
        lax.psum_scatter(
            grad_down.astype(jnp.bfloat16), "fsdp", scatter_dimension=0, tiled=True
        ).astype(jnp.float32),
    )
    (
        final_g1,
        final_query,
        final_key,
        final_value,
        final_out,
        final_g2,
        final_gate,
        final_up,
        final_down,
    ) = (
        lax.psum(share_g1.astype(jnp.bfloat16), "ctx").astype(jnp.float32),
        lax.psum(share_query.astype(jnp.bfloat16), "ctx").astype(jnp.float32),
        lax.psum(share_key.astype(jnp.bfloat16), "ctx").astype(jnp.float32),
        lax.psum(share_value.astype(jnp.bfloat16), "ctx").astype(jnp.float32),
        lax.psum(share_out.astype(jnp.bfloat16), "ctx").astype(jnp.float32),
        lax.psum(share_g2.astype(jnp.bfloat16), "ctx").astype(jnp.float32),
        lax.psum(share_gate.astype(jnp.bfloat16), "ctx").astype(jnp.float32),
        lax.psum(share_up.astype(jnp.bfloat16), "ctx").astype(jnp.float32),
        lax.psum(share_down.astype(jnp.bfloat16), "ctx").astype(jnp.float32),
    )
    return (
        output[None],
        input_grad[None],
        final_g1,
        final_query,
        final_key,
        final_value,
        final_out,
        final_g2,
        final_gate,
        final_up,
        final_down,
    )


def solution(mesh):
    in_specs = (
        P("fsdp", "ctx", None),
        P("fsdp", "ctx", None),
        P("fsdp", None, None),
        P("fsdp", None),
        P("fsdp"),
        P("fsdp", None),
        P("fsdp", None),
        P("fsdp", None),
        P("fsdp", None),
        P("fsdp"),
        P(None, "fsdp"),
        P(None, "fsdp"),
        P("fsdp", None),
    )
    out_specs = (
        P("fsdp", "ctx", None),
        P("fsdp", "ctx", None),
        P("fsdp"),
        P("fsdp", None),
        P("fsdp", None),
        P("fsdp", None),
        P("fsdp", None),
        P("fsdp"),
        P(None, "fsdp"),
        P(None, "fsdp"),
        P("fsdp", None),
    )
    return jax.shard_map(
        on_device, mesh=mesh, in_specs=in_specs, out_specs=out_specs, check_vma=False
    )
```

profile of v0, /device:TPU:0, one launch (start us, length us, event | category | flops | bytes accessed | tf_op | source)
XLA Modules:
  0.0 1336.2 jit_solution(17492908793618276053)
XLA Ops:
  11.7 13.5 %all-reduce.10 = (bf16[960]{0:T(1024)(128)(2,1)S(1)}, bf16[960]{0:T(1024)(128)(2,1)S(1)}) all-reduce(bf16[960]{0:T(1024)(128)(2,1)S(1)} %dynamic-update-slice.4, bf16[960]{0:T(1024)(128)(2,1)S(1)} %dynamic-update-slice.5), channel_id=1, replica_groups=mesh['ctx'=8,'fsdp'=4] {'fsdp'}, use_global_device_ids=true, to_apply=%add.3 | all-reduce | flops 1920 | bytes 7680
  25.3 25.9 %all-gather.1 = bf16[4,240,320]{1,2,0:T(8,128)(2,1)S(1)} all-gather(bf16[1,240,320]{1,2,0:T(8,128)(2,1)} %bitcast.399), channel_id=1, replica_groups=mesh['ctx'=8,'fsdp'=4] {'fsdp'}, dimensions={0}, use_global_device_ids=true | all-gather | bytes 768000 | tf_op jit(solution)/shard_map/all_gather | solution.py:197
  54.5 22.7 %all-gather = bf16[4,240,320]{1,2,0:T(8,128)(2,1)S(1)} all-gather(bf16[1,240,320]{1,2,0:T(8,128)(2,1)S(1)} %bitcast.400), channel_id=1, replica_groups=mesh['ctx'=8,'fsdp'=4] {'fsdp'}, dimensions={0}, use_global_device_ids=true | all-gather | bytes 768000 | tf_op jit(solution)/shard_map/all_gather | solution.py:196
  101.2 11.5 all-gather.14.cloned.1.call-done
  123.0 27.8 %all-gather.12.cloned.1.call-done = bf16[6144,320]{0,1:T(8,128)(2,1)} async-done(((bf16[768,320]{0,1:T(8,128)(2,1)}), bf16[6144,320]{0,1:T(8,128)(2,1)}) %all-gather.12.cloned.1.call-update) | async-done | bytes 3932176 | tf_op jit(solution)/shard_map/all_gather | solution.py:215
  172.8 32.1 %while.65 = (s32[]{:T(128)}, bf16[7168,320]{0,1:T(8,128)(2,1)}, s32[6,2]{0,1:T(2,128)S(1)}, bf16[6,1152,320]{1,2,0:T(8,128)(2,1)}) while((s32[]{:T(128)}, bf16[7168,320]{0,1:T(8,128)(2,1)}, s32[6,2]{0,1:T(2,128)S(1)}, bf16[6,1152,320]{1,2,0:T(8,128)(2,1)}) %tuple.197), condition=%wide.while_cond.1.clone, body=%wide.while_body.1.sunk.clone | while | flops 2 | bytes 5898337 | solution.py:224
  215.3 32.5 %while.64 = (s32[]{:T(128)}, bf16[7168,320]{0,1:T(8,128)(2,1)}, s32[6,2]{0,1:T(2,128)S(1)}, bf16[6,1152,320]{1,2,0:T(8,128)(2,1)}) while((s32[]{:T(128)}, bf16[7168,320]{0,1:T(8,128)(2,1)}, s32[6,2]{0,1:T(2,128)S(1)}, bf16[6,1152,320]{1,2,0:T(8,128)(2,1)}) %tuple.254), condition=%wide.while_cond.clone, body=%wide.while_body.sunk.clone | while | flops 2 | bytes 5898337 | solution.py:224
  252.6 71.3 %while.66 = (s32[]{:T(128)}, bf16[5,6,3,128,64]{3,4,2,1,0:T(8,128)(2,1)}, f32[5,6,3,128,1]{3,2,1,4,0:T(4,128)}, bf16[5,6,3,128,64]{3,4,2,1,0:T(8,128)(2,1)S(1)},...) while((s32[]{:T(128)}, ...), condition=%wide.region_9.11_spmd.clone.clone, body=%wide.region_6.10_spmd.clone.sunk.clone | while | flops 717518592 | bytes 38190968 | solution.py:243
  344.0 37.3 %all-gather.18.cloned.1.call-done = bf16[960,2560]{1,0:T(8,128)(2,1)} async-done(((bf16[960,640]{1,0:T(8,128)(2,1)}), bf16[960,2560]{1,0:T(8,128)(2,1)}) %all-gather.18.cloned.1.call-update) | async-done | bytes 4915216 | tf_op jit(solution)/shard_map/all_gather | solution.py:200
  381.3 10.5 fusion.108
  391.8 82.2 %all-gather.22.cloned.1.call-done = bf16[2560,960]{0,1:T(8,128)(2,1)} async-done(((bf16[640,960]{0,1:T(8,128)(2,1)}), bf16[2560,960]{0,1:T(8,128)(2,1)}) %all-gather.22.cloned.1.call-update) | async-done | bytes 4915216 | tf_op jit(solution)/shard_map/all_gather | solution.py:202
  474.0 14.1 %multiply_convert_fusion.1 = (bf16[768,2560]{1,0:T(8,128)(2,1)S(1)}, bf16[768,2560]{1,0:T(8,128)(2,1)S(1)}, bf16[768,2560]{1,0:T(8,128)(2,1)}) fusion(f32[768,2560]{1,0:T(8,128)} %fusion.108, f32[768,2560]{1,0:T(8,128)} %fusion.109, bf16[2560,960]{0,1:T(8,128)(2,1)} %all-gather.22.cloned.1.call-done, bf16[1,768,960]{1,2,0:T(8,128)(2,1)S(1)} %copy-done.18), kind=kOutput, calls=%fused_computation.81 | convolution fusion | flops 3804364800 | bytes 33914880 | tf_op jit(solution)/shard_map/dot_general | solution.py:24
  508.4 102.8 %while.67 = (s32[]{:T(128)}, f32[5,6,3,128,64]{3,4,2,1,0:T(8,128)}, f32[5,6,1152,64]{2,3,0,1:T(8,128)}, f32[5,6,1152,64]{2,3,0,1:T(8,128)}, bf16[5,6,3,128,64]{3...) while((s32[]{:T(128)}, f32[5,6,3,128,64]{3,4,2,1,0:T(8,128)}, ...), condition=%wide.region_14.16_spmd.clone.clone, body=%wide.region_12.15_spmd.clone.sunk.clone | while | flops 1729361664 | bytes 89481104 | solution.py:275
  615.9 40.6 %while.63 = (s32[]{:T(128)}, f32[7168,320]{1,0:T(8,128)}, s32[6]{0:T(128)S(1)}, f32[6,1152,320]{1,2,0:T(8,128)}, s32[1]{0:T(128)}) while((s32[]{:T(128)}, f32[7168,320]{1,0:T(8,128)}, s32[6]{0:T(128)S(1)}, f32[6,1152,320]{1,2,0:T(8,128)}, s32[1]{0:T(128)}) %tuple.255), condition=%wide.region_19.22_spmd.clone, body=%wide.region_18.21_spmd.sunk.clone | while | flops 368646 | bytes 10911879 | solution.py:291
  680.0 41.5 %while.62 = (s32[]{:T(128)}, f32[7168,320]{1,0:T(8,128)}, s32[6]{0:T(128)S(1)}, f32[6,1152,320]{1,2,0:T(8,128)}, s32[1]{0:T(128)}) while((s32[]{:T(128)}, f32[7168,320]{1,0:T(8,128)}, s32[6]{0:T(128)S(1)}, f32[6,1152,320]{1,2,0:T(8,128)}, s32[1]{0:T(128)}) %tuple.256), condition=%wide.region_16.18_spmd.clone, body=%wide.region_15.17_spmd.sunk.clone | while | flops 368646 | bytes 10911879 | solution.py:291
  749.2 44.5 %reduce-scatter.20.cloned.1.call-done = bf16[768,320]{0,1:T(8,128)(2,1)} async-done(((bf16[6144,320]{0,1:T(8,128)(2,1)}), bf16[768,320]{0,1:T(8,128)(2,1)}) %reduce-scatter.20.cloned.1.call-update) | async-done | bytes 491536 | tf_op jit(solution)/shard_map/reduce_scatter | solution.py:298
  880.6 58.8 %reduce-scatter.32.cloned.1.call-done = bf16[640,960]{1,0:T(8,128)(2,1)} async-done(((bf16[2560,960]{1,0:T(8,128)(2,1)}), bf16[640,960]{1,0:T(8,128)(2,1)}) %reduce-scatter.32.cloned.1.call-update) | async-done | bytes 1228816
  941.8 94.2 %reduce-scatter.34.cloned.1.call-done = bf16[640,960]{1,0:T(8,128)(2,1)} async-done(((bf16[2560,960]{1,0:T(8,128)(2,1)}), bf16[640,960]{1,0:T(8,128)(2,1)}) %reduce-scatter.34.cloned.1.call-update) | async-done | bytes 1228816
  1038.4 94.0 %reduce-scatter.36.cloned.1.call-done = bf16[640,960]{1,0:T(8,128)(2,1)} async-done(((bf16[2560,960]{1,0:T(8,128)(2,1)}), bf16[640,960]{1,0:T(8,128)(2,1)}) %reduce-scatter.36.cloned.1.call-update) | async-done | bytes 1228816
  1134.9 42.3 %reduce-scatter.26.cloned.1.call-done = bf16[240,960]{1,0:T(8,128)(2,1)} async-done(((bf16[960,960]{1,0:T(8,128)(2,1)}), bf16[240,960]{1,0:T(8,128)(2,1)}) %reduce-scatter.26.cloned.1.call-update) | async-done | bytes 460816 | tf_op jit(solution)/shard_map/reduce_scatter | solution.py:349
  1177.2 43.4 %reduce-scatter.24.cloned.1.call-done = bf16[240,960]{1,0:T(8,128)(2,1)} async-done(((bf16[960,960]{1,0:T(8,128)(2,1)}), bf16[240,960]{1,0:T(8,128)(2,1)}) %reduce-scatter.24.cloned.1.call-update) | async-done | bytes 460816 | tf_op jit(solution)/shard_map/reduce_scatter | solution.py:340
  1220.7 9.7 fusion.91
  1245.9 12.3 all-reduce.7
  1264.2 52.8 %all-reduce.13.cloned.1.call-done = (bf16[240,960]{1,0:T(8,128)(2,1)}, bf16[240,320]{0,1:T(8,128)(2,1)}, bf16[240,320]{0,1:T(8,128)(2,1)}, bf16[240,960]{1,0:T(8...) async-done(((bf16[240,960]{1,0:T(8,128)(2,1)}, bf16[240,320]{0,1:T(8,128)(2,1)}, bf16[240,320]{0,1:T(8,128)(2,1)}, ...) | async-done | bytes 4915216 | tf_op jit(solution)/shard_map/psum | solution.py:377
  (439 shorter events, 613.2 us)
Async XLA Ops:
  7.2 45.0 %copy-start.1 = (bf16[1,768,960]{1,2,0:T(8,128)(2,1)S(1)}, bf16[1,768,960]{1,2,0:T(8,128)(2,1)}, u32[]{:S(2)}) copy-start(bf16[1,768,960]{1,2,0:T(8,128)(2,1)} %param.25) | copy-start | bytes 4423684
  7.2 83.9 %all-gather.10.cloned.1.call-start = ((), (), s32[]{:S(2)}) async-start(), calls=%async_computation.9 | async-start | bytes 2457600 | tf_op jit(solution)/shard_map/all_gather | solution.py:195
  7.9 104.8 %all-gather.14.cloned.1.call-start = ((), (), s32[]{:S(2)}) async-start(), calls=%async_computation.11 | async-start | bytes 4423680 | tf_op jit(solution)/shard_map/all_gather | solution.py:216
  25.3 69.8 %copy-start.30 = (f32[960]{0:T(1024)}, f32[960]{0:T(1024)S(1)}, u32[]{:S(2)}) copy-start(f32[960]{0:T(1024)S(1)} %convert_element_type.220) | copy-start | bytes 11524
  52.6 42.5 %copy-start.32 = (f32[768]{0:T(1024)}, f32[768]{0:T(1024)S(1)}, u32[]{:S(2)}) copy-start(f32[768]{0:T(1024)S(1)} %add_rsqrt_fusion.1) | copy-start | bytes 9220
  54.2 24.0 %copy-start.37 = (s32[1,48]{1,0:T(1,128)S(1)}, s32[1,48]{1,0:T(1,128)}, u32[]{:S(2)}) copy-start(s32[1,48]{1,0:T(1,128)} %param.28) | copy-start | bytes 580
  54.2 96.6 %all-gather.12.cloned.1.call-start = ((), (), s32[]{:S(2)}) async-start(), calls=%async_computation.10 | async-start | bytes 4423680 | tf_op jit(solution)/shard_map/all_gather | solution.py:215
  84.1 243.8 %all-gather.16.cloned.1.call-start = ((), (), s32[]{:S(2)}) async-start(), calls=%async_computation.12 | async-start | bytes 2457600 | tf_op jit(solution)/shard_map/all_gather | solution.py:198
  84.7 249.3 %all-gather.20.cloned.1.call-start = ((), (), s32[]{:S(2)}) async-start(), calls=%async_computation.14 | async-start | bytes 6144000 | tf_op jit(solution)/shard_map/all_gather | solution.py:201
  85.3 296.0 %all-gather.18.cloned.1.call-start = ((), (), s32[]{:S(2)}) async-start(), calls=%async_computation.13 | async-start | bytes 6144000 | tf_op jit(solution)/shard_map/all_gather | solution.py:200
  85.9 388.1 %all-gather.22.cloned.1.call-start = ((), (), s32[]{:S(2)}) async-start(), calls=%async_computation.15 | async-start | bytes 6144000 | tf_op jit(solution)/shard_map/all_gather | solution.py:202
  86.6 658.2 %reduce-scatter.22.cloned.1.call-start = ((), (), s32[]{:S(2)}) async-start(), calls=%async_computation.17 | async-start | bytes 5308416 | tf_op jit(solution)/shard_map/reduce_scatter | solution.py:304
  344.0 130.0 %copy-start.18 = (bf16[1,768,960]{1,2,0:T(8,128)(2,1)S(1)}, bf16[1,768,960]{1,2,0:T(8,128)(2,1)}, u32[]{:S(2)}) copy-start(bf16[1,768,960]{1,2,0:T(8,128)(2,1)} %param.26) | copy-start | bytes 4423684
  675.2 118.5 %reduce-scatter.20.cloned.1.call-start = ((), (), s32[]{:S(2)}) async-start(), calls=%async_computation.16 | async-start | bytes 4423680 | tf_op jit(solution)/shard_map/reduce_scatter | solution.py:298
  744.8 50.1 %copy-start.13 = (f32[768,32]{0,1:T(8,128)S(1)}, f32[768,32]{0,1:T(8,128)}, u32[]{:S(2)}) copy-start(f32[768,32]{0,1:T(8,128)} %copy-done.12) | copy-start | bytes 294916
  744.8 50.1 %copy-start.26 = (f32[768,32]{0,1:T(8,128)S(1)}, f32[768,32]{0,1:T(8,128)}, u32[]{:S(2)}) copy-start(f32[768,32]{0,1:T(8,128)} %get-tuple-element.745) | copy-start | bytes 294916
  744.8 132.4 %reduce-scatter.30.cloned.1.call-start = ((), (), s32[]{:S(2)}) async-start(), calls=%async_computation.21 | async-start | bytes 921600
  749.2 129.7 %reduce-scatter.28.cloned.1.call-start = ((), (), s32[]{:S(2)}) async-start(), calls=%async_computation.20 | async-start | bytes 921600
  799.7 139.7 %reduce-scatter.32.cloned.1.call-start = ((), (), s32[]{:S(2)}) async-start(), calls=%async_computation.22 | async-start | bytes 6553600
  815.5 220.5 %reduce-scatter.34.cloned.1.call-start = ((), (), s32[]{:S(2)}) async-start(), calls=%async_computation.23 | async-start | bytes 6553600
  831.3 301.2 %reduce-scatter.36.cloned.1.call-start = ((), (), s32[]{:S(2)}) async-start(), calls=%async_computation.24 | async-start | bytes 6553600
  848.3 328.9 %reduce-scatter.26.cloned.1.call-start = ((), (), s32[]{:S(2)}) async-start(), calls=%async_computation.19 | async-start | bytes 2457600 | tf_op jit(solution)/shard_map/reduce_scatter | solution.py:349
  854.7 365.9 %reduce-scatter.24.cloned.1.call-start = ((), (), s32[]{:S(2)}) async-start(), calls=%async_computation.18 | async-start | bytes 2457600 | tf_op jit(solution)/shard_map/reduce_scatter | solution.py:340
  871.8 445.2 %all-reduce.13.cloned.1.call-start = ((), (), s32[]{:S(2)}) async-start(), calls=%async_computation.25 | async-start | bytes 9994240 | tf_op jit(solution)/shard_map/psum | solution.py:377
  (38 other events, 162.7 us)
Sparse Core Ops, SparseCore 0:
  9.6 66.4 all-gather.9
  78.6 34.0 all-gather.13
  115.2 35.5 all-gather.11
  152.2 43.5 all-gather.15
  197.2 91.4 all-gather.19
  290.2 91.0 all-gather.17
  382.9 91.0 all-gather.21
  675.3 52.4 reduce-scatter.21
  744.9 48.8 reduce-scatter.19
  796.5 22.8 reduce-scatter.29
  822.2 22.0 reduce-scatter.27
  846.5 92.9 reduce-scatter.31
  941.7 94.2 reduce-scatter.33
  1038.2 94.2 reduce-scatter.35
  1135.2 41.9 reduce-scatter.25
  1179.9 40.6 reduce-scatter.23
  1225.9 91.0 all-reduce.12
where the time goes:
time: 1350 us; the launch traced here: 1340 us
  waiting for transfers between devices  592 us (44%)
  local copies, waits for them, and re-layouts  270 us (20%)
  matrix products  233 us (17%)
  other arithmetic  130 us (10%)
  blocking collectives  83.9 us (6%)
  between operations  16.2 us (1%)
    unnamed x22, waiting for transfers between devices  250 us
    all_gather x1, waiting for transfers between devices, on_device(): lax.all_gather(w_down, 'fsdp', axis=0, tiled=True)  82.2 us
    unnamed x115, local copies, waits for them, and re-layouts  71 us
    gather x72, local copies, waits for them, and re-layouts  64 us
    psum x1, waiting for transfers between devices, on_device(): lax.psum(share_query.astype(jnp.bfloat16), 'ctx').astype(jnp.float32)  52.8 us
    reduce_scatter x1, waiting for transfers between devices, on_device(): lax.psum_scatter(spread(merge_keys(grad_k_heads)).astype(jnp.bfloat16), '...  44.5 us
    reduce_scatter x1, waiting for transfers between devices, on_device(): lax.psum_scatter(grad_query.astype(jnp.bfloat16), 'fsdp', scatter_dimensi...  43.4 us
    reduce_scatter x1, waiting for transfers between devices, on_device(): lax.psum_scatter(grad_out_proj.astype(jnp.bfloat16), 'fsdp', scatter_dime...  42.3 us
  transfers between devices with their start and end apart: 17, of which 11 were waited for; matrix products, arithmetic and copies ran while one was open for 31% of the time, Pallas kernels for 0%

commit v1 on v0

v1 whole, which is shorter than its diff:
```python
import jax
import jax.numpy as jnp
from jax import lax
from jax.experimental import pallas as pl
from jax.experimental.pallas import tpu as pltpu
from jax.sharding import PartitionSpec as P

HQ = 15
KVH = 5
HD = 64
BLK = 128
WIN = 1024
D = 960
KVW = 320
GRP = HQ // KVH
SPAN = WIN + BLK
NWB = SPAN // BLK
ROWS = 256
ZR = 240
ZP = 256
UNITS = 256

NORM_EPS = 1e-05
ROPE_THETA = 100000.0
MASK_FILL = -1e30
F32 = jnp.float32
BF16 = jnp.bfloat16
MIB = 1024 * 1024

VMEM = pl.BlockSpec(memory_space=pltpu.VMEM)
SMEM = pl.BlockSpec(memory_space=pltpu.SMEM)
ANY = pl.BlockSpec(memory_space=pl.ANY)


def dot(a, b):
    return jnp.dot(a, b, preferred_element_type=F32)


def dot_nt(a, b):
    return lax.dot_general(a, b, (((1,), (1,)), ((), ())), preferred_element_type=F32)


def dot_tn(a, b):
    return lax.dot_general(a, b, (((0,), (0,)), ((), ())), preferred_element_type=F32)


def params(mib, grid_dims=0):
    return pltpu.CompilerParams(
        vmem_limit_bytes=mib * MIB,
        dimension_semantics=("arbitrary",) * grid_dims if grid_dims else None,
    )


def cost(flops, moved, exps=0):
    return pl.CostEstimate(flops=int(flops), bytes_accessed=int(moved), transcendentals=int(exps))


def rope_slab(t, cos, sin_signed, first_half):
    swapped = jnp.where(first_half, pltpu.roll(t, 96, 1), pltpu.roll(t, 32, 1))
    return t * cos + swapped * sin_signed


def lane_masks(rows):
    lane = lax.broadcasted_iota(jnp.int32, (rows, 128), 1)
    return (lane % HD) < HD // 2, lane < HD


def pre_kernel(
    info, x_ref, gain_ref, cos_ref, sin_ref,
    a_own, b_own, m_up, m_dn, m_t1, m_t2, o_up, o_dn, o_t1, o_t2,
    attn_ref, q_ref, kv_ref, w_ref, sems,
):
    z, core = info[0], info[1]
    other = 1 - core
    half = 640

    def rows(shift):
        return pl.ds(pl.multiple_of(lax.rem(z + shift, 4) * ZR, 16), ZR)

    pairs = [
        (a_own, w_ref.at[0, rows(0)]),
        (b_own, w_ref.at[1, rows(0)]),
    ]
    for idx, (up, dn, t1, t2) in ((core, (m_up, m_dn, m_t1, m_t2)), (other, (o_up, o_dn, o_t1, o_t2))):
        pairs += [
            (up, w_ref.at[idx, rows(3)]),
            (dn, w_ref.at[idx, rows(1)]),
            (t1, w_ref.at[idx, rows(2), pl.ds(0, half)]),
            (t2, w_ref.at[idx, rows(2), pl.ds(half, half)]),
        ]
    copies = [pltpu.make_async_copy(s, d, sems.at[i]) for i, (s, d) in enumerate(pairs)]
    for c in copies:
        c.start()
    for c in copies:
        c.wait()
    first_half, low_head = lane_masks(ROWS)
    steps = x_ref.shape[0] // ROWS

    def body(i, _):
        r = pl.ds(pl.multiple_of(i * ROWS, ROWS), ROWS)
        x = x_ref[r, :].astype(F32)
        factor = lax.rsqrt(jnp.mean(x * x, axis=-1, keepdims=True) + NORM_EPS)
        a = (x * factor * gain_ref[...]).astype(BF16)
        attn_ref[r, :] = a
        qk = dot(a, w_ref[0])
        vv = dot(a, w_ref[1, :, 896:1280])
        cos, sin = cos_ref[r, :], sin_ref[r, :]
        slabs = [
            rope_slab(qk[:, 128 * j : 128 * j + 128], cos, sin, first_half) for j in range(10)
        ]
        for j in range(7):
            q_ref[r, 128 * j : 128 * j + 128] = slabs[j].astype(BF16)
        q_ref[r, 896:960] = slabs[7][:, :64].astype(BF16)
        mixed = jnp.where(low_head, pltpu.roll(slabs[7], 64, 1), vv[:, 0:128])
        for j, part in enumerate((slabs[8], slabs[9], mixed, vv[:, 128:256], vv[:, 256:384])):
            kv_ref[r, 128 * j : 128 * j + 128] = part.astype(BF16)
        return 0

    lax.fori_loop(0, steps, body, 0)


def pre_call(info, x, gain, cos, sin, pieces):
    t = x.shape[0]
    return pl.pallas_call(
        pre_kernel,
        out_shape=(
            jax.ShapeDtypeStruct((t, D), BF16),
            jax.ShapeDtypeStruct((t, D), BF16),
            jax.ShapeDtypeStruct((t, 2 * KVW), BF16),
            jax.ShapeDtypeStruct((2, D, 1280), BF16),
        ),
        in_specs=[SMEM] + [VMEM] * 4 + [ANY] * 10,
        out_specs=(VMEM,) * 4,
        scratch_shapes=[pltpu.SemaphoreType.DMA((10,))],
        compiler_params=params(40),
        cost_estimate=cost(2 * t * D * 1600, 15e6),
        name="pre",
    )(info, x, gain, cos, sin, *pieces)


PAIRS = ((0, 3, (0, 1)), (1, 4, (2, 3)), (2, 2, (4,)))


def start_window(tab, kvs, win, sem, blk, slot):
    def body(j, _):
        entry = tab[blk, j]
        which = entry // 1024
        idx = lax.rem(entry, 1024)
        dst = win.at[slot, pl.ds(pl.multiple_of(j * BLK, BLK), BLK)]
        for n, ref in enumerate(kvs):
            @pl.when(which == n)
            def _():
                src = ref.at[pl.ds(pl.multiple_of(idx * BLK, BLK), BLK)]
                pltpu.make_async_copy(src, dst, sem.at[slot]).start()
        return 0

    lax.fori_loop(0, NWB, body, 0)


def next_window(tab, kvs, win, sem):
    i = pl.program_id(0)
    slot = lax.rem(i, 2)

    @pl.when(i == 0)
    def _():
        start_window(tab, kvs, win, sem, i, slot)

    @pl.when(i + 1 < pl.num_programs(0))
    def _():
        start_window(tab, kvs, win, sem, i + 1, 1 - slot)

    pltpu.make_async_copy(win.at[slot], win.at[slot], sem.at[slot]).wait()
    return slot


def turned_heads(flat):
    rows = flat.astype(F32)
    padded = jnp.concatenate([rows, jnp.zeros((BLK, 64), F32)], axis=1)
    return padded.T


def spread_heads(turned, heads, low):
    width = GRP * BLK
    sides = []
    for g in heads:
        sides.append(
            jnp.concatenate(
                [turned[HD * h : HD * h + HD] for h in range(GRP * g, GRP * g + GRP)], axis=1
            )
        )
    empty = jnp.zeros((HD, width), turned.dtype)
    if len(heads) == 2:
        return jnp.concatenate(
            [jnp.concatenate([sides[0], empty], axis=1), jnp.concatenate([empty, sides[1]], axis=1)],
            axis=0,
        )
    return jnp.concatenate([sides[0], empty] if low else [empty, sides[0]], axis=0)


def fwd_kernel(n_kv, tab, lo_ref, q_ref, *refs):
    kvs = refs[:n_kv]
    mid_ref, rl_ref, p_ref, win, bias, scores, sem = refs[n_kv:]
    slot = next_window(tab, kvs, win, sem)
    row = lax.broadcasted_iota(jnp.int32, (SPAN, BLK), 0)
    lane = lax.broadcasted_iota(jnp.int32, (SPAN, BLK), 1)
    allowed = (row >= lo_ref[0]) & (row <= lane + WIN)
    bias[...] = jnp.where(allowed, 0.0, MASK_FILL)
    turned = (turned_heads(q_ref[...]) * (HD ** -0.5)).astype(BF16)
    outs, recips = [], []
    for k_slab, v_slab, heads in PAIRS:
        keys = win[slot, :, 128 * k_slab : 128 * k_slab + 128]
        vals = win[slot, :, 128 * v_slab : 128 * v_slab + 128]
        count = GRP * len(heads)
        width = BLK * count
        base = BLK * GRP * heads[0]
        scores[:, :width] = dot(keys, spread_heads(turned, heads, True))
        for j in range(count):
            s = scores[:, BLK * j : BLK * j + BLK] + bias[...]
            top = jnp.max(s, axis=0, keepdims=True)
            p_ref[0, :, base + BLK * j : base + BLK * j + BLK] = jnp.exp(s - top).astype(BF16)
        lhs = jnp.concatenate([vals.T, jnp.ones((16, SPAN), BF16)], axis=0)
        product = dot(lhs, p_ref[0, :, base : base + width])
        recip = 1.0 / product[128:129, :]
        for j in range(count):
            upper = (heads[0] == 4) or j >= GRP
            cols = slice(BLK * j, BLK * j + BLK)
            part = product[64:128, cols] if upper else product[0:64, cols]
            outs.append(part * recip[:, cols])
            recips.append(recip[:, cols])
    outs.append(jnp.zeros((64, BLK), F32))
    recips.append(jnp.zeros((1, BLK), F32))
    mid_ref[...] = jnp.concatenate(outs, axis=0).T[:, :D].astype(BF16)
    rl_ref[0] = jnp.concatenate(recips, axis=0)


def fwd_call(tab, lo, q, kvs):
    blocks = q.shape[0] // BLK
    n_kv = len(kvs)
    return pl.pallas_call(
        lambda *refs: fwd_kernel(n_kv, *refs),
        grid=(blocks,),
        out_shape=(
            jax.ShapeDtypeStruct((q.shape[0], D), BF16),
            jax.ShapeDtypeStruct((blocks, 16, BLK), F32),
            jax.ShapeDtypeStruct((blocks, SPAN, HQ * BLK), BF16),
        ),
        in_specs=[
            SMEM,
            pl.BlockSpec((1, 1, BLK), lambda i: (i, 0, 0)),
            pl.BlockSpec((BLK, D), lambda i: (i, 0)),
        ]
        + [ANY] * n_kv,
        out_specs=(
            pl.BlockSpec((BLK, D), lambda i: (i, 0)),
            pl.BlockSpec((1, 16, BLK), lambda i: (i, 0, 0)),
            pl.BlockSpec((1, SPAN, HQ * BLK), lambda i: (i, 0, 0)),
        ),
        scratch_shapes=[
            pltpu.VMEM((2, SPAN, 2 * KVW), BF16),
            pltpu.VMEM((SPAN, BLK), F32),
            pltpu.VMEM((SPAN, 2 * GRP * BLK), F32),
            pltpu.SemaphoreType.DMA((2,)),
        ],
        compiler_params=params(48, 1),
        cost_estimate=cost(8e9 * blocks, 8e6 * blocks, 2.2e6 * blocks),
        name="attend",
    )(tab, lo, q, *kvs)


def bwd_kernel(n_kv, n_out, n_slots, tab, slots, q_ref, do_ref, mid_ref, rl_ref, p_ref, cos_ref, sin_ref, *refs):
    kvs = refs[:n_kv]
    dq_ref = refs[n_kv]
    outs = refs[n_kv + 1 : n_kv + 1 + n_out]
    win, acc, scores, stage, sem, out_sem = refs[n_kv + 1 + n_out :]
    i = pl.program_id(0)
    slot = next_window(tab, kvs, win, sem)

    @pl.when(i == 0)
    def _():
        def clear(b, _):
            acc[pl.ds(pl.multiple_of(b * BLK, BLK), BLK), :] = jnp.zeros((BLK, 2 * KVW), F32)
            return 0

        lax.fori_loop(0, n_slots, clear, 0)

    def add(lanes, value):
        for j in range(NWB):
            r = pl.ds(pl.multiple_of(slots[i, j] * BLK, BLK), BLK)
            acc[r, lanes : lanes + 128] += value[BLK * j : BLK * j + BLK]

    turned_q = (turned_heads(q_ref[...]) * (HD ** -0.5)).astype(BF16)
    turned_do = turned_heads(do_ref[...])
    turned_o = turned_heads(mid_ref[...])
    scaled, dots = [], []
    for h in range(HQ):
        r = rl_ref[0, h : h + 1, :]
        do_h = turned_do[HD * h : HD * h + HD] * r
        scaled.append(do_h)
        dots.append(jnp.sum(do_h * turned_o[HD * h : HD * h + HD], axis=0, keepdims=True))
    scaled = jnp.concatenate(scaled, axis=0).astype(BF16)
    cos, sin = cos_ref[0], sin_ref[0]
    grads = []
    for k_slab, v_slab, heads in PAIRS:
        keys = win[slot, :, 128 * k_slab : 128 * k_slab + 128]
        vals = win[slot, :, 128 * v_slab : 128 * v_slab + 128]
        count = GRP * len(heads)
        width = BLK * count
        base = BLK * GRP * heads[0]
        q_rows = spread_heads(turned_q, heads, True)
        do_rows = spread_heads(scaled, heads, False)
        scores[:, :width] = dot(vals, do_rows)
        ds = []
        for j in range(count):
            p = p_ref[0, :, base + BLK * j : base + BLK * j + BLK].astype(F32)
            head = GRP * heads[0] + j
            ds.append((p * (scores[:, BLK * j : BLK * j + BLK] - dots[head])).astype(BF16))
        ds = jnp.concatenate(ds, axis=1)
        probs = p_ref[0, :, base : base + width]
        if len(heads) == 2:
            add(128 * k_slab, dot_nt(ds, q_rows))
            add(128 * v_slab, dot_nt(probs, do_rows))
        else:
            add(
                128 * k_slab,
                dot_nt(
                    jnp.concatenate([ds, probs], axis=1),
                    jnp.concatenate([q_rows, do_rows], axis=1),
                ),
            )
        dq = dot(keys.T, ds) * (HD ** -0.5)
        for j in range(count):
            top = HD if j >= GRP else 0
            cols = slice(BLK * j, BLK * j + BLK)
            first = dq[top : top + 32, cols]
            second = dq[top + 32 : top + 64, cols]
            grads.append(first * cos + second * sin)
            grads.append(second * cos - first * sin)
    grads.append(jnp.zeros((64, BLK), F32))
    dq_ref[...] = jnp.concatenate(grads, axis=0).T[:, :D].astype(BF16)

    @pl.when(i == pl.num_programs(0) - 1)
    def _():
        per = 6 * BLK
        total = n_slots // 6
        each = total // n_out
        copies = []
        for t in range(total):
            s = t % 2
            if t >= 2:
                copies[t - 2].wait()
            stage[s] = acc[per * t : per * t + per, :].astype(BF16)
            out = outs[t // each]
            c = pltpu.make_async_copy(
                stage.at[s], out.at[pl.ds(per * (t % each), per)], out_sem.at[s]
            )
            c.start()
            copies.append(c)
        copies[-2].wait()
        copies[-1].wait()


def bwd_call(tab, slots, n_slots, n_out, q, do, mid, rl, p, cos, sin, kvs):
    blocks = q.shape[0] // BLK
    n_kv = len(kvs)
    flat = pl.BlockSpec((BLK, D), lambda i: (i, 0))
    table = pl.BlockSpec((1, 32, BLK), lambda i: (i, 0, 0))
    return pl.pallas_call(
        lambda *refs: bwd_kernel(n_kv, n_out, n_slots, *refs),
        grid=(blocks,),
        out_shape=(jax.ShapeDtypeStruct((q.shape[0], D), BF16),)
        + (jax.ShapeDtypeStruct((n_slots // n_out * BLK, 2 * KVW), BF16),) * n_out,
        in_specs=[
            SMEM,
            SMEM,
            flat,
            flat,
            flat,
            pl.BlockSpec((1, 16, BLK), lambda i: (i, 0, 0)),
            pl.BlockSpec((1, SPAN, HQ * BLK), lambda i: (i, 0, 0)),
            table,
            table,
        ]
        + [ANY] * n_kv,
        out_specs=(flat,) + (ANY,) * n_out,
        scratch_shapes=[
            pltpu.VMEM((2, SPAN, 2 * KVW), BF16),
            pltpu.VMEM((n_slots * BLK, 2 * KVW), F32),
            pltpu.VMEM((SPAN, 2 * GRP * BLK), F32),
            pltpu.VMEM((2, 6 * BLK, 2 * KVW), BF16),
            pltpu.SemaphoreType.DMA((2,)),
            pltpu.SemaphoreType.DMA((2,)),
        ],
        compiler_params=params(58, 1),
        cost_estimate=cost(14e9 * blocks, 8e6 * blocks),
        name="attend_back",
    )(tab, slots, q, do, mid, rl, p, cos, sin, *kvs)


def mid_kernel(
    info, mid_ref, x_ref, cot_ref, gain_ref, w_ref, *refs,
):
    pieces = refs[:10]
    out_ref, gh_ref, gm_ref, go_ref, keep_ref, send_ref = refs[10:16]
    w_out, wbuf, h1, low, acc_o, acc_g, stage, w_sem, out_sem = refs[16:]
    z = info[0]
    units = wbuf.shape[1]
    half = units // 2
    copies = [pltpu.make_async_copy(w_ref.at[1, :, pl.ds(0, 1024)], w_out, w_sem.at[10])]
    at = 0
    for n, piece in enumerate(pieces):
        size = piece.shape[1]
        copies.append(
            pltpu.make_async_copy(piece, wbuf.at[:, pl.ds(at, size), :], w_sem.at[n])
        )
        at += size
    for c in copies:
        c.start()
    copies[0].wait()
    steps = x_ref.shape[0] // ROWS
    gain = gain_ref[...]

    def first(i, _):
        r = pl.ds(pl.multiple_of(i * ROWS, ROWS), ROWS)
        h = x_ref[r, :].astype(F32) + dot(mid_ref[r, :], w_out[:, :D])
        factor = lax.rsqrt(jnp.mean(h * h, axis=-1, keepdims=True) + NORM_EPS)
        h1[r, :] = h
        low[r, :] = (h * factor * gain).astype(BF16)
        acc_o[r, :] = h
        acc_g[r, :] = jnp.zeros((ROWS, D), F32)
        return 0

    lax.fori_loop(0, steps, first, 0)
    for c in copies[1:]:
        c.wait()
    n_chunks = units // UNITS
    half_chunks = n_chunks // 2

    def out_copy(c, slot, ref, start):
        rows = pl.ds(pl.multiple_of((c - start) * UNITS, UNITS), UNITS)
        return pltpu.make_async_copy(stage.at[slot], ref.at[:, rows, :], out_sem.at[slot])

    def chunk(c, _):
        u = pl.ds(pl.multiple_of(c * UNITS, UNITS), UNITS)
        slot = lax.rem(c, 2)
        a = low[...]
        gate = dot_nt(a, wbuf[0, u, :])
        up = dot_nt(a, wbuf[1, u, :])
        grad = dot_nt(cot_ref[...], wbuf[2, u, :])
        sig = lax.logistic(gate)
        swish = gate * sig
        hid = (swish * up).astype(BF16)
        g_gate = (grad * up * sig * (1.0 + gate * (1.0 - sig))).astype(BF16)
        g_up = (grad * swish).astype(BF16)
        acc_o[...] += dot(hid, wbuf[2, u, :])
        acc_g[...] += dot(g_gate, wbuf[0, u, :]) + dot(g_up, wbuf[1, u, :])

        @pl.when(c >= 2)
        def _():
            out_copy(0, slot, keep_ref, 0).wait()

        stage[slot, 0] = dot_tn(g_gate, a).astype(BF16)
        stage[slot, 1] = dot_tn(g_up, a).astype(BF16)
        stage[slot, 2] = dot_tn(hid, cot_ref[...]).astype(BF16)

        @pl.when(c < half_chunks)
        def _():
            out_copy(c, slot, keep_ref, 0).start()

        @pl.when(c >= half_chunks)
        def _():
            out_copy(c, slot, send_ref, half_chunks).start()

        return 0

    lax.fori_loop(0, n_chunks, chunk, 0)
    out_copy(0, 0, keep_ref, 0).wait()
    out_copy(0, 1, keep_ref, 0).wait()

    def last(i, total):
        r = pl.ds(pl.multiple_of(i * ROWS, ROWS), ROWS)
        h = h1[r, :]
        factor = lax.rsqrt(jnp.mean(h * h, axis=-1, keepdims=True) + NORM_EPS)
        normed = h * factor
        g = acc_g[r, :]
        out_ref[r, :] = acc_o[r, :].astype(BF16)
        scaled = g * gain
        back = factor * (scaled - normed * jnp.mean(scaled * normed, axis=-1, keepdims=True))
        full = cot_ref[r, :].astype(F32) + back
        gh_ref[r, :] = full
        res = full.astype(BF16)
        low[r, :] = res
        gm_ref[r, :] = dot_nt(res, w_out[:, :D]).astype(BF16)
        return total + jnp.sum(g * normed, axis=0, keepdims=True)

    gain_grad = lax.fori_loop(0, steps, last, jnp.zeros((1, D), F32))
    product = dot_tn(mid_ref[...], low[...])
    put_shards(z, go_ref, product, gain_grad, 0)


def put_shards(z, ref, product, gain_grad, lead):
    width = product.shape[1]
    first_row = lax.broadcasted_iota(jnp.int32, (ZP - ZR, width), 0) == 0
    for n in range(4):
        s = lax.rem(z - n + 4, 4)
        ref[s, 0:ZR, :] = product[ZR * n : ZR * n + ZR].astype(BF16)
        if gain_grad is None:
            ref[s, ZR:ZP, :] = jnp.zeros((ZP - ZR, width), BF16)
        else:
            part = jnp.concatenate(
                [gain_grad[:, ZR * n : ZR * n + ZR], jnp.zeros((1, width - ZR), F32)], axis=1
            )
            ref[s, ZR:ZP, :] = jnp.where(first_row, part, 0.0).astype(BF16)


def mid_call(info, mid, x, cot, gain, w, pieces):
    t = x.shape[0]
    units = sum(p.shape[1] for p in pieces)
    wide = jax.ShapeDtypeStruct((t, D), BF16)
    half = jax.ShapeDtypeStruct((3, units // 2, D), BF16)
    return pl.pallas_call(
        mid_kernel,
        out_shape=(
            wide,
            jax.ShapeDtypeStruct((t, D), F32),
            wide,
            jax.ShapeDtypeStruct((4, ZP, D), BF16),
            half,
            half,
        ),
        in_specs=[SMEM] + [VMEM] * 4 + [ANY] * 11,
        out_specs=(VMEM,) * 4 + (ANY,) * 2,
        scratch_shapes=[
            pltpu.VMEM((D, 1024), BF16),
            pltpu.VMEM((3, units, D), BF16),
            pltpu.VMEM((t, D), F32),
            pltpu.VMEM((t, D), BF16),
            pltpu.VMEM((t, D), F32),
            pltpu.VMEM((t, D), F32),
            pltpu.VMEM((2, 3, UNITS, D), BF16),
            pltpu.SemaphoreType.DMA((11,)),
            pltpu.SemaphoreType.DMA((2,)),
        ],
        compiler_params=params(60),
        cost_estimate=cost(2 * t * D * (9 * units + 3 * D), 45e6),
        name="feed_forward",
    )(info, mid, x, cot, gain, w, *pieces)


def post_q_kernel(info, a_ref, qg_ref, w_ref, gq_ref, part_ref):
    put_shards(info[0], gq_ref, dot_tn(a_ref[...], qg_ref[...]), None, 0)
    part_ref[...] = dot_nt(qg_ref[...], w_ref[0, :, :D])


def post_q_call(info, a, qg, w):
    t = a.shape[0]
    return pl.pallas_call(
        post_q_kernel,
        out_shape=(
            jax.ShapeDtypeStruct((4, ZP, D), BF16),
            jax.ShapeDtypeStruct((t, D), F32),
        ),
        in_specs=[SMEM] + [VMEM] * 3,
        out_specs=(VMEM,) * 2,
        compiler_params=params(40),
        cost_estimate=cost(4 * t * D * D, 14e6),
        name="query_back",
    )(info, a, qg, w)


def post_kv_kernel(
    info, s0, s1, s2, cos_ref, sin_ref, a_ref, part_ref, w_ref, x_ref, gh_ref, gain_ref,
    keep_ref, send_ref, ig_ref, kg, vg,
):
    z, core = info[0], info[1]
    first_half, low_head = lane_masks(ROWS)
    steps = x_ref.shape[0] // ROWS
    gain = gain_ref[...]

    def body(i, total):
        r = pl.ds(pl.multiple_of(i * ROWS, ROWS), ROWS)

        def slab(j):
            c = slice(128 * j, 128 * j + 128)
            return s0[r, c].astype(F32) + s1[r, c].astype(F32) + s2[r, c].astype(F32)

        cos, sin = cos_ref[r, :], -sin_ref[r, :]
        mixed = slab(2)
        k4 = jnp.where(low_head, 0.0, rope_slab(pltpu.roll(mixed, 64, 1), cos, sin, first_half))
        k_low = jnp.concatenate(
            [k4, rope_slab(slab(0), cos, sin, first_half), rope_slab(slab(1), cos, sin, first_half)],
            axis=1,
        ).astype(BF16)
        v_low = jnp.concatenate(
            [jnp.where(low_head, 0.0, mixed), slab(3), slab(4)], axis=1
        ).astype(BF16)
        kg[r, :] = k_low
        vg[r, :] = v_low
        g = (
            part_ref[r, :]
            + dot_nt(k_low, w_ref[0, :, 896:1280])
            + dot_nt(v_low, w_ref[1, :, 896:1280])
        )
        x = x_ref[r, :].astype(F32)
        factor = lax.rsqrt(jnp.mean(x * x, axis=-1, keepdims=True) + NORM_EPS)
        normed = x * factor
        scaled = g * gain
        back = factor * (scaled - normed * jnp.mean(scaled * normed, axis=-1, keepdims=True))
        ig_ref[r, :] = (gh_ref[r, :] + back).astype(BF16)
        return total + jnp.sum(g * normed, axis=0, keepdims=True)

    gain_grad = lax.fori_loop(0, steps, body, jnp.zeros((1, D), F32))
    mine = core == 0
    k_side = dot_tn(a_ref[...], kg[...])
    v_side = dot_tn(a_ref[...], vg[...])
    put_shards(z, keep_ref, jnp.where(mine, k_side, v_side), jnp.where(mine, gain_grad, 0.0), 0)
    put_shards(z, send_ref, jnp.where(mine, v_side, k_side), jnp.where(mine, 0.0, gain_grad), 0)


def post_kv_call(info, sums, cos, sin, a, part, w, x, gh, gain):
    t = x.shape[0]
    piece = jax.ShapeDtypeStruct((4, ZP, 384), BF16)
    return pl.pallas_call(
        post_kv_kernel,
        out_shape=(piece, piece, jax.ShapeDtypeStruct((t, D), BF16)),
        in_specs=[SMEM] + [VMEM] * 11,
        out_specs=(VMEM,) * 3,
        scratch_shapes=[pltpu.VMEM((t, 384), BF16), pltpu.VMEM((t, 384), BF16)],
        compiler_params=params(50),
        cost_estimate=cost(8 * t * D * 384, 25e6),
        name="key_value_back",
    )(info, *sums, cos, sin, a, part, w, x, gh, gain)


def z_shift(x, step):
    n = 4
    return lax.ppermute(x, "fsdp", [(i, (i + step) % n) for i in range(n)])


def c_swap(x, bit):
    n = lax.axis_size("ctx")
    return lax.ppermute(x, "ctx", [(i, i ^ bit) for i in range(n)])


def z_gather(mine, axis):
    up, dn = z_shift(mine, 1), z_shift(mine, -1)
    cut = mine.shape[axis] // 2
    t1 = z_shift(lax.slice_in_dim(up, 0, cut, axis=axis), 1)
    t2 = z_shift(lax.slice_in_dim(dn, cut, 2 * cut, axis=axis), -1)
    return up, dn, t1, t2


def z_reduce(s0, s1, s2, s3):
    axis = s0.ndim - 2
    cut = s0.shape[axis] // 2
    r1 = z_shift(lax.slice_in_dim(s2, 0, cut, axis=axis), -1)
    r3 = z_shift(lax.slice_in_dim(s2, cut, 2 * cut, axis=axis), 1)

    def join(left, right):
        return jnp.concatenate([left, right], axis=axis)

    lo1, hi1 = lax.slice_in_dim(s1, 0, cut, axis=axis), lax.slice_in_dim(s1, cut, 2 * cut, axis=axis)
    lo3, hi3 = lax.slice_in_dim(s3, 0, cut, axis=axis), lax.slice_in_dim(s3, cut, 2 * cut, axis=axis)
    f1 = z_shift(join(lo1 + r1, hi1), -1)
    f3 = z_shift(join(lo3, hi3 + r3), 1)
    return s0 + f1 + f3


def chips_sum(x):
    n = lax.axis_size("ctx")
    bits = []
    b = 2
    while b < n:
        bits.append(b)
        b *= 2
    axis = x.ndim - 2
    cut = x.shape[axis] // 2
    left = lax.slice_in_dim(x, 0, cut, axis=axis)
    right = lax.slice_in_dim(x, cut, 2 * cut, axis=axis)
    for b in bits:
        left = left + c_swap(left, b)
    for b in reversed(bits):
        right = right + c_swap(right, b)
    return jnp.concatenate([left, right], axis=axis)


def gather_kv(kv):
    n = lax.axis_size("ctx")
    if n != 8:
        return [lax.all_gather(kv, "ctx", axis=0, tiled=True)]
    cut = kv.shape[0] // 2
    across_x, across_y = c_swap(kv, 2), c_swap(kv, 4)
    far_lo = c_swap(across_x[:cut], 4)
    far_hi = c_swap(across_y[cut:], 2)
    chip = [kv, across_x, across_y, far_lo, far_hi]
    return chip + [c_swap(part, 1) for part in chip]


def kv_entry(position, per_dev, me, n):
    if n != 8:
        return position
    owner, within = position // per_dev, position % per_dev
    rel = owner ^ me
    cut = per_dev // 2
    far = (rel // 2) == 3
    late = far & (within >= cut)
    which = (rel % 2) * 5 + rel // 2 + late.astype(jnp.int32)
    return which * 1024 + jnp.where(late, within - cut, within)


def kv_slot(position, per_dev, me):
    owner, within = position // per_dev, position % per_dev
    rel = owner ^ me
    return ((rel % 2) * 4 + rel // 2) * per_dev + within


def return_kv(keep, send):
    rows = keep.shape[0] // 4
    cut = rows // 2
    total = keep + c_swap(send, 1)
    own, to_x, to_y, far = (total[rows * j : rows * j + rows] for j in range(4))
    from_x = c_swap(far[:cut], 2)
    from_y = c_swap(far[cut:], 4)
    to_y = jnp.concatenate([to_y[:cut] + from_x, to_y[cut:]], axis=0)
    to_x = jnp.concatenate([to_x[:cut], to_x[cut:] + from_y], axis=0)
    return own, c_swap(to_x, 2), c_swap(to_y, 4)


def on_device(
    tokens,
    cotangent,
    doc_lengths,
    deal,
    attn_gain,
    w_query,
    w_key,
    w_value,
    w_out,
    mlp_gain,
    w_gate,
    w_up,
    w_down,
):
    me = lax.axis_index("ctx")
    n_ctx = lax.axis_size("ctx")
    z = lax.axis_index("fsdp")
    core = me % 2
    even = core == 0
    info = jnp.stack([z, core]).astype(jnp.int32)
    tok_rows = tokens.shape[1]
    per_dev = tok_rows // BLK
    deal_row = deal[0]
    blocks = deal_row.shape[0]
    group_size = blocks * BLK
    doc_lens = doc_lengths[0]
    seq_count = doc_lens.shape[0]
    length = group_size // seq_count
    x = tokens[0]
    cot = cotangent[0]

    k_last, k_rest = w_key[:, 256:], w_key[:, :256]
    v_last, v_rest = w_value[:, 256:], w_value[:, :256]
    side_a = jnp.concatenate([w_query, k_last, k_rest], axis=1)
    side_b = jnp.concatenate([w_out, v_last, v_rest], axis=1)
    mine_ab = jnp.where(even, side_a, side_b)
    got = z_gather(mine_ab, 1)
    swapped = [c_swap(p, 1) for p in got]
    pieces_ab = [side_a, side_b, *got, *swapped]

    gains = jnp.stack([attn_gain, mlp_gain])
    rel_gains = jnp.stack([gains, z_shift(gains, 1), z_shift(gains, 2), z_shift(gains, 3)])
    rel_of = (z - jnp.arange(4, dtype=jnp.int32)) % 4
    pick = rel_of[:, None] == jnp.arange(4, dtype=jnp.int32)[None, :]
    full_gains = jnp.sum(
        jnp.where(pick[:, :, None, None], rel_gains[None].astype(F32), 0.0), axis=1
    )
    gain_one = full_gains[:, 0].reshape(1, D)
    gain_two = full_gains[:, 1].reshape(1, D)

    block_ids = jnp.arange(blocks, dtype=jnp.int32)
    mine = lax.dynamic_slice_in_dim(deal_row, me * per_dev, per_dev)
    seq_blocks = jnp.maximum(
        mine[:, None] - (NWB - 1) + jnp.arange(NWB, dtype=jnp.int32)[None, :], 0
    )
    position = jnp.sum(
        jnp.where(seq_blocks[:, :, None] == deal_row[None, None, :], block_ids, 0), axis=-1
    )
    tab = kv_entry(position, per_dev, me, n_ctx).astype(jnp.int32)
    doc_ends = (
        jnp.cumsum(doc_lens, axis=1) + (jnp.arange(seq_count, dtype=jnp.int32) * length)[:, None]
    ).reshape(-1)
    doc_starts = doc_ends - doc_lens.reshape(-1)
    q_time = mine[:, None] * BLK + jnp.arange(BLK, dtype=jnp.int32)[None, :]
    begin = jnp.max(jnp.where(q_time[..., None] >= doc_starts, doc_starts, 0), axis=-1)
    lo = jnp.maximum(begin, q_time - (WIN - 1)) - (mine[:, None] * BLK - WIN)
    lo = lo[:, None, :].astype(jnp.int32)
    pos = (q_time - begin).reshape(-1)
    half_dim = HD // 2
    freqs = ROPE_THETA ** (-jnp.arange(half_dim, dtype=F32) * (2.0 / HD))
    angle = pos.astype(F32)[:, None] * freqs[None, :]
    cos_tab, sin_tab = jnp.cos(angle), jnp.sin(angle)
    cos_wide = jnp.tile(cos_tab, (1, 4))
    sin_wide = jnp.tile(jnp.concatenate([-sin_tab, sin_tab], axis=1), (1, 2))
    cos_turn = cos_tab.reshape(per_dev, BLK, half_dim).transpose(0, 2, 1)
    sin_turn = sin_tab.reshape(per_dev, BLK, half_dim).transpose(0, 2, 1)

    attn_in, q_low, kv_low, w_ab = pre_call(info, x, gain_one, cos_wide, sin_wide, pieces_ab)

    stacked = jnp.stack([w_gate.T, w_up.T, w_down])
    unit_half = stacked.shape[1] // 2
    ffn_mine = jnp.where(even, stacked[:, :unit_half], stacked[:, unit_half:])
    ffn_other = jnp.where(even, stacked[:, unit_half:], stacked[:, :unit_half])
    up, dn, t1, t2 = z_gather(ffn_mine, 1)
    near = [up, t1, t2, dn]
    pieces_ffn = [ffn_mine, *near, ffn_other, *[c_swap(p, 1) for p in near]]

    kvs = gather_kv(kv_low)
    mid_low, recips, probs = fwd_call(tab, lo, q_low, kvs)
    output, grad_hidden, grad_mid, go, keep, send = mid_call(
        info, mid_low, x, cot, gain_two, w_ab, pieces_ffn
    )

    both = keep + c_swap(send, 1)
    parts = [both[:, unit_half * s : unit_half * s + unit_half] for s in range(4)]
    ffn_sum = chips_sum(z_reduce(*parts))

    if n_ctx == 8:
        slots = kv_slot(position, per_dev, me).astype(jnp.int32)
        q_grad, kv_keep, kv_send = bwd_call(
            tab, slots, blocks, 2, q_low, grad_mid, mid_low, recips, probs, cos_turn, sin_turn, kvs
        )
        sums = return_kv(kv_keep, kv_send)
    else:
        n_slots = per_dev * NWB
        flat_pos = position.reshape(-1)
        order = jnp.arange(n_slots, dtype=jnp.int32)
        slots = jnp.min(
            jnp.where(flat_pos[:, None] == flat_pos[None, :], order[None, :], n_slots), axis=1
        ).reshape(per_dev, NWB)
        q_grad, compact = bwd_call(
            tab, slots, n_slots, 1, q_low, grad_mid, mid_low, recips, probs, cos_turn, sin_turn, kvs
        )
        source = jnp.min(
            jnp.where(block_ids[:, None] == flat_pos[None, :], order[None, :], n_slots), axis=1
        )
        padded = jnp.concatenate(
            [compact.reshape(n_slots, BLK, 2 * KVW), jnp.zeros((1, BLK, 2 * KVW), BF16)], axis=0
        )
        spread = jnp.take(padded, source, axis=0).reshape(group_size, 2 * KVW)
        own = lax.psum_scatter(spread, "ctx", scatter_dimension=0, tiled=True)
        sums = (own, jnp.zeros_like(own), jnp.zeros_like(own))

    gq, part = post_q_call(info, attn_in, q_grad, w_ab)
    both_qo = jnp.where(even, gq, go) + c_swap(jnp.where(even, go, gq), 1)
    qo_sum = chips_sum(z_reduce(*(both_qo[s] for s in range(4))))

    kv_g_keep, kv_g_send, input_grad = post_kv_call(
        info, sums, cos_wide, sin_wide, attn_in, part, w_ab, x, grad_hidden, gain_one
    )
    both_kv = kv_g_keep + c_swap(kv_g_send, 1)
    kv_sum = chips_sum(z_reduce(*(both_kv[s] for s in range(4))))

    ffn_far = c_swap(ffn_sum, 1)
    ffn_full = jnp.where(
        even,
        jnp.concatenate([ffn_sum, ffn_far], axis=1),
        jnp.concatenate([ffn_far, ffn_sum], axis=1),
    ).astype(F32)
    qo_far = c_swap(qo_sum, 1)
    q_final = jnp.where(even, qo_sum, qo_far).astype(F32)
    o_final = jnp.where(even, qo_far, qo_sum).astype(F32)
    kv_far = c_swap(kv_sum, 1)
    k_final = jnp.where(even, kv_sum, kv_far).astype(F32)
    v_final = jnp.where(even, kv_far, kv_sum).astype(F32)

    def heads_back(arr):
        return jnp.concatenate([arr[:ZR, 128:384], arr[:ZR, 64:128]], axis=1)

    return (
        output[None],
        input_grad[None],
        k_final[ZR, :ZR],
        q_final[:ZR],
        heads_back(k_final),
        heads_back(v_final),
        o_final[:ZR],
        o_final[ZR, :ZR],
        ffn_full[0].T,
        ffn_full[1].T,
        ffn_full[2],
    )


def solution(mesh):
    in_specs = (
        P("fsdp", "ctx", None),
        P("fsdp", "ctx", None),
        P("fsdp", None, None),
        P("fsdp", None),
        P("fsdp"),
        P("fsdp", None),
        P("fsdp", None),
        P("fsdp", None),
        P("fsdp", None),
        P("fsdp"),
        P(None, "fsdp"),
        P(None, "fsdp"),
        P("fsdp", None),
    )
    out_specs = (
        P("fsdp", "ctx", None),
        P("fsdp", "ctx", None),
        P("fsdp"),
        P("fsdp", None),
        P("fsdp", None),
        P("fsdp", None),
        P("fsdp", None),
        P("fsdp"),
        P(None, "fsdp"),
        P(None, "fsdp"),
        P("fsdp", None),
    )
    return jax.shard_map(
        on_device, mesh=mesh, in_specs=in_specs, out_specs=out_specs, check_vma=False
    )
```

time: 1350 us -> 651 us (0.48)
  waiting for transfers between devices: 592 us -> 216 us
  matrix products: 233 us -> 0 us
  local copies, waits for them, and re-layouts: 270 us -> 95.6 us
  Pallas kernels: 0 us -> 156 us
  starting transfers between devices: 0.9 us -> 120 us
  blocking collectives: 83.9 us -> 0 us
  other arithmetic: 130 us -> 54.3 us
  between operations: 16.2 us -> 2.06 us
    unnamed x22 -> x0, waiting for transfers between devices: 250 us -> none
    dot_general x56 -> x0, matrix products: 233 us -> none  [the longest x10 42.3 us: head_scores(): jnp.einsum('efow,ejw->efoj', query_head_slice, key_head_slice, preferred_...]
    ppermute x0 -> x63, waiting for transfers between devices: none -> 216 us  [the longest x23 158 us: z_shift(): return lax.ppermute(x, 'fsdp', [(i, (i + step) % n) for i in range(n)])]
    all_gather x7 -> x0, waiting for transfers between devices: 159 us -> none  [the longest x1 82.2 us: on_device(): lax.all_gather(w_down, 'fsdp', axis=0, tiled=True)]
    pallas_call x0 -> x6, Pallas kernels: none -> 156 us  [the longest x1 59.8 us: mid_call(): pl.pallas_call(mid_kernel, out_shape=(wide, jax.ShapeDtypeStruct((t, D),...]
    reduce_scatter x4 -> x0, waiting for transfers between devices: 130 us -> none  [the longest x1 44.5 us: on_device(): lax.psum_scatter(spread(merge_keys(grad_k_heads)).astype(jnp.bfloat16), '...]
    ppermute x0 -> x63, starting transfers between devices: none -> 120 us  [the longest x23 82.2 us: z_shift(): return lax.ppermute(x, 'fsdp', [(i, (i + step) % n) for i in range(n)])]
    gather x76 -> x0, local copies, waits for them, and re-layouts: 85.7 us -> none
  transfers between devices with their start and end apart: 17 -> 63, of which waited for: 11 -> 20; matrix products, arithmetic and copies ran while one was open for 31% -> 16% of each run, Pallas kernels for 0% -> 15%
where the time goes in v1:
time: 651 us; the launch traced here: 645 us
  waiting for transfers between devices  216 us (33%)
  Pallas kernels  156 us (24%)
  starting transfers between devices  120 us (18%)
  local copies, waits for them, and re-layouts  95.6 us (15%)
  other arithmetic  54.3 us (8%)
    ppermute x23, waiting for transfers between devices, z_shift(): return lax.ppermute(x, 'fsdp', [(i, (i + step) % n) for i in range(n)])  158 us
    ppermute x23, starting transfers between devices, z_shift(): return lax.ppermute(x, 'fsdp', [(i, (i + step) % n) for i in range(n)])  82.2 us
    pallas_call x1, Pallas kernels, mid_call(): pl.pallas_call(mid_kernel, out_shape=(wide, jax.ShapeDtypeStruct((t, D),...  59.8 us
    ppermute x40, waiting for transfers between devices, c_swap(): return lax.ppermute(x, 'ctx', [(i, i ^ bit) for i in range(n)])  58.1 us
    unnamed x106, local copies, waits for them, and re-layouts  40 us
    pallas_call x1, Pallas kernels, bwd_call(): pl.pallas_call(lambda *refs: bwd_kernel(n_kv, n_out, n_slots, *refs), gri...  39.9 us
    ppermute x40, starting transfers between devices, c_swap(): return lax.ppermute(x, 'ctx', [(i, i ^ bit) for i in range(n)])  38.3 us
    pallas_call x1, Pallas kernels, fwd_call(): pl.pallas_call(lambda *refs: fwd_kernel(n_kv, *refs), grid=(blocks,), out...  32.8 us
  transfers between devices with their start and end apart: 63, of which 20 were waited for; matrix products, arithmetic and copies ran while one was open for 16% of the time, Pallas kernels for 15%

profile of v1, /device:TPU:0, one launch (start us, length us, event | category | flops | bytes accessed | tf_op | source)
XLA Modules:
  0.0 644.5 jit_solution(10477452156302533099)
XLA Ops:
  6.1 5.1 collective-permute-start.4
  11.9 4.4 collective-permute-start.1
  48.7 45.2 %collective-permute-done.5.m_t1 = bf16[240,640]{1,0:T(8,128)(2,1)} collective-permute-done((bf16[240,640]{1,0:T(8,128)(2,1)}, bf16[240,640]{1,0:T(8,128)(2,1)}, u32[]{:S(2)}, u32[]{:S(2)}) %collective-permute-start.5) | collective-permute-done | bytes 307232 | tf_op jit(solution)/shard_map/ppermute | solution.py:636
  99.7 7.9 %pre.1 = (bf16[768,960]{1,0:T(8,128)(2,1)S(1)}, bf16[768,960]{1,0:T(8,128)(2,1)S(1)}, bf16[768,640]{1,0:T(8,128)(2,1)}, bf16[2,960,1280]{2,1,0:T(8,128)(2,1)}) custom-call(s32[2]{0:T(128)S(1)} %pad_add_fusion.info, bf16[768,960]{1,0:T(8,128)(2,1)S(1)} %bitcast.95, f32[1,960]{1,0:T(1,128)S(1)} %reshape_squeeze.10.gain_ref, f32[768,128]{1,0:T(8,128)S(1)} %copy-done.5, ...), custom_call_target="tpu_custom_call" | custom-call | flops 2359296000 | bytes 15000000 | tf_op jit(solution)/shard_map/pre/pallas_call | solution.py:124
  111.8 21.1 %collective-permute-done.11.refs_4_.refs_10_ = bf16[768,640]{1,0:T(8,128)(2,1)S(1)} collective-permute-done((bf16[768,640]{1,0:T(8,128)(2,1)}, bf16[768,640]{1,0:T(8,128)(2,1)S(1)}, u32[]{:S(2)}, u32[]{:S(2)}) %collective-permute-start.11) | collective-permute-done | bytes 983072 | tf_op jit(solution)/shard_map/ppermute | solution.py:641
  150.4 13.2 %collective-permute-done.21.refs_2_ = bf16[3,160,960]{2,1,0:T(8,128)(2,1)} collective-permute-done((bf16[3,160,960]{2,1,0:T(8,128)(2,1)}, bf16[3,160,960]{2,1,0:T(8,128)(2,1)}, u32[]{:S(2)}, u32[]{:S(2)}) %collective-permute-start.21) | collective-permute-done | bytes 921632 | tf_op jit(solution)/shard_map/ppermute | solution.py:636
  169.4 14.7 %collective-permute-done.23.refs_3_ = bf16[3,160,960]{2,1,0:T(8,128)(2,1)} collective-permute-done((bf16[3,160,960]{2,1,0:T(8,128)(2,1)}, bf16[3,160,960]{2,1,0:T(8,128)(2,1)}, u32[]{:S(2)}, u32[]{:S(2)}) %collective-permute-start.23) | collective-permute-done | bytes 921632 | tf_op jit(solution)/shard_map/ppermute | solution.py:636
  185.1 32.8 %attend.1 = (bf16[768,960]{1,0:T(8,128)(2,1)}, f32[6,16,128]{2,1,0:T(8,128)S(1)}, bf16[6,1152,1920]{2,1,0:T(8,128)(2,1)}) custom-call(s32[6,9]{1,0:T(8,128)S(1)} %get-tuple-element.201.refs_0_, s32[6,1,128]{2,1,0:T(1,128)S(1)} %maximum_subtract_fusion.refs_1_, bf16[768,960]{1,0:T(8,128)(2,1)} %copy-done.15, ...), custom_call_target="tpu_custom_call" | custom-call | flops 48000000000 | bytes 48000000 | tf_op jit(solution)/shard_map/attend/pallas_call | solution.py:239
  219.9 59.8 %feed_forward.1 = (bf16[768,960]{1,0:T(8,128)(2,1)}, f32[768,960]{1,0:T(8,128)}, bf16[768,960]{1,0:T(8,128)(2,1)}, bf16[4,256,960]{2,1,0:T(8,128)(2,1)}, bf16[3,...) custom-call(s32[2]{0:T(128)} %copy-done.10, bf16[768,960]{1,0:T(8,128)(2,1)} %get-tuple-element.34.mid_ref.refs_4_, ...), custom_call_target="tpu_custom_call" | custom-call | flops 38220595200 | bytes 45000000 | tf_op jit(solution)/shard_map/feed_forward/pallas_call | solution.py:520
  279.7 10.3 %copy.260 = bf16[3,1280,960]{1,2,0:T(8,128)(2,1)} copy(bf16[3,1280,960]{2,1,0:T(8,128)(2,1)} %get-tuple-element.52) | data formatting | bytes 14745600 | tf_op jit(solution)/shard_map/feed_forward/pallas_call | solution.py:520
  291.2 39.9 %attend_back.1 = (bf16[768,960]{1,0:T(8,128)(2,1)}, bf16[3072,640]{1,0:T(8,128)(2,1)}, bf16[3072,640]{1,0:T(8,128)(2,1)}) custom-call(s32[6,9]{1,0:T(8,128)} %copy-done.9, s32[6,9]{1,0:T(8,128)} %get-tuple-element.200.refs_1_, bf16[768,960]{1,0:T(8,128)(2,1)} %copy-done.15, bf16[768,960]{1,0:T(8,128)(2,1)} %get-tuple-element.37.refs_3_, ...), custom_call_target="tpu_custom_call" | custom-call | flops 83999997952 | bytes 48000000 | tf_op jit(solution)/shard_map/attend_back/pallas_call | solution.py:367
  346.5 10.8 %copy.261 = bf16[3,1280,960]{2,1,0:T(8,128)(2,1)} copy(bf16[3,1280,960]{1,2,0:T(8,128)(2,1)} %collective-permute-done.53) | data formatting | bytes 14745600 | tf_op jit(solution)/shard_map/ppermute | solution.py:641
  357.3 13.1 %add.254 = bf16[3,1280,960]{2,1,0:T(8,128)(2,1)} add(bf16[3,1280,960]{2,1,0:T(8,128)(2,1)} %get-tuple-element.51, bf16[3,1280,960]{2,1,0:T(8,128)(2,1)} %copy.261) | non-fusion elementwise | flops 3686400 | bytes 22118400 | tf_op jit(solution)/shard_map/add | solution.py:822
  376.1 4.4 add.233
  381.5 15.8 %collective-permute-done.54 = bf16[3,160,960]{2,1,0:T(8,128)(2,1)S(1)} collective-permute-done((bf16[3,160,960]{2,1,0:T(8,128)(2,1)S(1)}, bf16[3,160,960]{2,1,0:T(8,128)(2,1)S(1)}, u32[]{:S(2)}, u32[]{:S(2)}) %collective-permute-start.54) | collective-permute-done | bytes 921632 | tf_op jit(solution)/shard_map/ppermute | solution.py:636
  412.4 13.9 %collective-permute-done.56 = bf16[3,160,960]{2,1,0:T(8,128)(2,1)} collective-permute-done((bf16[3,160,960]{2,1,0:T(8,128)(2,1)}, bf16[3,160,960]{2,1,0:T(8,128)(2,1)}, u32[]{:S(2)}, u32[]{:S(2)}) %collective-permute-start.56) | collective-permute-done | bytes 921632 | tf_op jit(solution)/shard_map/ppermute | solution.py:636
  428.2 36.6 %collective-permute-start.57 = (bf16[3,320,960]{2,1,0:T(8,128)(2,1)S(1)}, bf16[3,320,960]{2,1,0:T(8,128)(2,1)S(1)}, u32[]{:S(2)}, u32[]{:S(2)}) collective-permute-start(bf16[3,320,960]{2,1,0:T(8,128)(2,1)S(1)} %pad_maximum_fusion.2), channel_id=1, source_target_pairs={{0,1},{1,2},{2,3},{3,0},{4,5},{5,6},{6,7},{7,4},{8,9},{9,10},{10,1... | collective-permute-start | bytes 5529608 | tf_op jit(solution)/shard_map/ppermute | solution.py:636
  464.9 5.8 collective-permute-start.44
  475.8 38.6 %collective-permute-done.44 = bf16[128,960]{1,0:T(8,128)(2,1)S(1)} collective-permute-done((bf16[128,960]{1,0:T(8,128)(2,1)S(1)}, bf16[128,960]{1,0:T(8,128)(2,1)S(1)}, u32[]{:S(2)}, u32[]{:S(2)}) %collective-permute-start.44) | collective-permute-done | bytes 245792 | tf_op jit(solution)/shard_map/ppermute | solution.py:636
  517.0 5.7 collective-permute-done.46
  527.2 12.0 %key_value_back.1 = (bf16[4,256,384]{2,1,0:T(8,128)(2,1)S(1)}, bf16[4,256,384]{2,1,0:T(8,128)(2,1)S(1)}, bf16[768,960]{1,0:T(8,128)(2,1)}) custom-call(s32[2]{0:T(128)S(1)} %copy-done.11, bf16[768,640]{1,0:T(8,128)(2,1)S(1)} %slice.336.s0, bf16[768,640]{1,0:T(8,128)(2,1)} %copy-done.24, bf16[768,640]{1,0:T(8,128)(2,1)} %copy-done.23, ...), custom_call_target="tpu_custom_call" | custom-call | flops 2264924160 | bytes 25000000 | tf_op jit(solution)/shard_map/key_value_back/pallas_call | solution.py:622
  556.8 16.3 %collective-permute-done.48 = bf16[128,960]{1,0:T(8,128)(2,1)S(1)} collective-permute-done((bf16[128,960]{1,0:T(8,128)(2,1)S(1)}, bf16[128,960]{1,0:T(8,128)(2,1)S(1)}, u32[]{:S(2)}, u32[]{:S(2)}) %collective-permute-start.48) | collective-permute-done | bytes 245792 | tf_op jit(solution)/shard_map/ppermute | solution.py:641
  587.5 4.4 collective-permute-done.36
  595.0 10.4 %collective-permute-done.59 = bf16[3,160,960]{2,1,0:T(8,128)(2,1)S(1)} collective-permute-done((bf16[3,160,960]{2,1,0:T(8,128)(2,1)S(1)}, bf16[3,160,960]{2,1,0:T(8,128)(2,1)S(1)}, u32[]{:S(2)}, u32[]{:S(2)}) %collective-permute-start.59) | collective-permute-done | bytes 921632 | tf_op jit(solution)/shard_map/ppermute | solution.py:641
  (329 shorter events, 200.3 us)
Async XLA Ops:
  39.7 94.8 %collective-permute-start.20 = (bf16[3,320,960]{2,1,0:T(8,128)(2,1)}, bf16[3,320,960]{2,1,0:T(8,128)(2,1)}, u32[]{:S(2)}, u32[]{:S(2)}) collective-permute-start(bf16[3,320,960]{2,1,0:T(8,128)(2,1)} %get-tuple-element.168.refs_0_), channel_id=1, source_target_pairs={{0,1},{1,2},{2,3},{3,0},{4,5},{5,6},{6,7},{7,4},{8,9},{9,10},{10,1... | collective-permute-start | bytes 5529608 | tf_op jit(solution)/shard_map/ppermute | solution.py:636
  43.0 50.9 %collective-permute-start.5 = (bf16[240,640]{1,0:T(8,128)(2,1)}, bf16[240,640]{1,0:T(8,128)(2,1)}, u32[]{:S(2)}, u32[]{:S(2)}) collective-permute-start(bf16[240,640]{1,0:T(8,128)(2,1)} %slice.327), channel_id=1, source_target_pairs={{0,1},{1,2},{2,3},{3,0},{4,5},{5,6},{6,7},{7,4},{8,9},{9,10},{10,1... | collective-permute-start | bytes 921608 | tf_op jit(solution)/shard_map/ppermute | solution.py:636
  43.0 54.7 %collective-permute-start.7 = (bf16[240,1280]{1,0:T(8,128)(2,1)}, bf16[240,1280]{1,0:T(8,128)(2,1)}, u32[]{:S(2)}, u32[]{:S(2)}) collective-permute-start(bf16[240,1280]{1,0:T(8,128)(2,1)} %collective-permute-done.3.m_up), channel_id=1, source_target_pairs={{0,4},{4,0},{8,12},{12,8},{16,20},{20,16},{24,28},{28,24},{1,5},{5... | collective-permute-start | bytes 1843208 | tf_op jit(solution)/shard_map/ppermute | solution.py:641
  43.1 54.6 %collective-permute-start.8 = (bf16[240,1280]{1,0:T(8,128)(2,1)}, bf16[240,1280]{1,0:T(8,128)(2,1)}, u32[]{:S(2)}, u32[]{:S(2)}) collective-permute-start(bf16[240,1280]{1,0:T(8,128)(2,1)} %collective-permute-done.4.m_dn), channel_id=1, source_target_pairs={{0,4},{4,0},{8,12},{12,8},{16,20},{20,16},{24,28},{28,24},{1,5},{5... | collective-permute-start | bytes 1843208 | tf_op jit(solution)/shard_map/ppermute | solution.py:641
  46.5 47.4 %collective-permute-start.10 = (bf16[240,640]{1,0:T(8,128)(2,1)S(1)}, bf16[240,640]{1,0:T(8,128)(2,1)S(1)}, u32[]{:S(2)}, u32[]{:S(2)}) collective-permute-start(bf16[240,640]{1,0:T(8,128)(2,1)S(1)} %collective-permute-done.6.m_t2), channel_id=1, source_target_pairs={{0,4},{4,0},{8,12},{12,8},{16,20},{20,16},{24,28},{28,24},{1,5},{5... | collective-permute-start | bytes 921608 | tf_op jit(solution)/shard_map/ppermute | solution.py:641
  94.7 46.3 %collective-permute-start.22 = (bf16[3,320,960]{2,1,0:T(8,128)(2,1)}, bf16[3,320,960]{2,1,0:T(8,128)(2,1)}, u32[]{:S(2)}, u32[]{:S(2)}) collective-permute-start(bf16[3,320,960]{2,1,0:T(8,128)(2,1)} %get-tuple-element.168.refs_0_), channel_id=1, source_target_pairs={{0,3},{1,0},{2,1},{3,2},{4,7},{5,4},{6,5},{7,6},{8,11},{9,8},{10,9... | collective-permute-start | bytes 5529608 | tf_op jit(solution)/shard_map/ppermute | solution.py:636
  111.8 35.7 %collective-permute-start.15 = (bf16[768,640]{1,0:T(8,128)(2,1)}, bf16[768,640]{1,0:T(8,128)(2,1)}, u32[]{:S(2)}, u32[]{:S(2)}) collective-permute-start(bf16[768,640]{1,0:T(8,128)(2,1)} %get-tuple-element.33.refs_3_.refs_9_), channel_id=1, source_target_pairs={{0,4},{4,0},{8,12},{12,8},{16,20},{20,16},{24,28},{28,24},{1,5},{5... | collective-permute-start | bytes 2949128 | tf_op jit(solution)/shard_map/ppermute | solution.py:641
  143.1 40.9 %collective-permute-start.23 = (bf16[3,160,960]{2,1,0:T(8,128)(2,1)}, bf16[3,160,960]{2,1,0:T(8,128)(2,1)}, u32[]{:S(2)}, u32[]{:S(2)}) collective-permute-start(bf16[3,160,960]{2,1,0:T(8,128)(2,1)} %slice.335), channel_id=1, source_target_pairs={{0,3},{1,0},{2,1},{3,2},{4,7},{5,4},{6,5},{7,6},{8,11},{9,8},{10,9... | collective-permute-start | bytes 2764808 | tf_op jit(solution)/shard_map/ppermute | solution.py:636
  147.4 37.3 %collective-permute-start.16 = (bf16[768,640]{1,0:T(8,128)(2,1)S(1)}, bf16[768,640]{1,0:T(8,128)(2,1)}, u32[]{:S(2)}, u32[]{:S(2)}) collective-permute-start(bf16[768,640]{1,0:T(8,128)(2,1)S(1)} %collective-permute-done.11.refs_4_.refs_10_), channel_id=1, source_target_pairs={{0,4},{4,0},{8,12},{12,8},{16,20},{20,16},{24,28},{28,24},{1,5},{5... | collective-permute-start | bytes 2949128 | tf_op jit(solution)/shard_map/ppermute | solution.py:641
  147.5 37.7 %collective-permute-start.17 = (bf16[768,640]{1,0:T(8,128)(2,1)S(1)}, bf16[768,640]{1,0:T(8,128)(2,1)}, u32[]{:S(2)}, u32[]{:S(2)}) collective-permute-start(bf16[768,640]{1,0:T(8,128)(2,1)S(1)} %collective-permute-done.12.refs_5_.refs_11_), channel_id=1, source_target_pairs={{0,4},{4,0},{8,12},{12,8},{16,20},{20,16},{24,28},{28,24},{1,5},{5... | collective-permute-start | bytes 2949128 | tf_op jit(solution)/shard_map/ppermute | solution.py:641
  184.1 35.8 %collective-permute-start.24 = (bf16[3,320,960]{2,1,0:T(8,128)(2,1)}, bf16[3,320,960]{2,1,0:T(8,128)(2,1)}, u32[]{:S(2)}, u32[]{:S(2)}) collective-permute-start(bf16[3,320,960]{2,1,0:T(8,128)(2,1)} %collective-permute-done.20.refs_1_), channel_id=1, source_target_pairs={{0,4},{4,0},{8,12},{12,8},{16,20},{20,16},{24,28},{28,24},{1,5},{5... | collective-permute-start | bytes 5529608 | tf_op jit(solution)/shard_map/ppermute | solution.py:641
  184.1 35.8 %collective-permute-start.27 = (bf16[3,320,960]{2,1,0:T(8,128)(2,1)}, bf16[3,320,960]{2,1,0:T(8,128)(2,1)}, u32[]{:S(2)}, u32[]{:S(2)}) collective-permute-start(bf16[3,320,960]{2,1,0:T(8,128)(2,1)} %collective-permute-done.22.refs_4_), channel_id=1, source_target_pairs={{0,4},{4,0},{8,12},{12,8},{16,20},{20,16},{24,28},{28,24},{1,5},{5... | collective-permute-start | bytes 5529608 | tf_op jit(solution)/shard_map/ppermute | solution.py:641
  184.7 34.3 %collective-permute-start.26 = (bf16[3,160,960]{2,1,0:T(8,128)(2,1)}, bf16[3,160,960]{2,1,0:T(8,128)(2,1)S(1)}, u32[]{:S(2)}, u32[]{:S(2)}) collective-permute-start(bf16[3,160,960]{2,1,0:T(8,128)(2,1)} %collective-permute-done.23.refs_3_), channel_id=1, source_target_pairs={{0,4},{4,0},{8,12},{12,8},{16,20},{20,16},{24,28},{28,24},{1,5},{5... | collective-permute-start | bytes 2764808 | tf_op jit(solution)/shard_map/ppermute | solution.py:641
  290.0 56.5 %collective-permute-start.53 = (bf16[3,1280,960]{1,2,0:T(8,128)(2,1)}, bf16[3,1280,960]{1,2,0:T(8,128)(2,1)}, u32[]{:S(2)}, u32[]{:S(2)}) collective-permute-start(bf16[3,1280,960]{1,2,0:T(8,128)(2,1)} %copy.260), channel_id=1, source_target_pairs={{0,4},{4,0},{8,12},{12,8},{16,20},{20,16},{24,28},{28,24},{1,5},{5... | collective-permute-start | bytes 22118408 | tf_op jit(solution)/shard_map/ppermute | solution.py:641
  331.1 45.0 %collective-permute-start.28 = (bf16[3072,640]{1,0:T(8,128)(2,1)}, bf16[3072,640]{1,0:T(8,128)(2,1)}, u32[]{:S(2)}, u32[]{:S(2)}) collective-permute-start(bf16[3072,640]{1,0:T(8,128)(2,1)} %get-tuple-element.41), channel_id=1, source_target_pairs={{0,4},{4,0},{8,12},{12,8},{16,20},{20,16},{24,28},{28,24},{1,5},{5... | collective-permute-start | bytes 11796488 | tf_op jit(solution)/shard_map/ppermute | solution.py:641
  346.0 53.0 %collective-permute-start.43 = (bf16[4,256,960]{1,2,0:T(8,128)(2,1)}, bf16[4,256,960]{1,2,0:T(8,128)(2,1)}, u32[]{:S(2)}, u32[]{:S(2)}) collective-permute-start(bf16[4,256,960]{1,2,0:T(8,128)(2,1)} %copy.258), channel_id=1, source_target_pairs={{0,4},{4,0},{8,12},{12,8},{16,20},{20,16},{24,28},{28,24},{1,5},{5... | collective-permute-start | bytes 5898248 | tf_op jit(solution)/shard_map/ppermute | solution.py:641
  406.7 65.5 %collective-permute-start.29 = (bf16[384,640]{1,0:T(8,128)(2,1)S(1)}, bf16[384,640]{1,0:T(8,128)(2,1)S(1)}, u32[]{:S(2)}, u32[]{:S(2)}) collective-permute-start(bf16[384,640]{1,0:T(8,128)(2,1)S(1)} %get-tuple-element.165), channel_id=1, source_target_pairs={{0,16},{4,20},{8,24},{12,28},{16,0},{20,4},{24,8},{28,12},{1,17},{... | collective-permute-start | bytes 1474568 | tf_op jit(solution)/shard_map/ppermute | solution.py:641
  408.1 131.1 %collective-permute-start.55 = (bf16[3,320,960]{2,1,0:T(8,128)(2,1)S(1)}, bf16[3,320,960]{2,1,0:T(8,128)(2,1)}, u32[]{:S(2)}, u32[]{:S(2)}) collective-permute-start(bf16[3,320,960]{2,1,0:T(8,128)(2,1)S(1)} %pad_maximum_fusion.1), channel_id=1, source_target_pairs={{0,3},{1,0},{2,1},{3,2},{4,7},{5,4},{6,5},{7,6},{8,11},{9,8},{10,9... | collective-permute-start | bytes 5529608 | tf_op jit(solution)/shard_map/ppermute | solution.py:636
  428.2 111.0 %collective-permute-start.57 = (bf16[3,320,960]{2,1,0:T(8,128)(2,1)S(1)}, bf16[3,320,960]{2,1,0:T(8,128)(2,1)S(1)}, u32[]{:S(2)}, u32[]{:S(2)}) collective-permute-start(bf16[3,320,960]{2,1,0:T(8,128)(2,1)S(1)} %pad_maximum_fusion.2), channel_id=1, source_target_pairs={{0,1},{1,2},{2,3},{3,0},{4,5},{5,6},{6,7},{7,4},{8,9},{9,10},{10,1... | collective-permute-start | bytes 5529608 | tf_op jit(solution)/shard_map/ppermute | solution.py:636
  464.9 49.6 %collective-permute-start.44 = (bf16[128,960]{1,0:T(8,128)(2,1)S(1)}, bf16[128,960]{1,0:T(8,128)(2,1)S(1)}, u32[]{:S(2)}, u32[]{:S(2)}) collective-permute-start(bf16[128,960]{1,0:T(8,128)(2,1)S(1)} %get-tuple-element.171), channel_id=1, source_target_pairs={{0,3},{1,0},{2,1},{3,2},{4,7},{5,4},{6,5},{7,6},{8,11},{9,8},{10,9... | collective-permute-start | bytes 737288 | tf_op jit(solution)/shard_map/ppermute | solution.py:636
  470.7 53.8 %collective-permute-start.32 = (bf16[768,640]{1,0:T(8,128)(2,1)S(1)}, bf16[768,640]{1,0:T(8,128)(2,1)S(1)}, u32[]{:S(2)}, u32[]{:S(2)}) collective-permute-start(bf16[768,640]{1,0:T(8,128)(2,1)S(1)} %pad_maximum_fusion.5), channel_id=1, source_target_pairs={{0,16},{4,20},{8,24},{12,28},{16,0},{20,4},{24,8},{28,12},{1,17},{... | collective-permute-start | bytes 2949128 | tf_op jit(solution)/shard_map/ppermute | solution.py:641
  472.4 53.8 %collective-permute-start.30 = (bf16[768,640]{1,0:T(8,128)(2,1)S(1)}, bf16[768,640]{1,0:T(8,128)(2,1)S(1)}, u32[]{:S(2)}, u32[]{:S(2)}) collective-permute-start(bf16[768,640]{1,0:T(8,128)(2,1)S(1)} %pad_maximum_fusion.4), channel_id=1, source_target_pairs={{0,8},{4,12},{8,0},{12,4},{16,24},{20,28},{24,16},{28,20},{1,9},{5... | collective-permute-start | bytes 2949128 | tf_op jit(solution)/shard_map/ppermute | solution.py:641
  539.2 39.1 %collective-permute-start.33 = (bf16[4,256,384]{2,1,0:T(8,128)(2,1)S(1)}, bf16[4,256,384]{2,1,0:T(8,128)(2,1)S(1)}, u32[]{:S(2)}, u32[]{:S(2)}) collective-permute-start(bf16[4,256,384]{2,1,0:T(8,128)(2,1)S(1)} %get-tuple-element.48), channel_id=1, source_target_pairs={{0,4},{4,0},{8,12},{12,8},{16,20},{20,16},{24,28},{28,24},{1,5},{5... | collective-permute-start | bytes 2359304 | tf_op jit(solution)/shard_map/ppermute | solution.py:641
  541.8 36.6 %collective-permute-start.58 = (bf16[3,160,960]{2,1,0:T(8,128)(2,1)S(1)}, bf16[3,160,960]{2,1,0:T(8,128)(2,1)S(1)}, u32[]{:S(2)}, u32[]{:S(2)}) collective-permute-start(bf16[3,160,960]{2,1,0:T(8,128)(2,1)S(1)} %get-tuple-element.177), channel_id=1, source_target_pairs={{0,8},{4,12},{8,0},{12,4},{16,24},{20,28},{24,16},{28,20},{1,9},{5... | collective-permute-start | bytes 2764808 | tf_op jit(solution)/shard_map/ppermute | solution.py:641
  (84 other events, 1523.4 us)

commit v2 on v1

v2 whole, which is shorter than its diff:
```python
import jax
import jax.numpy as jnp
from jax import lax
from jax.experimental import pallas as pl
from jax.experimental.pallas import tpu as pltpu
from jax.sharding import PartitionSpec as P

HQ = 15
KVH = 5
HD = 64
BLK = 128
WIN = 1024
D = 960
GRP = HQ // KVH
SPAN = WIN + BLK
NWB = SPAN // BLK
ROWS = 256
ZR = 240
ZP = 256
UNITS = 256
WIDE = 1024
QKV = 1664

NORM_EPS = 1e-05
ROPE_THETA = 100000.0
MASK_FILL = -1e30
F32 = jnp.float32
BF16 = jnp.bfloat16
MIB = 1024 * 1024

VMEM = pl.BlockSpec(memory_space=pltpu.VMEM)
SMEM = pl.BlockSpec(memory_space=pltpu.SMEM)
ANY = pl.BlockSpec(memory_space=pl.ANY)

KV_LANES = 640
PAIRS = (
    (0, 3, (0, 1), True, True),
    (1, 4, (2, 3), True, True),
    (2, 2, (4,), False, True),
)

CORE_UNITS = 320
QUARTER = 160
OUT_ROWS = 64
OUT_AT = 3 * QUARTER
PACKED = OUT_AT + OUT_ROWS
CUT = 3 * PACKED // 2

P_ROWS = 128
Q_ROWS = 48
SEG = 64


def dot(a, b):
    return jnp.dot(a, b, preferred_element_type=F32)


def dot_nt(a, b):
    return lax.dot_general(a, b, (((1,), (1,)), ((), ())), preferred_element_type=F32)


def dot_tn(a, b):
    return lax.dot_general(a, b, (((0,), (0,)), ((), ())), preferred_element_type=F32)


def params(mib, grid_dims=0):
    return pltpu.CompilerParams(
        vmem_limit_bytes=mib * MIB,
        dimension_semantics=("arbitrary",) * grid_dims if grid_dims else None,
    )


def cost(flops, moved, exps=0):
    return pl.CostEstimate(flops=1, bytes_accessed=1, transcendentals=0)


def rope_slab(t, cos, sin_signed, first_half):
    swapped = jnp.where(first_half, pltpu.roll(t, 96, 1), pltpu.roll(t, 32, 1))
    return t * cos + swapped * sin_signed


def lane_masks(rows):
    lane = lax.broadcasted_iota(jnp.int32, (rows, 128), 1)
    return (lane % HD) < HD // 2, lane < HD


def rel_z(z, i):
    return lax.rem(z + 1 + i, 4)


def each(found, act):
    for cond, c in found:
        if cond is None:
            act(c)
        else:
            pl.when(cond)(lambda c=c: act(c))


def start(c):
    c.start()


def wait(c):
    c.wait()


def run_copies(pairs, sems):
    copies = [pltpu.make_async_copy(a, b, sems.at[i]) for i, (a, b) in enumerate(pairs)]
    for c in copies:
        c.start()
    for c in copies:
        c.wait()


def step_call(
    name, body, info, ins, outs, moved, where=None, out_where=None, scratch=(), aliases=None
):
    n_in, n_out = len(ins), len(outs)

    def kernel(info_ref, *refs):
        body(info_ref, refs[:n_in], refs[n_in : n_in + n_out], refs[n_in + n_out :])

    return pl.pallas_call(
        kernel,
        out_shape=tuple(jax.ShapeDtypeStruct(shape, dtype) for shape, dtype in outs),
        in_specs=[SMEM] + list(where or [VMEM] * n_in),
        out_specs=tuple(out_where or [VMEM] * n_out),
        scratch_shapes=list(scratch),
        input_output_aliases=aliases or {},
        compiler_params=params(40),
        cost_estimate=cost(1e6, moved),
        name=name,
    )(info, *ins)


def prep_weights(info, w_gate, w_up, w_down_turned, w_out):
    def body(info, ins, outs, scratch):
        core, parity = info[1], info[4]
        own, packed = outs
        turn = scratch[0]
        row = jnp.minimum(OUT_ROWS * (2 * core + parity), ZR - OUT_ROWS)
        packed[OUT_AT:PACKED, :] = ins[3][pl.ds(pl.multiple_of(row, 16), OUT_ROWS), :]
        base = core * CORE_UNITS
        for n in range(3):
            turn[...] = ins[n][...].T
            own[n] = turn[pl.ds(pl.multiple_of(base, 16), CORE_UNITS), :]
            quarter = pl.ds(pl.multiple_of(base + QUARTER * parity, 16), QUARTER)
            packed[QUARTER * n : QUARTER * n + QUARTER, :] = turn[quarter, :]

    return step_call(
        "prep_weights",
        body,
        info,
        (w_gate, w_up, w_down_turned, w_out),
        (((3, CORE_UNITS, D), BF16), ((PACKED, D), BF16)),
        8e6,
        scratch=(pltpu.VMEM((2 * CORE_UNITS, D), BF16),),
    )


def stack_weights(info, parts, packed):
    def body(info, ins, outs, scratch):
        c = pltpu.make_async_copy(ins[3], outs[1], scratch[0])
        c.start()
        for n in range(3):
            outs[0][n] = ins[n][...]
        c.wait()

    return step_call(
        "stack_weights",
        body,
        info,
        (*parts, packed),
        (((3,) + parts[0].shape, BF16), (packed.shape, BF16)),
        4e6,
        [VMEM] * 3 + [ANY],
        [VMEM, ANY],
        scratch=(pltpu.SemaphoreType.DMA,),
    )


def split_quarters(info, over_z, deps):
    at = CUT - PACKED

    def body(info, ins, outs, scratch):
        src = ins[0]
        z = info[0]
        zs = [rel_z(z, i) for i in range(3)]
        pairs = [
            (src.at[zs[0]], outs[0].at[pl.ds(0, PACKED)]),
            (src.at[zs[1], pl.ds(0, at)], outs[0].at[pl.ds(PACKED, at)]),
            (src.at[zs[1], pl.ds(at, PACKED - at)], outs[1].at[pl.ds(0, PACKED - at)]),
            (src.at[zs[2]], outs[1].at[pl.ds(PACKED - at, PACKED)]),
        ]
        pairs += [(src.at[zs[i], pl.ds(OUT_AT, OUT_ROWS)], outs[2].at[i]) for i in range(3)]
        run_copies(pairs, scratch[0])

    half = (CUT, D)
    return step_call(
        "split_quarters",
        body,
        info,
        (over_z, *deps),
        ((half, BF16), (half, BF16), ((3, OUT_ROWS, D), BF16)),
        8e6,
        [ANY] * (1 + len(deps)),
        [ANY] * 3,
        scratch=(pltpu.SemaphoreType.DMA((7,)),),
    )


def pick_out_rows(info, first_on, second_on, dep):
    def body(info, ins, outs, scratch):
        rows = (OUT_AT, PACKED + OUT_AT - CUT, 2 * PACKED + OUT_AT - CUT)
        pairs = [
            (ins[min(i, 1)].at[pl.ds(row, OUT_ROWS)], outs[0].at[i]) for i, row in enumerate(rows)
        ]
        run_copies(pairs, scratch[0])

    return step_call(
        "pick_out_rows",
        body,
        info,
        (first_on, second_on, dep),
        (((3, OUT_ROWS, D), BF16),),
        1e6,
        [ANY] * 3,
        [ANY],
        scratch=(pltpu.SemaphoreType.DMA((3,)),),
    )[0]


def pre_kernel(info, xt_ref, cos_ref, sin_ref, *refs):
    own, pieces = refs[0], refs[1:9]
    attn_ref, q_ref, kv_ref, w_ref, gains_ref, x_ref, cos_t, sin_t, sems = refs[9:]
    z, me = info[0], info[2]
    found = []

    def add(src, row, size, cond=None):
        view = w_ref.at[pl.ds(pl.multiple_of(row, 16), size)]
        found.append((cond, pltpu.make_async_copy(src, view, sems.at[len(found)])))

    add(own, z * ZR, ZR)
    for rel, piece in enumerate(pieces):
        c = me ^ rel
        for i in range(3):
            base = rel_z(z, i) * ZR
            add(piece.at[i, pl.ds(0, 16)], base + 32 * c, 16, c < 7)
            add(piece.at[i, pl.ds(16, 16)], base + jnp.minimum(32 * c + 16, ZR - 16), 16)
    each(found, start)
    steps = x_ref.shape[0] // ROWS
    cos_t[...] = cos_ref[...].T[0:32]
    sin_t[...] = sin_ref[...].T[32:64]

    def turn(i, _):
        r = pl.ds(pl.multiple_of(i * ROWS, ROWS), ROWS)
        x_ref[r, :] = xt_ref[:, r].T
        return 0

    lax.fori_loop(0, steps, turn, 0)
    each(found, wait)
    gains_ref[...] = w_ref[:, 1536:QKV].astype(F32).T[64:72]
    first_half, low_head = lane_masks(ROWS)

    def body(i, _):
        r = pl.ds(pl.multiple_of(i * ROWS, ROWS), ROWS)
        x = x_ref[r, :].astype(F32)
        factor = lax.rsqrt(jnp.mean(x * x, axis=-1, keepdims=True) + NORM_EPS)
        a = (x * factor * gains_ref[0:1, :]).astype(BF16)
        attn_ref[r, :] = a
        qk = dot(a, w_ref[:, 0:1280])
        vv = dot(a, w_ref[:, 1280:QKV])
        cos, sin = cos_ref[r, :], sin_ref[r, :]
        slabs = [
            rope_slab(qk[:, 128 * j : 128 * j + 128], cos, sin, first_half) for j in range(10)
        ]
        for j in range(7):
            q_ref[r, 128 * j : 128 * j + 128] = slabs[j].astype(BF16)
        q_ref[r, 896:960] = slabs[7][:, :64].astype(BF16)
        mixed = jnp.where(low_head, vv[:, 256:384], slabs[7])
        for j, part in enumerate((slabs[8], slabs[9], mixed, vv[:, 0:128], vv[:, 128:256])):
            kv_ref[r, 128 * j : 128 * j + 128] = part.astype(BF16)
        return 0

    lax.fori_loop(0, steps, body, 0)


def pre_call(info, xt, cos, sin, pieces):
    t = xt.shape[1]
    return pl.pallas_call(
        pre_kernel,
        out_shape=(
            jax.ShapeDtypeStruct((t, D), BF16),
            jax.ShapeDtypeStruct((t, D), BF16),
            jax.ShapeDtypeStruct((t, KV_LANES), BF16),
            jax.ShapeDtypeStruct((D, QKV), BF16),
            jax.ShapeDtypeStruct((8, D), F32),
            jax.ShapeDtypeStruct((t, D), BF16),
            jax.ShapeDtypeStruct((32, t), F32),
            jax.ShapeDtypeStruct((32, t), F32),
        ),
        in_specs=[SMEM] + [VMEM] * 3 + [ANY] * 9,
        out_specs=(VMEM,) * 8,
        scratch_shapes=[pltpu.SemaphoreType.DMA((49,))],
        compiler_params=params(40),
        cost_estimate=cost(2 * t * D * QKV, 13e6),
        name="pre",
    )(info, xt, cos, sin, *pieces)


def start_window(tab, kvs, win, sem, blk, slot):
    def body(j, _):
        entry = tab[blk, j]
        which = entry // 1024
        idx = lax.rem(entry, 1024)
        dst = win.at[slot, pl.ds(pl.multiple_of(j * BLK, BLK), BLK)]
        for n, ref in enumerate(kvs):
            @pl.when(which == n)
            def _():
                src = ref.at[pl.ds(pl.multiple_of(idx * BLK, BLK), BLK)]
                pltpu.make_async_copy(src, dst, sem.at[slot]).start()
        return 0

    lax.fori_loop(0, NWB, body, 0)


def next_window(tab, kvs, win, sem, first=0):
    i = pl.program_id(0)
    slot = lax.rem(i, 2)

    @pl.when(i == 0)
    def _():
        start_window(tab, kvs, win, sem, i + first, slot)

    @pl.when(i + 1 < pl.num_programs(0))
    def _():
        start_window(tab, kvs, win, sem, i + first + 1, 1 - slot)

    pltpu.make_async_copy(win.at[slot], win.at[slot], sem.at[slot]).wait()
    return slot


def turned(flat):
    rows = flat.astype(F32)
    extra = -rows.shape[1] % 128
    if extra:
        rows = jnp.concatenate([rows, jnp.zeros((rows.shape[0], extra), F32)], axis=1)
    return rows.T


def unturned(parts):
    rows = sum(p.shape[0] for p in parts)
    extra = -rows % 128
    if extra:
        parts = parts + [jnp.zeros((extra, parts[0].shape[1]), F32)]
    return jnp.concatenate(parts, axis=0).T[:, :rows].astype(BF16)


def spread_heads(rows, count, low):
    width = GRP * BLK
    sides = [jnp.concatenate(rows[GRP * n : GRP * n + GRP], axis=1) for n in range(count)]
    empty = jnp.zeros((HD, width), rows[0].dtype)
    if count == 2:
        return jnp.concatenate(
            [jnp.concatenate([sides[0], empty], axis=1), jnp.concatenate([empty, sides[1]], axis=1)],
            axis=0,
        )
    return jnp.concatenate([sides[0], empty] if low else [empty, sides[0]], axis=0)


def head_half(j, kv_heads, low):
    upper = j >= GRP if len(kv_heads) == 2 else not low
    return HD if upper else 0


def fwd_kernel(n_kv, tab, lo_ref, q_ref, *refs):
    kvs = refs[:n_kv]
    mid_ref, rl_ref, p_ref, win, bias, scores, sem = refs[n_kv:]
    slot = next_window(tab, kvs, win, sem)
    row = lax.broadcasted_iota(jnp.int32, (SPAN, BLK), 0)
    lane = lax.broadcasted_iota(jnp.int32, (SPAN, BLK), 1)
    allowed = (row >= lo_ref[0]) & (row <= lane + WIN)
    bias[...] = jnp.where(allowed, 0.0, MASK_FILL)
    q_all = (turned(q_ref[...]) * (HD ** -0.5)).astype(BF16)
    outs, recips = [], []
    at = 0
    for k_slab, v_slab, kv_heads, k_low, v_low in PAIRS:
        keys = win[slot, :, 128 * k_slab : 128 * k_slab + 128]
        vals = win[slot, :, 128 * v_slab : 128 * v_slab + 128]
        count = GRP * len(kv_heads)
        width = BLK * count
        base = BLK * at
        q_rows = [q_all[HD * (at + j) : HD * (at + j) + HD] for j in range(count)]
        scores[:, :width] = dot(keys, spread_heads(q_rows, len(kv_heads), k_low))
        for j in range(count):
            s = scores[:, BLK * j : BLK * j + BLK] + bias[...]
            top = jnp.max(s, axis=0, keepdims=True)
            p_ref[0, :, base + BLK * j : base + BLK * j + BLK] = jnp.exp(s - top).astype(BF16)
        lhs = jnp.concatenate([vals.T, jnp.ones((16, SPAN), BF16)], axis=0)
        product = dot(lhs, p_ref[0, :, base : base + width])
        recip = 1.0 / product[128:129, :]
        for j in range(count):
            cols = slice(BLK * j, BLK * j + BLK)
            half = head_half(j, kv_heads, v_low)
            outs.append(product[half : half + HD, cols] * recip[:, cols])
            recips.append(recip[:, cols])
        at += count
    mid_ref[...] = unturned(outs)
    recips.append(jnp.zeros((16 - len(recips), BLK), F32))
    rl_ref[0] = jnp.concatenate(recips, axis=0)


def fwd_call(tab, lo, q, kvs):
    blocks = q.shape[0] // BLK
    n_kv = len(kvs)
    lanes, heads = D, HQ
    return pl.pallas_call(
        lambda *refs: fwd_kernel(n_kv, *refs),
        grid=(blocks,),
        out_shape=(
            jax.ShapeDtypeStruct((q.shape[0], lanes), BF16),
            jax.ShapeDtypeStruct((blocks, 16, BLK), F32),
            jax.ShapeDtypeStruct((blocks, SPAN, heads * BLK), BF16),
        ),
        in_specs=[
            SMEM,
            pl.BlockSpec((1, 1, BLK), lambda i: (i, 0, 0)),
            pl.BlockSpec((BLK, lanes), lambda i: (i, 0)),
        ]
        + [ANY] * n_kv,
        out_specs=(
            pl.BlockSpec((BLK, lanes), lambda i: (i, 0)),
            pl.BlockSpec((1, 16, BLK), lambda i: (i, 0, 0)),
            pl.BlockSpec((1, SPAN, heads * BLK), lambda i: (i, 0, 0)),
        ),
        scratch_shapes=[
            pltpu.VMEM((2, SPAN, KV_LANES), BF16),
            pltpu.VMEM((SPAN, BLK), F32),
            pltpu.VMEM((SPAN, 2 * GRP * BLK), F32),
            pltpu.SemaphoreType.DMA((2,)),
        ],
        compiler_params=params(48, 1),
        cost_estimate=cost(0.5e9 * heads * blocks, 0.5e6 * heads * blocks, 0.15e6 * heads * blocks),
        name="attend",
    )(tab, lo, q, *kvs)


def bwd_kernel(
    n_kv, n_dep, first, prev, out_units, n_slots, tab, slots, q_ref, do_ref, mid_ref, rl_ref, p_ref, cos_ref, sin_ref, *refs
):
    kvs = refs[:n_kv]
    n_out = len(out_units)
    refs = refs[n_kv + n_dep :]
    earlier = refs[:n_out] if prev else ()
    refs = refs[len(earlier) :]
    dq_ref = refs[0]
    outs = refs[1 : 1 + n_out]
    win, acc, scores, stage, stage_in, sem, out_sem, in_sem = refs[1 + n_out :]
    i = pl.program_id(0)
    blk = i + first
    slot = next_window(tab, kvs, win, sem, first)
    lanes = acc.shape[1]

    @pl.when(i == 0)
    def _():
        def clear(b, _):
            acc[pl.ds(pl.multiple_of(b * BLK, BLK), BLK), :] = jnp.zeros((BLK, lanes), F32)
            return 0

        lax.fori_loop(0, n_slots, clear, 0)

    def add(slab, value):
        for j in range(NWB):
            r = pl.ds(pl.multiple_of(slots[blk, j] * BLK, BLK), BLK)
            acc[r, 128 * slab : 128 * slab + 128] += value[BLK * j : BLK * j + BLK]

    q_all = (turned(q_ref[...]) * (HD ** -0.5)).astype(BF16)
    do_all = turned(do_ref[...])
    o_all = turned(mid_ref[...])
    cos, sin = cos_ref[...], sin_ref[...]
    grads = []
    at = 0
    for k_slab, v_slab, kv_heads, k_low, v_low in PAIRS:
        keys = win[slot, :, 128 * k_slab : 128 * k_slab + 128]
        vals = win[slot, :, 128 * v_slab : 128 * v_slab + 128]
        count = GRP * len(kv_heads)
        width = BLK * count
        base = BLK * at
        q_rows, do_rows, dots = [], [], []
        for j in range(count):
            r = slice(HD * (at + j), HD * (at + j) + HD)
            q_rows.append(q_all[r])
            scaled = do_all[r] * rl_ref[0, at + j : at + j + 1, :]
            dots.append(jnp.sum(scaled * o_all[r], axis=0, keepdims=True))
            do_rows.append(scaled.astype(BF16))
        q_wide = spread_heads(q_rows, len(kv_heads), k_low)
        do_wide = spread_heads(do_rows, len(kv_heads), v_low)
        scores[:, :width] = dot(vals, do_wide)
        ds = []
        for j in range(count):
            p = p_ref[0, :, base + BLK * j : base + BLK * j + BLK].astype(F32)
            ds.append((p * (scores[:, BLK * j : BLK * j + BLK] - dots[j])).astype(BF16))
        ds = jnp.concatenate(ds, axis=1)
        probs = p_ref[0, :, base : base + width]
        if len(kv_heads) == 2:
            add(k_slab, dot_nt(ds, q_wide))
            add(v_slab, dot_nt(probs, do_wide))
        else:
            add(
                k_slab,
                dot_nt(
                    jnp.concatenate([ds, probs], axis=1),
                    jnp.concatenate([q_wide, do_wide], axis=1),
                ),
            )
        dq = dot(keys.T, ds) * (HD ** -0.5)
        for j in range(count):
            top = head_half(j, kv_heads, k_low)
            cols = slice(BLK * j, BLK * j + BLK)
            first = dq[top : top + 32, cols]
            second = dq[top + 32 : top + 64, cols]
            grads.append(first * cos + second * sin)
            grads.append(second * cos - first * sin)
        at += count
    dq_ref[...] = unturned(grads)

    @pl.when(i == pl.num_programs(0) - 1)
    def _():
        per = 6 * BLK
        places = [(n, u) for n, units in enumerate(out_units) for u in range(units)]
        copies, loads = [], []

        def load(t):
            if prev and t < len(places):
                n, u = places[t]
                c = pltpu.make_async_copy(
                    earlier[n].at[pl.ds(per * u, per)], stage_in.at[t % 2], in_sem.at[t % 2]
                )
                c.start()
                loads.append(c)

        load(0)
        load(1)
        for t, (n, u) in enumerate(places):
            s = t % 2
            if t >= 2:
                copies[t - 2].wait()
            value = acc[per * t : per * t + per, :]
            if prev:
                loads[t].wait()
                value = value + stage_in[s].astype(F32)
            stage[s] = value.astype(BF16)
            load(t + 2)
            c = pltpu.make_async_copy(stage.at[s], outs[n].at[pl.ds(per * u, per)], out_sem.at[s])
            c.start()
            copies.append(c)
        copies[-2].wait()
        copies[-1].wait()


def bwd_call(first, blocks, earlier, deps, tab, slots, out_units, q, do, mid, rl, p, cos, sin, kvs):
    n_kv = len(kvs)
    lanes, heads, width = D, HQ, KV_LANES
    n_slots = 6 * sum(out_units)
    flat = pl.BlockSpec((BLK, lanes), lambda i: (i + first, 0))
    table = pl.BlockSpec((32, BLK), lambda i: (0, i + first))
    prev = bool(earlier)
    return pl.pallas_call(
        lambda *refs: bwd_kernel(n_kv, len(deps), first, prev, out_units, n_slots, *refs),
        grid=(blocks,),
        out_shape=(jax.ShapeDtypeStruct((blocks * BLK, lanes), BF16),)
        + tuple(jax.ShapeDtypeStruct((6 * BLK * u, width), BF16) for u in out_units),
        in_specs=[
            SMEM,
            SMEM,
            flat,
            flat,
            flat,
            pl.BlockSpec((1, 16, BLK), lambda i: (i + first, 0, 0)),
            pl.BlockSpec((1, SPAN, heads * BLK), lambda i: (i + first, 0, 0)),
            table,
            table,
        ]
        + [ANY] * (n_kv + len(deps) + len(earlier)),
        out_specs=(pl.BlockSpec((BLK, lanes), lambda i: (i, 0)),) + (ANY,) * len(out_units),
        scratch_shapes=[
            pltpu.VMEM((2, SPAN, width), BF16),
            pltpu.VMEM((n_slots * BLK, width), F32),
            pltpu.VMEM((SPAN, 2 * GRP * BLK), F32),
            pltpu.VMEM((2, 6 * BLK, width), BF16),
            pltpu.VMEM((2, 6 * BLK, width), BF16),
            pltpu.SemaphoreType.DMA((2,)),
            pltpu.SemaphoreType.DMA((2,)),
            pltpu.SemaphoreType.DMA((2,)),
        ],
        compiler_params=params(60, 1),
        cost_estimate=cost(0.5e9 * heads * blocks, 0.5e6 * heads * blocks),
        name=f"attend_back_{first}",
    )(tab, slots, q, do, mid, rl, p, cos, sin, *kvs, *deps, *earlier)


def pro_kernel(info, mid_ref, x_ref, gain_ref, own, *refs):
    here, there = refs[0:4], refs[4:6]
    h1_ref, low_ref, w_ref, sems = refs[7:]
    z, core, parity = info[0], info[1], info[4]
    found = []

    def bring(src, row, size, cond=None):
        dst = w_ref.at[pl.ds(pl.multiple_of(row, 16), size)]
        found.append((cond, pltpu.make_async_copy(src, dst, sems.at[len(found)])))

    bring(own, z * ZR, ZR)
    for n, (side, par) in enumerate(
        ((core, parity), (core, 1 - parity), (1 - core, parity), (1 - core, 1 - parity))
    ):
        qd = 2 * side + par
        for i in range(3):
            if n < 2:
                a = PACKED * i + OUT_AT
                src = here[2 * n + (a >= CUT)]
                a -= CUT if a >= CUT else 0
                view = lambda at, size, src=src, a=a: src.at[pl.ds(a + at, size)]
            else:
                view = lambda at, size, src=there[n - 2], i=i: src.at[i, pl.ds(at, size)]
            base = rel_z(z, i) * ZR + jnp.minimum(OUT_ROWS * qd, ZR - OUT_ROWS)
            bring(view(0, 16), base, 16, qd < 3)
            bring(view(16, OUT_ROWS - 16), base + 16, OUT_ROWS - 16)
    each(found, start)
    gain = gain_ref[1:2, :]
    each(found, wait)

    def body(i, _):
        r = pl.ds(pl.multiple_of(i * ROWS, ROWS), ROWS)
        h = x_ref[r, :].astype(F32) + dot(mid_ref[r, :], w_ref[...])
        factor = lax.rsqrt(jnp.mean(h * h, axis=-1, keepdims=True) + NORM_EPS)
        h1_ref[r, :] = h
        low_ref[r, 0:D] = (h * factor * gain).astype(BF16)
        low_ref[r, D:WIDE] = jnp.zeros((ROWS, WIDE - D), BF16)
        return 0

    lax.fori_loop(0, x_ref.shape[0] // ROWS, body, 0)


def pro_call(info, mid, x, gains, own, here, there, dep):
    t = x.shape[0]
    return pl.pallas_call(
        pro_kernel,
        out_shape=(
            jax.ShapeDtypeStruct((t, D), F32),
            jax.ShapeDtypeStruct((t, WIDE), BF16),
            jax.ShapeDtypeStruct((D, D), BF16),
        ),
        in_specs=[SMEM] + [VMEM] * 3 + [ANY] * 8,
        out_specs=(VMEM,) * 3,
        scratch_shapes=[pltpu.SemaphoreType.DMA((25,))],
        compiler_params=params(40),
        cost_estimate=cost(2 * t * D * D, 12e6),
        name="out_projection",
    )(info, mid, x, gains, own, *here, *there, dep)


def ffn_kernel(info, a0, a1, c0, c1, own, *refs):
    here = refs[:4]
    acc_outs, p_ref, q_refs = refs[4:8], refs[8], refs[9:13]
    (
        wbuf, a_all, c_all, c_turn, hid_s, gg_s, gu_s, stage, acc_o, acc_g, send_o, send_g,
        io_sem, w_sem, out_sem, acc_sem,
    ) = refs[13:]
    z, chip, parity = info[0], info[3], info[4]
    t = a0.shape[0]
    units = wbuf.shape[1]
    ins = [
        pltpu.make_async_copy(a0, a_all.at[pl.ds(0, t)], io_sem.at[0]),
        pltpu.make_async_copy(a1, a_all.at[pl.ds(t, t)], io_sem.at[1]),
        pltpu.make_async_copy(c0, c_turn.at[0], io_sem.at[2]),
        pltpu.make_async_copy(c1, c_turn.at[1], io_sem.at[3]),
    ]
    copies = [pltpu.make_async_copy(own, wbuf.at[:, pl.ds(0, CORE_UNITS)], w_sem.at[0])]
    for n_par, par in enumerate((parity, 1 - parity)):
        for i in range(3):
            for n in range(3):
                a0_row = PACKED * i + QUARTER * n
                for ref, p0, p1 in ((here[2 * n_par], 0, CUT), (here[2 * n_par + 1], CUT, 2 * CUT)):
                    a, b = max(p0, a0_row), min(p1, a0_row + QUARTER)
                    if a < b:
                        row = CORE_UNITS * (i + 1) + QUARTER * par + (a - a0_row)
                        dst = wbuf.at[n, pl.ds(pl.multiple_of(row, 16), b - a)]
                        copies.append(
                            pltpu.make_async_copy(
                                ref.at[pl.ds(a - p0, b - a)], dst, w_sem.at[len(copies)]
                            )
                        )
    for c in ins[2:] + ins[:2] + copies:
        c.start()
    for h in range(2):
        ins[2 + h].wait()
        c_all[t * h : t * h + t, :] = c_turn[h].T
    for c in ins[:2] + copies:
        c.wait()

    def forward(c, _):
        u = pl.ds(pl.multiple_of(c * UNITS, UNITS), UNITS)
        for h in range(2 * t // ROWS):
            r = slice(ROWS * h, ROWS * h + ROWS)
            gate = dot_nt(a_all[r, 0:D], wbuf[0, u, :])
            up = dot_nt(a_all[r, 0:D], wbuf[1, u, :])
            grad = dot_nt(c_all[r, :], wbuf[2, u, :])
            sig = lax.logistic(gate)
            swish = gate * sig
            hid_s[r, u] = (swish * up).astype(BF16)
            gg_s[r, u] = (grad * up * (sig * (1.0 + gate * (1.0 - sig)))).astype(BF16)
            gu_s[r, u] = (grad * swish).astype(BF16)
        return 0

    lax.fori_loop(0, units // UNITS, forward, 0)

    def sums(r):
        left = dot(hid_s[r, :], wbuf[2])
        right = dot(gg_s[r, :], wbuf[0]) + dot(gu_s[r, :], wbuf[1])
        return left, right

    def mine(i, _):
        r = pl.ds(pl.multiple_of(i * ROWS, ROWS), ROWS)
        acc_o[r, :], acc_g[r, :] = sums(r)
        return 0

    def others(i, _):
        r = pl.ds(pl.multiple_of(i * ROWS, ROWS), ROWS)
        left, right = sums(pl.ds(pl.multiple_of(t + i * ROWS, ROWS), ROWS))
        for ref, value in ((send_o, left), (send_g, right)):
            ref[r, 0:D] = value.astype(BF16)
            ref[r, D:WIDE] = jnp.zeros((ROWS, WIDE - D), BF16)
        return 0

    lax.fori_loop(0, t // ROWS, others, 0)
    lax.fori_loop(0, t // ROWS, mine, 0)
    acc_copies = [
        pltpu.make_async_copy(src, dst, acc_sem.at[n])
        for n, (src, dst) in enumerate(zip((acc_o, acc_g, send_o, send_g), acc_outs))
    ]
    for c in acc_copies:
        c.start()

    def back_copies(c, slot):
        found = []
        per = CORE_UNITS // SEG
        for n in range(UNITS // SEG):
            j = c * (UNITS // SEG) + n
            within = lax.rem(j, per)
            zz = lax.rem(z + j // per, 4)
            n_p = P_ROWS // SEG
            first = within < n_p
            row = pl.multiple_of(jnp.minimum(within, n_p - 1) * SEG, SEG)
            src = stage.at[slot, :, pl.ds(SEG * n, SEG)]
            dst = p_ref.at[zz, :, pl.ds(row, SEG)]
            found.append((first, pltpu.make_async_copy(src, dst, out_sem.at[slot, 24 + n])))
            piece = 6 * n
            for k in range(per - n_p):
                at = SEG * k
                while at < SEG * k + SEG:
                    owner = at // Q_ROWS
                    size = min(SEG * k + SEG, Q_ROWS * (owner + 1)) - at
                    src = stage.at[slot, :, pl.ds(SEG * n + at - SEG * k, size)]
                    for r in range(4):
                        dst = q_refs[r].at[zz, :, pl.ds(at - Q_ROWS * owner, size)]
                        copy = pltpu.make_async_copy(src, dst, out_sem.at[slot, piece])
                        found.append(((within == n_p + k) & (chip ^ owner == r), copy))
                    at += size
                    piece += 1
        return found

    def backward(c, _):
        u = pl.ds(pl.multiple_of(c * UNITS, UNITS), UNITS)
        slot = lax.rem(c, 2)

        @pl.when(c >= 2)
        def _():
            each(back_copies(c - 2, slot), wait)

        stage[slot, 0] = dot_tn(gg_s[:, u], a_all[:, 0:D]).astype(BF16)
        stage[slot, 1] = dot_tn(gu_s[:, u], a_all[:, 0:D]).astype(BF16)
        stage[slot, 2] = dot_tn(hid_s[:, u], c_all[...]).astype(BF16)
        each(back_copies(c, slot), start)
        return 0

    n_chunks = units // UNITS
    lax.fori_loop(0, n_chunks, backward, 0)
    for c in (n_chunks - 2, n_chunks - 1):
        each(back_copies(jnp.int32(c), c % 2), wait)
    for c in acc_copies:
        c.wait()


def ffn_call(info, a0, a1, c0, c1, own, here):
    t = a0.shape[0]
    units = 4 * CORE_UNITS
    return pl.pallas_call(
        ffn_kernel,
        out_shape=(
            jax.ShapeDtypeStruct((t, D), F32),
            jax.ShapeDtypeStruct((t, D), F32),
            jax.ShapeDtypeStruct((t, WIDE), BF16),
            jax.ShapeDtypeStruct((t, WIDE), BF16),
            jax.ShapeDtypeStruct((4, 3, P_ROWS, D), BF16),
            *[jax.ShapeDtypeStruct((4, 3, Q_ROWS, D), BF16)] * 4,
        ),
        in_specs=[SMEM] + [ANY] * 9,
        out_specs=(ANY,) * 9,
        scratch_shapes=[
            pltpu.VMEM((3, units, D), BF16),
            pltpu.VMEM((2 * t, WIDE), BF16),
            pltpu.VMEM((2 * t, D), BF16),
            pltpu.VMEM((2, D, t), BF16),
            pltpu.VMEM((2 * t, units), BF16),
            pltpu.VMEM((2 * t, units), BF16),
            pltpu.VMEM((2 * t, units), BF16),
            pltpu.VMEM((2, 3, UNITS, D), BF16),
            pltpu.VMEM((t, D), F32),
            pltpu.VMEM((t, D), F32),
            pltpu.VMEM((t, WIDE), BF16),
            pltpu.VMEM((t, WIDE), BF16),
            pltpu.SemaphoreType.DMA((4,)),
            pltpu.SemaphoreType.DMA((24,)),
            pltpu.SemaphoreType.DMA((2, 28)),
            pltpu.SemaphoreType.DMA((4,)),
        ],
        compiler_params=params(60),
        cost_estimate=cost(2 * 2 * t * D * 9 * units, 40e6),
        name="feed_forward",
    )(info, a0, a1, c0, c1, own, *here)


def put_shards(ref, product, gain_grad):
    extra = ref.shape[-1] - product.shape[1]
    if extra:
        product = jnp.concatenate([product, jnp.zeros((product.shape[0], extra), F32)], axis=1)
    width = product.shape[1]
    first_row = lax.broadcasted_iota(jnp.int32, (ZP - ZR, width), 0) == 0
    for n in range(4):
        ref[n, 0:ZR, :] = product[ZR * n : ZR * n + ZR].astype(BF16)
        if gain_grad is None:
            ref[n, ZR:ZP, :] = jnp.zeros((ZP - ZR, width), BF16)
        else:
            part = jnp.concatenate(
                [gain_grad[:, ZR * n : ZR * n + ZR], jnp.zeros((1, width - ZR), F32)], axis=1
            )
            ref[n, ZR:ZP, :] = jnp.where(first_row, part, 0.0).astype(BF16)


def epi_kernel(info, h1_ref, acc_g, got_ref, ct_ref, gain_ref, w_ref, mid_ref, gh_ref, gm_ref, go_ref, acc, total):
    i = pl.program_id(0)

    @pl.when(i == 0)
    def _():
        acc[...] = jnp.zeros((D, D), F32)
        total[...] = jnp.zeros((8, D), F32)

    h = h1_ref[...]
    factor = lax.rsqrt(jnp.mean(h * h, axis=-1, keepdims=True) + NORM_EPS)
    normed = h * factor
    g = acc_g[...] + got_ref[:, 0:D].astype(F32)
    scaled = g * gain_ref[1:2, :]
    back = factor * (scaled - normed * jnp.mean(scaled * normed, axis=-1, keepdims=True))
    full = ct_ref[...].T.astype(F32) + back
    gh_ref[...] = full
    res = full.astype(BF16)
    gm_ref[...] = dot_nt(res, w_ref[...]).astype(BF16)
    total[0:1, :] += jnp.sum(g * normed, axis=0, keepdims=True)
    acc[...] += dot_tn(mid_ref[...], res)

    @pl.when(i == pl.num_programs(0) - 1)
    def _():
        put_shards(go_ref, acc[...], total[0:1, :])


def epi_call(info, h1, acc_g, got, cot_t, gains, w_out, mid):
    t = h1.shape[0]
    rows = pl.BlockSpec((ROWS, D), lambda i: (i, 0))
    return pl.pallas_call(
        epi_kernel,
        grid=(t // ROWS,),
        out_shape=(
            jax.ShapeDtypeStruct((t, D), F32),
            jax.ShapeDtypeStruct((t, D), BF16),
            jax.ShapeDtypeStruct((4, ZP, WIDE), BF16),
        ),
        in_specs=[
            SMEM,
            rows,
            rows,
            pl.BlockSpec((ROWS, WIDE), lambda i: (i, 0)),
            pl.BlockSpec((D, ROWS), lambda i: (0, i)),
            VMEM,
            VMEM,
            rows,
        ],
        out_specs=(rows, rows, pl.BlockSpec((4, ZP, WIDE), lambda i: (0, 0, 0))),
        scratch_shapes=[pltpu.VMEM((D, D), F32), pltpu.VMEM((8, D), F32)],
        compiler_params=params(48, 1),
        cost_estimate=cost(4 * t * D * D, 20e6),
        name="feed_forward_norm_back",
    )(info, h1, acc_g, got, cot_t, gains, w_out, mid)


def post_q_kernel(info, a_ref, g_ref, w_ref, go_ref, _, keep_ref, send_ref, part_ref):
    core = info[1]
    g = g_ref[...]
    product = dot_tn(a_ref[...], g)

    @pl.when(core == 0)
    def _():
        put_shards(keep_ref, product, None)
        send_ref[...] = go_ref[...]

    @pl.when(core == 1)
    def _():
        put_shards(send_ref, product, None)
        keep_ref[...] = go_ref[...]

    part_ref[...] = dot_nt(g, w_ref[:, :D])


def post_q_call(info, a, g, w, go, dep):
    t = a.shape[0]
    return pl.pallas_call(
        post_q_kernel,
        out_shape=(
            jax.ShapeDtypeStruct((4, ZP, 1024), BF16),
            jax.ShapeDtypeStruct((4, ZP, 1024), BF16),
            jax.ShapeDtypeStruct((t, D), F32),
        ),
        in_specs=[SMEM] + [VMEM] * 4 + [ANY],
        out_specs=(VMEM,) * 3,
        compiler_params=params(40),
        cost_estimate=cost(4 * t * D * D, 12e6),
        name="query_back",
    )(info, a, g, w, go, dep)


def post_kv_kernel(
    info, s0, s1, s2, cos_ref, sin_ref, a_ref, part_ref, w_ref, x_ref, gh_ref, gain_ref,
    keep_ref, send_ref, ig_ref, kg, vg,
):
    core = info[1]
    first_half, low_head = lane_masks(ROWS)
    steps = x_ref.shape[0] // ROWS
    gain = gain_ref[0:1, :]

    def body(i, total):
        r = pl.ds(pl.multiple_of(i * ROWS, ROWS), ROWS)

        def slab(j):
            c = slice(128 * j, 128 * j + 128)
            return s0[r, c].astype(F32) + s1[r, c].astype(F32) + s2[r, c].astype(F32)

        cos, sin = cos_ref[r, :], -sin_ref[r, :]
        mixed = slab(2)
        k4 = jnp.where(low_head, 0.0, rope_slab(mixed, cos, sin, first_half))
        k01 = rope_slab(slab(0), cos, sin, first_half)
        k23 = rope_slab(slab(1), cos, sin, first_half)
        k_low = jnp.concatenate([k4, k01, k23], axis=1).astype(BF16)
        v4 = jnp.where(low_head, mixed, 0.0)
        v_low = jnp.concatenate([slab(3), slab(4), v4], axis=1).astype(BF16)
        kg[r, :] = k_low
        vg[r, :] = v_low
        g = (
            part_ref[r, :]
            + dot_nt(k_low, w_ref[:, 896:1280])
            + dot_nt(v_low[:, 0:320], w_ref[:, 1280:1600])
        )
        x = x_ref[r, :].astype(F32)
        factor = lax.rsqrt(jnp.mean(x * x, axis=-1, keepdims=True) + NORM_EPS)
        normed = x * factor
        scaled = g * gain
        back = factor * (scaled - normed * jnp.mean(scaled * normed, axis=-1, keepdims=True))
        ig_ref[:, r] = (gh_ref[r, :] + back).astype(BF16).T
        return total + jnp.sum(g * normed, axis=0, keepdims=True)

    gain_grad = lax.fori_loop(0, steps, body, jnp.zeros((1, D), F32))
    mine = core == 0
    k_side = dot_tn(a_ref[...], kg[...])
    v_side = dot_tn(a_ref[...], vg[...])
    put_shards(keep_ref, jnp.where(mine, k_side, v_side), jnp.where(mine, gain_grad, 0.0))
    put_shards(send_ref, jnp.where(mine, v_side, k_side), jnp.where(mine, 0.0, gain_grad))


def post_kv_call(info, sums, cos, sin, a, part, w, x, gh, gain, deps):
    t = x.shape[0]
    n_deps = len(deps)
    piece = jax.ShapeDtypeStruct((4, ZP, 384), BF16)
    return pl.pallas_call(
        lambda *refs: post_kv_kernel(*refs[:12], *refs[12 + n_deps :]),
        out_shape=(piece, piece, jax.ShapeDtypeStruct((D, t), BF16)),
        in_specs=[SMEM] + [VMEM] * 11 + [ANY] * n_deps,
        out_specs=(VMEM,) * 3,
        scratch_shapes=[pltpu.VMEM((t, 384), BF16), pltpu.VMEM((t, 384), BF16)],
        compiler_params=params(50),
        cost_estimate=cost(8 * t * D * 384, 25e6),
        name="key_value_back",
    )(info, *sums, cos, sin, a, part, w, x, gh, gain, *deps)


def finish_ffn_kernel(info, pm_ref, po_ref, qm_ref, qo_ref, gate_ref, up_ref, down_ref, rows):
    core, chip = info[1], info[3]
    for n, out in enumerate((gate_ref, up_ref, down_ref)):
        for p_ref, q_ref, side in ((pm_ref, qm_ref, core), (po_ref, qo_ref, 1 - core)):
            base = side * CORE_UNITS
            rows[pl.ds(pl.multiple_of(base, 16), P_ROWS), :] = p_ref[n].astype(F32)
            for r in range(4):
                row = base + P_ROWS + Q_ROWS * (chip ^ r)
                rows[pl.ds(pl.multiple_of(row, 16), Q_ROWS), :] = q_ref[r, n].astype(F32)
        out[...] = rows[...].T


def finish_ffn_call(info, pm, po, qm, qo):
    out = jax.ShapeDtypeStruct((D, 2 * CORE_UNITS), F32)
    return pl.pallas_call(
        finish_ffn_kernel,
        out_shape=(out,) * 3,
        in_specs=[SMEM] + [VMEM] * 4,
        out_specs=(VMEM,) * 3,
        scratch_shapes=[pltpu.VMEM((2 * CORE_UNITS, D), F32)],
        compiler_params=params(32),
        cost_estimate=cost(1e6, 12e6),
        name="finish_feed_forward",
    )(info, pm, po, qm, qo)


def finish_rest_kernel(info, qm_ref, qo_ref, km_ref, ko_ref, wq_ref, wo_ref, wk_ref, wv_ref, gains_ref):
    def emit(q_ref, o_ref, k_ref, v_ref):
        wq_ref[...] = q_ref[0:ZR, 0:D].astype(F32)
        wo_ref[...] = o_ref[0:ZR, 0:D].astype(F32)
        k = k_ref[...].astype(F32).T
        wk_ref[...] = jnp.concatenate([k[128:384], k[64:128]], axis=0)[:, 0:ZR]
        wv_ref[...] = v_ref[...].astype(F32).T[0:320, 0:ZR]
        gains_ref[0:1, :] = k_ref[ZR:ZP, :].astype(F32)[0:1, 0:256]
        gains_ref[1:2, :] = o_ref[ZR:ZP, :].astype(F32)[0:1, 0:256]

    @pl.when(info[1] == 0)
    def _():
        emit(qm_ref, qo_ref, km_ref, ko_ref)

    @pl.when(info[1] == 1)
    def _():
        emit(qo_ref, qm_ref, ko_ref, km_ref)


def finish_rest_call(info, qm, qo, km, ko):
    return pl.pallas_call(
        finish_rest_kernel,
        out_shape=(
            jax.ShapeDtypeStruct((ZR, D), F32),
            jax.ShapeDtypeStruct((ZR, D), F32),
            jax.ShapeDtypeStruct((320, ZR), F32),
            jax.ShapeDtypeStruct((320, ZR), F32),
            jax.ShapeDtypeStruct((2, 256), F32),
        ),
        in_specs=[SMEM] + [VMEM] * 4,
        out_specs=(VMEM,) * 5,
        compiler_params=params(32),
        cost_estimate=cost(1e6, 4e6),
        name="finish_rest",
    )(info, qm, qo, km, ko)


def sum_chips(info, terms, passed, dep):
    n_terms = len(terms)

    def body(info, ins, outs, scratch):
        z = info[0]
        for n in range(4):
            zz = lax.rem(z + n, 4)
            outs[n][...] = sum(ins[k][zz].astype(F32) for k in range(n_terms)).astype(BF16)

    return step_call(
        "sum_chips",
        body,
        info,
        (*terms, *passed, dep),
        (((3, Q_ROWS, D), BF16),) * 4 + tuple((p.shape, p.dtype) for p in passed),
        8e6,
        [VMEM] * n_terms + [ANY] * (len(passed) + 1),
        [VMEM] * 4 + [ANY] * len(passed),
        aliases={1 + n_terms + n: 4 + n for n in range(len(passed))},
    )


def join_near(info, keep, recv, from_x, from_y, dep):
    rows = keep.shape[0] // 3
    cut = rows // 2

    def body(info, ins, outs, scratch):
        keep, recv, from_x, from_y, _ = ins
        outs[0][...] = keep[0:rows, :] + recv[0:rows, :]
        for n, (lo, hi) in ((1, (None, from_y)), (2, (from_x, None))):
            for h, extra in enumerate((lo, hi)):
                r = slice(rows * n + cut * h, rows * n + cut * h + cut)
                value = keep[r, :].astype(F32) + recv[r, :].astype(F32)
                if extra is not None:
                    value = value + extra[...].astype(F32)
                outs[n][cut * h : cut * h + cut, :] = value.astype(BF16)

    out = ((rows, KV_LANES), BF16)
    return step_call(
        "join_near",
        body,
        info,
        (keep, recv, from_x, from_y, dep),
        (out,) * 3,
        10e6,
        [VMEM] * 4 + [ANY],
    )


def join_projections(info, keep, recv, h1, acc_o, got_o, dep):
    t = h1.shape[0]

    def body(info, ins, outs, scratch):
        outs[0][...] = ins[0][...] + ins[1][...]
        for i in range(t // ROWS):
            r = slice(ROWS * i, ROWS * i + ROWS)
            value = ins[2][r, :] + ins[3][r, :] + ins[4][r, 0:D].astype(F32)
            outs[1][:, r] = value.astype(BF16).T

    return step_call(
        "join_projections",
        body,
        info,
        (keep, recv, h1, acc_o, got_o, dep),
        ((keep.shape, BF16), ((D, t), BF16)),
        14e6,
        [VMEM] * 5 + [ANY],
    )


def halve_rows(info, whole, dep, axis):
    cut = whole.shape[axis] // 2
    shape = whole.shape[:axis] + (cut,) + whole.shape[axis + 1 :]
    at = (slice(None),) * axis

    def body(info, ins, outs, scratch):
        for n in range(2):
            outs[n][...] = ins[0][at + (slice(cut * n, cut * n + cut),)]

    return step_call(
        "halve_rows", body, info, (whole, dep), ((shape, BF16),) * 2, 2e6, [VMEM, ANY]
    )


def join_pairs(info, name, pairs, deps):
    flat = [a for pair in pairs for a in pair]

    def body(info, ins, outs, scratch):
        at = 0
        for n, pair in enumerate(pairs):
            terms = [ins[at + k][...].astype(F32) for k in range(len(pair))]
            at += len(pair)
            outs[n][...] = sum(terms).astype(BF16)

    return step_call(
        name,
        body,
        info,
        (*flat, *deps),
        tuple((pair[0].shape, BF16) for pair in pairs),
        4e6,
        [VMEM] * len(flat) + [ANY] * len(deps),
    )


def cut_for_chips(info, keep, recv, deps):
    rows = ZP // 4

    def body(info, ins, outs, scratch):
        chip = info[3]
        for r in range(4):
            at = pl.ds(pl.multiple_of((chip ^ r) * rows, 16), rows)
            outs[r][...] = ins[0][:, at, :] + ins[1][:, at, :]

    piece = ((4, rows, keep.shape[2]), BF16)
    return step_call(
        "cut_for_chips", body, info, (keep, recv, *deps), (piece,) * 4, 3e6, [VMEM] * 2 + [ANY] * len(deps)
    )


def cut_for_z(info, terms, whole):
    shape = terms[0].shape[1:]
    cut = whole.shape[0] // 2

    def body(info, ins, outs, scratch):
        z = info[0]
        for n in range(4):
            zz = lax.rem(z + n, 4)
            outs[n][...] = sum(ins[k][zz].astype(F32) for k in range(4)).astype(BF16)
        for n in range(2):
            outs[4 + n][...] = ins[4][cut * n : cut * n + cut, :]

    half = ((cut, whole.shape[1]), BF16)
    return step_call(
        "cut_for_z", body, info, (*terms, whole), ((shape, BF16),) * 4 + (half,) * 2, 3e6
    )


def place_chips(info, pieces, pairs):
    rows, width = pieces[0].shape
    cut = pairs[0][0].shape[0]

    def body(info, ins, outs, scratch):
        chip = info[3]
        for r in range(4):
            outs[0][pl.ds(pl.multiple_of((chip ^ r) * rows, 16), rows), :] = ins[r][...]
        for n in range(2):
            outs[1][cut * n : cut * n + cut, :] = ins[4 + 2 * n][...] + ins[5 + 2 * n][...]

    return step_call(
        "place_chips",
        body,
        info,
        (*pieces, *pairs[0], *pairs[1]),
        (((4 * rows, width), BF16), ((2 * cut, pairs[0][0].shape[1]), BF16)),
        2e6,
    )


def rows_after(x, start, size, tok, axis=0):
    return lax.dynamic_slice_in_dim(x, start + tok, size, axis=axis)


def z_shift(x, step):
    n = 4
    return lax.ppermute(x, "fsdp", [(i, (i + step) % n) for i in range(n)])


def c_swap(x, bit):
    n = lax.axis_size("ctx")
    return lax.ppermute(x, "ctx", [(i, i ^ bit) for i in range(n)])


def bits_from(b):
    bits = []
    while b < lax.axis_size("ctx"):
        bits.append(b)
        b *= 2
    return bits


def chip_near(kv):
    if lax.axis_size("ctx") != 8:
        return ()
    return c_swap(kv, 2), c_swap(kv, 4)


def chip_far(kv, near):
    if not near:
        return [lax.all_gather(kv, "ctx", axis=0, tiled=True)]
    cut = kv.shape[0] // 2
    across_x, across_y = near
    far_lo = c_swap(across_x[:cut], 4)
    far_hi = c_swap(across_y[cut:], 2)
    chip = [kv, across_x, across_y, far_lo, far_hi]
    return chip + [c_swap(part, 1) for part in chip]


def kv_entry(position, per_dev, me, n):
    if n != 8:
        return position
    owner, within = position // per_dev, position % per_dev
    rel = owner ^ me
    cut = per_dev // 2
    far = (rel // 2) == 3
    late = far & (within >= cut)
    which = (rel % 2) * 5 + rel // 2 + late.astype(jnp.int32)
    return which * 1024 + jnp.where(late, within - cut, within)


def kv_slot(position, per_dev, me):
    owner, within = position // per_dev, position % per_dev
    rel = owner ^ me
    return ((rel % 2) * 4 + rel // 2) * per_dev + within


def on_device(
    tokens,
    cotangent,
    doc_lengths,
    deal,
    attn_gain,
    w_query,
    w_key,
    w_value,
    w_out,
    mlp_gain,
    w_gate,
    w_up,
    w_down,
):
    me = lax.axis_index("ctx")
    n_ctx = lax.axis_size("ctx")
    z = lax.axis_index("fsdp")
    core = me % 2
    near_me = me % 8
    chip = near_me // 2
    parity = (chip + chip // 2) % 2
    info = jnp.stack([z, core, near_me, chip, parity]).astype(jnp.int32)
    tok_rows = tokens.shape[1]
    per_dev = tok_rows // BLK
    deal_row = deal[0]
    blocks = deal_row.shape[0]
    group_size = blocks * BLK
    doc_lens = doc_lengths[0]
    seq_count = doc_lens.shape[0]
    length = group_size // seq_count
    x_turned = tokens[0].T
    cot_turned = cotangent[0].T

    gains_wide = jnp.concatenate(
        [attn_gain[:, None], mlp_gain[:, None], jnp.zeros((ZR, QKV - 1602), BF16)], axis=1
    )
    w_parts = [w_query, w_key[:, 256:], w_key[:, :256], w_value, gains_wide]
    start = jnp.minimum(32 * near_me, ZR - 32)
    w_mine = jnp.concatenate(
        [lax.dynamic_slice_in_dim(w, start, 32, axis=0) for w in w_parts], axis=1
    )
    w_z = [z_shift(w_mine, -1), z_shift(w_mine, 2), z_shift(w_mine, 1)]
    own_half, packed = prep_weights(info, w_gate, w_up, w_down.T, w_out)
    w_got, packed = stack_weights(info, w_z, packed)
    over_z = lax.all_gather(packed, "fsdp", axis=0, tiled=False)
    cot_there = c_swap(cot_turned, 1)
    w_chips = [w_got, c_swap(w_got, 2), c_swap(w_got, 4), c_swap(w_got, 6)]
    w_pieces = [jnp.concatenate(w_parts, axis=1)]
    for piece in w_chips:
        w_pieces += [piece, c_swap(piece, 1)]

    block_ids = jnp.arange(blocks, dtype=jnp.int32)
    mine = lax.dynamic_slice_in_dim(deal_row, me * per_dev, per_dev)
    seq_blocks = jnp.maximum(
        mine[:, None] - (NWB - 1) + jnp.arange(NWB, dtype=jnp.int32)[None, :], 0
    )
    position = jnp.sum(
        jnp.where(seq_blocks[:, :, None] == deal_row[None, None, :], block_ids, 0), axis=-1
    )
    tab = kv_entry(position, per_dev, me, n_ctx).astype(jnp.int32)
    doc_ends = (
        jnp.cumsum(doc_lens, axis=1) + (jnp.arange(seq_count, dtype=jnp.int32) * length)[:, None]
    ).reshape(-1)
    doc_starts = doc_ends - doc_lens.reshape(-1)
    q_time = mine[:, None] * BLK + jnp.arange(BLK, dtype=jnp.int32)[None, :]
    begin = jnp.max(jnp.where(q_time[..., None] >= doc_starts, doc_starts, 0), axis=-1)
    lo = jnp.maximum(begin, q_time - (WIN - 1)) - (mine[:, None] * BLK - WIN)
    lo = lo[:, None, :].astype(jnp.int32)
    pos = (q_time - begin).reshape(-1)
    half_dim = HD // 2
    freqs = ROPE_THETA ** (-jnp.arange(half_dim, dtype=F32) * (2.0 / HD))
    angle = pos.astype(F32)[:, None] * freqs[None, :]
    cos_tab, sin_tab = jnp.cos(angle), jnp.sin(angle)
    cos_wide = jnp.tile(cos_tab, (1, 4))
    sin_wide = jnp.tile(jnp.concatenate([-sin_tab, sin_tab], axis=1), (1, 2))

    attn_in, q_low, kv_low, w_all, gains, x, cos_turn, sin_turn = pre_call(
        info, x_turned, cos_wide, sin_wide, w_pieces
    )
    kvs = chip_far(kv_low, chip_near(kv_low))

    first, second, out_here = split_quarters(info, over_z, kvs[3:5] if n_ctx == 8 else kvs)
    first_on, second_on = c_swap(first, 2), c_swap(second, 4)
    mid_low, recips, probs = fwd_call(tab, lo, q_low, kvs)
    out_there = [
        c_swap(out_here, 1),
        c_swap(pick_out_rows(info, first_on, second_on, mid_low), 1),
    ]
    here = (first, second, first_on, second_on)
    h1, mlp_in, w_out_all = pro_call(
        info, mid_low, x, gains, w_out, here, out_there, cot_there
    )
    acc_o, acc_g, send_o, send_g, p_both, *q_both = ffn_call(
        info, mlp_in, c_swap(mlp_in, 1), cot_turned, cot_there, own_half, here
    )
    p_sum = lax.psum_scatter(p_both, "fsdp", scatter_dimension=0, tiled=True)[0]
    q_got = [c_swap(q_both[r], 2 * r) for r in range(1, 4)]
    grad_hidden, grad_mid, go = epi_call(
        info, h1, acc_g, c_swap(send_g, 1), cot_turned, gains, w_out_all, mid_low
    )
    got_o = c_swap(send_o, 1)

    if n_ctx == 8:
        out_units = (3, 1, 3, 1)
        slots = kv_slot(position, per_dev, me).astype(jnp.int32)
    else:
        out_units = (NWB,)
        n_slots = per_dev * NWB
        flat_pos = position.reshape(-1)
        order = jnp.arange(n_slots, dtype=jnp.int32)
        slots = jnp.min(
            jnp.where(flat_pos[:, None] == flat_pos[None, :], order[None, :], n_slots), axis=1
        ).reshape(per_dev, NWB)
        source = jnp.min(
            jnp.where(block_ids[:, None] == flat_pos[None, :], order[None, :], n_slots), axis=1
        )

    def own_rows(parts):
        width = parts[0].shape[1]
        padded = jnp.concatenate(
            [parts[0].reshape(n_slots, BLK, width), jnp.zeros((1, BLK, width), BF16)], axis=0
        )
        spread = jnp.take(padded, source, axis=0).reshape(group_size, width)
        own = lax.psum_scatter(spread, "ctx", scatter_dimension=0, tiled=True)
        return own, (own, jnp.zeros_like(own), jnp.zeros_like(own))

    back_args = (
        tab, slots, out_units, q_low, grad_mid, mid_low, recips, probs, cos_turn, sin_turn, kvs
    )
    dq, *kv_parts = bwd_call(0, per_dev, (), (), *back_args)
    q_terms = (q_both[0], *q_got)
    if n_ctx == 8:
        keep_near, keep_far, send_near, send_far = kv_parts
        *q_parts, send_near, send_far = sum_chips(info, q_terms, (send_near, send_far), dq)
        recv_far, recv_near = c_swap(send_far, 1), c_swap(send_near, 1)
        cut = keep_far.shape[0] // 2
        far_lo = keep_far[:cut] + recv_far[:cut]
        far_hi = keep_far[cut:] + recv_far[cut:]
        from_x, from_y = c_swap(far_lo, 2), c_swap(far_hi, 4)
        far = far_lo
    else:
        q_parts = sum_chips(info, q_terms, (), dq)
        ready, sums = own_rows(kv_parts)
        far = ready
    q_z = [z_shift(q_parts[step], step) for step in (1, 2, 3)]
    qo_keep, qo_send, part = post_q_call(info, attn_in, dq, w_all, go, far)
    qo_recv = c_swap(qo_send, 1)
    qo_both, output = join_projections(info, qo_keep, qo_recv, h1, acc_o, got_o, far)
    if n_ctx == 8:
        own, to_x, to_y = join_near(info, keep_near, recv_near, from_x, from_y, qo_both)
        sums = (own, c_swap(to_x, 2), c_swap(to_y, 4))
        ready = to_x
    qo_sum = lax.psum_scatter(qo_both, "fsdp", scatter_dimension=0, tiled=True)[0]

    p_l, p_r = halve_rows(info, p_sum, ready, 1)
    p_l, p_r, q_mine = join_pairs(
        info,
        "join_chips",
        ((p_l, c_swap(p_l, 2)), (p_r, c_swap(p_r, 4)), (q_parts[0], *q_z)),
        sums[1:],
    )
    p_got = c_swap(p_l, 4), c_swap(p_r, 2)
    for b in bits_from(8):
        q_mine = q_mine + c_swap(q_mine, b)
    q_all = [q_mine, c_swap(q_mine, 2), c_swap(q_mine, 4), c_swap(q_mine, 6)]
    kv_keep, kv_send, input_grad = post_kv_call(
        info, sums, cos_wide, sin_wide, attn_in, part, w_all, x, grad_hidden, gains, (p_l, q_mine)
    )
    kv_pieces = cut_for_chips(info, kv_keep, c_swap(kv_send, 1), ())
    kv_pieces = [kv_pieces[0]] + [c_swap(kv_pieces[r], 2 * r) for r in range(1, 4)]
    p_l, p_r = join_pairs(
        info, "join_chips", ((p_l, p_got[0]), (p_r, p_got[1])), (kv_pieces[0], *q_all[1:])
    )
    p_sum = jnp.concatenate([p_l, p_r], axis=1)
    for b in bits_from(8):
        p_sum = p_sum + c_swap(p_sum, b)
    q_all = jnp.stack(q_all)
    *kv_z, qo_l, qo_r = cut_for_z(info, kv_pieces, qo_sum)
    kv_terms = [kv_z[0]] + [z_shift(kv_z[step], step) for step in (1, 2, 3)]
    kv_mine, qo_l, qo_r = join_pairs(
        info, "join_z", (kv_terms, (qo_l, c_swap(qo_l, 2)), (qo_r, c_swap(qo_r, 4))), ()
    )
    for b in bits_from(8):
        kv_mine = kv_mine + c_swap(kv_mine, b)
    kv_all = [kv_mine] + [c_swap(kv_mine, 2 * r) for r in range(1, 4)]
    kv_sum, qo_sum = place_chips(
        info, kv_all, ((qo_l, c_swap(qo_l, 4)), (qo_r, c_swap(qo_r, 2)))
    )
    for b in bits_from(8):
        qo_sum = qo_sum + c_swap(qo_sum, b)

    gate_grad, up_grad, down_grad = finish_ffn_call(
        info, p_sum, c_swap(p_sum, 1), q_all, c_swap(q_all, 1)
    )
    query_grad, out_grad, key_grad, value_grad, gain_grads = finish_rest_call(
        info, qo_sum, c_swap(qo_sum, 1), kv_sum, c_swap(kv_sum, 1)
    )

    return (
        output.T[None],
        input_grad.T[None],
        gain_grads[0, :ZR],
        query_grad,
        key_grad.T,
        value_grad.T,
        out_grad,
        gain_grads[1, :ZR],
        gate_grad,
        up_grad,
        down_grad.T,
    )


def solution(mesh):
    in_specs = (
        P("fsdp", "ctx", None),
        P("fsdp", "ctx", None),
        P("fsdp", None, None),
        P("fsdp", None),
        P("fsdp"),
        P("fsdp", None),
        P("fsdp", None),
        P("fsdp", None),
        P("fsdp", None),
        P("fsdp"),
        P(None, "fsdp"),
        P(None, "fsdp"),
        P("fsdp", None),
    )
    out_specs = (
        P("fsdp", "ctx", None),
        P("fsdp", "ctx", None),
        P("fsdp"),
        P("fsdp", None),
        P("fsdp", None),
        P("fsdp", None),
        P("fsdp", None),
        P("fsdp"),
        P(None, "fsdp"),
        P(None, "fsdp"),
        P("fsdp", None),
    )
    return jax.shard_map(
        on_device, mesh=mesh, in_specs=in_specs, out_specs=out_specs, check_vma=False
    )
```

time: 651 us -> 507 us (0.78)
  starting transfers between devices: 120 us -> 59.5 us
  waiting for transfers between devices: 216 us -> 161 us
  other arithmetic: 54.3 us -> 6.93 us
  Pallas kernels: 156 us -> 201 us
  local copies, waits for them, and re-layouts: 95.6 us -> 55 us
  between operations: 2.06 us -> 15.1 us
    ppermute x23 -> x9, waiting for transfers between devices: 158 us -> 40.3 us  [z_shift(): return lax.ppermute(x, 'fsdp', [(i, (i + step) % n) for i in range(n)])]
    ppermute x23 -> x9, starting transfers between devices: 82.2 us -> 16.1 us  [z_shift(): return lax.ppermute(x, 'fsdp', [(i, (i + step) % n) for i in range(n)])]
    ppermute x40 -> x56, waiting for transfers between devices: 58.1 us -> 108 us  [c_swap(): return lax.ppermute(x, 'ctx', [(i, i ^ bit) for i in range(n)])]
    pallas_call x4 -> x22, Pallas kernels: 116 us -> 158 us  [the longest x1 50.3 us: ffn_call(): pl.pallas_call(ffn_kernel, out_shape=(jax.ShapeDtypeStruct((t, D), F32),...]
    add x22 -> x1, other arithmetic: 29.4 us -> 0.89 us  [on_device(): far_hi = keep_far[cut:] + recv_far[cut:]]
    slice x26 -> x5, local copies, waits for them, and re-layouts: 18 us -> 3.48 us  [the longest x2 1.79 us: on_device(): w_parts = [w_query, w_key[:, 256:], w_key[:, :256], w_value, gains_wide]]
    ppermute x2 -> x1, local copies, waits for them, and re-layouts: 14.6 us -> 1.39 us  [c_swap(): return lax.ppermute(x, 'ctx', [(i, i ^ bit) for i in range(n)])]
    all_gather x0 -> x1, waiting for transfers between devices: none -> 11.8 us  [on_device(): over_z = lax.all_gather(packed, 'fsdp', axis=0, tiled=False)]
  transfers between devices with their start and end apart: 63 -> 68, of which waited for: 20 -> 29; matrix products, arithmetic and copies ran while one was open for 16% -> 3% of each run, Pallas kernels for 15% -> 28%
where the time goes in v2:
time: 507 us; the launch traced here: 498 us
  Pallas kernels  201 us (40%)
  waiting for transfers between devices  161 us (32%)
  starting transfers between devices  59.5 us (12%)
  local copies, waits for them, and re-layouts  55 us (11%)
  between operations  15.1 us (3%)
  other arithmetic  6.93 us (1%)
    ppermute x56, waiting for transfers between devices, c_swap(): return lax.ppermute(x, 'ctx', [(i, i ^ bit) for i in range(n)])  108 us
    pallas_call x1, Pallas kernels, ffn_call(): pl.pallas_call(ffn_kernel, out_shape=(jax.ShapeDtypeStruct((t, D), F32),...  50.3 us
    ppermute x56, starting transfers between devices, c_swap(): return lax.ppermute(x, 'ctx', [(i, i ^ bit) for i in range(n)])  43 us
    unnamed x146, local copies, waits for them, and re-layouts  41.2 us
    ppermute x9, waiting for transfers between devices, z_shift(): return lax.ppermute(x, 'fsdp', [(i, (i + step) % n) for i in range(n)])  40.3 us
    pallas_call x1, Pallas kernels, bwd_call(): pl.pallas_call(lambda *refs: bwd_kernel(n_kv, len(deps), first, prev, out...  39.4 us
    pallas_call x1, Pallas kernels, fwd_call(): pl.pallas_call(lambda *refs: fwd_kernel(n_kv, *refs), grid=(blocks,), out...  34.7 us
    pallas_call x14, Pallas kernels, step_call(): pl.pallas_call(kernel, out_shape=tuple((jax.ShapeDtypeStruct(shape, dtype...  25 us
  transfers between devices with their start and end apart: 68, of which 29 were waited for; matrix products, arithmetic and copies ran while one was open for 3% of the time, Pallas kernels for 28%

profile of v2, /device:TPU:0, one launch (start us, length us, event | category | flops | bytes accessed | tf_op | source)
XLA Modules:
  0.0 497.8 jit_solution(16453461362405108723)
XLA Ops:
  32.7 7.9 %collective-permute-done.8.refs_7_ = bf16[3,32,1664]{2,1,0:T(8,128)(2,1)} collective-permute-done((bf16[3,32,1664]{2,1,0:T(8,128)(2,1)S(1)}, bf16[3,32,1664]{2,1,0:T(8,128)(2,1)}, u32[]{:S(2)}, u32[]{:S(2)}) %collective-permute-start.8) | collective-permute-done | bytes 319520 | tf_op jit(solution)/shard_map/ppermute | solution.py:1236
  40.5 5.7 %collective-permute-done.6.refs_5_ = bf16[3,32,1664]{2,1,0:T(8,128)(2,1)} collective-permute-done((bf16[3,32,1664]{2,1,0:T(8,128)(2,1)S(1)}, bf16[3,32,1664]{2,1,0:T(8,128)(2,1)}, u32[]{:S(2)}, u32[]{:S(2)}) %collective-permute-start.6) | collective-permute-done | bytes 319520 | tf_op jit(solution)/shard_map/ppermute | solution.py:1236
  51.1 8.1 %pre.1 = (bf16[768,960]{1,0:T(8,128)(2,1)S(1)}, bf16[768,960]{1,0:T(8,128)(2,1)S(1)}, bf16[768,640]{1,0:T(8,128)(2,1)}, bf16[960,1664]{1,0:T(8,128)(2,1)}, f32[8...) custom-call(s32[5]{0:T(128)S(1)} %stack.38.info_ref.info.refs_0_, ...), custom_call_target="tpu_custom_call" | custom-call | flops 1 | bytes 1 | tf_op jit(solution)/shard_map/pre/pallas_call | solution.py:290
  65.0 21.6 %collective-permute-done.11.refs_5_.refs_11_ = bf16[768,640]{1,0:T(8,128)(2,1)S(1)} collective-permute-done((bf16[768,640]{1,0:T(8,128)(2,1)}, bf16[768,640]{1,0:T(8,128)(2,1)S(1)}, u32[]{:S(2)}, u32[]{:S(2)}) %collective-permute-start.11) | collective-permute-done | bytes 983072 | tf_op jit(solution)/shard_map/ppermute | solution.py:1236
  89.9 9.3 %collective-permute-done.13.refs_7_.refs_2_.refs_13_ = bf16[384,640]{1,0:T(8,128)(2,1)S(1)} collective-permute-done((bf16[384,640]{1,0:T(8,128)(2,1)S(1)}, bf16[384,640]{1,0:T(8,128)(2,1)S(1)}, u32[]{:S(2)}, u32[]{:S(2)}) %collective-permute-start.13) | collective-permute-done | bytes 491552 | tf_op jit(solution)/shard_map/ppermute | solution.py:1236
  102.3 11.8 %all-gather.3.cloned.1.call-done = bf16[2176,960]{1,0:T(8,128)(2,1)} async-done(((bf16[544,960]{1,0:T(8,128)(2,1)}), bf16[2176,960]{1,0:T(8,128)(2,1)}) %all-gather.3.cloned.1.call-update) | async-done | bytes 4177936 | tf_op jit(solution)/shard_map/all_gather | solution.py:1327
  135.8 34.7 %attend.1 = (bf16[768,960]{1,0:T(8,128)(2,1)}, f32[6,16,128]{2,1,0:T(8,128)S(1)}, bf16[6,1152,1920]{2,1,0:T(8,128)(2,1)}) custom-call(s32[6,9]{1,0:T(8,128)S(1)} %get-tuple-element.189.refs_0_, s32[6,1,128]{2,1,0:T(1,128)S(1)} %maximum_subtract_fusion.refs_1_, bf16[768,960]{1,0:T(8,128)(2,1)} %copy-done.4, ...), custom_call_target="tpu_custom_call" | custom-call | flops 1 | bytes 1 | tf_op jit(solution)/shard_map/attend/pallas_call | solution.py:417
  176.6 6.6 %out_projection.1 = (f32[768,960]{1,0:T(8,128)}, bf16[768,1024]{1,0:T(8,128)(2,1)S(1)}, bf16[960,960]{1,0:T(8,128)(2,1)}) custom-call(s32[5]{0:T(128)S(1)} %stack.38.info_ref.info.refs_0_, bf16[768,960]{1,0:T(8,128)(2,1)S(1)} %copy-done.1, bf16[768,960]{1,0:T(8,128)(2,1)S(1)} %copy-done.8, f32[8,960]{1,0:T(8,128)S(1)} %copy-done.48, ...), custom_call_target="tpu_custom_call" | custom-call | flops 1 | bytes 1 | tf_op jit(solution)/shard_map/out_projection/pallas_call | solution.py:646
  189.1 50.3 %feed_forward.1 = (f32[768,960]{1,0:T(8,128)}, f32[768,960]{1,0:T(8,128)}, bf16[768,1024]{1,0:T(8,128)(2,1)}, bf16[768,1024]{1,0:T(8,128)(2,1)}, bf16[4,3,128,96...) custom-call(s32[5]{0:T(128)} %copy-done.51, ...), custom_call_target="tpu_custom_call" | custom-call | flops 1 | bytes 1 | tf_op jit(solution)/shard_map/feed_forward/pallas_call | solution.py:797
  240.2 3.5 collective-permute-start.28
  243.7 10.9 %feed_forward_norm_back.1 = (f32[768,960]{1,0:T(8,128)}, bf16[768,960]{1,0:T(8,128)(2,1)S(1)}, bf16[4,256,1024]{2,1,0:T(8,128)(2,1)}) custom-call(s32[5]{0:T(128)S(1)} %copy-done.52, f32[768,960]{1,0:T(8,128)} %get-tuple-element.108.h1_ref.refs_2_, f32[768,960]{1,0:T(8,128)} %get-tuple-element.111.acc_g, ...), custom_call_target="tpu_custom_call" | custom-call | flops 1 | bytes 1 | tf_op jit(solution)/shard_map/feed_forward_norm_back/pallas_call | solution.py:879
  255.7 39.4 %attend_back_0.1 = (bf16[768,960]{1,0:T(8,128)(2,1)}, bf16[2304,640]{1,0:T(8,128)(2,1)}, bf16[768,640]{1,0:T(8,128)(2,1)}, bf16[2304,640]{1,0:T(8,128)(2,1)}, bf16[768,640]{1,0:T(8,128)(2,1)}) custom-call(s32[6,9]{1,0:T(8,128)} %copy-done.58, s32[6,9]{1,0:T(8,128)} %get-tuple-element.188.refs_1_, bf16[768,960]{1,0:T(8,128)(2,1)} %copy-done.4, ...), custom_call_target="tpu_custom_call" | custom-call | flops 1 | bytes 1 | tf_op jit(solution)/shard_map/attend_back_0/pallas_call | solution.py:568
  311.4 6.2 %query_back.1 = (bf16[4,256,1024]{2,1,0:T(8,128)(2,1)S(1)}, bf16[4,256,1024]{2,1,0:T(8,128)(2,1)S(1)}, f32[768,960]{1,0:T(8,128)S(1)}) custom-call(s32[5]{0:T(128)S(1)} %copy-done.52, bf16[768,960]{1,0:T(8,128)(2,1)S(1)} %copy-done.6, bf16[768,960]{1,0:T(8,128)(2,1)S(1)} %copy-done.10, bf16[960,1664]{1,0:T(8,128)(2,1)} %get-tuple-element.120.w_ref.refs_8_, ...), custom_call_target="tpu_custom_call" | custom-call | flops 1 | bytes 1 | tf_op jit(solution)/shard_map/query_back/pallas_call | solution.py:925
  319.9 8.0 %collective-permute-done.31.refs_4_ = bf16[768,1024]{1,0:T(8,128)(2,1)S(1)} collective-permute-done((bf16[768,1024]{1,0:T(8,128)(2,1)S(1)}, bf16[768,1024]{1,0:T(8,128)(2,1)S(1)}, u32[]{:S(2)}, u32[]{:S(2)}) %collective-permute-start.31) | collective-permute-done | bytes 1572896 | tf_op jit(solution)/shard_map/ppermute | solution.py:1236
  327.9 4.4 join_projections.1
  334.6 12.1 %collective-permute-done.34.refs_3_ = bf16[384,640]{1,0:T(8,128)(2,1)S(1)} collective-permute-done((bf16[384,640]{1,0:T(8,128)(2,1)S(1)}, bf16[384,640]{1,0:T(8,128)(2,1)S(1)}, u32[]{:S(2)}, u32[]{:S(2)}) %collective-permute-start.34) | collective-permute-done | bytes 491552 | tf_op jit(solution)/shard_map/ppermute | solution.py:1236
  359.4 14.0 %collective-permute-done.39.refs_5_ = bf16[3,48,960]{2,1,0:T(8,128)(2,1)} collective-permute-done((bf16[3,48,960]{2,1,0:T(8,128)(2,1)}, bf16[3,48,960]{2,1,0:T(8,128)(2,1)}, u32[]{:S(2)}, u32[]{:S(2)}) %collective-permute-start.39) | collective-permute-done | bytes 276512 | tf_op jit(solution)/shard_map/ppermute | solution.py:1231
  374.3 17.0 %collective-permute-done.40.refs_6_ = bf16[3,48,960]{2,1,0:T(8,128)(2,1)} collective-permute-done((bf16[3,48,960]{2,1,0:T(8,128)(2,1)}, bf16[3,48,960]{2,1,0:T(8,128)(2,1)}, u32[]{:S(2)}, u32[]{:S(2)}) %collective-permute-start.40) | collective-permute-done | bytes 276512 | tf_op jit(solution)/shard_map/ppermute | solution.py:1231
  393.2 6.6 %collective-permute-done.41.refs_7_ = bf16[3,48,960]{2,1,0:T(8,128)(2,1)S(1)} collective-permute-done((bf16[3,48,960]{2,1,0:T(8,128)(2,1)S(1)}, bf16[3,48,960]{2,1,0:T(8,128)(2,1)S(1)}, u32[]{:S(2)}, u32[]{:S(2)}) %collective-permute-start.41) | collective-permute-done | bytes 276512 | tf_op jit(solution)/shard_map/ppermute | solution.py:1231
  402.4 10.5 %key_value_back.1 = (bf16[4,256,384]{2,1,0:T(8,128)(2,1)S(1)}, bf16[4,256,384]{2,1,0:T(8,128)(2,1)S(1)}, bf16[960,768]{1,0:T(8,128)(2,1)}) custom-call(s32[5]{0:T(128)S(1)} %copy-done.52, bf16[768,640]{1,0:T(8,128)(2,1)S(1)} %copy-done.43, bf16[768,640]{1,0:T(8,128)(2,1)} %copy-done.18, bf16[768,640]{1,0:T(8,128)(2,1)} %copy-done.17, ...), custom_call_target="tpu_custom_call" | custom-call | flops 1 | bytes 1 | tf_op jit(solution)/shard_map/key_value_back/pallas_call | solution.py:991
  425.2 10.3 %collective-permute-done.44.refs_2_ = bf16[4,64,384]{2,1,0:T(8,128)(2,1)S(1)} collective-permute-done((bf16[4,64,384]{2,1,0:T(8,128)(2,1)S(1)}, bf16[4,64,384]{2,1,0:T(8,128)(2,1)S(1)}, u32[]{:S(2)}, u32[]{:S(2)}) %collective-permute-start.44) | collective-permute-done | bytes 196640 | tf_op jit(solution)/shard_map/ppermute | solution.py:1236
  443.7 5.3 %collective-permute-done.59.refs_3_ = bf16[3,64,960]{2,1,0:T(8,128)(2,1)S(1)} collective-permute-done((bf16[3,64,960]{2,1,0:T(8,128)(2,1)}, bf16[3,64,960]{2,1,0:T(8,128)(2,1)S(1)}, u32[]{:S(2)}, u32[]{:S(2)}) %collective-permute-start.59) | collective-permute-done | bytes 368672 | tf_op jit(solution)/shard_map/ppermute | solution.py:1236
  464.8 4.2 collective-permute-done.53.refs_3_
  481.3 6.1 %finish_feed_forward.1 = (f32[960,640]{1,0:T(8,128)}, f32[960,640]{1,0:T(8,128)}, f32[960,640]{1,0:T(8,128)}) custom-call(s32[5]{0:T(128)S(1)} %copy-done.52, bf16[3,128,960]{2,1,0:T(8,128)(2,1)S(1)} %constant_dynamic-update-slice_fusion.pm_ref, bf16[3,128,960]{2,1,0:T(8,128)(2,1)S(1)} %copy.73.po_ref, bf16[4,3,48,960]{3,2,1,0:T(8,128)(2,1)S(1)} %pad_maximum_fusion.qm_ref, ...), custom_call_target="tpu_custom_call" | custom-call | flops 1 | bytes 1 | tf_op jit(solution)/shard_map/finish_feed_forward/pallas_call | solution.py:1017
  (326 shorter events, 168.1 us)
Async XLA Ops:
  7.2 106.9 %all-gather.3.cloned.1.call-start = ((), (), s32[]{:S(2)}) async-start(), calls=%async_computation.4 | async-start | bytes 5570560 | tf_op jit(solution)/shard_map/all_gather | solution.py:1327
  27.5 329.9 %reduce-scatter.3.cloned.1.call-start = ((), (), s32[]{:S(2)}) async-start(), calls=%async_computation.2 | async-start | bytes 3932160 | tf_op jit(solution)/shard_map/reduce_scatter | solution.py:1378
  62.7 24.0 %collective-permute-start.11 = (bf16[768,640]{1,0:T(8,128)(2,1)}, bf16[768,640]{1,0:T(8,128)(2,1)S(1)}, u32[]{:S(2)}, u32[]{:S(2)}) collective-permute-start(bf16[768,640]{1,0:T(8,128)(2,1)} %get-tuple-element.100.refs_3_.refs_9_), channel_id=1, source_target_pairs={{0,16},{4,20},{8,24},{12,28},{16,0},{20,4},{24,8},{28,12},{1,17},{... | collective-permute-start | bytes 2949128 | tf_op jit(solution)/shard_map/ppermute | solution.py:1236
  64.2 24.0 %collective-permute-start.10 = (bf16[768,640]{1,0:T(8,128)(2,1)}, bf16[768,640]{1,0:T(8,128)(2,1)}, u32[]{:S(2)}, u32[]{:S(2)}) collective-permute-start(bf16[768,640]{1,0:T(8,128)(2,1)} %get-tuple-element.100.refs_3_.refs_9_), channel_id=1, source_target_pairs={{0,8},{4,12},{8,0},{12,4},{16,24},{20,28},{24,16},{28,20},{1,9},{5... | collective-permute-start | bytes 2949128 | tf_op jit(solution)/shard_map/ppermute | solution.py:1236
  65.0 59.0 %collective-permute-start.14 = (bf16[768,640]{1,0:T(8,128)(2,1)}, bf16[768,640]{1,0:T(8,128)(2,1)}, u32[]{:S(2)}, u32[]{:S(2)}) collective-permute-start(bf16[768,640]{1,0:T(8,128)(2,1)} %get-tuple-element.100.refs_3_.refs_9_), channel_id=1, source_target_pairs={{0,4},{4,0},{8,12},{12,8},{16,20},{20,16},{24,28},{28,24},{1,5},{5... | collective-permute-start | bytes 2949128 | tf_op jit(solution)/shard_map/ppermute | solution.py:1236
  120.5 50.1 %collective-permute-start.19 = (bf16[816,960]{1,0:T(8,128)(2,1)}, bf16[816,960]{1,0:T(8,128)(2,1)S(1)}, u32[]{:S(2)}, u32[]{:S(2)}) collective-permute-start(bf16[816,960]{1,0:T(8,128)(2,1)} %get-tuple-element.105.refs_0_), channel_id=1, source_target_pairs={{0,8},{4,12},{8,0},{12,4},{16,24},{20,28},{24,16},{28,20},{1,9},{5... | collective-permute-start | bytes 4700168 | tf_op jit(solution)/shard_map/ppermute | solution.py:1236
  122.0 48.6 %collective-permute-start.20 = (bf16[816,960]{1,0:T(8,128)(2,1)}, bf16[816,960]{1,0:T(8,128)(2,1)}, u32[]{:S(2)}, u32[]{:S(2)}) collective-permute-start(bf16[816,960]{1,0:T(8,128)(2,1)} %get-tuple-element.106.refs_1_), channel_id=1, source_target_pairs={{0,16},{4,20},{8,24},{12,28},{16,0},{20,4},{24,8},{28,12},{1,17},{... | collective-permute-start | bytes 4700168 | tf_op jit(solution)/shard_map/ppermute | solution.py:1236
  124.0 51.3 %collective-permute-start.23 = (bf16[960,768]{1,0:T(8,128)(2,1)}, bf16[960,768]{1,0:T(8,128)(2,1)}, u32[]{:S(2)}, u32[]{:S(2)}) collective-permute-start(bf16[960,768]{1,0:T(8,128)(2,1)} %bitcast.21.c0.ct_ref), channel_id=1, source_target_pairs={{0,4},{4,0},{8,12},{12,8},{16,20},{20,16},{24,28},{28,24},{1,5},{5... | collective-permute-start | bytes 4423688 | tf_op jit(solution)/shard_map/ppermute | solution.py:1236
  239.5 198.3 %reduce-scatter.5.cloned.1.call-start = ((), (), s32[]{:S(2)}) async-start(), calls=%async_computation.3 | async-start | bytes 2621440 | tf_op jit(solution)/shard_map/reduce_scatter | solution.py:1435
  240.2 55.0 %collective-permute-start.26 = (bf16[4,3,48,960]{3,2,1,0:T(8,128)(2,1)}, bf16[4,3,48,960]{3,2,1,0:T(8,128)(2,1)S(1)}, u32[]{:S(2)}, u32[]{:S(2)}) collective-permute-start(bf16[4,3,48,960]{3,2,1,0:T(8,128)(2,1)} %get-tuple-element.124), channel_id=1, source_target_pairs={{0,8},{4,12},{8,0},{12,4},{16,24},{20,28},{24,16},{28,20},{1,9},{5... | collective-permute-start | bytes 3317768 | tf_op jit(solution)/shard_map/ppermute | solution.py:1236
  240.2 56.0 %collective-permute-start.27 = (bf16[4,3,48,960]{3,2,1,0:T(8,128)(2,1)}, bf16[4,3,48,960]{3,2,1,0:T(8,128)(2,1)S(1)}, u32[]{:S(2)}, u32[]{:S(2)}) collective-permute-start(bf16[4,3,48,960]{3,2,1,0:T(8,128)(2,1)} %get-tuple-element.125), channel_id=1, source_target_pairs={{0,16},{4,20},{8,24},{12,28},{16,0},{20,4},{24,8},{28,12},{1,17},{... | collective-permute-start | bytes 3317768 | tf_op jit(solution)/shard_map/ppermute | solution.py:1236
  240.2 57.1 %collective-permute-start.28 = (bf16[4,3,48,960]{3,2,1,0:T(8,128)(2,1)}, bf16[4,3,48,960]{3,2,1,0:T(8,128)(2,1)S(1)}, u32[]{:S(2)}, u32[]{:S(2)}) collective-permute-start(bf16[4,3,48,960]{3,2,1,0:T(8,128)(2,1)} %get-tuple-element.126), channel_id=1, source_target_pairs={{0,24},{4,28},{8,16},{12,20},{16,8},{20,12},{24,0},{28,4},{1,25},{... | collective-permute-start | bytes 3317768 | tf_op jit(solution)/shard_map/ppermute | solution.py:1236
  319.8 27.8 %collective-permute-start.32 = (bf16[2304,640]{1,0:T(8,128)(2,1)}, bf16[2304,640]{1,0:T(8,128)(2,1)}, u32[]{:S(2)}, u32[]{:S(2)}) collective-permute-start(bf16[2304,640]{1,0:T(8,128)(2,1)} %get-tuple-element.136), channel_id=1, source_target_pairs={{0,4},{4,0},{8,12},{12,8},{16,20},{20,16},{24,28},{28,24},{1,5},{5... | collective-permute-start | bytes 8847368 | tf_op jit(solution)/shard_map/ppermute | solution.py:1236
  353.6 46.2 %collective-permute-start.36 = (bf16[768,640]{1,0:T(8,128)(2,1)}, bf16[768,640]{1,0:T(8,128)(2,1)S(1)}, u32[]{:S(2)}, u32[]{:S(2)}) collective-permute-start(bf16[768,640]{1,0:T(8,128)(2,1)} %get-tuple-element.140), channel_id=1, source_target_pairs={{0,16},{4,20},{8,24},{12,28},{16,0},{20,4},{24,8},{28,12},{1,17},{... | collective-permute-start | bytes 2949128 | tf_op jit(solution)/shard_map/ppermute | solution.py:1236
  354.4 45.4 %collective-permute-start.35 = (bf16[768,640]{1,0:T(8,128)(2,1)S(1)}, bf16[768,640]{1,0:T(8,128)(2,1)S(1)}, u32[]{:S(2)}, u32[]{:S(2)}) collective-permute-start(bf16[768,640]{1,0:T(8,128)(2,1)S(1)} %get-tuple-element.139.refs_1_), channel_id=1, source_target_pairs={{0,8},{4,12},{8,0},{12,4},{16,24},{20,28},{24,16},{28,20},{1,9},{5... | collective-permute-start | bytes 2949128 | tf_op jit(solution)/shard_map/ppermute | solution.py:1236
  354.9 18.5 %collective-permute-start.39 = (bf16[3,48,960]{2,1,0:T(8,128)(2,1)}, bf16[3,48,960]{2,1,0:T(8,128)(2,1)}, u32[]{:S(2)}, u32[]{:S(2)}) collective-permute-start(bf16[3,48,960]{2,1,0:T(8,128)(2,1)} %get-tuple-element.147), channel_id=1, source_target_pairs={{0,1},{1,2},{2,3},{3,0},{4,5},{5,6},{6,7},{7,4},{8,9},{9,10},{10,1... | collective-permute-start | bytes 829448 | tf_op jit(solution)/shard_map/ppermute | solution.py:1231
  354.9 36.4 %collective-permute-start.40 = (bf16[3,48,960]{2,1,0:T(8,128)(2,1)}, bf16[3,48,960]{2,1,0:T(8,128)(2,1)}, u32[]{:S(2)}, u32[]{:S(2)}) collective-permute-start(bf16[3,48,960]{2,1,0:T(8,128)(2,1)} %get-tuple-element.148), channel_id=1, source_target_pairs={{0,2},{1,3},{2,0},{3,1},{4,6},{5,7},{6,4},{7,5},{8,10},{9,11},{10,... | collective-permute-start | bytes 829448 | tf_op jit(solution)/shard_map/ppermute | solution.py:1231
  359.1 40.7 %collective-permute-start.37 = (bf16[3,64,960]{2,1,0:T(8,128)(2,1)S(1)}, bf16[3,64,960]{2,1,0:T(8,128)(2,1)S(1)}, u32[]{:S(2)}, u32[]{:S(2)}) collective-permute-start(bf16[3,64,960]{2,1,0:T(8,128)(2,1)S(1)} %get-tuple-element.144.refs_0_), channel_id=1, source_target_pairs={{0,8},{4,12},{8,0},{12,4},{16,24},{20,28},{24,16},{28,20},{1,9},{5... | collective-permute-start | bytes 1105928 | tf_op jit(solution)/shard_map/ppermute | solution.py:1236
  373.4 26.4 %collective-permute-start.38 = (bf16[3,64,960]{2,1,0:T(8,128)(2,1)S(1)}, bf16[3,64,960]{2,1,0:T(8,128)(2,1)S(1)}, u32[]{:S(2)}, u32[]{:S(2)}) collective-permute-start(bf16[3,64,960]{2,1,0:T(8,128)(2,1)S(1)} %get-tuple-element.145.refs_2_), channel_id=1, source_target_pairs={{0,16},{4,20},{8,24},{12,28},{16,0},{20,4},{24,8},{28,12},{1,17},{... | collective-permute-start | bytes 1105928 | tf_op jit(solution)/shard_map/ppermute | solution.py:1236
  419.5 20.1 %collective-permute-start.62 = (bf16[3,48,960]{2,1,0:T(8,128)(2,1)S(1)}, bf16[3,48,960]{2,1,0:T(8,128)(2,1)S(1)}, u32[]{:S(2)}, u32[]{:S(2)}) collective-permute-start(bf16[3,48,960]{2,1,0:T(8,128)(2,1)S(1)} %get-tuple-element.151.refs_13_), channel_id=1, source_target_pairs={{0,24},{4,28},{8,16},{12,20},{16,8},{20,12},{24,0},{28,4},{1,25},{... | collective-permute-start | bytes 829448 | tf_op jit(solution)/shard_map/ppermute | solution.py:1236
  421.8 20.1 %collective-permute-start.61 = (bf16[3,48,960]{2,1,0:T(8,128)(2,1)S(1)}, bf16[3,48,960]{2,1,0:T(8,128)(2,1)S(1)}, u32[]{:S(2)}, u32[]{:S(2)}) collective-permute-start(bf16[3,48,960]{2,1,0:T(8,128)(2,1)S(1)} %get-tuple-element.151.refs_13_), channel_id=1, source_target_pairs={{0,16},{4,20},{8,24},{12,28},{16,0},{20,4},{24,8},{28,12},{1,17},{... | collective-permute-start | bytes 829448 | tf_op jit(solution)/shard_map/ppermute | solution.py:1236
  423.7 19.8 %collective-permute-start.60 = (bf16[3,48,960]{2,1,0:T(8,128)(2,1)S(1)}, bf16[3,48,960]{2,1,0:T(8,128)(2,1)S(1)}, u32[]{:S(2)}, u32[]{:S(2)}) collective-permute-start(bf16[3,48,960]{2,1,0:T(8,128)(2,1)S(1)} %get-tuple-element.151.refs_13_), channel_id=1, source_target_pairs={{0,8},{4,12},{8,0},{12,4},{16,24},{20,28},{24,16},{28,20},{1,9},{5... | collective-permute-start | bytes 829448 | tf_op jit(solution)/shard_map/ppermute | solution.py:1236
  439.5 19.9 %collective-permute-start.49 = (bf16[128,1024]{1,0:T(8,128)(2,1)S(1)}, bf16[128,1024]{1,0:T(8,128)(2,1)S(1)}, u32[]{:S(2)}, u32[]{:S(2)}) collective-permute-start(bf16[128,1024]{1,0:T(8,128)(2,1)S(1)} %get-tuple-element.163.refs_4_), channel_id=1, source_target_pairs={{0,8},{4,12},{8,0},{12,4},{16,24},{20,28},{24,16},{28,20},{1,9},{5... | collective-permute-start | bytes 786440 | tf_op jit(solution)/shard_map/ppermute | solution.py:1236
  443.7 37.6 %collective-permute-start.64 = (bf16[4,3,48,960]{3,2,1,0:T(8,128)(2,1)S(1)}, bf16[4,3,48,960]{3,2,1,0:T(8,128)(2,1)}, u32[]{:S(2)}, u32[]{:S(2)}) collective-permute-start(bf16[4,3,48,960]{3,2,1,0:T(8,128)(2,1)S(1)} %pad_maximum_fusion.qm_ref), channel_id=1, source_target_pairs={{0,4},{4,0},{8,12},{12,8},{16,20},{20,16},{24,28},{28,24},{1,5},{5... | collective-permute-start | bytes 3317768 | tf_op jit(solution)/shard_map/ppermute | solution.py:1236
  (115 other events, 1113.8 us)
Sparse Core Ops, SparseCore 0:
  27.6 86.4 all-gather.2
  239.6 57.4 reduce-scatter.2
  332.5 53.9 reduce-scatter.4

commit v3 on v2

v3 whole, which is shorter than its diff:
```python
import jax
import jax.numpy as jnp
from jax import lax
from jax.experimental import pallas as pl
from jax.experimental.pallas import tpu as pltpu
from jax.sharding import PartitionSpec as P

HQ = 15
KVH = 5
HD = 64
BLK = 128
WIN = 1024
D = 960
GRP = HQ // KVH
SPAN = WIN + BLK
NWB = SPAN // BLK
ROWS = 256
ZR = 240
ZP = 256
UNITS = 256
WIDE = 1024
QKV = 1664

NORM_EPS = 1e-05
ROPE_THETA = 100000.0
MASK_FILL = -1e30
F32 = jnp.float32
BF16 = jnp.bfloat16
MIB = 1024 * 1024

VMEM = pl.BlockSpec(memory_space=pltpu.VMEM)
SMEM = pl.BlockSpec(memory_space=pltpu.SMEM)
ANY = pl.BlockSpec(memory_space=pl.ANY)

KV_LANES = 640
PAIRS = (
    (0, 3, (0, 1), True, True),
    (1, 4, (2, 3), True, True),
    (2, 2, (4,), False, True),
)

CORE_UNITS = 320
QUARTER = 160
OUT_ROWS = 128
PACKED = 3 * QUARTER
CUT = 3 * PACKED // 2

P_ROWS = 128
Q_ROWS = 48
SEG = 64


def dot(a, b):
    return jnp.dot(a, b, preferred_element_type=F32)


def dot_nt(a, b):
    return lax.dot_general(a, b, (((1,), (1,)), ((), ())), preferred_element_type=F32)


def dot_tn(a, b):
    return lax.dot_general(a, b, (((0,), (0,)), ((), ())), preferred_element_type=F32)


def params(mib, grid_dims=0):
    return pltpu.CompilerParams(
        vmem_limit_bytes=mib * MIB,
        dimension_semantics=("arbitrary",) * grid_dims if grid_dims else None,
    )


def cost(micros):
    return pl.CostEstimate(flops=int(3.5e8 * micros), bytes_accessed=1, transcendentals=0)


def rope_slab(t, cos, sin_signed, first_half):
    swapped = jnp.where(first_half, pltpu.roll(t, 96, 1), pltpu.roll(t, 32, 1))
    return t * cos + swapped * sin_signed


def wide_tables(cos, sin):
    return (
        jnp.concatenate([cos] * 4, axis=0).T,
        jnp.concatenate([-sin, sin, -sin, sin], axis=0).T,
    )


def lane_masks(rows):
    lane = lax.broadcasted_iota(jnp.int32, (rows, 128), 1)
    return (lane % HD) < HD // 2, lane < HD


def rel_z(z, i):
    return lax.rem(z + 1 + i, 4)


def each(found, act):
    for cond, c in found:
        if cond is None:
            act(c)
        else:
            pl.when(cond)(lambda c=c: act(c))


def start(c):
    c.start()


def wait(c):
    c.wait()


def run_copies(pairs, sems):
    copies = [pltpu.make_async_copy(a, b, sems.at[i]) for i, (a, b) in enumerate(pairs)]
    for c in copies:
        c.start()
    for c in copies:
        c.wait()


MICROS = {
    "stack_two": 1,
    "meet": 1,
    "prep_weights": 5,
    "stack_weights": 2,
    "split_quarters": 5,
    "pick_out_rows": 3,
    "sum_chips": 4,
    "join_cores": 5,
    "key_value_weights_back": 11,
    "join_near": 4,
    "join_projections": 7,
    "add_pairs": 3,
    "stack_pairs": 2,
    "halve_rows": 2,
    "join_feed_forward": 3,
    "finish_feed_forward": 6,
    "finish_rest": 4,
}


def whole(shape):
    return pl.BlockSpec(shape, lambda i: (0,) * len(shape))


def step_call(
    name, body, info, ins, outs, far=(), scratch=(), behind=(), passed=()
):
    n_in, n_out, n_behind, n_passed = len(ins), len(outs), len(behind), len(passed)

    def kernel(info_ref, *refs):
        after = refs[n_in + n_behind + n_passed :]
        body(info_ref, refs[:n_in], after[:n_out], after[n_out + n_passed :])

    return pl.pallas_call(
        kernel,
        grid=(1,),
        out_shape=tuple(jax.ShapeDtypeStruct(shape, dtype) for shape, dtype in outs)
        + tuple(jax.ShapeDtypeStruct(p.shape, p.dtype) for p in passed),
        in_specs=[SMEM]
        + [ANY if n in far else whole(x.shape) for n, x in enumerate(ins)]
        + [ANY] * (n_behind + n_passed),
        out_specs=tuple(whole(shape) for shape, _ in outs) + (ANY,) * n_passed,
        scratch_shapes=list(scratch),
        input_output_aliases={1 + n_in + n_behind + n: n_out + n for n in range(n_passed)},
        compiler_params=params(60, 1),
        cost_estimate=cost(MICROS[name]),
        name=name,
    )(info, *ins, *behind, *passed)


def meet(info, passed, behind=()):
    return step_call("meet", lambda *refs: None, info, (), (), behind=behind, passed=passed)


def prep_weights(info, w_gate, w_up, w_down_turned):
    def body(info, ins, outs, scratch):
        core, parity = info[1], info[4]
        turn, given, sems = scratch
        base = core * CORE_UNITS
        copies = [pltpu.make_async_copy(ins[n], given.at[n], sems.at[n]) for n in range(3)]
        for c in copies:
            c.start()
        for n in range(3):
            copies[n].wait()
            turn[...] = given[n].T
            outs[0][n] = turn[pl.ds(pl.multiple_of(base, 16), CORE_UNITS), :]
            quarter = pl.ds(pl.multiple_of(base + QUARTER * parity, 16), QUARTER)
            outs[1][QUARTER * n : QUARTER * n + QUARTER, :] = turn[quarter, :]

    weights = (w_gate, w_up, w_down_turned)
    return step_call(
        "prep_weights",
        body,
        info,
        weights,
        (((3, CORE_UNITS, D), BF16), ((PACKED, D), BF16)),
        far=range(3),
        scratch=(
            pltpu.VMEM((2 * CORE_UNITS, D), BF16),
            pltpu.VMEM((3,) + w_gate.shape, BF16),
            pltpu.SemaphoreType.DMA((3,)),
        ),
    )


def stack_weights(info, parts, behind, passed):
    def body(info, ins, outs, scratch):
        for n in range(3):
            outs[0][n] = ins[n][...]

    out = ((3,) + parts[0].shape, BF16)
    return step_call("stack_weights", body, info, parts, (out,), behind=behind, passed=passed)


def split_quarters(info, over_z, deps):
    at = CUT - PACKED

    def body(info, ins, outs, scratch):
        src = ins[0]
        z = info[0]
        zs = [rel_z(z, i) for i in range(3)]
        pairs = [
            (src.at[zs[0]], outs[0].at[pl.ds(0, PACKED)]),
            (src.at[zs[1], pl.ds(0, at)], outs[0].at[pl.ds(PACKED, at)]),
            (src.at[zs[1], pl.ds(at, PACKED - at)], outs[1].at[pl.ds(0, PACKED - at)]),
            (src.at[zs[2]], outs[1].at[pl.ds(PACKED - at, PACKED)]),
        ]
        run_copies(pairs, scratch[0])

    half = (CUT, D)
    return step_call(
        "split_quarters",
        body,
        info,
        (over_z, *deps),
        ((half, BF16), (half, BF16)),
        range(1 + len(deps)),
        scratch=(pltpu.SemaphoreType.DMA((4,)),),
    )


def pre_kernel(info, xt_ref, cos_ref, sin_ref, *refs):
    own, pieces = refs[0], refs[1:9]
    attn_ref, attn_up, attn_lo, q_ref, kv_ref, x_ref, gains_ref, wq_out, wkv_out = refs[9:18]
    w_ref, sems, out_sems = refs[18:]
    step = pl.program_id(0)
    z, me = info[0], info[2]
    outs = [
        pltpu.make_async_copy(w_ref.at[:, pl.ds(0, WIDE)], wq_out, out_sems.at[0]),
        pltpu.make_async_copy(w_ref.at[:, pl.ds(896, QKV - 896)], wkv_out, out_sems.at[1]),
    ]

    def pieces_do(act):
        found = []

        def add(src, row, size, cond=None):
            view = w_ref.at[pl.ds(pl.multiple_of(row, 16), size)]
            found.append((cond, pltpu.make_async_copy(src, view, sems.at[len(found)])))

        add(own, z * ZR, ZR)
        for rel, piece in enumerate(pieces):
            c = me ^ rel
            for i in range(3):
                base = rel_z(z, i) * ZR
                add(piece.at[i, pl.ds(0, 16)], base + 32 * c, 16, c < 7)
                add(piece.at[i, pl.ds(16, 16)], base + jnp.minimum(32 * c + 16, ZR - 16), 16)
        each(found, act)

    @pl.when(step == 0)
    def _():
        pieces_do(start)

    first_half, low_head = lane_masks(ROWS)
    cos, sin = wide_tables(cos_ref[...], sin_ref[...])
    x_low = xt_ref[...].T
    x_ref[...] = x_low
    x = x_low.astype(F32)
    factor = lax.rsqrt(jnp.mean(x * x, axis=-1, keepdims=True) + NORM_EPS)

    @pl.when(step == 0)
    def _():
        pieces_do(wait)
        for c in outs:
            c.start()
        gains_ref[...] = w_ref[:, 1536:QKV].astype(F32).T[64:72]

    a = (x * factor * gains_ref[0:1, :]).astype(BF16)
    attn_ref[...] = a
    turned_a = a.T
    attn_up[...] = turned_a[0 : D // 2]
    attn_lo[...] = turned_a[D // 2 :]
    qk = dot(a, w_ref[:, 0:1280])
    vv = dot(a, w_ref[:, 1280:QKV])
    slabs = [rope_slab(qk[:, 128 * j : 128 * j + 128], cos, sin, first_half) for j in range(10)]
    for j in range(7):
        q_ref[:, 128 * j : 128 * j + 128] = slabs[j].astype(BF16)
    q_ref[:, 896:960] = slabs[7][:, :64].astype(BF16)
    mixed = jnp.where(low_head, vv[:, 256:384], slabs[7])
    for j, part in enumerate((slabs[8], slabs[9], mixed, vv[:, 0:128], vv[:, 128:256])):
        kv_ref[:, 128 * j : 128 * j + 128] = part.astype(BF16)

    @pl.when(step == pl.num_programs(0) - 1)
    def _():
        for c in outs:
            c.wait()


def by_rows(width):
    return pl.BlockSpec((ROWS, width), lambda i: (i, 0))


def by_lanes(height):
    return pl.BlockSpec((height, ROWS), lambda i: (0, i))


def pre_call(info, xt, cos, sin, pieces):
    t = xt.shape[1]
    return pl.pallas_call(
        pre_kernel,
        grid=(t // ROWS,),
        out_shape=(
            jax.ShapeDtypeStruct((t, D), BF16),
            jax.ShapeDtypeStruct((D // 2, t), BF16),
            jax.ShapeDtypeStruct((D // 2, t), BF16),
            jax.ShapeDtypeStruct((t, D), BF16),
            jax.ShapeDtypeStruct((t, KV_LANES), BF16),
            jax.ShapeDtypeStruct((t, D), BF16),
            jax.ShapeDtypeStruct((8, D), F32),
            jax.ShapeDtypeStruct((D, WIDE), BF16),
            jax.ShapeDtypeStruct((D, QKV - 896), BF16),
        ),
        in_specs=[SMEM, by_lanes(D), by_lanes(32), by_lanes(32)] + [ANY] * 9,
        out_specs=(
            by_rows(D), by_lanes(D // 2), by_lanes(D // 2), by_rows(D), by_rows(KV_LANES), by_rows(D), whole((8, D)),
            ANY, ANY,
        ),
        scratch_shapes=[
            pltpu.VMEM((D, QKV), BF16),
            pltpu.SemaphoreType.DMA((49,)),
            pltpu.SemaphoreType.DMA((2,)),
        ],
        compiler_params=params(60, 1),
        cost_estimate=cost(12),
        name="pre",
    )(info, xt, cos, sin, *pieces)


def start_window(tab, kvs, win, sem, blk, slot):
    def body(j, _):
        entry = tab[blk, j]
        which = entry // 1024
        idx = lax.rem(entry, 1024)
        dst = win.at[slot, pl.ds(pl.multiple_of(j * BLK, BLK), BLK)]
        for n, ref in enumerate(kvs):
            @pl.when(which == n)
            def _():
                src = ref.at[pl.ds(pl.multiple_of(idx * BLK, BLK), BLK)]
                pltpu.make_async_copy(src, dst, sem.at[slot]).start()
        return 0

    lax.fori_loop(0, NWB, body, 0)


def next_window(tab, kvs, win, sem, first=0):
    i = pl.program_id(0)
    slot = lax.rem(i, 2)

    @pl.when(i == 0)
    def _():
        start_window(tab, kvs, win, sem, i + first, slot)

    @pl.when(i + 1 < pl.num_programs(0))
    def _():
        start_window(tab, kvs, win, sem, i + first + 1, 1 - slot)

    pltpu.make_async_copy(win.at[slot], win.at[slot], sem.at[slot]).wait()
    return slot


def turned(flat):
    rows = flat.astype(F32)
    extra = -rows.shape[1] % 128
    if extra:
        rows = jnp.concatenate([rows, jnp.zeros((rows.shape[0], extra), F32)], axis=1)
    return rows.T


def unturned(parts):
    rows = sum(p.shape[0] for p in parts)
    extra = -rows % 128
    if extra:
        parts = parts + [jnp.zeros((extra, parts[0].shape[1]), F32)]
    return jnp.concatenate(parts, axis=0).T[:, :rows].astype(BF16)


def spread_heads(rows, count, low):
    width = GRP * BLK
    sides = [jnp.concatenate(rows[GRP * n : GRP * n + GRP], axis=1) for n in range(count)]
    empty = jnp.zeros((HD, width), rows[0].dtype)
    if count == 2:
        return jnp.concatenate(
            [jnp.concatenate([sides[0], empty], axis=1), jnp.concatenate([empty, sides[1]], axis=1)],
            axis=0,
        )
    return jnp.concatenate([sides[0], empty] if low else [empty, sides[0]], axis=0)


def head_half(j, kv_heads, low):
    upper = j >= GRP if len(kv_heads) == 2 else not low
    return HD if upper else 0


def fwd_kernel(n_kv, tab, lo_ref, q_ref, *refs):
    kvs = refs[:n_kv]
    mid_ref, rl_ref, p_ref, win, bias, scores, sem = refs[n_kv:]
    slot = next_window(tab, kvs, win, sem)
    row = lax.broadcasted_iota(jnp.int32, (SPAN, BLK), 0)
    lane = lax.broadcasted_iota(jnp.int32, (SPAN, BLK), 1)
    allowed = (row >= lo_ref[0]) & (row <= lane + WIN)
    bias[...] = jnp.where(allowed, 0.0, MASK_FILL)
    q_all = (turned(q_ref[...]) * (HD ** -0.5)).astype(BF16)
    outs, recips = [], []
    at = 0
    for k_slab, v_slab, kv_heads, k_low, v_low in PAIRS:
        keys = win[slot, :, 128 * k_slab : 128 * k_slab + 128]
        vals = win[slot, :, 128 * v_slab : 128 * v_slab + 128]
        count = GRP * len(kv_heads)
        width = BLK * count
        base = BLK * at
        q_rows = [q_all[HD * (at + j) : HD * (at + j) + HD] for j in range(count)]
        scores[:, :width] = dot(keys, spread_heads(q_rows, len(kv_heads), k_low))
        for j in range(count):
            s = scores[:, BLK * j : BLK * j + BLK] + bias[...]
            top = jnp.max(s, axis=0, keepdims=True)
            p_ref[0, :, base + BLK * j : base + BLK * j + BLK] = jnp.exp(s - top).astype(BF16)
        lhs = jnp.concatenate([vals.T, jnp.ones((16, SPAN), BF16)], axis=0)
        product = dot(lhs, p_ref[0, :, base : base + width])
        recip = 1.0 / product[128:129, :]
        for j in range(count):
            cols = slice(BLK * j, BLK * j + BLK)
            half = head_half(j, kv_heads, v_low)
            outs.append(product[half : half + HD, cols] * recip[:, cols])
            recips.append(recip[:, cols])
        at += count
    mid_ref[...] = unturned(outs)
    recips.append(jnp.zeros((16 - len(recips), BLK), F32))
    rl_ref[0] = jnp.concatenate(recips, axis=0)


def fwd_call(tab, lo, q, kvs):
    blocks = q.shape[0] // BLK
    n_kv = len(kvs)
    lanes, heads = D, HQ
    return pl.pallas_call(
        lambda *refs: fwd_kernel(n_kv, *refs),
        grid=(blocks,),
        out_shape=(
            jax.ShapeDtypeStruct((q.shape[0], lanes), BF16),
            jax.ShapeDtypeStruct((blocks, 16, BLK), F32),
            jax.ShapeDtypeStruct((blocks, SPAN, heads * BLK), BF16),
        ),
        in_specs=[
            SMEM,
            pl.BlockSpec((1, 1, BLK), lambda i: (i, 0, 0)),
            pl.BlockSpec((BLK, lanes), lambda i: (i, 0)),
        ]
        + [ANY] * n_kv,
        out_specs=(
            pl.BlockSpec((BLK, lanes), lambda i: (i, 0)),
            pl.BlockSpec((1, 16, BLK), lambda i: (i, 0, 0)),
            pl.BlockSpec((1, SPAN, heads * BLK), lambda i: (i, 0, 0)),
        ),
        scratch_shapes=[
            pltpu.VMEM((2, SPAN, KV_LANES), BF16),
            pltpu.VMEM((SPAN, BLK), F32),
            pltpu.VMEM((SPAN, 2 * GRP * BLK), F32),
            pltpu.SemaphoreType.DMA((2,)),
        ],
        compiler_params=params(60, 1),
        cost_estimate=cost(32),
        name="attend",
    )(tab, lo, q, *kvs)


def bwd_kernel(
    n_kv, n_dep, first, prev, out_units, n_slots, tab, slots, q_ref, do_ref, mid_ref, rl_ref, p_ref, cos_ref, sin_ref, *refs
):
    kvs = refs[:n_kv]
    n_out = len(out_units)
    refs = refs[n_kv + n_dep :]
    earlier = refs[:n_out] if prev else ()
    refs = refs[len(earlier) :]
    dq_ref = refs[0]
    outs = refs[1 : 1 + n_out]
    win, acc, scores, stage, stage_in, sem, out_sem, in_sem = refs[1 + n_out :]
    i = pl.program_id(0)
    blk = i + first
    slot = next_window(tab, kvs, win, sem, first)
    lanes = acc.shape[1]

    @pl.when(i == 0)
    def _():
        def clear(b, _):
            acc[pl.ds(pl.multiple_of(b * BLK, BLK), BLK), :] = jnp.zeros((BLK, lanes), F32)
            return 0

        lax.fori_loop(0, n_slots, clear, 0)

    def add(slab, value):
        for j in range(NWB):
            r = pl.ds(pl.multiple_of(slots[blk, j] * BLK, BLK), BLK)
            acc[r, 128 * slab : 128 * slab + 128] += value[BLK * j : BLK * j + BLK]

    q_all = (turned(q_ref[...]) * (HD ** -0.5)).astype(BF16)
    do_all = turned(do_ref[...])
    o_all = turned(mid_ref[...])
    cos, sin = cos_ref[...], sin_ref[...]
    grads = []
    at = 0
    for k_slab, v_slab, kv_heads, k_low, v_low in PAIRS:
        keys = win[slot, :, 128 * k_slab : 128 * k_slab + 128]
        vals = win[slot, :, 128 * v_slab : 128 * v_slab + 128]
        count = GRP * len(kv_heads)
        width = BLK * count
        base = BLK * at
        q_rows, do_rows, dots = [], [], []
        for j in range(count):
            r = slice(HD * (at + j), HD * (at + j) + HD)
            q_rows.append(q_all[r])
            scaled = do_all[r] * rl_ref[0, at + j : at + j + 1, :]
            dots.append(jnp.sum(scaled * o_all[r], axis=0, keepdims=True))
            do_rows.append(scaled.astype(BF16))
        q_wide = spread_heads(q_rows, len(kv_heads), k_low)
        do_wide = spread_heads(do_rows, len(kv_heads), v_low)
        scores[:, :width] = dot(vals, do_wide)
        ds = []
        for j in range(count):
            p = p_ref[0, :, base + BLK * j : base + BLK * j + BLK].astype(F32)
            ds.append((p * (scores[:, BLK * j : BLK * j + BLK] - dots[j])).astype(BF16))
        ds = jnp.concatenate(ds, axis=1)
        probs = p_ref[0, :, base : base + width]
        if len(kv_heads) == 2:
            add(k_slab, dot_nt(ds, q_wide))
            add(v_slab, dot_nt(probs, do_wide))
        else:
            add(
                k_slab,
                dot_nt(
                    jnp.concatenate([ds, probs], axis=1),
                    jnp.concatenate([q_wide, do_wide], axis=1),
                ),
            )
        dq = dot(keys.T, ds) * (HD ** -0.5)
        for j in range(count):
            top = head_half(j, kv_heads, k_low)
            cols = slice(BLK * j, BLK * j + BLK)
            first = dq[top : top + 32, cols]
            second = dq[top + 32 : top + 64, cols]
            grads.append(first * cos + second * sin)
            grads.append(second * cos - first * sin)
        at += count
    dq_ref[...] = unturned(grads)

    @pl.when(i == pl.num_programs(0) - 1)
    def _():
        per = 6 * BLK
        places = [(n, u) for n, units in enumerate(out_units) for u in range(units)]
        copies, loads = [], []

        def load(t):
            if prev and t < len(places):
                n, u = places[t]
                c = pltpu.make_async_copy(
                    earlier[n].at[pl.ds(per * u, per)], stage_in.at[t % 2], in_sem.at[t % 2]
                )
                c.start()
                loads.append(c)

        load(0)
        load(1)
        for t, (n, u) in enumerate(places):
            s = t % 2
            if t >= 2:
                copies[t - 2].wait()
            value = acc[per * t : per * t + per, :]
            if prev:
                loads[t].wait()
                value = value + stage_in[s].astype(F32)
            stage[s] = value.astype(BF16)
            load(t + 2)
            c = pltpu.make_async_copy(stage.at[s], outs[n].at[pl.ds(per * u, per)], out_sem.at[s])
            c.start()
            copies.append(c)
        copies[-2].wait()
        copies[-1].wait()


def bwd_call(first, blocks, earlier, deps, tab, slots, out_units, q, do, mid, rl, p, cos, sin, kvs):
    n_kv = len(kvs)
    lanes, heads, width = D, HQ, KV_LANES
    n_slots = 6 * sum(out_units)
    flat = pl.BlockSpec((BLK, lanes), lambda i: (i + first, 0))
    table = pl.BlockSpec((32, BLK), lambda i: (0, i + first))
    prev = bool(earlier)
    return pl.pallas_call(
        lambda *refs: bwd_kernel(n_kv, len(deps), first, prev, out_units, n_slots, *refs),
        grid=(blocks,),
        out_shape=(jax.ShapeDtypeStruct((blocks * BLK, lanes), BF16),)
        + tuple(jax.ShapeDtypeStruct((6 * BLK * u, width), BF16) for u in out_units),
        in_specs=[
            SMEM,
            SMEM,
            flat,
            flat,
            flat,
            pl.BlockSpec((1, 16, BLK), lambda i: (i + first, 0, 0)),
            pl.BlockSpec((1, SPAN, heads * BLK), lambda i: (i + first, 0, 0)),
            table,
            table,
        ]
        + [ANY] * (n_kv + len(deps) + len(earlier)),
        out_specs=(pl.BlockSpec((BLK, lanes), lambda i: (i, 0)),) + (ANY,) * len(out_units),
        scratch_shapes=[
            pltpu.VMEM((2, SPAN, width), BF16),
            pltpu.VMEM((n_slots * BLK, width), F32),
            pltpu.VMEM((SPAN, 2 * GRP * BLK), F32),
            pltpu.VMEM((2, 6 * BLK, width), BF16),
            pltpu.VMEM((2, 6 * BLK, width), BF16),
            pltpu.SemaphoreType.DMA((2,)),
            pltpu.SemaphoreType.DMA((2,)),
            pltpu.SemaphoreType.DMA((2,)),
        ],
        compiler_params=params(60, 1),
        cost_estimate=cost(10000),
        name=f"attend_back_{first}",
    )(tab, slots, q, do, mid, rl, p, cos, sin, *kvs, *deps, *earlier)


def pro_kernel(info, mid_ref, x_ref, gain_ref, own, *refs):
    here, there = refs[0:3], refs[3:6]
    h1_ref, low_ref, w_out, _, _, w_ref, sems, out_sem = refs[9:]
    z, core = info[0], info[1]
    step = pl.program_id(0)
    out_copy = pltpu.make_async_copy(w_ref, w_out, out_sem)
    found = []

    def bring(src, row, size):
        dst = w_ref.at[pl.ds(pl.multiple_of(row, 16), size)]
        found.append((None, pltpu.make_async_copy(src, dst, sems.at[len(found)])))

    bring(own, z * ZR, ZR)
    skip = 16 * (1 - core)
    for i in range(3):
        base = rel_z(z, i) * ZR
        bring(here[i], base + (ZR - OUT_ROWS) * core, OUT_ROWS)
        bring(
            there[i].at[pl.ds(pl.multiple_of(skip, 16), OUT_ROWS - 16)],
            base + (ZR - OUT_ROWS) * (1 - core) + skip,
            OUT_ROWS - 16,
        )

    @pl.when(step == 0)
    def _():
        each(found, start)
        each(found, wait)
        out_copy.start()

    h = x_ref[...].astype(F32) + dot(mid_ref[...], w_ref[...])
    factor = lax.rsqrt(jnp.mean(h * h, axis=-1, keepdims=True) + NORM_EPS)
    h1_ref[...] = h
    low_ref[:, 0:D] = (h * factor * gain_ref[1:2, :]).astype(BF16)
    low_ref[:, D:WIDE] = jnp.zeros((ROWS, WIDE - D), BF16)

    @pl.when(step == pl.num_programs(0) - 1)
    def _():
        out_copy.wait()


def pro_call(info, mid, x, gains, own, here, there, dep, passed):
    t = x.shape[0]
    return pl.pallas_call(
        pro_kernel,
        grid=(t // ROWS,),
        out_shape=(
            jax.ShapeDtypeStruct((t, D), F32),
            jax.ShapeDtypeStruct((t, WIDE), BF16),
            jax.ShapeDtypeStruct((D, D), BF16),
            *[jax.ShapeDtypeStruct(p.shape, p.dtype) for p in passed],
        ),
        in_specs=[SMEM, by_rows(D), by_rows(D), whole((8, D))] + [ANY] * 10,
        out_specs=(by_rows(D), by_rows(WIDE), ANY, ANY, ANY),
        input_output_aliases={12: 3, 13: 4},
        scratch_shapes=[
            pltpu.VMEM((D, D), BF16),
            pltpu.SemaphoreType.DMA((7,)),
            pltpu.SemaphoreType.DMA,
        ],
        compiler_params=params(60, 1),
        cost_estimate=cost(7),
        name="out_projection",
    )(info, mid, x, gains, own, *here, *there, dep, *passed)


def ffn_kernel(info, a0, a1, c0, c1, own, *refs):
    here = refs[:4]
    acc_outs, p_ref, q_refs = refs[4:9], refs[9], refs[10:14]
    (
        wbuf, a_all, c_all, c_turn, hid_s, gg_s, gu_s, stage, acc_o, acc_g, send_o, send_lo, send_hi,
        io_sem, w_sem, out_sem, acc_sem,
    ) = refs[14:]
    z, chip, parity = info[0], info[3], info[4]
    t = a0.shape[0]
    units = wbuf.shape[1]
    ins = [
        pltpu.make_async_copy(a0, a_all.at[pl.ds(0, t)], io_sem.at[0]),
        pltpu.make_async_copy(a1, a_all.at[pl.ds(t, t)], io_sem.at[1]),
        pltpu.make_async_copy(c0, c_turn.at[0], io_sem.at[2]),
        pltpu.make_async_copy(c1, c_turn.at[1], io_sem.at[3]),
    ]
    copies = [pltpu.make_async_copy(own, wbuf.at[:, pl.ds(0, CORE_UNITS)], w_sem.at[0])]
    for n_par, par in enumerate((parity, 1 - parity)):
        for i in range(3):
            for n in range(3):
                a0_row = PACKED * i + QUARTER * n
                for ref, p0, p1 in ((here[2 * n_par], 0, CUT), (here[2 * n_par + 1], CUT, 2 * CUT)):
                    a, b = max(p0, a0_row), min(p1, a0_row + QUARTER)
                    if a < b:
                        row = CORE_UNITS * (i + 1) + QUARTER * par + (a - a0_row)
                        dst = wbuf.at[n, pl.ds(pl.multiple_of(row, 16), b - a)]
                        copies.append(
                            pltpu.make_async_copy(
                                ref.at[pl.ds(a - p0, b - a)], dst, w_sem.at[len(copies)]
                            )
                        )
    for c in ins[2:] + ins[:2] + copies:
        c.start()
    for h in range(2):
        ins[2 + h].wait()
        c_all[t * h : t * h + t, :] = c_turn[h].T
    for c in ins[:2] + copies:
        c.wait()

    def forward(c, _):
        u = pl.ds(pl.multiple_of(c * UNITS, UNITS), UNITS)
        for h in range(2 * t // ROWS):
            r = slice(ROWS * h, ROWS * h + ROWS)
            gate = dot_nt(a_all[r, 0:D], wbuf[0, u, :])
            up = dot_nt(a_all[r, 0:D], wbuf[1, u, :])
            grad = dot_nt(c_all[r, :], wbuf[2, u, :])
            sig = lax.logistic(gate)
            swish = gate * sig
            hid_s[r, u] = (swish * up).astype(BF16)
            gg_s[r, u] = (grad * up * (sig * (1.0 + gate * (1.0 - sig)))).astype(BF16)
            gu_s[r, u] = (grad * swish).astype(BF16)
        return 0

    lax.fori_loop(0, units // UNITS, forward, 0)

    def sums(r):
        left = dot(hid_s[r, :], wbuf[2])
        right = dot(gg_s[r, :], wbuf[0]) + dot(gu_s[r, :], wbuf[1])
        return left, right

    def mine(i, _):
        r = pl.ds(pl.multiple_of(i * ROWS, ROWS), ROWS)
        acc_o[r, :], acc_g[r, :] = sums(r)
        return 0

    def others(i, _):
        r = pl.ds(pl.multiple_of(i * ROWS, ROWS), ROWS)
        left, right = sums(pl.ds(pl.multiple_of(t + i * ROWS, ROWS), ROWS))
        empty = jnp.zeros((ROWS, WIDE - D), BF16)
        send_o[r, 0:D] = left.astype(BF16)
        send_o[r, D:WIDE] = empty
        half = WIDE // 2
        send_lo[r, :] = right[:, 0:half].astype(BF16)
        send_hi[r, 0 : D - half] = right[:, half:D].astype(BF16)
        send_hi[r, D - half : half] = empty
        return 0

    lax.fori_loop(0, t // ROWS, others, 0)
    lax.fori_loop(0, t // ROWS, mine, 0)
    acc_copies = [
        pltpu.make_async_copy(src, dst, acc_sem.at[n])
        for n, (src, dst) in enumerate(zip((acc_o, acc_g, send_o, send_lo, send_hi), acc_outs))
    ]
    for c in acc_copies:
        c.start()

    def back_copies(c, slot):
        found = []
        per = CORE_UNITS // SEG
        for n in range(UNITS // SEG):
            j = c * (UNITS // SEG) + n
            within = lax.rem(j, per)
            zz = lax.rem(z + j // per, 4)
            n_p = P_ROWS // SEG
            first = within < n_p
            row = pl.multiple_of(jnp.minimum(within, n_p - 1) * SEG, SEG)
            src = stage.at[slot, :, pl.ds(SEG * n, SEG)]
            dst = p_ref.at[zz, :, pl.ds(row, SEG)]
            found.append((first, pltpu.make_async_copy(src, dst, out_sem.at[slot, 24 + n])))
            piece = 6 * n
            for k in range(per - n_p):
                at = SEG * k
                while at < SEG * k + SEG:
                    owner = at // Q_ROWS
                    size = min(SEG * k + SEG, Q_ROWS * (owner + 1)) - at
                    src = stage.at[slot, :, pl.ds(SEG * n + at - SEG * k, size)]
                    for r in range(4):
                        dst = q_refs[r].at[zz, :, pl.ds(at - Q_ROWS * owner, size)]
                        copy = pltpu.make_async_copy(src, dst, out_sem.at[slot, piece])
                        found.append(((within == n_p + k) & (chip ^ owner == r), copy))
                    at += size
                    piece += 1
        return found

    def backward(c, _):
        u = pl.ds(pl.multiple_of(c * UNITS, UNITS), UNITS)
        slot = lax.rem(c, 2)

        @pl.when(c >= 2)
        def _():
            each(back_copies(c - 2, slot), wait)

        stage[slot, 0] = dot_tn(gg_s[:, u], a_all[:, 0:D]).astype(BF16)
        stage[slot, 1] = dot_tn(gu_s[:, u], a_all[:, 0:D]).astype(BF16)
        stage[slot, 2] = dot_tn(hid_s[:, u], c_all[...]).astype(BF16)
        each(back_copies(c, slot), start)
        return 0

    n_chunks = units // UNITS
    lax.fori_loop(0, n_chunks, backward, 0)
    for c in (n_chunks - 2, n_chunks - 1):
        each(back_copies(jnp.int32(c), c % 2), wait)
    for c in acc_copies:
        c.wait()


def ffn_call(info, a0, a1, c0, c1, own, here):
    t = a0.shape[0]
    units = 4 * CORE_UNITS
    return pl.pallas_call(
        ffn_kernel,
        out_shape=(
            jax.ShapeDtypeStruct((t, D), F32),
            jax.ShapeDtypeStruct((t, D), F32),
            jax.ShapeDtypeStruct((t, WIDE), BF16),
            jax.ShapeDtypeStruct((t, WIDE // 2), BF16),
            jax.ShapeDtypeStruct((t, WIDE // 2), BF16),
            jax.ShapeDtypeStruct((4, 3, P_ROWS, D), BF16),
            *[jax.ShapeDtypeStruct((4, 3, Q_ROWS, D), BF16)] * 4,
        ),
        in_specs=[SMEM] + [ANY] * 9,
        out_specs=(ANY,) * 10,
        scratch_shapes=[
            pltpu.VMEM((3, units, D), BF16),
            pltpu.VMEM((2 * t, WIDE), BF16),
            pltpu.VMEM((2 * t, D), BF16),
            pltpu.VMEM((2, D, t), BF16),
            pltpu.VMEM((2 * t, units), BF16),
            pltpu.VMEM((2 * t, units), BF16),
            pltpu.VMEM((2 * t, units), BF16),
            pltpu.VMEM((2, 3, UNITS, D), BF16),
            pltpu.VMEM((t, D), F32),
            pltpu.VMEM((t, D), F32),
            pltpu.VMEM((t, WIDE), BF16),
            pltpu.VMEM((t, WIDE // 2), BF16),
            pltpu.VMEM((t, WIDE // 2), BF16),
            pltpu.SemaphoreType.DMA((4,)),
            pltpu.SemaphoreType.DMA((24,)),
            pltpu.SemaphoreType.DMA((2, 28)),
            pltpu.SemaphoreType.DMA((5,)),
        ],
        compiler_params=params(60),
        cost_estimate=cost(50),
        name="feed_forward",
    )(info, a0, a1, c0, c1, own, *here)


def put_shards(ref, product, gain_grad):
    extra = ref.shape[-1] - product.shape[1]
    if extra:
        product = jnp.concatenate([product, jnp.zeros((product.shape[0], extra), F32)], axis=1)
    width = product.shape[1]
    first_row = lax.broadcasted_iota(jnp.int32, (ZP - ZR, width), 0) == 0
    for n in range(4):
        ref[n, 0:ZR, :] = product[ZR * n : ZR * n + ZR].astype(BF16)
        if gain_grad is None:
            ref[n, ZR:ZP, :] = jnp.zeros((ZP - ZR, width), BF16)
        else:
            part = jnp.concatenate(
                [gain_grad[:, ZR * n : ZR * n + ZR], jnp.zeros((1, width - ZR), F32)], axis=1
            )
            ref[n, ZR:ZP, :] = jnp.where(first_row, part, 0.0).astype(BF16)


def put_halves(core, keep_ref, send_ref, product, gain_grad):
    extra = jnp.zeros((product.shape[0], WIDE - product.shape[1]), F32)
    wide = jnp.concatenate([product, extra], axis=1)
    half = WIDE // 2
    for side, (first, second) in enumerate(((keep_ref, send_ref), (send_ref, keep_ref))):
        @pl.when(core == side)
        def _():
            put_shards(first, wide[:, :half], gain_grad)
            put_shards(second, wide[:, half:], None)


def epi_kernel(
    info, h1_ref, acc_g, got_lo, got_hi, ct_ref, gain_ref, w_ref, mid_ref, *refs
):
    gh_ref, gm_ref, keep_ref, send_ref, acc, total = refs
    i = pl.program_id(0)

    @pl.when(i == 0)
    def _():
        acc[...] = jnp.zeros((D, D), F32)
        total[...] = jnp.zeros((8, D), F32)

    h = h1_ref[...]
    factor = lax.rsqrt(jnp.mean(h * h, axis=-1, keepdims=True) + NORM_EPS)
    normed = h * factor
    got = jnp.concatenate([got_lo[...], got_hi[...]], axis=1)
    g = acc_g[...] + got[:, 0:D].astype(F32)
    scaled = g * gain_ref[1:2, :]
    back = factor * (scaled - normed * jnp.mean(scaled * normed, axis=-1, keepdims=True))
    full = ct_ref[...].T.astype(F32) + back
    gh_ref[...] = full
    res = full.astype(BF16)
    gm_ref[...] = dot_nt(res, w_ref[...]).astype(BF16)
    total[0:1, :] += jnp.sum(g * normed, axis=0, keepdims=True)
    acc[...] += dot_tn(mid_ref[...], res)

    @pl.when(i == pl.num_programs(0) - 1)
    def _():
        put_halves(info[1], keep_ref, send_ref, acc[...], total[0:1, :])


def epi_call(info, h1, acc_g, got_lo, got_hi, cot_t, gains, w_out, mid):
    t = h1.shape[0]
    rows = pl.BlockSpec((ROWS, D), lambda i: (i, 0))
    return pl.pallas_call(
        epi_kernel,
        grid=(t // ROWS,),
        out_shape=(
            jax.ShapeDtypeStruct((t, D), F32),
            jax.ShapeDtypeStruct((t, D), BF16),
            jax.ShapeDtypeStruct((4, ZP, WIDE // 2), BF16),
            jax.ShapeDtypeStruct((4, ZP, WIDE // 2), BF16),
        ),
        in_specs=[
            SMEM,
            rows,
            rows,
            by_rows(WIDE // 2),
            by_rows(WIDE // 2),
            by_lanes(D),
            whole((8, D)),
            whole((D, D)),
            rows,
        ],
        out_specs=(rows, rows) + (whole((4, ZP, WIDE // 2)),) * 2,
        scratch_shapes=[pltpu.VMEM((D, D), F32), pltpu.VMEM((8, D), F32)],
        compiler_params=params(60, 1),
        cost_estimate=cost(12),
        name="feed_forward_norm_back",
    )(info, h1, acc_g, got_lo, got_hi, cot_t, gains, w_out, mid)


def post_q_kernel(info, a_ref, g_ref, w_ref, _, keep_ref, send_ref, part_ref, acc):
    step = pl.program_id(0)

    @pl.when(step == 0)
    def _():
        acc[...] = jnp.zeros((D, D), F32)

    g = g_ref[...]
    part_ref[...] = dot_nt(g, w_ref[:, 0:D])
    acc[...] += dot_tn(a_ref[...], g)

    @pl.when(step == pl.num_programs(0) - 1)
    def _():
        put_halves(info[1], keep_ref, send_ref, acc[...], None)


def post_q_call(info, a, g, w, dep):
    t = a.shape[0]
    piece = (4, ZP, WIDE // 2)
    return pl.pallas_call(
        post_q_kernel,
        grid=(t // ROWS,),
        out_shape=(
            jax.ShapeDtypeStruct(piece, BF16),
            jax.ShapeDtypeStruct(piece, BF16),
            jax.ShapeDtypeStruct((t, D), F32),
        ),
        in_specs=[SMEM, by_rows(D), by_rows(D), whole(w.shape), ANY],
        out_specs=(whole(piece), whole(piece), by_rows(D)),
        scratch_shapes=[pltpu.VMEM((D, D), F32)],
        compiler_params=params(60, 1),
        cost_estimate=cost(8),
        name="query_back",
    )(info, a, g, w, dep)


def turn_back(slab, cos, sin, first_half, low_head):
    mixed = slab(2)
    k4 = jnp.where(low_head, 0.0, rope_slab(mixed, cos, sin, first_half))
    k01 = rope_slab(slab(0), cos, sin, first_half)
    k23 = rope_slab(slab(1), cos, sin, first_half)
    v4 = jnp.where(low_head, mixed, 0.0)
    return jnp.concatenate([k4, k01, k23, slab(3), slab(4), v4], axis=1).astype(BF16)


def kv_weights_back(info, cos, sin, turned, totals, dep):
    t = turned[0].shape[1]
    half = t // 2
    piece = ((4, ZP, 384), BF16)
    n_all = len(totals)

    def body(info, ins, outs, scratch):
        cos_ref, sin_ref = ins[0], ins[1]
        a_refs, g_refs = ins[2 : 2 + len(turned)], ins[2 + len(turned) :]
        first_half, low_head = lane_masks(ROWS)
        low, acc = scratch
        for c in range(n_all if n_all < 4 else 4):
            for i in range(t // ROWS):
                at = ROWS * i

                def slab(j):
                    lanes = slice(128 * j, 128 * j + 128)
                    if c < 3:
                        return g_refs[c][at : at + ROWS, lanes].astype(F32)
                    if at + ROWS <= half:
                        return g_refs[3][at : at + ROWS, lanes].astype(F32)
                    if at >= half:
                        return g_refs[4][at - half : at - half + ROWS, lanes].astype(F32)
                    parts = [g_refs[3][at:half, lanes], g_refs[4][0 : at + ROWS - half, lanes]]
                    return jnp.concatenate([p.astype(F32) for p in parts], axis=0)

                r = slice(t * c + at, t * c + at + ROWS)
                cos, sin = wide_tables(cos_ref[:, r], -sin_ref[:, r])
                low[at : at + ROWS, :] = turn_back(slab, cos, sin, first_half, low_head)
            for n, rows in enumerate((slice(0, D // 2), slice(D // 2, D))):
                value = dot(a_refs[2 * c + n][...], low[...])
                if c == 0:
                    acc[rows, :] = value
                else:
                    acc[rows, :] += value
        for core, (k_out, v_out) in enumerate(((outs[0], outs[1]), (outs[1], outs[0]))):
            @pl.when(info[1] == core)
            def _():
                put_shards(k_out, acc[:, 0:384], None)
                put_shards(v_out, acc[:, 384:768], None)

    return step_call(
        "key_value_weights_back",
        body,
        info,
        (cos, sin, *turned, *totals),
        (piece, piece),
        scratch=(pltpu.VMEM((t, 768), BF16), pltpu.VMEM((D, 768), F32)),
        behind=(dep,),
    )


def post_kv_kernel(
    info, s0, s1, s2, cos_ref, sin_ref, part_ref, w_ref, x_ref, gh_ref, gain_ref, ig_ref,
):
    first_half, low_head = lane_masks(ROWS)

    def slab(j):
        c = slice(128 * j, 128 * j + 128)
        return s0[:, c].astype(F32) + s1[:, c].astype(F32) + s2[:, c].astype(F32)

    cos, sin = wide_tables(cos_ref[...], -sin_ref[...])
    low = turn_back(slab, cos, sin, first_half, low_head)
    g = (
        part_ref[...]
        + dot_nt(low[:, 0:384], w_ref[:, 0:384])
        + dot_nt(low[:, 384:704], w_ref[:, 384:704])
    )
    x = x_ref[...].astype(F32)
    factor = lax.rsqrt(jnp.mean(x * x, axis=-1, keepdims=True) + NORM_EPS)
    normed = x * factor
    scaled = g * gain_ref[0:1, :]
    back = factor * (scaled - normed * jnp.mean(scaled * normed, axis=-1, keepdims=True))
    ig_ref[...] = (gh_ref[...] + back).astype(BF16).T


def post_kv_call(info, sums, cos, sin, part, w, x, gh, gain, dep):
    t = x.shape[0]
    return pl.pallas_call(
        lambda *refs: post_kv_kernel(*refs[:11], refs[12]),
        grid=(t // ROWS,),
        out_shape=jax.ShapeDtypeStruct((D, t), BF16),
        in_specs=[SMEM]
        + [by_rows(KV_LANES)] * 3
        + [by_lanes(32)] * 2
        + [by_rows(D), whole(w.shape)]
        + [by_rows(D)] * 2
        + [whole((8, D)), ANY],
        out_specs=by_lanes(D),
        compiler_params=params(60, 1),
        cost_estimate=cost(8),
        name="key_value_back",
    )(info, *sums, cos, sin, part, w, x, gh, gain, dep)


def finish_ffn(info, mine, other, dep):
    out = ((D, 2 * CORE_UNITS), F32)

    def body(info, ins, outs, scratch):
        rows = scratch[0]
        for n in range(3):
            for ref, side in ((ins[0], info[1]), (ins[1], 1 - info[1])):
                at = pl.multiple_of(side * CORE_UNITS, 16)
                rows[pl.ds(at, CORE_UNITS), :] = ref[n].astype(F32)
            outs[n][...] = rows[...].T

    return step_call(
        "finish_feed_forward",
        body,
        info,
        (mine, other),
        (out,) * 3,
        scratch=(pltpu.VMEM((2 * CORE_UNITS, D), F32),),
        behind=(dep,),
    )


def finish_rest(info, mine, other, w_own):
    half = WIDE // 2

    def body(info, ins, outs, scratch):
        wq_ref, wo_ref, wk_ref, wv_ref, one_ref, two_ref = outs

        def emit(first, second):
            def both(at):
                lanes = slice(at, at + half)
                return jnp.concatenate([first[0:ZR, lanes], second[0:ZR, lanes]], axis=1)

            wo_ref[...] = both(0).astype(F32)[:, 0:D]
            query = both(half).astype(F32)[:, 0:D]
            wq_ref[...] = query
            k = first[:, WIDE : WIDE + 384].astype(F32)
            v = second[:, WIDE : WIDE + 384].astype(F32)
            k_t = k.T
            wk_ref[...] = jnp.concatenate([k_t[128:384], k_t[64:128]], axis=0)[:, 0:ZR]
            wv_ref[...] = v.T[0:320, 0:ZR]
            w = ins[2][...].astype(F32)
            total = jnp.sum(query * w[:, 0:D], axis=1, keepdims=True)
            total += jnp.sum(k[0:ZR, 128:384] * w[:, 1024:1280], axis=1, keepdims=True)
            total += jnp.sum(k[0:ZR, 64:128] * w[:, 960:1024], axis=1, keepdims=True)
            total += jnp.sum(v[0:ZR, 0:320] * w[:, 1280:1600], axis=1, keepdims=True)
            total = total / w[:, 1600:1601]
            one_ref[...] = jnp.broadcast_to(total, (ZR, 128)).T[0:1, :]
            two_ref[...] = first[ZR:ZP, :].astype(F32)[0:1, 0:ZR]

        for core, refs in enumerate(((ins[0], ins[1]), (ins[1], ins[0]))):
            @pl.when(info[1] == core)
            def _():
                emit(*refs)

    outs = (((ZR, D), F32), ((ZR, D), F32), ((320, ZR), F32), ((320, ZR), F32), ((1, ZR), F32), ((1, ZR), F32))
    return step_call("finish_rest", body, info, (mine, other, w_own), outs)


def sum_chips(info, terms, over_z, passed, behind):
    n_terms = len(terms)
    cut = P_ROWS // 2

    def body(info, ins, outs, scratch):
        for zz in range(4):
            outs[0][zz] = sum(ins[k][zz].astype(F32) for k in range(n_terms)).astype(BF16)
        for n in range(2):
            outs[1 + n][...] = ins[n_terms][0, :, cut * n : cut * n + cut, :]

    outs = ((terms[0].shape, BF16),) + (((3, cut, D), BF16),) * 2
    return step_call(
        "sum_chips", body, info, (*terms, over_z), outs, behind=behind, passed=passed
    )


def join_cores(info, keep_near, recv_near, keep_far, recv_far, pairs):
    rows = keep_far.shape[0]
    cut = rows // 2

    def body(info, ins, outs, scratch):
        for n in range(3):
            r = slice(rows * n, rows * n + rows)
            outs[n][...] = ins[0][r, :] + ins[1][r, :]
        for n in range(2):
            r = slice(cut * n, cut * n + cut)
            outs[3 + n][...] = ins[2][r, :] + ins[3][r, :]
        for n in range(len(pairs)):
            outs[5 + n][...] = ins[4 + 2 * n][...] + ins[5 + 2 * n][...]

    outs = (((rows, KV_LANES), BF16),) * 3 + (((cut, KV_LANES), BF16),) * 2
    outs += tuple((a.shape, BF16) for a, _ in pairs)
    flat = [a for pair in pairs for a in pair]
    return step_call(
        "join_cores", body, info, (keep_near, recv_near, keep_far, recv_far, *flat), outs
    )


def join_near(info, to_x, to_y, from_x, from_y, pairs, passed):
    cut = from_x.shape[0]
    rows = pairs[0][0].shape[1]

    def body(info, ins, outs, scratch):
        to_x, to_y, from_x, from_y = ins[:4]
        outs[0][0:cut, :] = to_x[0:cut, :]
        outs[0][cut : 2 * cut, :] = to_x[cut : 2 * cut, :] + from_y[...]
        outs[1][0:cut, :] = to_y[0:cut, :] + from_x[...]
        outs[1][cut : 2 * cut, :] = to_y[cut : 2 * cut, :]
        for n in range(2):
            outs[2][:, rows * n : rows * n + rows, :] = ins[4 + 2 * n][...] + ins[5 + 2 * n][...]

    flat = [a for pair in pairs for a in pair]
    return step_call(
        "join_near",
        body,
        info,
        (to_x, to_y, from_x, from_y, *flat),
        ((to_x.shape, BF16),) * 2 + (((3, P_ROWS, D), BF16),),
        passed=passed,
    )


def join_projections(info, q_pair, kv_pair, h1, acc_o, got_o, dep):
    t = h1.shape[0]
    half = WIDE // 2

    def body(info, ins, outs, scratch):
        outs[0][:, :, 0:half] = ins[0][...] + ins[1][...]
        outs[0][:, :, half : half + 384] = ins[2][...] + ins[3][...]
        for i in range(t // ROWS):
            r = slice(ROWS * i, ROWS * i + ROWS)
            value = ins[4][r, :] + ins[5][r, :] + ins[6][r, 0:D].astype(F32)
            outs[1][:, r] = value.astype(BF16).T

    return step_call(
        "join_projections",
        body,
        info,
        (*q_pair, *kv_pair, h1, acc_o, got_o),
        (((4, ZP, half + 384), BF16), ((D, t), BF16)),
        behind=(dep,),
    )


def halve_rows(info, left, right, behind):
    rows = left.shape[1] // 2
    lanes = left.shape[2], right.shape[2]

    def body(info, ins, outs, scratch):
        for n in range(2):
            r = slice(rows * n, rows * n + rows)
            outs[n][:, 0 : lanes[0]] = ins[0][0, r, :]
            outs[n][:, lanes[0] : sum(lanes)] = ins[1][0, r, :]

    outs = (((rows, sum(lanes)), BF16),) * 2
    return step_call("halve_rows", body, info, (left, right), outs, behind=behind)


def add_pairs(info, pairs, behind=()):
    def body(info, ins, outs, scratch):
        for n in range(len(pairs)):
            outs[n][...] = ins[2 * n][...] + ins[2 * n + 1][...]

    flat = [a for pair in pairs for a in pair]
    outs = tuple((a.shape, BF16) for a, _ in pairs)
    return step_call("add_pairs", body, info, flat, outs, behind=behind)


def stack_two(info, first, second, behind):
    def body(info, ins, outs, scratch):
        for n in range(2):
            outs[0][n] = ins[n][...]

    out = ((2,) + first.shape, BF16)
    return step_call("stack_two", body, info, (first, second), (out,), behind=behind)[0]


def stack_pairs(info, pairs, dep):
    rows = pairs[0][0].shape[0]

    def body(info, ins, outs, scratch):
        for n in range(2):
            outs[0][rows * n : rows * n + rows, :] = ins[2 * n][...] + ins[2 * n + 1][...]

    flat = [a for pair in pairs for a in pair]
    shape = (2 * rows,) + pairs[0][0].shape[1:]
    return step_call("stack_pairs", body, info, flat, ((shape, BF16),), behind=(dep,))[0]


def join_ffn(info, first, near, far, dep):
    def body(info, ins, outs, scratch):
        chip = info[3]
        out = outs[0]
        out[:, 0:P_ROWS, :] = ins[0][...]
        for r in range(4):
            at = pl.multiple_of(P_ROWS + Q_ROWS * (chip ^ r), 16)
            out[:, pl.ds(at, Q_ROWS), :] = ins[1 + r // 2][r % 2]

    return step_call(
        "join_feed_forward",
        body,
        info,
        (first, near, far),
        (((3, CORE_UNITS, D), BF16),),
        behind=(dep,),
    )[0]


def rows_after(x, start, size, tok, axis=0):
    return lax.dynamic_slice_in_dim(x, start + tok, size, axis=axis)


def z_shift(x, step):
    n = 4
    return lax.ppermute(x, "fsdp", [(i, (i + step) % n) for i in range(n)])


def c_swap(x, bit):
    n = lax.axis_size("ctx")
    return lax.ppermute(x, "ctx", [(i, i ^ bit) for i in range(n)])


def bits_from(b):
    bits = []
    while b < lax.axis_size("ctx"):
        bits.append(b)
        b *= 2
    return bits


def chip_near(kv):
    if lax.axis_size("ctx") != 8:
        return ()
    return c_swap(kv, 2), c_swap(kv, 4)


def chip_far(kv, near):
    if not near:
        return [lax.all_gather(kv, "ctx", axis=0, tiled=True)]
    cut = kv.shape[0] // 2
    across_x, across_y = near
    far_lo = c_swap(across_x[:cut], 4)
    far_hi = c_swap(across_y[cut:], 2)
    chip = [kv, across_x, across_y, far_lo, far_hi]
    return chip + [c_swap(part, 1) for part in chip]


def kv_entry(position, per_dev, me, n):
    if n != 8:
        return position
    owner, within = position // per_dev, position % per_dev
    rel = owner ^ me
    cut = per_dev // 2
    far = (rel // 2) == 3
    late = far & (within >= cut)
    which = (rel % 2) * 5 + rel // 2 + late.astype(jnp.int32)
    return which * 1024 + jnp.where(late, within - cut, within)


def kv_slot(position, per_dev, me):
    owner, within = position // per_dev, position % per_dev
    rel = owner ^ me
    return ((rel % 2) * 4 + rel // 2) * per_dev + within


def on_device(
    tokens,
    cotangent,
    doc_lengths,
    deal,
    attn_gain,
    w_query,
    w_key,
    w_value,
    w_out,
    mlp_gain,
    w_gate,
    w_up,
    w_down,
):
    me = lax.axis_index("ctx")
    n_ctx = lax.axis_size("ctx")
    z = lax.axis_index("fsdp")
    core = me % 2
    near_me = me % 8
    chip = near_me // 2
    parity = (chip + chip // 2) % 2
    info = jnp.stack([z, core, near_me, chip, parity]).astype(jnp.int32)
    tok_rows = tokens.shape[1]
    per_dev = tok_rows // BLK
    deal_row = deal[0]
    blocks = deal_row.shape[0]
    group_size = blocks * BLK
    doc_lens = doc_lengths[0]
    seq_count = doc_lens.shape[0]
    length = group_size // seq_count
    x_turned = tokens[0].T
    cot_turned = cotangent[0].T

    block_ids = jnp.arange(blocks, dtype=jnp.int32)
    mine = lax.dynamic_slice_in_dim(deal_row, me * per_dev, per_dev)
    seq_blocks = jnp.maximum(
        mine[:, None] - (NWB - 1) + jnp.arange(NWB, dtype=jnp.int32)[None, :], 0
    )
    position = jnp.sum(
        jnp.where(seq_blocks[:, :, None] == deal_row[None, None, :], block_ids, 0), axis=-1
    )
    tab = kv_entry(position, per_dev, me, n_ctx).astype(jnp.int32)
    doc_ends = (
        jnp.cumsum(doc_lens, axis=1) + (jnp.arange(seq_count, dtype=jnp.int32) * length)[:, None]
    ).reshape(-1)
    doc_starts = doc_ends - doc_lens.reshape(-1)
    q_time = mine[:, None] * BLK + jnp.arange(BLK, dtype=jnp.int32)[None, :]
    begin = jnp.max(jnp.where(q_time[..., None] >= doc_starts, doc_starts, 0), axis=-1)
    lo = jnp.maximum(begin, q_time - (WIN - 1)) - (mine[:, None] * BLK - WIN)
    lo = lo[:, None, :].astype(jnp.int32)
    n_chips = 4 if n_ctx == 8 else 1
    owners = jnp.stack([me ^ (2 * r) for r in range(n_chips)])
    theirs = jnp.sum(
        jnp.where(
            block_ids == (owners[:, None] * per_dev + jnp.arange(per_dev, dtype=jnp.int32))[..., None],
            deal_row,
            0,
        ),
        axis=-1,
    )
    their_time = theirs[:, :, None] * BLK + jnp.arange(BLK, dtype=jnp.int32)
    their_begin = jnp.max(jnp.where(their_time[..., None] >= doc_starts, doc_starts, 0), axis=-1)
    pos = (their_time - their_begin).reshape(-1)
    half_dim = HD // 2
    freqs = ROPE_THETA ** (-jnp.arange(half_dim, dtype=F32) * (2.0 / HD))
    angle = freqs[:, None] * pos.astype(F32)[None, :]
    cos_turn, sin_turn = jnp.cos(angle), jnp.sin(angle)

    gains_wide = jnp.concatenate(
        [attn_gain[:, None], mlp_gain[:, None], jnp.zeros((ZR, QKV - 1602), BF16)], axis=1
    )
    w_parts = [w_query, w_key[:, 256:], w_key[:, :256], w_value, gains_wide]
    start = jnp.minimum(32 * near_me, ZR - 32)
    w_mine = jnp.concatenate(
        [lax.dynamic_slice_in_dim(w, start, 32, axis=0) for w in w_parts], axis=1
    )
    w_z = [z_shift(w_mine, -1), z_shift(w_mine, 2), z_shift(w_mine, 1)]
    own_half, packed = prep_weights(info, w_gate, w_up, w_down.T)
    w_got, packed = stack_weights(info, w_z, (cos_turn, sin_turn), (packed,))
    over_z = lax.all_gather(packed, "fsdp", axis=0, tiled=False)
    cot_there = c_swap(cot_turned, 1)
    w_chips = [w_got, c_swap(w_got, 2), c_swap(w_got, 4), c_swap(w_got, 6)]
    w_pieces = [jnp.concatenate(w_parts, axis=1)]
    for piece in w_chips:
        w_pieces += [piece, c_swap(piece, 1)]

    attn_in, attn_up, attn_lo, q_low, kv_low, x, gains, w_q, w_kv = pre_call(
        info, x_turned, cos_turn, sin_turn, w_pieces
    )
    kvs = chip_far(kv_low, chip_near(kv_low))

    first, second = split_quarters(info, over_z, kvs[3:5] if n_ctx == 8 else kvs)
    first_on, second_on = c_swap(first, 2), c_swap(second, 4)
    out_mine = lax.dynamic_slice_in_dim(w_out, (ZR - OUT_ROWS) * core, OUT_ROWS, axis=0)
    out_mine = meet(info, (out_mine,), (first,))[0]
    out_here = [z_shift(out_mine, -1), z_shift(out_mine, 2), z_shift(out_mine, 1)]
    mid_low, recips, probs = fwd_call(tab, lo, q_low, kvs)
    *out_here, first_on, second_on = meet(info, (*out_here, first_on, second_on), (mid_low,))
    out_there = [c_swap(p, 1) for p in out_here]
    here = (first, second, first_on, second_on)
    h1, mlp_in, w_out_all, attn_up, attn_lo = pro_call(
        info, mid_low, x, gains, w_out, out_here, out_there, cot_there, (attn_up, attn_lo)
    )
    acc_o, acc_g, send_o, send_lo, send_hi, p_both, *q_both = ffn_call(
        info, mlp_in, c_swap(mlp_in, 1), cot_turned, cot_there, own_half, here
    )
    p_sum = lax.psum_scatter(p_both, "fsdp", scatter_dimension=0, tiled=True)
    q_got = [c_swap(q_both[r], 2 * r) for r in range(1, 4)]
    got_o = c_swap(send_o, 1)
    attn_turned = [attn_up, attn_lo]
    a_x = [c_swap(a, 2) for a in attn_turned]
    a_y = [c_swap(a, 4) for a in attn_turned]
    send_lo, send_hi, *a_near = meet(info, (send_lo, send_hi, *a_x, *a_y))
    got_lo, got_hi = c_swap(send_lo, 1), c_swap(send_hi, 1)
    grad_hidden, grad_mid, go_keep, go_send = epi_call(
        info, h1, acc_g, got_lo, got_hi, cot_turned, gains, w_out_all, mid_low
    )
    a_turned = [*attn_turned, *a_near, c_swap(a_near[0], 4), c_swap(a_near[3], 2)]

    if n_ctx == 8:
        out_units = (3, 1, 3, 1)
        slots = kv_slot(position, per_dev, me).astype(jnp.int32)
    else:
        out_units = (NWB,)
        n_slots = per_dev * NWB
        flat_pos = position.reshape(-1)
        order = jnp.arange(n_slots, dtype=jnp.int32)
        slots = jnp.min(
            jnp.where(flat_pos[:, None] == flat_pos[None, :], order[None, :], n_slots), axis=1
        ).reshape(per_dev, NWB)
        source = jnp.min(
            jnp.where(block_ids[:, None] == flat_pos[None, :], order[None, :], n_slots), axis=1
        )

    def own_rows(parts):
        width = parts[0].shape[1]
        padded = jnp.concatenate(
            [parts[0].reshape(n_slots, BLK, width), jnp.zeros((1, BLK, width), BF16)], axis=0
        )
        spread = jnp.take(padded, source, axis=0).reshape(group_size, width)
        own = lax.psum_scatter(spread, "ctx", scatter_dimension=0, tiled=True)
        return own, (own, jnp.zeros_like(own), jnp.zeros_like(own))

    back_args = (
        tab, slots, out_units, q_low, grad_mid, mid_low, recips, probs, cos_turn, sin_turn, kvs
    )
    dq, *kv_parts = bwd_call(0, per_dev, (), (), *back_args)
    q_terms = (q_both[0], *q_got)
    go_pair = (go_keep, c_swap(go_send, 1))
    if n_ctx == 8:
        keep_near, keep_far, send_near, send_far = kv_parts
        q_sum, p_l, p_r, send_near, send_far, a_lo, a_hi = sum_chips(
            info, q_terms, p_sum, (send_near, send_far, *a_turned[6:]), (dq,)
        )
        a_turned[6:] = [a_lo, a_hi]
        own, to_x, to_y, far_lo, far_hi, go_both, p_l, p_r = join_cores(
            info,
            keep_near,
            c_swap(send_near, 1),
            keep_far,
            c_swap(send_far, 1),
            (go_pair, (p_l, c_swap(p_l, 2)), (p_r, c_swap(p_r, 4))),
        )
        totals = (own, to_x, to_y, far_lo, far_hi)
    else:
        q_sum, p_l, p_r = sum_chips(info, q_terms, p_sum, (), (dq,))
        own, sums = own_rows(kv_parts)
        a_turned, totals = a_turned[:2], (own,)
        go_both, p_l, p_r = add_pairs(
            info, (go_pair, (p_l, c_swap(p_l, 2)), (p_r, c_swap(p_r, 4)))
        )
    q_mine = lax.psum_scatter(q_sum, "fsdp", scatter_dimension=0, tiled=True)[0]
    for b in bits_from(8):
        q_mine = q_mine + c_swap(q_mine, b)
    gq_keep, gq_send, part = post_q_call(info, attn_in, dq, w_q, own)
    go_sum = lax.psum_scatter(go_both, "fsdp", scatter_dimension=0, tiled=True)
    gkv_keep, gkv_send = kv_weights_back(info, cos_turn, sin_turn, a_turned, totals, gq_keep)
    p_pairs = ((p_l, c_swap(p_l, 4)), (p_r, c_swap(p_r, 2)))
    if n_ctx == 8:
        to_x, to_y, p_sum, gq_send, gkv_send, q_mine = join_near(
            info,
            to_x,
            to_y,
            c_swap(far_lo, 2),
            c_swap(far_hi, 4),
            p_pairs,
            (gq_send, gkv_send, q_mine),
        )
        sums = (own, c_swap(to_x, 2), c_swap(to_y, 4))
    else:
        p_sum = jnp.concatenate([a + b for a, b in p_pairs], axis=1)
    g_both, output = join_projections(
        info, (gq_keep, c_swap(gq_send, 1)), (gkv_keep, c_swap(gkv_send, 1)), h1, acc_o, got_o, p_sum
    )
    g_sum = lax.psum_scatter(g_both, "fsdp", scatter_dimension=0, tiled=True)
    q_near = stack_two(info, q_mine, c_swap(q_mine, 2), (output,))
    q_far = c_swap(q_near, 4)
    input_grad = post_kv_call(
        info, sums, cos_turn, sin_turn, part, w_kv, x, grad_hidden, gains, q_near
    )
    for b in bits_from(8):
        p_sum = p_sum + c_swap(p_sum, b)
    ffn_sum = join_ffn(info, p_sum, q_near, q_far, input_grad)
    g_l, g_r = halve_rows(info, go_sum, g_sum, (ffn_sum,))
    g_l, g_r = add_pairs(info, ((g_l, c_swap(g_l, 2)), (g_r, c_swap(g_r, 4))))
    gate_grad, up_grad, down_grad = finish_ffn(info, ffn_sum, c_swap(ffn_sum, 1), g_l)
    g_sum = stack_pairs(info, ((g_l, c_swap(g_l, 4)), (g_r, c_swap(g_r, 2))), gate_grad)
    for b in bits_from(8):
        g_sum = g_sum + c_swap(g_sum, b)
    query_grad, out_grad, key_grad, value_grad, gain_one, gain_two = finish_rest(
        info, g_sum, c_swap(g_sum, 1), w_pieces[0]
    )

    return (
        output.T[None],
        input_grad.T[None],
        gain_one.reshape(ZR),
        query_grad,
        key_grad.T,
        value_grad.T,
        out_grad,
        gain_two.reshape(ZR),
        gate_grad,
        up_grad,
        down_grad.T,
    )


def solution(mesh):
    in_specs = (
        P("fsdp", "ctx", None),
        P("fsdp", "ctx", None),
        P("fsdp", None, None),
        P("fsdp", None),
        P("fsdp"),
        P("fsdp", None),
        P("fsdp", None),
        P("fsdp", None),
        P("fsdp", None),
        P("fsdp"),
        P(None, "fsdp"),
        P(None, "fsdp"),
        P("fsdp", None),
    )
    out_specs = (
        P("fsdp", "ctx", None),
        P("fsdp", "ctx", None),
        P("fsdp"),
        P("fsdp", None),
        P("fsdp", None),
        P("fsdp", None),
        P("fsdp", None),
        P("fsdp"),
        P(None, "fsdp"),
        P(None, "fsdp"),
        P("fsdp", None),
    )
    return jax.shard_map(
        on_device, mesh=mesh, in_specs=in_specs, out_specs=out_specs, check_vma=False
    )
```

time: 507 us -> 467 us (0.921)
  Pallas kernels: 201 us -> 233 us
  local copies, waits for them, and re-layouts: 55 us -> 26.4 us
  waiting for transfers between devices: 161 us -> 135 us
  starting transfers between devices: 59.5 us -> 46.3 us
    pallas_call x20 -> x22, Pallas kernels: 65.3 us -> 101 us  [the longest x18 66.6 us: step_call(): pl.pallas_call(kernel, grid=(1,), out_shape=tuple((jax.ShapeDtypeStruct(s...]
    ppermute x9 -> x6, waiting for transfers between devices: 40.3 us -> 6.67 us  [z_shift(): return lax.ppermute(x, 'fsdp', [(i, (i + step) % n) for i in range(n)])]
    unnamed x146 -> x107, local copies, waits for them, and re-layouts: 41.2 us -> 17.3 us
    ppermute x56, waiting for transfers between devices: 108 us -> 121 us  [c_swap(): return lax.ppermute(x, 'ctx', [(i, i ^ bit) for i in range(n)])]
    ppermute x9 -> x6, starting transfers between devices: 16.1 us -> 8.48 us  [z_shift(): return lax.ppermute(x, 'fsdp', [(i, (i + step) % n) for i in range(n)])]
    ppermute x56, starting transfers between devices: 43 us -> 37.6 us  [c_swap(): return lax.ppermute(x, 'ctx', [(i, i ^ bit) for i in range(n)])]
  transfers between devices with their start and end apart: 68 -> 67, of which waited for: 29 -> 24; matrix products, arithmetic and copies ran while one was open for 3% -> 2% of each run, Pallas kernels for 28% -> 46%
where the time goes in v3:
time: 467 us; the launch traced here: 460 us
  Pallas kernels  233 us (50%)
  waiting for transfers between devices  135 us (29%)
  starting transfers between devices  46.3 us (10%)
  local copies, waits for them, and re-layouts  26.4 us (6%)
  between operations  14.7 us (3%)
  other arithmetic  5.17 us (1%)
    ppermute x56, waiting for transfers between devices, c_swap(): return lax.ppermute(x, 'ctx', [(i, i ^ bit) for i in range(n)])  121 us
    pallas_call x18, Pallas kernels, step_call(): pl.pallas_call(kernel, grid=(1,), out_shape=tuple((jax.ShapeDtypeStruct(s...  66.6 us
    pallas_call x1, Pallas kernels, ffn_call(): pl.pallas_call(ffn_kernel, out_shape=(jax.ShapeDtypeStruct((t, D), F32),...  50.7 us
    pallas_call x1, Pallas kernels, bwd_call(): pl.pallas_call(lambda *refs: bwd_kernel(n_kv, len(deps), first, prev, out...  39.4 us
    ppermute x56, starting transfers between devices, c_swap(): return lax.ppermute(x, 'ctx', [(i, i ^ bit) for i in range(n)])  37.6 us
    pallas_call x1, Pallas kernels, fwd_call(): pl.pallas_call(lambda *refs: fwd_kernel(n_kv, *refs), grid=(blocks,), out...  30.3 us
    unnamed x107, local copies, waits for them, and re-layouts  17.3 us
    pallas_call x1, Pallas kernels, epi_call(): pl.pallas_call(epi_kernel, grid=(t // ROWS,), out_shape=(jax.ShapeDtypeSt...  11.7 us
  transfers between devices with their start and end apart: 67, of which 24 were waited for; matrix products, arithmetic and copies ran while one was open for 2% of the time, Pallas kernels for 46%

profile of v3, /device:TPU:0, one launch (start us, length us, event | category | flops | bytes accessed | tf_op | source)
XLA Modules:
  0.0 460.2 jit_solution(12146933380125624207)
XLA Ops:
  13.0 5.1 %collective-permute-start = (bf16[32,1664]{1,0:T(8,128)(2,1)S(1)}, bf16[32,1664]{1,0:T(8,128)(2,1)S(1)}, u32[]{:S(2)}, u32[]{:S(2)}) collective-permute-start(bf16[32,1664]{1,0:T(8,128)(2,1)S(1)} %concatenate.16), channel_id=1, source_target_pairs={{0,3},{1,0},{2,1},{3,2},{4,7},{5,4},{6,5},{7,6},{8,11},{9,8},{10,9... | collective-permute-start | bytes 319496 | tf_op jit(solution)/shard_map/ppermute | solution.py:1324
  22.9 5.0 %prep_weights.1 = (bf16[3,320,960]{2,1,0:T(8,128)(2,1)}, bf16[480,960]{1,0:T(8,128)(2,1)}) custom-call(s32[5]{0:T(128)} %stack.38.info_ref.info.refs_0_, bf16[960,640]{1,0:T(8,128)(2,1)} %refs_0_.1, bf16[960,640]{1,0:T(8,128)(2,1)} %refs_1_.1, bf16[960,640]{1,0:T(8,128)(2,1)} %bitcast.56), custom_call_target="tpu_custom_call" | custom-call | flops 1750000000 | bytes 1 | tf_op jit(solution)/shard_map/prep_weights/pallas_call | solution.py:155
  34.1 7.2 %collective-permute-done.4.refs_3_ = bf16[3,32,1664]{2,1,0:T(8,128)(2,1)S(1)} collective-permute-done((bf16[3,32,1664]{2,1,0:T(8,128)(2,1)}, bf16[3,32,1664]{2,1,0:T(8,128)(2,1)S(1)}, u32[]{:S(2)}, u32[]{:S(2)}) %collective-permute-start.4) | collective-permute-done | bytes 319520 | tf_op jit(solution)/shard_map/ppermute | solution.py:1329
  41.3 6.0 %collective-permute-done.6.refs_5_ = bf16[3,32,1664]{2,1,0:T(8,128)(2,1)S(1)} collective-permute-done((bf16[3,32,1664]{2,1,0:T(8,128)(2,1)}, bf16[3,32,1664]{2,1,0:T(8,128)(2,1)S(1)}, u32[]{:S(2)}, u32[]{:S(2)}) %collective-permute-start.6) | collective-permute-done | bytes 319520 | tf_op jit(solution)/shard_map/ppermute | solution.py:1329
  49.9 9.3 %pre.1 = (bf16[768,960]{1,0:T(8,128)(2,1)}, bf16[480,768]{1,0:T(8,128)(2,1)}, bf16[480,768]{1,0:T(8,128)(2,1)}, bf16[768,960]{1,0:T(8,128)(2,1)}, bf16[768,640]{...) custom-call(s32[5]{0:T(128)} %stack.38.info_ref.info.refs_0_, ...), custom_call_target="tpu_custom_call" | custom-call | flops 4200000000 | bytes 1 | tf_op jit(solution)/shard_map/pre/pallas_call | solution.py:319
  61.5 21.9 %collective-permute-done.10.refs_4_.refs_10_ = bf16[768,640]{1,0:T(8,128)(2,1)} collective-permute-done((bf16[768,640]{1,0:T(8,128)(2,1)}, bf16[768,640]{1,0:T(8,128)(2,1)}, u32[]{:S(2)}, u32[]{:S(2)}) %collective-permute-start.10) | collective-permute-done | bytes 983072 | tf_op jit(solution)/shard_map/ppermute | solution.py:1329
  88.8 8.2 %collective-permute-done.12.refs_6_.refs_1_.refs_12_ = bf16[384,640]{1,0:T(8,128)(2,1)S(1)} collective-permute-done((bf16[384,640]{1,0:T(8,128)(2,1)S(1)}, bf16[384,640]{1,0:T(8,128)(2,1)S(1)}, u32[]{:S(2)}, u32[]{:S(2)}) %collective-permute-start.12) | collective-permute-done | bytes 491552 | tf_op jit(solution)/shard_map/ppermute | solution.py:1329
  100.7 6.8 %all-gather.3.cloned.1.call-done = bf16[1920,960]{1,0:T(8,128)(2,1)} async-done(((bf16[480,960]{1,0:T(8,128)(2,1)}), bf16[1920,960]{1,0:T(8,128)(2,1)}) %all-gather.3.cloned.1.call-update) | async-done | bytes 3686416 | tf_op jit(solution)/shard_map/all_gather | solution.py:1455
  117.8 6.7 %collective-permute-done.19.refs_1_ = bf16[128,960]{1,0:T(8,128)(2,1)S(1)} collective-permute-done((bf16[128,960]{1,0:T(8,128)(2,1)}, bf16[128,960]{1,0:T(8,128)(2,1)S(1)}, u32[]{:S(2)}, u32[]{:S(2)}) %collective-permute-start.19) | collective-permute-done | bytes 245792 | tf_op jit(solution)/shard_map/ppermute | solution.py:1324
  125.9 30.3 %attend.1 = (bf16[768,960]{1,0:T(8,128)(2,1)}, f32[6,16,128]{2,1,0:T(8,128)}, bf16[6,1152,1920]{2,1,0:T(8,128)(2,1)}) custom-call(s32[6,9]{1,0:T(8,128)} %get-tuple-element.204.refs_0_, s32[6,1,128]{2,1,0:T(1,128)} %maximum_subtract_fusion.refs_1_, bf16[768,960]{1,0:T(8,128)(2,1)} %get-tuple-element.108.refs_2_, ...), custom_call_target="tpu_custom_call" | custom-call | flops 11200000000 | bytes 1 | tf_op jit(solution)/shard_map/attend/pallas_call | solution.py:455
  161.5 7.7 %out_projection.1 = (f32[768,960]{1,0:T(8,128)}, bf16[768,1024]{1,0:T(8,128)(2,1)}, bf16[960,960]{1,0:T(8,128)(2,1)}, bf16[480,768]{1,0:T(8,128)(2,1)}, bf16[480,768]{1,0:T(8,128)(2,1)}) custom-call(s32[5]{0:T(128)} %stack.38.info_ref.info.refs_0_, ...), custom_call_target="tpu_custom_call", output_to_operand_aliasing={{3}: (12, {}), {4}: (13, {})} | custom-call | flops 2449999872 | bytes 1 | tf_op jit(solution)/shard_map/out_projection/pallas_call | solution.py:682
  173.5 50.7 %feed_forward.1 = (f32[768,960]{1,0:T(8,128)}, f32[768,960]{1,0:T(8,128)}, bf16[768,1024]{1,0:T(8,128)(2,1)}, bf16[768,512]{1,0:T(8,128)(2,1)}, bf16[768,512]{1,...) custom-call(s32[5]{0:T(128)} %stack.38.info_ref.info.refs_0_, ...), custom_call_target="tpu_custom_call" | custom-call | flops 17500000256 | bytes 1 | tf_op jit(solution)/shard_map/feed_forward/pallas_call | solution.py:844
  232.3 11.7 %feed_forward_norm_back.1 = (f32[768,960]{1,0:T(8,128)}, bf16[768,960]{1,0:T(8,128)(2,1)}, bf16[4,256,512]{2,1,0:T(8,128)(2,1)}, bf16[4,256,512]{2,1,0:T(8,128)(2,1)}) custom-call(s32[5]{0:T(128)} %stack.38.info_ref.info.refs_0_, f32[768,960]{1,0:T(8,128)} %get-tuple-element.121.h1_ref.refs_4_, f32[768,960]{1,0:T(8,128)} %get-tuple-element.126.acc_g, ...), custom_call_target="tpu_custom_call" | custom-call | flops 4200000000 | bytes 1 | tf_op jit(solution)/shard_map/feed_forward_norm_back/pallas_call | solution.py:943
  244.0 39.4 %attend_back_0.1 = (bf16[768,960]{1,0:T(8,128)(2,1)}, bf16[2304,640]{1,0:T(8,128)(2,1)}, bf16[768,640]{1,0:T(8,128)(2,1)}, bf16[2304,640]{1,0:T(8,128)(2,1)}, bf16[768,640]{1,0:T(8,128)(2,1)}) custom-call(s32[6,9]{1,0:T(8,128)} %get-tuple-element.204.refs_0_, s32[6,9]{1,0:T(8,128)} %get-tuple-element.203.refs_1_, ...), custom_call_target="tpu_custom_call" | custom-call | flops 3499999887360 | bytes 1 | tf_op jit(solution)/shard_map/attend_back_0/pallas_call | solution.py:606
  283.4 14.1 %collective-permute-done.37.refs_3_ = bf16[4,3,48,960]{3,2,1,0:T(8,128)(2,1)} collective-permute-done((bf16[4,3,48,960]{3,2,1,0:T(8,128)(2,1)}, bf16[4,3,48,960]{3,2,1,0:T(8,128)(2,1)}, u32[]{:S(2)}, u32[]{:S(2)}) %collective-permute-start.37) | collective-permute-done | bytes 1105952 | tf_op jit(solution)/shard_map/ppermute | solution.py:1329
  308.9 5.3 %collective-permute-done.43.refs_7_ = bf16[3,64,960]{2,1,0:T(8,128)(2,1)S(1)} collective-permute-done((bf16[3,64,960]{2,1,0:T(8,128)(2,1)}, bf16[3,64,960]{2,1,0:T(8,128)(2,1)S(1)}, u32[]{:S(2)}, u32[]{:S(2)}) %collective-permute-start.43) | collective-permute-done | bytes 368672 | tf_op jit(solution)/shard_map/ppermute | solution.py:1329
  316.6 7.0 %join_cores.1 = (bf16[768,640]{1,0:T(8,128)(2,1)}, bf16[768,640]{1,0:T(8,128)(2,1)}, bf16[768,640]{1,0:T(8,128)(2,1)}, bf16[384,640]{1,0:T(8,128)(2,1)}, bf16[38...) custom-call(s32[5]{0:T(128)} %stack.38.info_ref.info.refs_0_, ...), custom_call_target="tpu_custom_call" | custom-call | flops 1750000000 | bytes 1 | tf_op jit(solution)/shard_map/join_cores/pallas_call | solution.py:155
  327.9 8.7 %query_back.1 = (bf16[4,256,512]{2,1,0:T(8,128)(2,1)}, bf16[4,256,512]{2,1,0:T(8,128)(2,1)}, f32[768,960]{1,0:T(8,128)}) custom-call(s32[5]{0:T(128)} %stack.38.info_ref.info.refs_0_, bf16[768,960]{1,0:T(8,128)(2,1)} %get-tuple-element.107.a_ref, bf16[768,960]{1,0:T(8,128)(2,1)} %get-tuple-element.137.refs_5_.g_ref, ...), custom_call_target="tpu_custom_call" | custom-call | flops 2800000000 | bytes 1 | tf_op jit(solution)/shard_map/query_back/pallas_call | solution.py:990
  336.5 10.6 %key_value_weights_back.1 = (bf16[4,256,384]{2,1,0:T(8,128)(2,1)}, bf16[4,256,384]{2,1,0:T(8,128)(2,1)}) custom-call(s32[5]{0:T(128)} %stack.38.info_ref.info.refs_0_, f32[32,3072]{1,0:T(8,128)} %get-tuple-element.202.refs_3_.cos_ref.refs_7_.refs_0_.refs_4_, f32[32,3072]{1,0:T(8,128)} %get-tuple-element.201.refs_4_.sin_ref.refs_8_.refs_1_.refs_5_, ...), custom_call_target="tpu_custom_call" | custom-call | flops 3849999872 | bytes 1 | tf_op jit(solution)/shard_map/key_value_weights_back/pallas_call | solution.py:155
  357.6 6.6 %join_projections.1 = (bf16[4,256,896]{2,1,0:T(8,128)(2,1)}, bf16[960,768]{1,0:T(8,128)(2,1)}) custom-call(s32[5]{0:T(128)} %stack.38.info_ref.info.refs_0_, bf16[4,256,512]{2,1,0:T(8,128)(2,1)} %get-tuple-element.157.refs_15_.refs_0_, bf16[4,256,512]{2,1,0:T(8,128)(2,1)} %copy-done.6, bf16[4,256,384]{2,1,0:T(8,128)(2,1)} %get-tuple-element.172.refs_2_, ...), custom_call_target="tpu_custom_call" | custom-call | flops 2449999872 | bytes 1 | tf_op jit(solution)/shard_map/join_projections/pallas_call | solution.py:155
  367.4 27.1 %collective-permute-done.54.refs_1_ = bf16[3,48,960]{2,1,0:T(8,128)(2,1)S(1)} collective-permute-done((bf16[3,48,960]{2,1,0:T(8,128)(2,1)S(1)}, bf16[3,48,960]{2,1,0:T(8,128)(2,1)S(1)}, u32[]{:S(2)}, u32[]{:S(2)}) %collective-permute-start.54) | collective-permute-done | bytes 276512 | tf_op jit(solution)/shard_map/ppermute | solution.py:1329
  399.6 8.7 %key_value_back.1.refs_3_ = bf16[960,768]{1,0:T(8,128)(2,1)} custom-call(s32[5]{0:T(128)} %stack.38.info_ref.info.refs_0_, bf16[768,640]{1,0:T(8,128)(2,1)} %get-tuple-element.156._.refs_10_.refs_1_, bf16[768,640]{1,0:T(8,128)(2,1)} %copy-done.8, bf16[768,640]{1,0:T(8,128)(2,1)} %copy-done.9, ...), custom_call_target="tpu_custom_call" | custom-call | flops 2800000000 | bytes 1 | tf_op jit(solution)/shard_map/key_value_back/pallas_call | solution.py:1094
  419.9 8.9 %collective-permute-done.56.refs_1_ = bf16[128,1408]{1,0:T(8,128)(2,1)S(1)} collective-permute-done((bf16[128,1408]{1,0:T(8,128)(2,1)}, bf16[128,1408]{1,0:T(8,128)(2,1)S(1)}, u32[]{:S(2)}, u32[]{:S(2)}) %collective-permute-start.56) | collective-permute-done | bytes 360480 | tf_op jit(solution)/shard_map/ppermute | solution.py:1329
  435.9 6.2 %finish_feed_forward.1 = (f32[960,640]{1,0:T(8,128)}, f32[960,640]{1,0:T(8,128)}, f32[960,640]{1,0:T(8,128)}) custom-call(s32[5]{0:T(128)} %stack.38.info_ref.info.refs_0_, bf16[3,320,960]{2,1,0:T(8,128)(2,1)} %join_feed_forward.1.refs_2_.refs_0_, bf16[3,320,960]{2,1,0:T(8,128)(2,1)} %copy-done.31, bf16[128,1408]{1,0:T(8,128)(2,1)} %get-tuple-element.188.refs_2_.refs_0_), custom_call_target="tpu_custom_call" | custom-call | flops 2100000000 | bytes 1 | tf_op jit(solution)/shard_map/finish_feed_forward/pallas_call | solution.py:155
  (287 shorter events, 126.3 us)
Async XLA Ops:
  7.2 100.3 %all-gather.3.cloned.1.call-start = ((), (), s32[]{:S(2)}) async-start(), calls=%async_computation.8 | async-start | bytes 4915200 | tf_op jit(solution)/shard_map/all_gather | solution.py:1455
  30.5 267.1 %reduce-scatter.5.cloned.1.call-start = ((), (), s32[]{:S(2)}) async-start(), calls=%async_computation.4 | async-start | bytes 3932160 | tf_op jit(solution)/shard_map/reduce_scatter | solution.py:1482
  61.5 50.9 %collective-permute-start.14 = (bf16[768,640]{1,0:T(8,128)(2,1)}, bf16[768,640]{1,0:T(8,128)(2,1)}, u32[]{:S(2)}, u32[]{:S(2)}) collective-permute-start(bf16[768,640]{1,0:T(8,128)(2,1)} %get-tuple-element.109.refs_3_.refs_9_), channel_id=1, source_target_pairs={{0,4},{4,0},{8,12},{12,8},{16,20},{20,16},{24,28},{28,24},{1,5},{5... | collective-permute-start | bytes 2949128 | tf_op jit(solution)/shard_map/ppermute | solution.py:1329
  87.8 29.8 %collective-permute-start.16 = (bf16[768,640]{1,0:T(8,128)(2,1)}, bf16[768,640]{1,0:T(8,128)(2,1)}, u32[]{:S(2)}, u32[]{:S(2)}) collective-permute-start(bf16[768,640]{1,0:T(8,128)(2,1)} %collective-permute-done.11.refs_5_.refs_11_), channel_id=1, source_target_pairs={{0,4},{4,0},{8,12},{12,8},{16,20},{20,16},{24,28},{28,24},{1,5},{5... | collective-permute-start | bytes 2949128 | tf_op jit(solution)/shard_map/ppermute | solution.py:1329
  113.0 43.3 %collective-permute-start.22 = (bf16[720,960]{1,0:T(8,128)(2,1)S(1)}, bf16[720,960]{1,0:T(8,128)(2,1)S(1)}, u32[]{:S(2)}, u32[]{:S(2)}) collective-permute-start(bf16[720,960]{1,0:T(8,128)(2,1)S(1)} %copy-done.2), channel_id=1, source_target_pairs={{0,8},{4,12},{8,0},{12,4},{16,24},{20,28},{24,16},{28,20},{1,9},{5... | collective-permute-start | bytes 4147208 | tf_op jit(solution)/shard_map/ppermute | solution.py:1329
  114.5 41.8 %collective-permute-start.23 = (bf16[720,960]{1,0:T(8,128)(2,1)}, bf16[720,960]{1,0:T(8,128)(2,1)}, u32[]{:S(2)}, u32[]{:S(2)}) collective-permute-start(bf16[720,960]{1,0:T(8,128)(2,1)} %get-tuple-element.115.refs_1_), channel_id=1, source_target_pairs={{0,16},{4,20},{8,24},{12,28},{16,0},{20,4},{24,8},{28,12},{1,17},{... | collective-permute-start | bytes 4147208 | tf_op jit(solution)/shard_map/ppermute | solution.py:1329
  116.9 41.9 %collective-permute-start.27 = (bf16[960,768]{1,0:T(8,128)(2,1)}, bf16[960,768]{1,0:T(8,128)(2,1)}, u32[]{:S(2)}, u32[]{:S(2)}) collective-permute-start(bf16[960,768]{1,0:T(8,128)(2,1)} %bitcast.53), channel_id=1, source_target_pairs={{0,4},{4,0},{8,12},{12,8},{16,20},{20,16},{24,28},{28,24},{1,5},{5... | collective-permute-start | bytes 4423688 | tf_op jit(solution)/shard_map/ppermute | solution.py:1329
  117.7 38.6 %collective-permute-start.20 = (bf16[128,960]{1,0:T(8,128)(2,1)}, bf16[128,960]{1,0:T(8,128)(2,1)S(1)}, u32[]{:S(2)}, u32[]{:S(2)}) collective-permute-start(bf16[128,960]{1,0:T(8,128)(2,1)} %meet.3), channel_id=1, source_target_pairs={{0,2},{1,3},{2,0},{3,1},{4,6},{5,7},{6,4},{7,5},{8,10},{9,11},{10,... | collective-permute-start | bytes 737288 | tf_op jit(solution)/shard_map/ppermute | solution.py:1324
  124.5 31.8 %collective-permute-start.21 = (bf16[128,960]{1,0:T(8,128)(2,1)}, bf16[128,960]{1,0:T(8,128)(2,1)S(1)}, u32[]{:S(2)}, u32[]{:S(2)}) collective-permute-start(bf16[128,960]{1,0:T(8,128)(2,1)} %meet.3), channel_id=1, source_target_pairs={{0,1},{1,2},{2,3},{3,0},{4,5},{5,6},{6,7},{7,4},{8,9},{9,10},{10,1... | collective-permute-start | bytes 737288 | tf_op jit(solution)/shard_map/ppermute | solution.py:1324
  169.4 54.7 %collective-permute-start.29 = (bf16[480,768]{1,0:T(8,128)(2,1)}, bf16[480,768]{1,0:T(8,128)(2,1)S(1)}, u32[]{:S(2)}, u32[]{:S(2)}) collective-permute-start(bf16[480,768]{1,0:T(8,128)(2,1)} %get-tuple-element.129.refs_2_), channel_id=1, source_target_pairs={{0,8},{4,12},{8,0},{12,4},{16,24},{20,28},{24,16},{28,20},{1,9},{5... | collective-permute-start | bytes 2211848 | tf_op jit(solution)/shard_map/ppermute | solution.py:1329
  170.0 54.2 %collective-permute-start.31 = (bf16[480,768]{1,0:T(8,128)(2,1)}, bf16[480,768]{1,0:T(8,128)(2,1)S(1)}, u32[]{:S(2)}, u32[]{:S(2)}) collective-permute-start(bf16[480,768]{1,0:T(8,128)(2,1)} %get-tuple-element.129.refs_2_), channel_id=1, source_target_pairs={{0,16},{4,20},{8,24},{12,28},{16,0},{20,4},{24,8},{28,12},{1,17},{... | collective-permute-start | bytes 2211848 | tf_op jit(solution)/shard_map/ppermute | solution.py:1329
  171.0 53.1 %collective-permute-start.30 = (bf16[480,768]{1,0:T(8,128)(2,1)}, bf16[480,768]{1,0:T(8,128)(2,1)S(1)}, u32[]{:S(2)}, u32[]{:S(2)}) collective-permute-start(bf16[480,768]{1,0:T(8,128)(2,1)} %get-tuple-element.130.refs_3_), channel_id=1, source_target_pairs={{0,8},{4,12},{8,0},{12,4},{16,24},{20,28},{24,16},{28,20},{1,9},{5... | collective-permute-start | bytes 2211848 | tf_op jit(solution)/shard_map/ppermute | solution.py:1329
  172.0 52.2 %collective-permute-start.32 = (bf16[480,768]{1,0:T(8,128)(2,1)}, bf16[480,768]{1,0:T(8,128)(2,1)S(1)}, u32[]{:S(2)}, u32[]{:S(2)}) collective-permute-start(bf16[480,768]{1,0:T(8,128)(2,1)} %get-tuple-element.130.refs_3_), channel_id=1, source_target_pairs={{0,16},{4,20},{8,24},{12,28},{16,0},{20,4},{24,8},{28,12},{1,17},{... | collective-permute-start | bytes 2211848 | tf_op jit(solution)/shard_map/ppermute | solution.py:1329
  227.0 56.4 %collective-permute-start.38 = (bf16[480,768]{1,0:T(8,128)(2,1)}, bf16[480,768]{1,0:T(8,128)(2,1)}, u32[]{:S(2)}, u32[]{:S(2)}) collective-permute-start(bf16[480,768]{1,0:T(8,128)(2,1)} %get-tuple-element.147.refs_4_), channel_id=1, source_target_pairs={{0,16},{4,20},{8,24},{12,28},{16,0},{20,4},{24,8},{28,12},{1,17},{... | collective-permute-start | bytes 2211848 | tf_op jit(solution)/shard_map/ppermute | solution.py:1329
  227.6 55.8 %collective-permute-start.39 = (bf16[480,768]{1,0:T(8,128)(2,1)}, bf16[480,768]{1,0:T(8,128)(2,1)}, u32[]{:S(2)}, u32[]{:S(2)}) collective-permute-start(bf16[480,768]{1,0:T(8,128)(2,1)} %get-tuple-element.148.refs_7_), channel_id=1, source_target_pairs={{0,8},{4,12},{8,0},{12,4},{16,24},{20,28},{24,16},{28,20},{1,9},{5... | collective-permute-start | bytes 2211848 | tf_op jit(solution)/shard_map/ppermute | solution.py:1329
  228.6 54.8 %collective-permute-start.35 = (bf16[4,3,48,960]{3,2,1,0:T(8,128)(2,1)}, bf16[4,3,48,960]{3,2,1,0:T(8,128)(2,1)}, u32[]{:S(2)}, u32[]{:S(2)}) collective-permute-start(bf16[4,3,48,960]{3,2,1,0:T(8,128)(2,1)} %get-tuple-element.141), channel_id=1, source_target_pairs={{0,8},{4,12},{8,0},{12,4},{16,24},{20,28},{24,16},{28,20},{1,9},{5... | collective-permute-start | bytes 3317768 | tf_op jit(solution)/shard_map/ppermute | solution.py:1329
  229.6 117.5 %reduce-scatter.7.cloned.1.call-start = ((), (), s32[]{:S(2)}) async-start(), calls=%async_computation.5 | async-start | bytes 1474560 | tf_op jit(solution)/shard_map/reduce_scatter | solution.py:1547
  229.7 53.7 %collective-permute-start.36 = (bf16[4,3,48,960]{3,2,1,0:T(8,128)(2,1)}, bf16[4,3,48,960]{3,2,1,0:T(8,128)(2,1)}, u32[]{:S(2)}, u32[]{:S(2)}) collective-permute-start(bf16[4,3,48,960]{3,2,1,0:T(8,128)(2,1)} %get-tuple-element.142), channel_id=1, source_target_pairs={{0,16},{4,20},{8,24},{12,28},{16,0},{20,4},{24,8},{28,12},{1,17},{... | collective-permute-start | bytes 3317768 | tf_op jit(solution)/shard_map/ppermute | solution.py:1329
  231.2 66.3 %collective-permute-start.37 = (bf16[4,3,48,960]{3,2,1,0:T(8,128)(2,1)}, bf16[4,3,48,960]{3,2,1,0:T(8,128)(2,1)}, u32[]{:S(2)}, u32[]{:S(2)}) collective-permute-start(bf16[4,3,48,960]{3,2,1,0:T(8,128)(2,1)} %get-tuple-element.143), channel_id=1, source_target_pairs={{0,24},{4,28},{8,16},{12,20},{16,8},{20,12},{24,0},{28,4},{1,25},{... | collective-permute-start | bytes 3317768 | tf_op jit(solution)/shard_map/ppermute | solution.py:1329
  301.9 113.9 %reduce-scatter.9.cloned.1.call-start = ((), (), s32[]{:S(2)}) async-start(), calls=%async_computation.6 | async-start | bytes 1310720 | tf_op jit(solution)/shard_map/reduce_scatter | solution.py:1551
  323.6 92.2 %reduce-scatter.11.cloned.1.call-start = ((), (), s32[]{:S(2)}) async-start(), calls=%async_computation.7 | async-start | bytes 2293760 | tf_op jit(solution)/shard_map/reduce_scatter | solution.py:1570
  323.7 29.2 %collective-permute-start.51 = (bf16[768,1024]{1,0:T(8,128)(2,1)}, bf16[768,1024]{1,0:T(8,128)(2,1)S(1)}, u32[]{:S(2)}, u32[]{:S(2)}) collective-permute-start(bf16[768,1024]{1,0:T(8,128)(2,1)} %get-tuple-element.175), channel_id=1, source_target_pairs={{0,4},{4,0},{8,12},{12,8},{16,20},{20,16},{24,28},{28,24},{1,5},{5... | collective-permute-start | bytes 4718600 | tf_op jit(solution)/shard_map/ppermute | solution.py:1329
  364.2 34.1 %collective-permute-start.52 = (bf16[768,640]{1,0:T(8,128)(2,1)}, bf16[768,640]{1,0:T(8,128)(2,1)S(1)}, u32[]{:S(2)}, u32[]{:S(2)}) collective-permute-start(bf16[768,640]{1,0:T(8,128)(2,1)} %get-tuple-element.178), channel_id=1, source_target_pairs={{0,8},{4,12},{8,0},{12,4},{16,24},{20,28},{24,16},{28,20},{1,9},{5... | collective-permute-start | bytes 2949128 | tf_op jit(solution)/shard_map/ppermute | solution.py:1329
  365.7 32.6 %collective-permute-start.53 = (bf16[768,640]{1,0:T(8,128)(2,1)S(1)}, bf16[768,640]{1,0:T(8,128)(2,1)S(1)}, u32[]{:S(2)}, u32[]{:S(2)}) collective-permute-start(bf16[768,640]{1,0:T(8,128)(2,1)S(1)} %copy-done.32), channel_id=1, source_target_pairs={{0,16},{4,20},{8,24},{12,28},{16,0},{20,4},{24,8},{28,12},{1,17},{... | collective-permute-start | bytes 2949128 | tf_op jit(solution)/shard_map/ppermute | solution.py:1329
  (95 other events, 712.4 us)
Sparse Core Ops, SparseCore 0:
  30.6 76.8 all-gather.2
  229.8 60.1 reduce-scatter.4
  302.0 28.3 reduce-scatter.6
  332.5 25.8 reduce-scatter.8
  364.3 39.0 reduce-scatter.10

commit v4 on v3

--- a/solution.py
+++ b/solution.py
@@ -173,7 +173,7 @@
     return step_call("meet", lambda *refs: None, info, (), (), behind=behind, passed=passed)
 
 
-def prep_weights(info, w_gate, w_up, w_down_turned):
+def prep_weights(info, w_gate, w_up, w_down_turned, w_out):
     def body(info, ins, outs, scratch):
         core, parity = info[1], info[4]
         turn, given, sems = scratch
@@ -181,6 +181,8 @@
         copies = [pltpu.make_async_copy(ins[n], given.at[n], sems.at[n]) for n in range(3)]
         for c in copies:
             c.start()
+        row = pl.multiple_of((ZR - OUT_ROWS) * core, 16)
+        outs[2][...] = ins[3][pl.ds(row, OUT_ROWS), :]
         for n in range(3):
             copies[n].wait()
             turn[...] = given[n].T
@@ -188,13 +190,12 @@
             quarter = pl.ds(pl.multiple_of(base + QUARTER * parity, 16), QUARTER)
             outs[1][QUARTER * n : QUARTER * n + QUARTER, :] = turn[quarter, :]
 
-    weights = (w_gate, w_up, w_down_turned)
     return step_call(
         "prep_weights",
         body,
         info,
-        weights,
-        (((3, CORE_UNITS, D), BF16), ((PACKED, D), BF16)),
+        (w_gate, w_up, w_down_turned, w_out),
+        (((3, CORE_UNITS, D), BF16), ((PACKED, D), BF16), ((OUT_ROWS, D), BF16)),
         far=range(3),
         scratch=(
             pltpu.VMEM((2 * CORE_UNITS, D), BF16),
@@ -738,10 +739,15 @@
     for h in range(2):
         ins[2 + h].wait()
         c_all[t * h : t * h + t, :] = c_turn[h].T
-    for c in ins[:2] + copies:
+    for c in ins[:2] + copies[:1]:
         c.wait()
 
     def forward(c, _):
+        @pl.when(c == 1)
+        def _():
+            for late in copies[1:]:
+                late.wait()
+
         u = pl.ds(pl.multiple_of(c * UNITS, UNITS), UNITS)
         for h in range(2 * t // ROWS):
             r = slice(ROWS * h, ROWS * h + ROWS)
@@ -1183,8 +1189,8 @@
     )
 
 
-def join_cores(info, keep_near, recv_near, keep_far, recv_far, pairs):
-    rows = keep_far.shape[0]
+def join_cores(info, keep, recv, pairs):
+    rows = keep.shape[0] // 4
     cut = rows // 2
 
     def body(info, ins, outs, scratch):
@@ -1192,22 +1198,19 @@
             r = slice(rows * n, rows * n + rows)
             outs[n][...] = ins[0][r, :] + ins[1][r, :]
         for n in range(2):
-            r = slice(cut * n, cut * n + cut)
-            outs[3 + n][...] = ins[2][r, :] + ins[3][r, :]
+            r = slice(3 * rows + cut * n, 3 * rows + cut * n + cut)
+            outs[3 + n][...] = ins[0][r, :] + ins[1][r, :]
         for n in range(len(pairs)):
-            outs[5 + n][...] = ins[4 + 2 * n][...] + ins[5 + 2 * n][...]
+            outs[5 + n][...] = ins[2 + 2 * n][...] + ins[3 + 2 * n][...]
 
     outs = (((rows, KV_LANES), BF16),) * 3 + (((cut, KV_LANES), BF16),) * 2
     outs += tuple((a.shape, BF16) for a, _ in pairs)
     flat = [a for pair in pairs for a in pair]
-    return step_call(
-        "join_cores", body, info, (keep_near, recv_near, keep_far, recv_far, *flat), outs
-    )
+    return step_call("join_cores", body, info, (keep, recv, *flat), outs)
 
 
 def join_near(info, to_x, to_y, from_x, from_y, pairs, passed):
     cut = from_x.shape[0]
-    rows = pairs[0][0].shape[1]
 
     def body(info, ins, outs, scratch):
         to_x, to_y, from_x, from_y = ins[:4]
@@ -1216,16 +1219,12 @@
         outs[1][0:cut, :] = to_y[0:cut, :] + from_x[...]
         outs[1][cut : 2 * cut, :] = to_y[cut : 2 * cut, :]
         for n in range(2):
-            outs[2][:, rows * n : rows * n + rows, :] = ins[4 + 2 * n][...] + ins[5 + 2 * n][...]
+            outs[2 + n][...] = ins[4 + 2 * n][...] + ins[5 + 2 * n][...]
 
     flat = [a for pair in pairs for a in pair]
+    outs = ((to_x.shape, BF16),) * 2 + tuple((a.shape, BF16) for a, _ in pairs)
     return step_call(
-        "join_near",
-        body,
-        info,
-        (to_x, to_y, from_x, from_y, *flat),
-        ((to_x.shape, BF16),) * 2 + (((3, P_ROWS, D), BF16),),
-        passed=passed,
+        "join_near", body, info, (to_x, to_y, from_x, from_y, *flat), outs, passed=passed
     )
 
 
@@ -1265,14 +1264,14 @@
     return step_call("halve_rows", body, info, (left, right), outs, behind=behind)
 
 
-def add_pairs(info, pairs, behind=()):
+def add_pairs(info, pairs, passed=()):
     def body(info, ins, outs, scratch):
         for n in range(len(pairs)):
             outs[n][...] = ins[2 * n][...] + ins[2 * n + 1][...]
 
     flat = [a for pair in pairs for a in pair]
     outs = tuple((a.shape, BF16) for a, _ in pairs)
-    return step_call("add_pairs", body, info, flat, outs, behind=behind)
+    return step_call("add_pairs", body, info, flat, outs, passed=passed)
 
 
 def stack_two(info, first, second, behind):
@@ -1296,20 +1295,24 @@
     return step_call("stack_pairs", body, info, flat, ((shape, BF16),), behind=(dep,))[0]
 
 
-def join_ffn(info, first, near, far, dep):
+def join_ffn(info, pairs, near, far, dep):
+    cut = P_ROWS // 2
+
     def body(info, ins, outs, scratch):
         chip = info[3]
         out = outs[0]
-        out[:, 0:P_ROWS, :] = ins[0][...]
+        for n in range(2):
+            out[:, cut * n : cut * n + cut, :] = ins[2 * n][...] + ins[2 * n + 1][...]
         for r in range(4):
             at = pl.multiple_of(P_ROWS + Q_ROWS * (chip ^ r), 16)
-            out[:, pl.ds(at, Q_ROWS), :] = ins[1 + r // 2][r % 2]
-
+            out[:, pl.ds(at, Q_ROWS), :] = ins[4 + r // 2][r % 2]
+
+    flat = [a for pair in pairs for a in pair]
     return step_call(
         "join_feed_forward",
         body,
         info,
-        (first, near, far),
+        (*flat, near, far),
         (((3, CORE_UNITS, D), BF16),),
         behind=(dep,),
     )[0]
@@ -1450,7 +1453,7 @@
         [lax.dynamic_slice_in_dim(w, start, 32, axis=0) for w in w_parts], axis=1
     )
     w_z = [z_shift(w_mine, -1), z_shift(w_mine, 2), z_shift(w_mine, 1)]
-    own_half, packed = prep_weights(info, w_gate, w_up, w_down.T)
+    own_half, packed, out_mine = prep_weights(info, w_gate, w_up, w_down.T, w_out)
     w_got, packed = stack_weights(info, w_z, (cos_turn, sin_turn), (packed,))
     over_z = lax.all_gather(packed, "fsdp", axis=0, tiled=False)
     cot_there = c_swap(cot_turned, 1)
@@ -1464,9 +1467,8 @@
     )
     kvs = chip_far(kv_low, chip_near(kv_low))
 
-    first, second = split_quarters(info, over_z, kvs[3:5] if n_ctx == 8 else kvs)
+    first, second = split_quarters(info, over_z, (*kvs, cot_there))
     first_on, second_on = c_swap(first, 2), c_swap(second, 4)
-    out_mine = lax.dynamic_slice_in_dim(w_out, (ZR - OUT_ROWS) * core, OUT_ROWS, axis=0)
     out_mine = meet(info, (out_mine,), (first,))[0]
     out_here = [z_shift(out_mine, -1), z_shift(out_mine, 2), z_shift(out_mine, 1)]
     mid_low, recips, probs = fwd_call(tab, lo, q_low, kvs)
@@ -1493,7 +1495,7 @@
     a_turned = [*attn_turned, *a_near, c_swap(a_near[0], 4), c_swap(a_near[3], 2)]
 
     if n_ctx == 8:
-        out_units = (3, 1, 3, 1)
+        out_units = (4, 4)
         slots = kv_slot(position, per_dev, me).astype(jnp.int32)
     else:
         out_units = (NWB,)
@@ -1523,36 +1525,29 @@
     q_terms = (q_both[0], *q_got)
     go_pair = (go_keep, c_swap(go_send, 1))
     if n_ctx == 8:
-        keep_near, keep_far, send_near, send_far = kv_parts
-        q_sum, p_l, p_r, send_near, send_far, a_lo, a_hi = sum_chips(
-            info, q_terms, p_sum, (send_near, send_far, *a_turned[6:]), (dq,)
+        kv_keep, kv_send = kv_parts
+        q_sum, p_l, p_r, kv_send, a_lo, a_hi = sum_chips(
+            info, q_terms, p_sum, (kv_send, *a_turned[6:]), (dq,)
         )
         a_turned[6:] = [a_lo, a_hi]
-        own, to_x, to_y, far_lo, far_hi, go_both, p_l, p_r = join_cores(
-            info,
-            keep_near,
-            c_swap(send_near, 1),
-            keep_far,
-            c_swap(send_far, 1),
-            (go_pair, (p_l, c_swap(p_l, 2)), (p_r, c_swap(p_r, 4))),
+        own, to_x, to_y, far_lo, far_hi, go_both = join_cores(
+            info, kv_keep, c_swap(kv_send, 1), (go_pair,)
         )
         totals = (own, to_x, to_y, far_lo, far_hi)
     else:
         q_sum, p_l, p_r = sum_chips(info, q_terms, p_sum, (), (dq,))
         own, sums = own_rows(kv_parts)
         a_turned, totals = a_turned[:2], (own,)
-        go_both, p_l, p_r = add_pairs(
-            info, (go_pair, (p_l, c_swap(p_l, 2)), (p_r, c_swap(p_r, 4)))
-        )
+        go_both = add_pairs(info, (go_pair,))[0]
     q_mine = lax.psum_scatter(q_sum, "fsdp", scatter_dimension=0, tiled=True)[0]
     for b in bits_from(8):
         q_mine = q_mine + c_swap(q_mine, b)
     gq_keep, gq_send, part = post_q_call(info, attn_in, dq, w_q, own)
     go_sum = lax.psum_scatter(go_both, "fsdp", scatter_dimension=0, tiled=True)
     gkv_keep, gkv_send = kv_weights_back(info, cos_turn, sin_turn, a_turned, totals, gq_keep)
-    p_pairs = ((p_l, c_swap(p_l, 4)), (p_r, c_swap(p_r, 2)))
+    p_pairs = ((p_l, c_swap(p_l, 2)), (p_r, c_swap(p_r, 4)))
     if n_ctx == 8:
-        to_x, to_y, p_sum, gq_send, gkv_send, q_mine = join_near(
+        to_x, to_y, p_l, p_r, gq_send, gkv_send, q_mine = join_near(
             info,
             to_x,
             to_y,
@@ -1563,9 +1558,10 @@
         )
         sums = (own, c_swap(to_x, 2), c_swap(to_y, 4))
     else:
-        p_sum = jnp.concatenate([a + b for a, b in p_pairs], axis=1)
+        p_l, p_r = (a + b for a, b in p_pairs)
+    p_pairs = ((p_l, c_swap(p_l, 4)), (p_r, c_swap(p_r, 2)))
     g_both, output = join_projections(
-        info, (gq_keep, c_swap(gq_send, 1)), (gkv_keep, c_swap(gkv_send, 1)), h1, acc_o, got_o, p_sum
+        info, (gq_keep, c_swap(gq_send, 1)), (gkv_keep, c_swap(gkv_send, 1)), h1, acc_o, got_o, p_l
     )
     g_sum = lax.psum_scatter(g_both, "fsdp", scatter_dimension=0, tiled=True)
     q_near = stack_two(info, q_mine, c_swap(q_mine, 2), (output,))
@@ -1574,10 +1570,12 @@
         info, sums, cos_turn, sin_turn, part, w_kv, x, grad_hidden, gains, q_near
     )
     for b in bits_from(8):
-        p_sum = p_sum + c_swap(p_sum, b)
-    ffn_sum = join_ffn(info, p_sum, q_near, q_far, input_grad)
-    g_l, g_r = halve_rows(info, go_sum, g_sum, (ffn_sum,))
-    g_l, g_r = add_pairs(info, ((g_l, c_swap(g_l, 2)), (g_r, c_swap(g_r, 4))))
+        p_pairs = tuple((a + c_swap(a, b), g + c_swap(g, b)) for a, g in p_pairs)
+    g_l, g_r = halve_rows(info, go_sum, g_sum, (input_grad,))
+    ffn_sum = join_ffn(info, p_pairs, q_near, q_far, g_l)
+    g_l, g_r, ffn_sum = add_pairs(
+        info, ((g_l, c_swap(g_l, 2)), (g_r, c_swap(g_r, 4))), (ffn_sum,)
+    )
     gate_grad, up_grad, down_grad = finish_ffn(info, ffn_sum, c_swap(ffn_sum, 1), g_l)
     g_sum = stack_pairs(info, ((g_l, c_swap(g_l, 4)), (g_r, c_swap(g_r, 2))), gate_grad)
     for b in bits_from(8):

time: 467 us -> 448 us (0.959)
  waiting for transfers between devices: 135 us -> 116 us
    ppermute x56 -> x55, waiting for transfers between devices: 121 us -> 110 us  [c_swap(): return lax.ppermute(x, 'ctx', [(i, i ^ bit) for i in range(n)])]
    ppermute x6, waiting for transfers between devices: 6.67 us -> 0.02 us  [z_shift(): return lax.ppermute(x, 'fsdp', [(i, (i + step) % n) for i in range(n)])]
    unnamed x107 -> x101, local copies, waits for them, and re-layouts: 17.3 us -> 16.6 us
    ppermute x56 -> x55, starting transfers between devices: 37.6 us -> 37.2 us  [c_swap(): return lax.ppermute(x, 'ctx', [(i, i ^ bit) for i in range(n)])]
  transfers between devices with their start and end apart: 67 -> 66, of which waited for: 24 -> 21; matrix products, arithmetic and copies ran while one was open for 2% -> 2% of each run, Pallas kernels for 46% -> 47%
where the time goes in v4:
time: 448 us; the launch traced here: 442 us
  Pallas kernels  234 us (52%)
  waiting for transfers between devices  116 us (26%)
  starting transfers between devices  46.7 us (10%)
  local copies, waits for them, and re-layouts  24.8 us (6%)
  between operations  14.7 us (3%)
  other arithmetic  5.17 us (1%)
    ppermute x55, waiting for transfers between devices, c_swap(): return lax.ppermute(x, 'ctx', [(i, i ^ bit) for i in range(n)])  110 us
    pallas_call x18, Pallas kernels, step_call(): pl.pallas_call(kernel, grid=(1,), out_shape=tuple((jax.ShapeDtypeStruct(s...  66.6 us
    pallas_call x1, Pallas kernels, ffn_call(): pl.pallas_call(ffn_kernel, out_shape=(jax.ShapeDtypeStruct((t, D), F32),...  50.6 us
    pallas_call x1, Pallas kernels, bwd_call(): pl.pallas_call(lambda *refs: bwd_kernel(n_kv, len(deps), first, prev, out...  39.7 us
    ppermute x55, starting transfers between devices, c_swap(): return lax.ppermute(x, 'ctx', [(i, i ^ bit) for i in range(n)])  37.2 us
    pallas_call x1, Pallas kernels, fwd_call(): pl.pallas_call(lambda *refs: fwd_kernel(n_kv, *refs), grid=(blocks,), out...  31 us
    unnamed x101, local copies, waits for them, and re-layouts  16.6 us
    pallas_call x1, Pallas kernels, epi_call(): pl.pallas_call(epi_kernel, grid=(t // ROWS,), out_shape=(jax.ShapeDtypeSt...  12.2 us
  transfers between devices with their start and end apart: 66, of which 21 were waited for; matrix products, arithmetic and copies ran while one was open for 2% of the time, Pallas kernels for 47%

profile of v4, /device:TPU:0, one launch (start us, length us, event | category | flops | bytes accessed | tf_op | source)
XLA Modules:
  0.0 441.8 jit_solution(2438221530545198457)
XLA Ops:
  13.0 5.1 %collective-permute-start = (bf16[32,1664]{1,0:T(8,128)(2,1)S(1)}, bf16[32,1664]{1,0:T(8,128)(2,1)S(1)}, u32[]{:S(2)}, u32[]{:S(2)}) collective-permute-start(bf16[32,1664]{1,0:T(8,128)(2,1)S(1)} %concatenate.16), channel_id=1, source_target_pairs={{0,3},{1,0},{2,1},{3,2},{4,7},{5,4},{6,5},{7,6},{8,11},{9,8},{10,9... | collective-permute-start | bytes 319496 | tf_op jit(solution)/shard_map/ppermute | solution.py:1327
  23.0 5.4 %prep_weights.1 = (bf16[3,320,960]{2,1,0:T(8,128)(2,1)}, bf16[480,960]{1,0:T(8,128)(2,1)}, bf16[128,960]{1,0:T(8,128)(2,1)}) custom-call(s32[5]{0:T(128)} %stack.38.info_ref.info.refs_0_, bf16[960,640]{1,0:T(8,128)(2,1)} %refs_0_.1, bf16[960,640]{1,0:T(8,128)(2,1)} %refs_1_.1, bf16[960,640]{1,0:T(8,128)(2,1)} %bitcast.56, bf16[240,960]{1,0:T(8,128)(2,1)} %own.1), custom_call_target="tpu_custom_call" | custom-call | flops 1750000000 | bytes 1 | tf_op jit(solution)/shard_map/prep_weights/pallas_call | solution.py:155
  34.6 7.2 %collective-permute-done.4.refs_3_ = bf16[3,32,1664]{2,1,0:T(8,128)(2,1)S(1)} collective-permute-done((bf16[3,32,1664]{2,1,0:T(8,128)(2,1)}, bf16[3,32,1664]{2,1,0:T(8,128)(2,1)S(1)}, u32[]{:S(2)}, u32[]{:S(2)}) %collective-permute-start.4) | collective-permute-done | bytes 319520 | tf_op jit(solution)/shard_map/ppermute | solution.py:1332
  41.8 6.0 %collective-permute-done.6.refs_5_ = bf16[3,32,1664]{2,1,0:T(8,128)(2,1)S(1)} collective-permute-done((bf16[3,32,1664]{2,1,0:T(8,128)(2,1)}, bf16[3,32,1664]{2,1,0:T(8,128)(2,1)S(1)}, u32[]{:S(2)}, u32[]{:S(2)}) %collective-permute-start.6) | collective-permute-done | bytes 319520 | tf_op jit(solution)/shard_map/ppermute | solution.py:1332
  50.2 9.3 %pre.1 = (bf16[768,960]{1,0:T(8,128)(2,1)}, bf16[480,768]{1,0:T(8,128)(2,1)}, bf16[480,768]{1,0:T(8,128)(2,1)}, bf16[768,960]{1,0:T(8,128)(2,1)}, bf16[768,640]{...) custom-call(s32[5]{0:T(128)} %stack.38.info_ref.info.refs_0_, ...), custom_call_target="tpu_custom_call" | custom-call | flops 4200000000 | bytes 1 | tf_op jit(solution)/shard_map/pre/pallas_call | solution.py:320
  61.7 21.9 %collective-permute-done.10.refs_4_.refs_2_.refs_10_ = bf16[768,640]{1,0:T(8,128)(2,1)S(1)} collective-permute-done((bf16[768,640]{1,0:T(8,128)(2,1)}, bf16[768,640]{1,0:T(8,128)(2,1)S(1)}, u32[]{:S(2)}, u32[]{:S(2)}) %collective-permute-start.10) | collective-permute-done | bytes 983072 | tf_op jit(solution)/shard_map/ppermute | solution.py:1332
  88.2 9.1 %collective-permute-done.12.refs_6_.refs_4_.refs_12_ = bf16[384,640]{1,0:T(8,128)(2,1)} collective-permute-done((bf16[384,640]{1,0:T(8,128)(2,1)}, bf16[384,640]{1,0:T(8,128)(2,1)}, u32[]{:S(2)}, u32[]{:S(2)}) %collective-permute-start.12) | collective-permute-done | bytes 491552 | tf_op jit(solution)/shard_map/ppermute | solution.py:1332
  102.3 5.8 %all-gather.3.cloned.1.call-done = bf16[1920,960]{1,0:T(8,128)(2,1)} async-done(((bf16[480,960]{1,0:T(8,128)(2,1)}), bf16[1920,960]{1,0:T(8,128)(2,1)}) %all-gather.3.cloned.1.call-update) | async-done | bytes 3686416 | tf_op jit(solution)/shard_map/all_gather | solution.py:1458
  108.0 4.1 split_quarters.1
  120.1 31.0 %attend.1 = (bf16[768,960]{1,0:T(8,128)(2,1)}, f32[6,16,128]{2,1,0:T(8,128)}, bf16[6,1152,1920]{2,1,0:T(8,128)(2,1)}) custom-call(s32[6,9]{1,0:T(8,128)} %get-tuple-element.200.refs_0_, s32[6,1,128]{2,1,0:T(1,128)} %maximum_subtract_fusion.refs_1_, bf16[768,960]{1,0:T(8,128)(2,1)} %get-tuple-element.106.refs_2_, ...), custom_call_target="tpu_custom_call" | custom-call | flops 11200000000 | bytes 1 | tf_op jit(solution)/shard_map/attend/pallas_call | solution.py:456
  156.9 7.8 %out_projection.1 = (f32[768,960]{1,0:T(8,128)}, bf16[768,1024]{1,0:T(8,128)(2,1)}, bf16[960,960]{1,0:T(8,128)(2,1)}, bf16[480,768]{1,0:T(8,128)(2,1)}, bf16[480,768]{1,0:T(8,128)(2,1)}) custom-call(s32[5]{0:T(128)} %stack.38.info_ref.info.refs_0_, ...), custom_call_target="tpu_custom_call", output_to_operand_aliasing={{3}: (12, {}), {4}: (13, {})} | custom-call | flops 2449999872 | bytes 1 | tf_op jit(solution)/shard_map/out_projection/pallas_call | solution.py:683
  169.0 50.6 %feed_forward.1 = (f32[768,960]{1,0:T(8,128)}, f32[768,960]{1,0:T(8,128)}, bf16[768,1024]{1,0:T(8,128)(2,1)}, bf16[768,512]{1,0:T(8,128)(2,1)}, bf16[768,512]{1,...) custom-call(s32[5]{0:T(128)} %stack.38.info_ref.info.refs_0_, ...), custom_call_target="tpu_custom_call" | custom-call | flops 17500000256 | bytes 1 | tf_op jit(solution)/shard_map/feed_forward/pallas_call | solution.py:850
  227.6 12.2 %feed_forward_norm_back.1 = (f32[768,960]{1,0:T(8,128)}, bf16[768,960]{1,0:T(8,128)(2,1)}, bf16[4,256,512]{2,1,0:T(8,128)(2,1)}, bf16[4,256,512]{2,1,0:T(8,128)(2,1)}) custom-call(s32[5]{0:T(128)} %stack.38.info_ref.info.refs_0_, f32[768,960]{1,0:T(8,128)} %get-tuple-element.120.h1_ref.refs_4_, f32[768,960]{1,0:T(8,128)} %get-tuple-element.125.acc_g, ...), custom_call_target="tpu_custom_call" | custom-call | flops 4200000000 | bytes 1 | tf_op jit(solution)/shard_map/feed_forward_norm_back/pallas_call | solution.py:949
  239.8 39.7 %attend_back_0.1 = (bf16[768,960]{1,0:T(8,128)(2,1)}, bf16[3072,640]{1,0:T(8,128)(2,1)}, bf16[3072,640]{1,0:T(8,128)(2,1)}) custom-call(s32[6,9]{1,0:T(8,128)} %get-tuple-element.200.refs_0_, s32[6,9]{1,0:T(8,128)} %get-tuple-element.199.refs_1_, bf16[768,960]{1,0:T(8,128)(2,1)} %get-tuple-element.106.refs_2_, bf16[768,960]{1,0:T(8,128)(2,1)} %get-tuple-element.133.refs_3_, ...), custom_call_target="tpu_custom_call" | custom-call | flops 3499999887360 | bytes 1 | tf_op jit(solution)/shard_map/attend_back_0/pallas_call | solution.py:607
  279.6 13.4 %collective-permute-done.37.refs_3_ = bf16[4,3,48,960]{3,2,1,0:T(8,128)(2,1)} collective-permute-done((bf16[4,3,48,960]{3,2,1,0:T(8,128)(2,1)}, bf16[4,3,48,960]{3,2,1,0:T(8,128)(2,1)}, u32[]{:S(2)}, u32[]{:S(2)}) %collective-permute-start.37) | collective-permute-done | bytes 1105952 | tf_op jit(solution)/shard_map/ppermute | solution.py:1332
  293.0 4.4 sum_chips.1
  298.0 7.3 %collective-permute-done.41.refs_3_ = bf16[4,256,512]{2,1,0:T(8,128)(2,1)S(1)} collective-permute-done((bf16[4,256,512]{2,1,0:T(8,128)(2,1)S(1)}, bf16[4,256,512]{2,1,0:T(8,128)(2,1)S(1)}, u32[]{:S(2)}, u32[]{:S(2)}) %collective-permute-start.41) | collective-permute-done | bytes 1048608 | tf_op jit(solution)/shard_map/ppermute | solution.py:1332
  306.3 6.4 %join_cores.1 = (bf16[768,640]{1,0:T(8,128)(2,1)}, bf16[768,640]{1,0:T(8,128)(2,1)}, bf16[768,640]{1,0:T(8,128)(2,1)}, bf16[384,640]{1,0:T(8,128)(2,1)}, bf16[38...) custom-call(s32[5]{0:T(128)} %stack.38.info_ref.info.refs_0_, bf16[3072,640]{1,0:T(8,128)(2,1)} %get-tuple-element.138.refs_0_, ...), custom_call_target="tpu_custom_call" | custom-call | flops 1750000000 | bytes 1 | tf_op jit(solution)/shard_map/join_cores/pallas_call | solution.py:155
  317.2 8.6 %query_back.1 = (bf16[4,256,512]{2,1,0:T(8,128)(2,1)}, bf16[4,256,512]{2,1,0:T(8,128)(2,1)}, f32[768,960]{1,0:T(8,128)}) custom-call(s32[5]{0:T(128)} %stack.38.info_ref.info.refs_0_, bf16[768,960]{1,0:T(8,128)(2,1)} %get-tuple-element.105.a_ref, bf16[768,960]{1,0:T(8,128)(2,1)} %get-tuple-element.136.refs_5_.g_ref, ...), custom_call_target="tpu_custom_call" | custom-call | flops 2800000000 | bytes 1 | tf_op jit(solution)/shard_map/query_back/pallas_call | solution.py:996
  325.8 10.5 %key_value_weights_back.1 = (bf16[4,256,384]{2,1,0:T(8,128)(2,1)}, bf16[4,256,384]{2,1,0:T(8,128)(2,1)}) custom-call(s32[5]{0:T(128)} %stack.38.info_ref.info.refs_0_, f32[32,3072]{1,0:T(8,128)} %get-tuple-element.198.refs_3_.cos_ref.refs_7_.refs_0_.refs_4_, f32[32,3072]{1,0:T(8,128)} %get-tuple-element.197.refs_4_.sin_ref.refs_8_.refs_1_.refs_5_, ...), custom_call_target="tpu_custom_call" | custom-call | flops 3849999872 | bytes 1 | tf_op jit(solution)/shard_map/key_value_weights_back/pallas_call | solution.py:155
  347.1 6.7 %join_projections.1 = (bf16[4,256,896]{2,1,0:T(8,128)(2,1)}, bf16[960,768]{1,0:T(8,128)(2,1)}) custom-call(s32[5]{0:T(128)} %stack.38.info_ref.info.refs_0_, bf16[4,256,512]{2,1,0:T(8,128)(2,1)} %get-tuple-element.151.refs_15_.refs_0_, bf16[4,256,512]{2,1,0:T(8,128)(2,1)} %copy-done.8, bf16[4,256,384]{2,1,0:T(8,128)(2,1)} %get-tuple-element.166.refs_2_, ...), custom_call_target="tpu_custom_call" | custom-call | flops 2449999872 | bytes 1 | tf_op jit(solution)/shard_map/join_projections/pallas_call | solution.py:155
  358.2 26.8 %collective-permute-done.51.refs_1_ = bf16[3,48,960]{2,1,0:T(8,128)(2,1)S(1)} collective-permute-done((bf16[3,48,960]{2,1,0:T(8,128)(2,1)S(1)}, bf16[3,48,960]{2,1,0:T(8,128)(2,1)S(1)}, u32[]{:S(2)}, u32[]{:S(2)}) %collective-permute-start.51) | collective-permute-done | bytes 276512 | tf_op jit(solution)/shard_map/ppermute | solution.py:1332
  389.2 8.7 %key_value_back.1.refs_2_ = bf16[960,768]{1,0:T(8,128)(2,1)} custom-call(s32[5]{0:T(128)} %stack.38.info_ref.info.refs_0_, bf16[768,640]{1,0:T(8,128)(2,1)} %get-tuple-element.150._.refs_10_.refs_1_, bf16[768,640]{1,0:T(8,128)(2,1)} %copy-done.10, bf16[768,640]{1,0:T(8,128)(2,1)} %copy-done.11, ...), custom_call_target="tpu_custom_call" | custom-call | flops 2800000000 | bytes 1 | tf_op jit(solution)/shard_map/key_value_back/pallas_call | solution.py:1100
  418.1 6.2 %finish_feed_forward.1 = (f32[960,640]{1,0:T(8,128)}, f32[960,640]{1,0:T(8,128)}, f32[960,640]{1,0:T(8,128)}) custom-call(s32[5]{0:T(128)} %stack.38.info_ref.info.refs_0_, bf16[3,320,960]{2,1,0:T(8,128)(2,1)} %get-tuple-element.185.refs_0_, bf16[3,320,960]{2,1,0:T(8,128)(2,1)} %copy-done.33, bf16[128,1408]{1,0:T(8,128)(2,1)} %get-tuple-element.183.refs_2_.refs_0_), custom_call_target="tpu_custom_call" | custom-call | flops 2100000000 | bytes 1 | tf_op jit(solution)/shard_map/finish_feed_forward/pallas_call | solution.py:155
  (278 shorter events, 113.1 us)
Async XLA Ops:
  7.2 100.8 %all-gather.3.cloned.1.call-start = ((), (), s32[]{:S(2)}) async-start(), calls=%async_computation.8 | async-start | bytes 4915200 | tf_op jit(solution)/shard_map/all_gather | solution.py:1458
  31.0 262.0 %reduce-scatter.5.cloned.1.call-start = ((), (), s32[]{:S(2)}) async-start(), calls=%async_computation.4 | async-start | bytes 3932160 | tf_op jit(solution)/shard_map/reduce_scatter | solution.py:1484
  48.3 39.1 %collective-permute-start.19 = (bf16[960,768]{1,0:T(8,128)(2,1)}, bf16[960,768]{1,0:T(8,128)(2,1)S(1)}, u32[]{:S(2)}, u32[]{:S(2)}) collective-permute-start(bf16[960,768]{1,0:T(8,128)(2,1)} %bitcast.53), channel_id=1, source_target_pairs={{0,4},{4,0},{8,12},{12,8},{16,20},{20,16},{24,28},{28,24},{1,5},{5... | collective-permute-start | bytes 4423688 | tf_op jit(solution)/shard_map/ppermute | solution.py:1332
  61.7 38.5 %collective-permute-start.14 = (bf16[768,640]{1,0:T(8,128)(2,1)}, bf16[768,640]{1,0:T(8,128)(2,1)}, u32[]{:S(2)}, u32[]{:S(2)}) collective-permute-start(bf16[768,640]{1,0:T(8,128)(2,1)} %get-tuple-element.107.refs_3_.refs_1_.refs_9_), channel_id=1, source_target_pairs={{0,4},{4,0},{8,12},{12,8},{16,20},{20,16},{24,28},{28,24},{1,5},{5... | collective-permute-start | bytes 2949128 | tf_op jit(solution)/shard_map/ppermute | solution.py:1332
  112.2 39.0 %collective-permute-start.23 = (bf16[720,960]{1,0:T(8,128)(2,1)}, bf16[720,960]{1,0:T(8,128)(2,1)S(1)}, u32[]{:S(2)}, u32[]{:S(2)}) collective-permute-start(bf16[720,960]{1,0:T(8,128)(2,1)} %get-tuple-element.112.refs_0_), channel_id=1, source_target_pairs={{0,8},{4,12},{8,0},{12,4},{16,24},{20,28},{24,16},{28,20},{1,9},{5... | collective-permute-start | bytes 4147208 | tf_op jit(solution)/shard_map/ppermute | solution.py:1332
  113.7 37.5 %collective-permute-start.24 = (bf16[720,960]{1,0:T(8,128)(2,1)}, bf16[720,960]{1,0:T(8,128)(2,1)S(1)}, u32[]{:S(2)}, u32[]{:S(2)}) collective-permute-start(bf16[720,960]{1,0:T(8,128)(2,1)} %get-tuple-element.114.refs_1_), channel_id=1, source_target_pairs={{0,16},{4,20},{8,24},{12,28},{16,0},{20,4},{24,8},{28,12},{1,17},{... | collective-permute-start | bytes 4147208 | tf_op jit(solution)/shard_map/ppermute | solution.py:1332
  116.9 34.2 %collective-permute-start.20 = (bf16[128,960]{1,0:T(8,128)(2,1)}, bf16[128,960]{1,0:T(8,128)(2,1)S(1)}, u32[]{:S(2)}, u32[]{:S(2)}) collective-permute-start(bf16[128,960]{1,0:T(8,128)(2,1)} %meet.3), channel_id=1, source_target_pairs={{0,3},{1,0},{2,1},{3,2},{4,7},{5,4},{6,5},{7,6},{8,11},{9,8},{10,9... | collective-permute-start | bytes 737288 | tf_op jit(solution)/shard_map/ppermute | solution.py:1327
  117.8 33.3 %collective-permute-start.21 = (bf16[128,960]{1,0:T(8,128)(2,1)}, bf16[128,960]{1,0:T(8,128)(2,1)S(1)}, u32[]{:S(2)}, u32[]{:S(2)}) collective-permute-start(bf16[128,960]{1,0:T(8,128)(2,1)} %meet.3), channel_id=1, source_target_pairs={{0,2},{1,3},{2,0},{3,1},{4,6},{5,7},{6,4},{7,5},{8,10},{9,11},{10,... | collective-permute-start | bytes 737288 | tf_op jit(solution)/shard_map/ppermute | solution.py:1327
  164.9 54.7 %collective-permute-start.29 = (bf16[480,768]{1,0:T(8,128)(2,1)}, bf16[480,768]{1,0:T(8,128)(2,1)S(1)}, u32[]{:S(2)}, u32[]{:S(2)}) collective-permute-start(bf16[480,768]{1,0:T(8,128)(2,1)} %get-tuple-element.128.refs_2_), channel_id=1, source_target_pairs={{0,8},{4,12},{8,0},{12,4},{16,24},{20,28},{24,16},{28,20},{1,9},{5... | collective-permute-start | bytes 2211848 | tf_op jit(solution)/shard_map/ppermute | solution.py:1332
  164.9 54.7 %collective-permute-start.31 = (bf16[480,768]{1,0:T(8,128)(2,1)}, bf16[480,768]{1,0:T(8,128)(2,1)S(1)}, u32[]{:S(2)}, u32[]{:S(2)}) collective-permute-start(bf16[480,768]{1,0:T(8,128)(2,1)} %get-tuple-element.128.refs_2_), channel_id=1, source_target_pairs={{0,16},{4,20},{8,24},{12,28},{16,0},{20,4},{24,8},{28,12},{1,17},{... | collective-permute-start | bytes 2211848 | tf_op jit(solution)/shard_map/ppermute | solution.py:1332
  166.2 53.4 %collective-permute-start.30 = (bf16[480,768]{1,0:T(8,128)(2,1)}, bf16[480,768]{1,0:T(8,128)(2,1)S(1)}, u32[]{:S(2)}, u32[]{:S(2)}) collective-permute-start(bf16[480,768]{1,0:T(8,128)(2,1)} %get-tuple-element.129.refs_3_), channel_id=1, source_target_pairs={{0,8},{4,12},{8,0},{12,4},{16,24},{20,28},{24,16},{28,20},{1,9},{5... | collective-permute-start | bytes 2211848 | tf_op jit(solution)/shard_map/ppermute | solution.py:1332
  166.9 52.7 %collective-permute-start.32 = (bf16[480,768]{1,0:T(8,128)(2,1)}, bf16[480,768]{1,0:T(8,128)(2,1)S(1)}, u32[]{:S(2)}, u32[]{:S(2)}) collective-permute-start(bf16[480,768]{1,0:T(8,128)(2,1)} %get-tuple-element.129.refs_3_), channel_id=1, source_target_pairs={{0,16},{4,20},{8,24},{12,28},{16,0},{20,4},{24,8},{28,12},{1,17},{... | collective-permute-start | bytes 2211848 | tf_op jit(solution)/shard_map/ppermute | solution.py:1332
  222.5 57.1 %collective-permute-start.38 = (bf16[480,768]{1,0:T(8,128)(2,1)}, bf16[480,768]{1,0:T(8,128)(2,1)}, u32[]{:S(2)}, u32[]{:S(2)}) collective-permute-start(bf16[480,768]{1,0:T(8,128)(2,1)} %get-tuple-element.145.refs_4_), channel_id=1, source_target_pairs={{0,16},{4,20},{8,24},{12,28},{16,0},{20,4},{24,8},{28,12},{1,17},{... | collective-permute-start | bytes 2211848 | tf_op jit(solution)/shard_map/ppermute | solution.py:1332
  222.5 57.1 %collective-permute-start.39 = (bf16[480,768]{1,0:T(8,128)(2,1)}, bf16[480,768]{1,0:T(8,128)(2,1)}, u32[]{:S(2)}, u32[]{:S(2)}) collective-permute-start(bf16[480,768]{1,0:T(8,128)(2,1)} %get-tuple-element.146.refs_7_), channel_id=1, source_target_pairs={{0,8},{4,12},{8,0},{12,4},{16,24},{20,28},{24,16},{28,20},{1,9},{5... | collective-permute-start | bytes 2211848 | tf_op jit(solution)/shard_map/ppermute | solution.py:1332
  223.8 55.8 %collective-permute-start.35 = (bf16[4,3,48,960]{3,2,1,0:T(8,128)(2,1)}, bf16[4,3,48,960]{3,2,1,0:T(8,128)(2,1)}, u32[]{:S(2)}, u32[]{:S(2)}) collective-permute-start(bf16[4,3,48,960]{3,2,1,0:T(8,128)(2,1)} %get-tuple-element.140), channel_id=1, source_target_pairs={{0,8},{4,12},{8,0},{12,4},{16,24},{20,28},{24,16},{28,20},{1,9},{5... | collective-permute-start | bytes 3317768 | tf_op jit(solution)/shard_map/ppermute | solution.py:1332
  224.5 112.5 %reduce-scatter.7.cloned.1.call-start = ((), (), s32[]{:S(2)}) async-start(), calls=%async_computation.5 | async-start | bytes 1474560 | tf_op jit(solution)/shard_map/reduce_scatter | solution.py:1542
  224.6 55.0 %collective-permute-start.36 = (bf16[4,3,48,960]{3,2,1,0:T(8,128)(2,1)}, bf16[4,3,48,960]{3,2,1,0:T(8,128)(2,1)}, u32[]{:S(2)}, u32[]{:S(2)}) collective-permute-start(bf16[4,3,48,960]{3,2,1,0:T(8,128)(2,1)} %get-tuple-element.141), channel_id=1, source_target_pairs={{0,16},{4,20},{8,24},{12,28},{16,0},{20,4},{24,8},{28,12},{1,17},{... | collective-permute-start | bytes 3317768 | tf_op jit(solution)/shard_map/ppermute | solution.py:1332
  226.7 66.3 %collective-permute-start.37 = (bf16[4,3,48,960]{3,2,1,0:T(8,128)(2,1)}, bf16[4,3,48,960]{3,2,1,0:T(8,128)(2,1)}, u32[]{:S(2)}, u32[]{:S(2)}) collective-permute-start(bf16[4,3,48,960]{3,2,1,0:T(8,128)(2,1)} %get-tuple-element.142), channel_id=1, source_target_pairs={{0,24},{4,28},{8,16},{12,20},{16,8},{20,12},{24,0},{28,4},{1,25},{... | collective-permute-start | bytes 3317768 | tf_op jit(solution)/shard_map/ppermute | solution.py:1332
  297.4 100.5 %reduce-scatter.9.cloned.1.call-start = ((), (), s32[]{:S(2)}) async-start(), calls=%async_computation.6 | async-start | bytes 1310720 | tf_op jit(solution)/shard_map/reduce_scatter | solution.py:1546
  312.6 85.2 %reduce-scatter.11.cloned.1.call-start = ((), (), s32[]{:S(2)}) async-start(), calls=%async_computation.7 | async-start | bytes 2293760 | tf_op jit(solution)/shard_map/reduce_scatter | solution.py:1566
  353.8 34.1 %collective-permute-start.49 = (bf16[768,640]{1,0:T(8,128)(2,1)}, bf16[768,640]{1,0:T(8,128)(2,1)S(1)}, u32[]{:S(2)}, u32[]{:S(2)}) collective-permute-start(bf16[768,640]{1,0:T(8,128)(2,1)} %get-tuple-element.172), channel_id=1, source_target_pairs={{0,8},{4,12},{8,0},{12,4},{16,24},{20,28},{24,16},{28,20},{1,9},{5... | collective-permute-start | bytes 2949128 | tf_op jit(solution)/shard_map/ppermute | solution.py:1332
  354.2 33.8 %collective-permute-start.50 = (bf16[768,640]{1,0:T(8,128)(2,1)}, bf16[768,640]{1,0:T(8,128)(2,1)S(1)}, u32[]{:S(2)}, u32[]{:S(2)}) collective-permute-start(bf16[768,640]{1,0:T(8,128)(2,1)} %get-tuple-element.173), channel_id=1, source_target_pairs={{0,16},{4,20},{8,24},{12,28},{16,0},{20,4},{24,8},{28,12},{1,17},{... | collective-permute-start | bytes 2949128 | tf_op jit(solution)/shard_map/ppermute | solution.py:1332
  356.2 45.8 %collective-permute-start.54 = (bf16[3,64,960]{2,1,0:T(8,128)(2,1)S(1)}, bf16[3,64,960]{2,1,0:T(8,128)(2,1)}, u32[]{:S(2)}, u32[]{:S(2)}) collective-permute-start(bf16[3,64,960]{2,1,0:T(8,128)(2,1)S(1)} %copy-done.3), channel_id=1, source_target_pairs={{0,16},{4,20},{8,24},{12,28},{16,0},{20,4},{24,8},{28,12},{1,17},{... | collective-permute-start | bytes 1105928 | tf_op jit(solution)/shard_map/ppermute | solution.py:1332
  357.9 44.1 %collective-permute-start.55 = (bf16[3,64,960]{2,1,0:T(8,128)(2,1)}, bf16[3,64,960]{2,1,0:T(8,128)(2,1)}, u32[]{:S(2)}, u32[]{:S(2)}) collective-permute-start(bf16[3,64,960]{2,1,0:T(8,128)(2,1)} %get-tuple-element.182.refs_2_), channel_id=1, source_target_pairs={{0,8},{4,12},{8,0},{12,4},{16,24},{20,28},{24,16},{28,20},{1,9},{5... | collective-permute-start | bytes 1105928 | tf_op jit(solution)/shard_map/ppermute | solution.py:1332
  (91 other events, 680.0 us)
Sparse Core Ops, SparseCore 0:
  31.1 76.8 all-gather.2
  224.7 58.8 reduce-scatter.4
  297.5 27.3 reduce-scatter.6
  327.0 25.8 reduce-scatter.8
  355.7 38.0 reduce-scatter.10

commit v5 on v4

--- a/solution.py
+++ b/solution.py
@@ -129,7 +129,8 @@
     "join_cores": 5,
     "key_value_weights_back": 11,
     "join_near": 4,
-    "join_projections": 7,
+    "join_projections": 3,
+    "join_output": 5,
     "add_pairs": 3,
     "stack_pairs": 2,
     "halve_rows": 2,
@@ -1021,35 +1022,36 @@
 
 def kv_weights_back(info, cos, sin, turned, totals, dep):
     t = turned[0].shape[1]
-    half = t // 2
     piece = ((4, ZP, 384), BF16)
-    n_all = len(totals)
+    n_chips = len(totals)
 
     def body(info, ins, outs, scratch):
         cos_ref, sin_ref = ins[0], ins[1]
-        a_refs, g_refs = ins[2 : 2 + len(turned)], ins[2 + len(turned) :]
+        low, acc, a_buf, g_buf, sems = scratch
         first_half, low_head = lane_masks(ROWS)
-        low, acc = scratch
-        for c in range(n_all if n_all < 4 else 4):
+        copies = []
+        for c in range(n_chips):
+            pairs = [(ins[2 + 2 * c + n], a_buf.at[2 * c + n]) for n in range(2)]
+            pairs.append((ins[2 + len(turned) + c], g_buf.at[pl.ds(t * c, t)]))
+            copies.append(
+                [pltpu.make_async_copy(a, b, sems.at[c, n]) for n, (a, b) in enumerate(pairs)]
+            )
+            for copy in copies[-1]:
+                copy.start()
+        for c in range(n_chips):
+            for copy in copies[c]:
+                copy.wait()
             for i in range(t // ROWS):
                 at = ROWS * i
 
                 def slab(j):
-                    lanes = slice(128 * j, 128 * j + 128)
-                    if c < 3:
-                        return g_refs[c][at : at + ROWS, lanes].astype(F32)
-                    if at + ROWS <= half:
-                        return g_refs[3][at : at + ROWS, lanes].astype(F32)
-                    if at >= half:
-                        return g_refs[4][at - half : at - half + ROWS, lanes].astype(F32)
-                    parts = [g_refs[3][at:half, lanes], g_refs[4][0 : at + ROWS - half, lanes]]
-                    return jnp.concatenate([p.astype(F32) for p in parts], axis=0)
+                    return g_buf[t * c + at : t * c + at + ROWS, 128 * j : 128 * j + 128].astype(F32)
 
                 r = slice(t * c + at, t * c + at + ROWS)
                 cos, sin = wide_tables(cos_ref[:, r], -sin_ref[:, r])
                 low[at : at + ROWS, :] = turn_back(slab, cos, sin, first_half, low_head)
             for n, rows in enumerate((slice(0, D // 2), slice(D // 2, D))):
-                value = dot(a_refs[2 * c + n][...], low[...])
+                value = dot(a_buf[2 * c + n], low[...])
                 if c == 0:
                     acc[rows, :] = value
                 else:
@@ -1066,7 +1068,14 @@
         info,
         (cos, sin, *turned, *totals),
         (piece, piece),
-        scratch=(pltpu.VMEM((t, 768), BF16), pltpu.VMEM((D, 768), F32)),
+        far=range(2, 2 + len(turned) + len(totals)),
+        scratch=(
+            pltpu.VMEM((t, 768), BF16),
+            pltpu.VMEM((D, 768), F32),
+            pltpu.VMEM((len(turned),) + turned[0].shape, BF16),
+            pltpu.VMEM((t * n_chips, KV_LANES), BF16),
+            pltpu.SemaphoreType.DMA((n_chips, 3)),
+        ),
         behind=(dep,),
     )
 
@@ -1173,25 +1182,24 @@
     return step_call("finish_rest", body, info, (mine, other, w_own), outs)
 
 
-def sum_chips(info, terms, over_z, passed, behind):
+def sum_chips(info, terms, pair, passed, behind):
     n_terms = len(terms)
-    cut = P_ROWS // 2
 
     def body(info, ins, outs, scratch):
         for zz in range(4):
             outs[0][zz] = sum(ins[k][zz].astype(F32) for k in range(n_terms)).astype(BF16)
-        for n in range(2):
-            outs[1 + n][...] = ins[n_terms][0, :, cut * n : cut * n + cut, :]
-
-    outs = ((terms[0].shape, BF16),) + (((3, cut, D), BF16),) * 2
+        outs[1][...] = ins[n_terms][...] + ins[n_terms + 1][...]
+
+    outs = ((terms[0].shape, BF16), (pair[0].shape, BF16))
     return step_call(
-        "sum_chips", body, info, (*terms, over_z), outs, behind=behind, passed=passed
-    )
-
-
-def join_cores(info, keep, recv, pairs):
+        "sum_chips", body, info, (*terms, *pair), outs, behind=behind, passed=passed
+    )
+
+
+def join_cores(info, keep, recv, over_z):
     rows = keep.shape[0] // 4
     cut = rows // 2
+    p_cut = P_ROWS // 2
 
     def body(info, ins, outs, scratch):
         for n in range(3):
@@ -1200,13 +1208,11 @@
         for n in range(2):
             r = slice(3 * rows + cut * n, 3 * rows + cut * n + cut)
             outs[3 + n][...] = ins[0][r, :] + ins[1][r, :]
-        for n in range(len(pairs)):
-            outs[5 + n][...] = ins[2 + 2 * n][...] + ins[3 + 2 * n][...]
+            outs[5 + n][...] = ins[2][0, :, p_cut * n : p_cut * n + p_cut, :]
 
     outs = (((rows, KV_LANES), BF16),) * 3 + (((cut, KV_LANES), BF16),) * 2
-    outs += tuple((a.shape, BF16) for a, _ in pairs)
-    flat = [a for pair in pairs for a in pair]
-    return step_call("join_cores", body, info, (keep, recv, *flat), outs)
+    outs += (((3, p_cut, D), BF16),) * 2
+    return step_call("join_cores", body, info, (keep, recv, over_z), outs)
 
 
 def join_near(info, to_x, to_y, from_x, from_y, pairs, passed):
@@ -1228,26 +1234,28 @@
     )
 
 
-def join_projections(info, q_pair, kv_pair, h1, acc_o, got_o, dep):
-    t = h1.shape[0]
+def join_projections(info, q_pair, kv_pair, dep):
     half = WIDE // 2
 
     def body(info, ins, outs, scratch):
         outs[0][:, :, 0:half] = ins[0][...] + ins[1][...]
         outs[0][:, :, half : half + 384] = ins[2][...] + ins[3][...]
+
+    out = ((4, ZP, half + 384), BF16)
+    return step_call("join_projections", body, info, (*q_pair, *kv_pair), (out,), behind=(dep,))[0]
+
+
+def join_output(info, h1, acc_o, got_o, dep):
+    t = h1.shape[0]
+
+    def body(info, ins, outs, scratch):
         for i in range(t // ROWS):
             r = slice(ROWS * i, ROWS * i + ROWS)
-            value = ins[4][r, :] + ins[5][r, :] + ins[6][r, 0:D].astype(F32)
-            outs[1][:, r] = value.astype(BF16).T
-
-    return step_call(
-        "join_projections",
-        body,
-        info,
-        (*q_pair, *kv_pair, h1, acc_o, got_o),
-        (((4, ZP, half + 384), BF16), ((D, t), BF16)),
-        behind=(dep,),
-    )
+            value = ins[0][r, :] + ins[1][r, :] + ins[2][r, 0:D].astype(F32)
+            outs[0][:, r] = value.astype(BF16).T
+
+    out = ((D, t), BF16)
+    return step_call("join_output", body, info, (h1, acc_o, got_o), (out,), behind=(dep,))[0]
 
 
 def halve_rows(info, left, right, behind):
@@ -1426,7 +1434,7 @@
     begin = jnp.max(jnp.where(q_time[..., None] >= doc_starts, doc_starts, 0), axis=-1)
     lo = jnp.maximum(begin, q_time - (WIN - 1)) - (mine[:, None] * BLK - WIN)
     lo = lo[:, None, :].astype(jnp.int32)
-    n_chips = 4 if n_ctx == 8 else 1
+    n_chips = 3 if n_ctx == 8 else 1
     owners = jnp.stack([me ^ (2 * r) for r in range(n_chips)])
     theirs = jnp.sum(
         jnp.where(
@@ -1492,7 +1500,7 @@
     grad_hidden, grad_mid, go_keep, go_send = epi_call(
         info, h1, acc_g, got_lo, got_hi, cot_turned, gains, w_out_all, mid_low
     )
-    a_turned = [*attn_turned, *a_near, c_swap(a_near[0], 4), c_swap(a_near[3], 2)]
+    a_turned = [*attn_turned, *a_near]
 
     if n_ctx == 8:
         out_units = (4, 4)
@@ -1526,43 +1534,43 @@
     go_pair = (go_keep, c_swap(go_send, 1))
     if n_ctx == 8:
         kv_keep, kv_send = kv_parts
-        q_sum, p_l, p_r, kv_send, a_lo, a_hi = sum_chips(
-            info, q_terms, p_sum, (kv_send, *a_turned[6:]), (dq,)
+        q_sum, go_both, kv_send = sum_chips(info, q_terms, go_pair, (kv_send,), (dq,))
+        own, to_x, to_y, far_lo, far_hi, p_l, p_r = join_cores(
+            info, kv_keep, c_swap(kv_send, 1), p_sum
         )
-        a_turned[6:] = [a_lo, a_hi]
-        own, to_x, to_y, far_lo, far_hi, go_both = join_cores(
-            info, kv_keep, c_swap(kv_send, 1), (go_pair,)
-        )
-        totals = (own, to_x, to_y, far_lo, far_hi)
     else:
-        q_sum, p_l, p_r = sum_chips(info, q_terms, p_sum, (), (dq,))
+        q_sum, go_both = sum_chips(info, q_terms, go_pair, (), (dq,))
         own, sums = own_rows(kv_parts)
-        a_turned, totals = a_turned[:2], (own,)
-        go_both = add_pairs(info, (go_pair,))[0]
+        a_turned = a_turned[:2]
+        p_cut = P_ROWS // 2
+        p_l, p_r = p_sum[0, :, :p_cut], p_sum[0, :, p_cut:]
     q_mine = lax.psum_scatter(q_sum, "fsdp", scatter_dimension=0, tiled=True)[0]
     for b in bits_from(8):
         q_mine = q_mine + c_swap(q_mine, b)
+    go_sum = lax.psum_scatter(go_both, "fsdp", scatter_dimension=0, tiled=True)
     gq_keep, gq_send, part = post_q_call(info, attn_in, dq, w_q, own)
-    go_sum = lax.psum_scatter(go_both, "fsdp", scatter_dimension=0, tiled=True)
-    gkv_keep, gkv_send = kv_weights_back(info, cos_turn, sin_turn, a_turned, totals, gq_keep)
     p_pairs = ((p_l, c_swap(p_l, 2)), (p_r, c_swap(p_r, 4)))
     if n_ctx == 8:
-        to_x, to_y, p_l, p_r, gq_send, gkv_send, q_mine = join_near(
+        to_x, to_y, p_l, p_r, gq_send, q_mine = join_near(
             info,
             to_x,
             to_y,
             c_swap(far_lo, 2),
             c_swap(far_hi, 4),
             p_pairs,
-            (gq_send, gkv_send, q_mine),
+            (gq_send, q_mine),
         )
+        totals = (own, to_x, to_y)
         sums = (own, c_swap(to_x, 2), c_swap(to_y, 4))
     else:
         p_l, p_r = (a + b for a, b in p_pairs)
+        totals = (own,)
+    gkv_keep, gkv_send = kv_weights_back(info, cos_turn, sin_turn, a_turned, totals, p_l)
     p_pairs = ((p_l, c_swap(p_l, 4)), (p_r, c_swap(p_r, 2)))
-    g_both, output = join_projections(
-        info, (gq_keep, c_swap(gq_send, 1)), (gkv_keep, c_swap(gkv_send, 1)), h1, acc_o, got_o, p_l
-    )
+    g_both = join_projections(
+        info, (gq_keep, c_swap(gq_send, 1)), (gkv_keep, c_swap(gkv_send, 1)), p_l
+    )
+    output = join_output(info, h1, acc_o, got_o, g_both)
     g_sum = lax.psum_scatter(g_both, "fsdp", scatter_dimension=0, tiled=True)
     q_near = stack_two(info, q_mine, c_swap(q_mine, 2), (output,))
     q_far = c_swap(q_near, 4)

time: 448 us -> 437 us (0.975)
  waiting for transfers between devices: 116 us -> 105 us
    ppermute x55 -> x53, waiting for transfers between devices: 110 us -> 90.3 us  [c_swap(): return lax.ppermute(x, 'ctx', [(i, i ^ bit) for i in range(n)])]
    reduce_scatter x1, waiting for transfers between devices: 0.01 us -> 7.24 us  [on_device(): q_mine = lax.psum_scatter(q_sum, 'fsdp', scatter_dimension=0, tiled=True)[0]]
    ppermute x55 -> x53, starting transfers between devices: 37.2 us -> 38.1 us  [c_swap(): return lax.ppermute(x, 'ctx', [(i, i ^ bit) for i in range(n)])]
    pallas_call x18 -> x19, Pallas kernels: 66.6 us -> 67.1 us  [step_call(): pl.pallas_call(kernel, grid=(1,), out_shape=tuple((jax.ShapeDtypeStruct(s...]
    unnamed x101 -> x93, local copies, waits for them, and re-layouts: 16.6 us -> 16.4 us
  transfers between devices with their start and end apart: 66 -> 64, of which waited for: 21 -> 22; matrix products, arithmetic and copies ran while one was open for 2% -> 2% of each run, Pallas kernels for 47% -> 49%
where the time goes in v5:
time: 437 us; the launch traced here: 430 us
  Pallas kernels  234 us (54%)
  waiting for transfers between devices  105 us (24%)
  starting transfers between devices  47.6 us (11%)
  local copies, waits for them, and re-layouts  24.4 us (6%)
  between operations  14.6 us (3%)
  other arithmetic  4.85 us (1%)
    ppermute x53, waiting for transfers between devices, c_swap(): return lax.ppermute(x, 'ctx', [(i, i ^ bit) for i in range(n)])  90.3 us
    pallas_call x19, Pallas kernels, step_call(): pl.pallas_call(kernel, grid=(1,), out_shape=tuple((jax.ShapeDtypeStruct(s...  67.1 us
    pallas_call x1, Pallas kernels, ffn_call(): pl.pallas_call(ffn_kernel, out_shape=(jax.ShapeDtypeStruct((t, D), F32),...  50.6 us
    pallas_call x1, Pallas kernels, bwd_call(): pl.pallas_call(lambda *refs: bwd_kernel(n_kv, len(deps), first, prev, out...  39.4 us
    ppermute x53, starting transfers between devices, c_swap(): return lax.ppermute(x, 'ctx', [(i, i ^ bit) for i in range(n)])  38.1 us
    pallas_call x1, Pallas kernels, fwd_call(): pl.pallas_call(lambda *refs: fwd_kernel(n_kv, *refs), grid=(blocks,), out...  30.5 us
    unnamed x93, local copies, waits for them, and re-layouts  16.4 us
    pallas_call x1, Pallas kernels, epi_call(): pl.pallas_call(epi_kernel, grid=(t // ROWS,), out_shape=(jax.ShapeDtypeSt...  11.6 us
  transfers between devices with their start and end apart: 64, of which 22 were waited for; matrix products, arithmetic and copies ran while one was open for 2% of the time, Pallas kernels for 49%

profile of v5, /device:TPU:0, one launch (start us, length us, event | category | flops | bytes accessed | tf_op | source)
XLA Modules:
  0.0 429.9 jit_solution(16464412835402472282)
XLA Ops:
  13.0 5.1 %collective-permute-start = (bf16[32,1664]{1,0:T(8,128)(2,1)S(1)}, bf16[32,1664]{1,0:T(8,128)(2,1)S(1)}, u32[]{:S(2)}, u32[]{:S(2)}) collective-permute-start(bf16[32,1664]{1,0:T(8,128)(2,1)S(1)} %concatenate.16), channel_id=1, source_target_pairs={{0,3},{1,0},{2,1},{3,2},{4,7},{5,4},{6,5},{7,6},{8,11},{9,8},{10,9... | collective-permute-start | bytes 319496 | tf_op jit(solution)/shard_map/ppermute | solution.py:1335
  22.5 5.4 %prep_weights.1 = (bf16[3,320,960]{2,1,0:T(8,128)(2,1)}, bf16[480,960]{1,0:T(8,128)(2,1)}, bf16[128,960]{1,0:T(8,128)(2,1)}) custom-call(s32[5]{0:T(128)} %stack.35.info_ref.info.refs_0_, bf16[960,640]{1,0:T(8,128)(2,1)} %refs_0_.1, bf16[960,640]{1,0:T(8,128)(2,1)} %refs_1_.1, bf16[960,640]{1,0:T(8,128)(2,1)} %bitcast.55, bf16[240,960]{1,0:T(8,128)(2,1)} %own.1), custom_call_target="tpu_custom_call" | custom-call | flops 1750000000 | bytes 1 | tf_op jit(solution)/shard_map/prep_weights/pallas_call | solution.py:156
  34.1 7.2 %collective-permute-done.4.refs_3_ = bf16[3,32,1664]{2,1,0:T(8,128)(2,1)S(1)} collective-permute-done((bf16[3,32,1664]{2,1,0:T(8,128)(2,1)}, bf16[3,32,1664]{2,1,0:T(8,128)(2,1)S(1)}, u32[]{:S(2)}, u32[]{:S(2)}) %collective-permute-start.4) | collective-permute-done | bytes 319520 | tf_op jit(solution)/shard_map/ppermute | solution.py:1340
  41.3 6.0 %collective-permute-done.6.refs_5_ = bf16[3,32,1664]{2,1,0:T(8,128)(2,1)S(1)} collective-permute-done((bf16[3,32,1664]{2,1,0:T(8,128)(2,1)}, bf16[3,32,1664]{2,1,0:T(8,128)(2,1)S(1)}, u32[]{:S(2)}, u32[]{:S(2)}) %collective-permute-start.6) | collective-permute-done | bytes 319520 | tf_op jit(solution)/shard_map/ppermute | solution.py:1340
  49.7 9.3 %pre.1 = (bf16[768,960]{1,0:T(8,128)(2,1)}, bf16[480,768]{1,0:T(8,128)(2,1)}, bf16[480,768]{1,0:T(8,128)(2,1)}, bf16[768,960]{1,0:T(8,128)(2,1)}, bf16[768,640]{...) custom-call(s32[5]{0:T(128)} %stack.35.info_ref.info.refs_0_, ...), custom_call_target="tpu_custom_call" | custom-call | flops 4200000000 | bytes 1 | tf_op jit(solution)/shard_map/pre/pallas_call | solution.py:321
  61.2 21.9 %collective-permute-done.10.refs_4_.refs_2_.refs_10_ = bf16[768,640]{1,0:T(8,128)(2,1)S(1)} collective-permute-done((bf16[768,640]{1,0:T(8,128)(2,1)}, bf16[768,640]{1,0:T(8,128)(2,1)S(1)}, u32[]{:S(2)}, u32[]{:S(2)}) %collective-permute-start.10) | collective-permute-done | bytes 983072 | tf_op jit(solution)/shard_map/ppermute | solution.py:1340
  87.8 9.1 %collective-permute-done.12.refs_6_.refs_4_.refs_12_ = bf16[384,640]{1,0:T(8,128)(2,1)} collective-permute-done((bf16[384,640]{1,0:T(8,128)(2,1)}, bf16[384,640]{1,0:T(8,128)(2,1)}, u32[]{:S(2)}, u32[]{:S(2)}) %collective-permute-start.12) | collective-permute-done | bytes 491552 | tf_op jit(solution)/shard_map/ppermute | solution.py:1340
  101.8 5.7 %all-gather.3.cloned.1.call-done = bf16[1920,960]{1,0:T(8,128)(2,1)} async-done(((bf16[480,960]{1,0:T(8,128)(2,1)}), bf16[1920,960]{1,0:T(8,128)(2,1)}) %all-gather.3.cloned.1.call-update) | async-done | bytes 3686416 | tf_op jit(solution)/shard_map/all_gather | solution.py:1466
  107.5 4.1 split_quarters.1
  119.6 30.5 %attend.1 = (bf16[768,960]{1,0:T(8,128)(2,1)}, f32[6,16,128]{2,1,0:T(8,128)}, bf16[6,1152,1920]{2,1,0:T(8,128)(2,1)}) custom-call(s32[6,9]{1,0:T(8,128)} %get-tuple-element.190.refs_0_, s32[6,1,128]{2,1,0:T(1,128)} %maximum_subtract_fusion.refs_1_, bf16[768,960]{1,0:T(8,128)(2,1)} %get-tuple-element.100.refs_2_, ...), custom_call_target="tpu_custom_call" | custom-call | flops 11200000000 | bytes 1 | tf_op jit(solution)/shard_map/attend/pallas_call | solution.py:457
  155.9 7.8 %out_projection.1 = (f32[768,960]{1,0:T(8,128)}, bf16[768,1024]{1,0:T(8,128)(2,1)}, bf16[960,960]{1,0:T(8,128)(2,1)}, bf16[480,768]{1,0:T(8,128)(2,1)}, bf16[480,768]{1,0:T(8,128)(2,1)}) custom-call(s32[5]{0:T(128)} %stack.35.info_ref.info.refs_0_, ...), custom_call_target="tpu_custom_call", output_to_operand_aliasing={{3}: (12, {}), {4}: (13, {})} | custom-call | flops 2449999872 | bytes 1 | tf_op jit(solution)/shard_map/out_projection/pallas_call | solution.py:684
  167.9 50.6 %feed_forward.1 = (f32[768,960]{1,0:T(8,128)}, f32[768,960]{1,0:T(8,128)}, bf16[768,1024]{1,0:T(8,128)(2,1)}, bf16[768,512]{1,0:T(8,128)(2,1)}, bf16[768,512]{1,...) custom-call(s32[5]{0:T(128)} %stack.35.info_ref.info.refs_0_, ...), custom_call_target="tpu_custom_call" | custom-call | flops 17500000256 | bytes 1 | tf_op jit(solution)/shard_map/feed_forward/pallas_call | solution.py:851
  226.1 11.6 %feed_forward_norm_back.1 = (f32[768,960]{1,0:T(8,128)}, bf16[768,960]{1,0:T(8,128)(2,1)}, bf16[4,256,512]{2,1,0:T(8,128)(2,1)}, bf16[4,256,512]{2,1,0:T(8,128)(2,1)}) custom-call(s32[5]{0:T(128)} %stack.35.info_ref.info.refs_0_, f32[768,960]{1,0:T(8,128)} %get-tuple-element.114.h1_ref.refs_0_, f32[768,960]{1,0:T(8,128)} %get-tuple-element.122.acc_g, ...), custom_call_target="tpu_custom_call" | custom-call | flops 4200000000 | bytes 1 | tf_op jit(solution)/shard_map/feed_forward_norm_back/pallas_call | solution.py:950
  237.8 39.4 %attend_back_0.1 = (bf16[768,960]{1,0:T(8,128)(2,1)}, bf16[3072,640]{1,0:T(8,128)(2,1)}, bf16[3072,640]{1,0:T(8,128)(2,1)}) custom-call(s32[6,9]{1,0:T(8,128)} %get-tuple-element.190.refs_0_, s32[6,9]{1,0:T(8,128)} %get-tuple-element.189.refs_1_, bf16[768,960]{1,0:T(8,128)(2,1)} %get-tuple-element.100.refs_2_, bf16[768,960]{1,0:T(8,128)(2,1)} %get-tuple-element.130.refs_3_, ...), custom_call_target="tpu_custom_call" | custom-call | flops 3499999887360 | bytes 1 | tf_op jit(solution)/shard_map/attend_back_0/pallas_call | solution.py:608
  277.3 5.0 %sum_chips.1 = (bf16[4,3,48,960]{3,2,1,0:T(8,128)(2,1)}, bf16[4,256,512]{2,1,0:T(8,128)(2,1)}, bf16[3072,640]{1,0:T(8,128)(2,1)}) custom-call(s32[5]{0:T(128)} %stack.35.info_ref.info.refs_0_, bf16[4,3,48,960]{3,2,1,0:T(8,128)(2,1)} %get-tuple-element.136.refs_0_, ...), custom_call_target="tpu_custom_call", output_to_operand_aliasing={{2}: (8, {})} | custom-call | flops 1400000000 | bytes 1 | tf_op jit(solution)/shard_map/sum_chips/pallas_call | solution.py:156
  283.7 6.1 %collective-permute-done.40.refs_1_ = bf16[3072,640]{1,0:T(8,128)(2,1)} collective-permute-done((bf16[3072,640]{1,0:T(8,128)(2,1)}, bf16[3072,640]{1,0:T(8,128)(2,1)}, u32[]{:S(2)}, u32[]{:S(2)}) %collective-permute-start.40) | collective-permute-done | bytes 3932192 | tf_op jit(solution)/shard_map/ppermute | solution.py:1340
  289.8 6.0 %join_cores.1 = (bf16[768,640]{1,0:T(8,128)(2,1)}, bf16[768,640]{1,0:T(8,128)(2,1)}, bf16[768,640]{1,0:T(8,128)(2,1)}, bf16[384,640]{1,0:T(8,128)(2,1)}, bf16[38...) custom-call(s32[5]{0:T(128)} %stack.35.info_ref.info.refs_0_, ...), custom_call_target="tpu_custom_call" | custom-call | flops 1750000000 | bytes 1 | tf_op jit(solution)/shard_map/join_cores/pallas_call | solution.py:156
  299.8 8.6 %query_back.1 = (bf16[4,256,512]{2,1,0:T(8,128)(2,1)}, bf16[4,256,512]{2,1,0:T(8,128)(2,1)}, f32[768,960]{1,0:T(8,128)}) custom-call(s32[5]{0:T(128)} %stack.35.info_ref.info.refs_0_, bf16[768,960]{1,0:T(8,128)(2,1)} %get-tuple-element.121.a_ref, bf16[768,960]{1,0:T(8,128)(2,1)} %get-tuple-element.133.refs_6_.g_ref, ...), custom_call_target="tpu_custom_call" | custom-call | flops 2800000000 | bytes 1 | tf_op jit(solution)/shard_map/query_back/pallas_call | solution.py:997
  308.4 7.2 %reduce-scatter.7.cloned.1.call-done = bf16[1,3,48,960]{3,2,1,0:T(8,128)(2,1)} async-done(((bf16[4,3,48,960]{3,2,1,0:T(8,128)(2,1)}), bf16[1,3,48,960]{3,2,1,0:T(8,128)(2,1)}) %reduce-scatter.7.cloned.1.call-update) | async-done | bytes 276496 | tf_op jit(solution)/shard_map/reduce_scatter | solution.py:1547
  323.0 9.0 %key_value_weights_back.1 = (bf16[4,256,384]{2,1,0:T(8,128)(2,1)}, bf16[4,256,384]{2,1,0:T(8,128)(2,1)}) custom-call(s32[5]{0:T(128)} %stack.35.info_ref.info.refs_0_, f32[32,2304]{1,0:T(8,128)} %get-tuple-element.188.refs_3_.cos_ref.refs_7_.refs_0_.refs_4_, f32[32,2304]{1,0:T(8,128)} %get-tuple-element.187.refs_4_.sin_ref.refs_8_.refs_1_.refs_5_, ...), custom_call_target="tpu_custom_call" | custom-call | flops 3849999872 | bytes 1 | tf_op jit(solution)/shard_map/key_value_weights_back/pallas_call | solution.py:156
  345.5 4.9 %join_output.1.refs_2_ = bf16[960,768]{1,0:T(8,128)(2,1)} custom-call(s32[5]{0:T(128)} %stack.35.info_ref.info.refs_0_, f32[768,960]{1,0:T(8,128)} %get-tuple-element.114.h1_ref.refs_0_, f32[768,960]{1,0:T(8,128)} %get-tuple-element.119.refs_1_, bf16[768,1024]{1,0:T(8,128)(2,1)} %copy-done.2, bf16[4,256,896]{2,1,0:T(8,128)(2,1)} %join_projections.1.refs_3_), custom_call_target="tpu_custom_call" | custom-call | flops 1750000000 | bytes 1 | tf_op jit(solution)/shard_map/join_output/pallas_call | solution.py:156
  350.4 20.6 %collective-permute-done.49.refs_1_ = bf16[3,48,960]{2,1,0:T(8,128)(2,1)S(1)} collective-permute-done((bf16[3,48,960]{2,1,0:T(8,128)(2,1)S(1)}, bf16[3,48,960]{2,1,0:T(8,128)(2,1)S(1)}, u32[]{:S(2)}, u32[]{:S(2)}) %collective-permute-start.49) | collective-permute-done | bytes 276512 | tf_op jit(solution)/shard_map/ppermute | solution.py:1340
  374.9 8.7 %key_value_back.1.refs_2_ = bf16[960,768]{1,0:T(8,128)(2,1)} custom-call(s32[5]{0:T(128)} %stack.35.info_ref.info.refs_0_, bf16[768,640]{1,0:T(8,128)(2,1)} %get-tuple-element.145._.refs_8_.refs_1_, bf16[768,640]{1,0:T(8,128)(2,1)} %copy-done.9, bf16[768,640]{1,0:T(8,128)(2,1)} %collective-permute-done.48.refs_3_, ...), custom_call_target="tpu_custom_call" | custom-call | flops 2800000000 | bytes 1 | tf_op jit(solution)/shard_map/key_value_back/pallas_call | solution.py:1109
  406.5 6.2 %finish_feed_forward.1 = (f32[960,640]{1,0:T(8,128)}, f32[960,640]{1,0:T(8,128)}, f32[960,640]{1,0:T(8,128)}) custom-call(s32[5]{0:T(128)} %stack.35.info_ref.info.refs_0_, bf16[3,320,960]{2,1,0:T(8,128)(2,1)} %get-tuple-element.175.refs_0_, bf16[3,320,960]{2,1,0:T(8,128)(2,1)} %copy-done.30, bf16[128,1408]{1,0:T(8,128)(2,1)} %get-tuple-element.173.refs_2_.refs_0_), custom_call_target="tpu_custom_call" | custom-call | flops 2100000000 | bytes 1 | tf_op jit(solution)/shard_map/finish_feed_forward/pallas_call | solution.py:156
  (266 shorter events, 119.3 us)
Async XLA Ops:
  7.2 100.3 %all-gather.3.cloned.1.call-start = ((), (), s32[]{:S(2)}) async-start(), calls=%async_computation.8 | async-start | bytes 4915200 | tf_op jit(solution)/shard_map/all_gather | solution.py:1466
  30.5 259.3 %reduce-scatter.5.cloned.1.call-start = ((), (), s32[]{:S(2)}) async-start(), calls=%async_computation.4 | async-start | bytes 3932160 | tf_op jit(solution)/shard_map/reduce_scatter | solution.py:1492
  47.8 39.1 %collective-permute-start.19 = (bf16[960,768]{1,0:T(8,128)(2,1)}, bf16[960,768]{1,0:T(8,128)(2,1)S(1)}, u32[]{:S(2)}, u32[]{:S(2)}) collective-permute-start(bf16[960,768]{1,0:T(8,128)(2,1)} %bitcast.52), channel_id=1, source_target_pairs={{0,4},{4,0},{8,12},{12,8},{16,20},{20,16},{24,28},{28,24},{1,5},{5... | collective-permute-start | bytes 4423688 | tf_op jit(solution)/shard_map/ppermute | solution.py:1340
  61.2 38.5 %collective-permute-start.14 = (bf16[768,640]{1,0:T(8,128)(2,1)}, bf16[768,640]{1,0:T(8,128)(2,1)}, u32[]{:S(2)}, u32[]{:S(2)}) collective-permute-start(bf16[768,640]{1,0:T(8,128)(2,1)} %get-tuple-element.101.refs_3_.refs_1_.refs_9_), channel_id=1, source_target_pairs={{0,4},{4,0},{8,12},{12,8},{16,20},{20,16},{24,28},{28,24},{1,5},{5... | collective-permute-start | bytes 2949128 | tf_op jit(solution)/shard_map/ppermute | solution.py:1340
  111.7 38.5 %collective-permute-start.23 = (bf16[720,960]{1,0:T(8,128)(2,1)}, bf16[720,960]{1,0:T(8,128)(2,1)S(1)}, u32[]{:S(2)}, u32[]{:S(2)}) collective-permute-start(bf16[720,960]{1,0:T(8,128)(2,1)} %get-tuple-element.106.refs_0_), channel_id=1, source_target_pairs={{0,8},{4,12},{8,0},{12,4},{16,24},{20,28},{24,16},{28,20},{1,9},{5... | collective-permute-start | bytes 4147208 | tf_op jit(solution)/shard_map/ppermute | solution.py:1340
  113.2 36.9 %collective-permute-start.24 = (bf16[720,960]{1,0:T(8,128)(2,1)}, bf16[720,960]{1,0:T(8,128)(2,1)S(1)}, u32[]{:S(2)}, u32[]{:S(2)}) collective-permute-start(bf16[720,960]{1,0:T(8,128)(2,1)} %get-tuple-element.108.refs_1_), channel_id=1, source_target_pairs={{0,16},{4,20},{8,24},{12,28},{16,0},{20,4},{24,8},{28,12},{1,17},{... | collective-permute-start | bytes 4147208 | tf_op jit(solution)/shard_map/ppermute | solution.py:1340
  116.4 33.6 %collective-permute-start.20 = (bf16[128,960]{1,0:T(8,128)(2,1)}, bf16[128,960]{1,0:T(8,128)(2,1)S(1)}, u32[]{:S(2)}, u32[]{:S(2)}) collective-permute-start(bf16[128,960]{1,0:T(8,128)(2,1)} %meet.3), channel_id=1, source_target_pairs={{0,3},{1,0},{2,1},{3,2},{4,7},{5,4},{6,5},{7,6},{8,11},{9,8},{10,9... | collective-permute-start | bytes 737288 | tf_op jit(solution)/shard_map/ppermute | solution.py:1335
  117.3 32.8 %collective-permute-start.21 = (bf16[128,960]{1,0:T(8,128)(2,1)}, bf16[128,960]{1,0:T(8,128)(2,1)S(1)}, u32[]{:S(2)}, u32[]{:S(2)}) collective-permute-start(bf16[128,960]{1,0:T(8,128)(2,1)} %meet.3), channel_id=1, source_target_pairs={{0,2},{1,3},{2,0},{3,1},{4,6},{5,7},{6,4},{7,5},{8,10},{9,11},{10,... | collective-permute-start | bytes 737288 | tf_op jit(solution)/shard_map/ppermute | solution.py:1335
  117.5 32.6 %collective-permute-start.22 = (bf16[128,960]{1,0:T(8,128)(2,1)}, bf16[128,960]{1,0:T(8,128)(2,1)S(1)}, u32[]{:S(2)}, u32[]{:S(2)}) collective-permute-start(bf16[128,960]{1,0:T(8,128)(2,1)} %meet.3), channel_id=1, source_target_pairs={{0,1},{1,2},{2,3},{3,0},{4,5},{5,6},{6,7},{7,4},{8,9},{9,10},{10,1... | collective-permute-start | bytes 737288 | tf_op jit(solution)/shard_map/ppermute | solution.py:1335
  163.9 54.7 %collective-permute-start.30 = (bf16[480,768]{1,0:T(8,128)(2,1)}, bf16[480,768]{1,0:T(8,128)(2,1)S(1)}, u32[]{:S(2)}, u32[]{:S(2)}) collective-permute-start(bf16[480,768]{1,0:T(8,128)(2,1)} %get-tuple-element.125.refs_2_), channel_id=1, source_target_pairs={{0,8},{4,12},{8,0},{12,4},{16,24},{20,28},{24,16},{28,20},{1,9},{5... | collective-permute-start | bytes 2211848 | tf_op jit(solution)/shard_map/ppermute | solution.py:1340
  164.4 54.1 %collective-permute-start.32 = (bf16[480,768]{1,0:T(8,128)(2,1)}, bf16[480,768]{1,0:T(8,128)(2,1)S(1)}, u32[]{:S(2)}, u32[]{:S(2)}) collective-permute-start(bf16[480,768]{1,0:T(8,128)(2,1)} %get-tuple-element.125.refs_2_), channel_id=1, source_target_pairs={{0,16},{4,20},{8,24},{12,28},{16,0},{20,4},{24,8},{28,12},{1,17},{... | collective-permute-start | bytes 2211848 | tf_op jit(solution)/shard_map/ppermute | solution.py:1340
  165.0 53.6 %collective-permute-start.31 = (bf16[480,768]{1,0:T(8,128)(2,1)}, bf16[480,768]{1,0:T(8,128)(2,1)S(1)}, u32[]{:S(2)}, u32[]{:S(2)}) collective-permute-start(bf16[480,768]{1,0:T(8,128)(2,1)} %get-tuple-element.126.refs_3_), channel_id=1, source_target_pairs={{0,8},{4,12},{8,0},{12,4},{16,24},{20,28},{24,16},{28,20},{1,9},{5... | collective-permute-start | bytes 2211848 | tf_op jit(solution)/shard_map/ppermute | solution.py:1340
  166.5 52.1 %collective-permute-start.33 = (bf16[480,768]{1,0:T(8,128)(2,1)}, bf16[480,768]{1,0:T(8,128)(2,1)S(1)}, u32[]{:S(2)}, u32[]{:S(2)}) collective-permute-start(bf16[480,768]{1,0:T(8,128)(2,1)} %get-tuple-element.126.refs_3_), channel_id=1, source_target_pairs={{0,16},{4,20},{8,24},{12,28},{16,0},{20,4},{24,8},{28,12},{1,17},{... | collective-permute-start | bytes 2211848 | tf_op jit(solution)/shard_map/ppermute | solution.py:1340
  221.4 55.9 %collective-permute-start.36 = (bf16[4,3,48,960]{3,2,1,0:T(8,128)(2,1)}, bf16[4,3,48,960]{3,2,1,0:T(8,128)(2,1)}, u32[]{:S(2)}, u32[]{:S(2)}) collective-permute-start(bf16[4,3,48,960]{3,2,1,0:T(8,128)(2,1)} %get-tuple-element.137), channel_id=1, source_target_pairs={{0,8},{4,12},{8,0},{12,4},{16,24},{20,28},{24,16},{28,20},{1,9},{5... | collective-permute-start | bytes 3317768 | tf_op jit(solution)/shard_map/ppermute | solution.py:1340
  222.0 55.3 %collective-permute-start.37 = (bf16[4,3,48,960]{3,2,1,0:T(8,128)(2,1)}, bf16[4,3,48,960]{3,2,1,0:T(8,128)(2,1)}, u32[]{:S(2)}, u32[]{:S(2)}) collective-permute-start(bf16[4,3,48,960]{3,2,1,0:T(8,128)(2,1)} %get-tuple-element.138), channel_id=1, source_target_pairs={{0,16},{4,20},{8,24},{12,28},{16,0},{20,4},{24,8},{28,12},{1,17},{... | collective-permute-start | bytes 3317768 | tf_op jit(solution)/shard_map/ppermute | solution.py:1340
  222.5 54.8 %collective-permute-start.38 = (bf16[4,3,48,960]{3,2,1,0:T(8,128)(2,1)}, bf16[4,3,48,960]{3,2,1,0:T(8,128)(2,1)}, u32[]{:S(2)}, u32[]{:S(2)}) collective-permute-start(bf16[4,3,48,960]{3,2,1,0:T(8,128)(2,1)} %get-tuple-element.139), channel_id=1, source_target_pairs={{0,24},{4,28},{8,16},{12,20},{16,8},{20,12},{24,0},{28,4},{1,25},{... | collective-permute-start | bytes 3317768 | tf_op jit(solution)/shard_map/ppermute | solution.py:1340
  224.9 90.8 %reduce-scatter.7.cloned.1.call-start = ((), (), s32[]{:S(2)}) async-start(), calls=%async_computation.5 | async-start | bytes 1474560 | tf_op jit(solution)/shard_map/reduce_scatter | solution.py:1547
  237.7 39.5 %collective-permute-start.39 = (bf16[4,256,512]{2,1,0:T(8,128)(2,1)}, bf16[4,256,512]{2,1,0:T(8,128)(2,1)}, u32[]{:S(2)}, u32[]{:S(2)}) collective-permute-start(bf16[4,256,512]{2,1,0:T(8,128)(2,1)} %get-tuple-element.141), channel_id=1, source_target_pairs={{0,4},{4,0},{8,12},{12,8},{16,20},{20,16},{24,28},{28,24},{1,5},{5... | collective-permute-start | bytes 3145736 | tf_op jit(solution)/shard_map/ppermute | solution.py:1340
  283.1 100.5 %reduce-scatter.9.cloned.1.call-start = ((), (), s32[]{:S(2)}) async-start(), calls=%async_computation.6 | async-start | bytes 1310720 | tf_op jit(solution)/shard_map/reduce_scatter | solution.py:1550
  283.6 101.0 %reduce-scatter.11.cloned.1.call-start = ((), (), s32[]{:S(2)}) async-start(), calls=%async_computation.7 | async-start | bytes 2293760 | tf_op jit(solution)/shard_map/reduce_scatter | solution.py:1574
  339.8 34.1 %collective-permute-start.47 = (bf16[768,640]{1,0:T(8,128)(2,1)}, bf16[768,640]{1,0:T(8,128)(2,1)S(1)}, u32[]{:S(2)}, u32[]{:S(2)}) collective-permute-start(bf16[768,640]{1,0:T(8,128)(2,1)} %get-tuple-element.160.refs_9_), channel_id=1, source_target_pairs={{0,8},{4,12},{8,0},{12,4},{16,24},{20,28},{24,16},{28,20},{1,9},{5... | collective-permute-start | bytes 2949128 | tf_op jit(solution)/shard_map/ppermute | solution.py:1340
  341.5 32.5 %collective-permute-start.48 = (bf16[768,640]{1,0:T(8,128)(2,1)}, bf16[768,640]{1,0:T(8,128)(2,1)}, u32[]{:S(2)}, u32[]{:S(2)}) collective-permute-start(bf16[768,640]{1,0:T(8,128)(2,1)} %get-tuple-element.161.refs_10_), channel_id=1, source_target_pairs={{0,16},{4,20},{8,24},{12,28},{16,0},{20,4},{24,8},{28,12},{1,17},{... | collective-permute-start | bytes 2949128 | tf_op jit(solution)/shard_map/ppermute | solution.py:1340
  342.2 47.3 %collective-permute-start.52 = (bf16[3,64,960]{2,1,0:T(8,128)(2,1)S(1)}, bf16[3,64,960]{2,1,0:T(8,128)(2,1)}, u32[]{:S(2)}, u32[]{:S(2)}) collective-permute-start(bf16[3,64,960]{2,1,0:T(8,128)(2,1)S(1)} %copy-done.3), channel_id=1, source_target_pairs={{0,16},{4,20},{8,24},{12,28},{16,0},{20,4},{24,8},{28,12},{1,17},{... | collective-permute-start | bytes 1105928 | tf_op jit(solution)/shard_map/ppermute | solution.py:1340
  343.9 45.7 %collective-permute-start.53 = (bf16[3,64,960]{2,1,0:T(8,128)(2,1)}, bf16[3,64,960]{2,1,0:T(8,128)(2,1)}, u32[]{:S(2)}, u32[]{:S(2)}) collective-permute-start(bf16[3,64,960]{2,1,0:T(8,128)(2,1)} %get-tuple-element.172.refs_2_), channel_id=1, source_target_pairs={{0,8},{4,12},{8,0},{12,4},{16,24},{20,28},{24,16},{28,20},{1,9},{5... | collective-permute-start | bytes 1105928 | tf_op jit(solution)/shard_map/ppermute | solution.py:1340
  (85 other events, 595.6 us)
Sparse Core Ops, SparseCore 0:
  30.6 76.8 all-gather.2
  225.0 58.4 reduce-scatter.4
  286.4 29.1 reduce-scatter.6
  317.8 25.8 reduce-scatter.8
  346.5 38.0 reduce-scatter.10

commit v6 on v5

--- a/solution.py
+++ b/solution.py
@@ -364,7 +364,7 @@
     lax.fori_loop(0, NWB, body, 0)
 
 
-def next_window(tab, kvs, win, sem, first=0):
+def next_window(tab, kvs, win, sem, first=0, meanwhile=None):
     i = pl.program_id(0)
     slot = lax.rem(i, 2)
 
@@ -376,6 +376,8 @@
     def _():
         start_window(tab, kvs, win, sem, i + first + 1, 1 - slot)
 
+    if meanwhile is not None:
+        meanwhile()
     pltpu.make_async_copy(win.at[slot], win.at[slot], sem.at[slot]).wait()
     return slot
 
@@ -498,16 +500,18 @@
     win, acc, scores, stage, stage_in, sem, out_sem, in_sem = refs[1 + n_out :]
     i = pl.program_id(0)
     blk = i + first
-    slot = next_window(tab, kvs, win, sem, first)
     lanes = acc.shape[1]
 
-    @pl.when(i == 0)
-    def _():
-        def clear(b, _):
-            acc[pl.ds(pl.multiple_of(b * BLK, BLK), BLK), :] = jnp.zeros((BLK, lanes), F32)
-            return 0
-
-        lax.fori_loop(0, n_slots, clear, 0)
+    def clear_all():
+        @pl.when(i == 0)
+        def _():
+            def clear(b, _):
+                acc[pl.ds(pl.multiple_of(b * BLK, BLK), BLK), :] = jnp.zeros((BLK, lanes), F32)
+                return 0
+
+            lax.fori_loop(0, n_slots, clear, 0)
+
+    slot = next_window(tab, kvs, win, sem, first, clear_all)
 
     def add(slab, value):
         for j in range(NWB):
@@ -1184,13 +1188,22 @@
 
 def sum_chips(info, terms, pair, passed, behind):
     n_terms = len(terms)
+    half, lanes = pair[0].shape[1] // 2, pair[0].shape[2]
+    q_rows = 3 * Q_ROWS
 
     def body(info, ins, outs, scratch):
+        out = outs[0]
         for zz in range(4):
-            outs[0][zz] = sum(ins[k][zz].astype(F32) for k in range(n_terms)).astype(BF16)
-        outs[1][...] = ins[n_terms][...] + ins[n_terms + 1][...]
-
-    outs = ((terms[0].shape, BF16), (pair[0].shape, BF16))
+            value = sum(ins[k][zz].astype(F32) for k in range(n_terms)).astype(BF16)
+            for n in range(3):
+                out[zz, Q_ROWS * n : Q_ROWS * n + Q_ROWS, 0:D] = value[n]
+            out[zz, 0:q_rows, D:WIDE] = jnp.zeros((q_rows, WIDE - D), BF16)
+        for n in range(2):
+            r = slice(half * n, half * n + half)
+            value = ins[n_terms][:, r, :] + ins[n_terms + 1][:, r, :]
+            out[:, q_rows : q_rows + half, lanes * n : lanes * n + lanes] = value
+
+    outs = (((4, q_rows + half, WIDE), BF16),)
     return step_call(
         "sum_chips", body, info, (*terms, *pair), outs, behind=behind, passed=passed
     )
@@ -1234,15 +1247,19 @@
     )
 
 
-def join_projections(info, q_pair, kv_pair, dep):
+def join_projections(info, q_pair, kv_pair, over_z, dep):
     half = WIDE // 2
 
     def body(info, ins, outs, scratch):
         outs[0][:, :, 0:half] = ins[0][...] + ins[1][...]
         outs[0][:, :, half : half + 384] = ins[2][...] + ins[3][...]
-
-    out = ((4, ZP, half + 384), BF16)
-    return step_call("join_projections", body, info, (*q_pair, *kv_pair), (out,), behind=(dep,))[0]
+        for n in range(3):
+            outs[1][n] = ins[4][0, Q_ROWS * n : Q_ROWS * n + Q_ROWS, 0:D]
+
+    outs = (((4, ZP, half + 384), BF16), ((3, Q_ROWS, D), BF16))
+    return step_call(
+        "join_projections", body, info, (*q_pair, *kv_pair, over_z), outs, behind=(dep,)
+    )
 
 
 def join_output(info, h1, acc_o, got_o, dep):
@@ -1259,14 +1276,14 @@
 
 
 def halve_rows(info, left, right, behind):
-    rows = left.shape[1] // 2
-    lanes = left.shape[2], right.shape[2]
+    rows = right.shape[1] // 2
+    lanes = left.shape[2] // 2, right.shape[2]
+    at = 3 * Q_ROWS
 
     def body(info, ins, outs, scratch):
         for n in range(2):
-            r = slice(rows * n, rows * n + rows)
-            outs[n][:, 0 : lanes[0]] = ins[0][0, r, :]
-            outs[n][:, lanes[0] : sum(lanes)] = ins[1][0, r, :]
+            outs[n][:, 0 : lanes[0]] = ins[0][0, at : at + rows, lanes[0] * n : lanes[0] * n + lanes[0]]
+            outs[n][:, lanes[0] : sum(lanes)] = ins[1][0, rows * n : rows * n + rows, :]
 
     outs = (((rows, sum(lanes)), BF16),) * 2
     return step_call("halve_rows", body, info, (left, right), outs, behind=behind)
@@ -1534,31 +1551,28 @@
     go_pair = (go_keep, c_swap(go_send, 1))
     if n_ctx == 8:
         kv_keep, kv_send = kv_parts
-        q_sum, go_both, kv_send = sum_chips(info, q_terms, go_pair, (kv_send,), (dq,))
+        both, kv_send = sum_chips(info, q_terms, go_pair, (kv_send,), (dq,))
         own, to_x, to_y, far_lo, far_hi, p_l, p_r = join_cores(
             info, kv_keep, c_swap(kv_send, 1), p_sum
         )
     else:
-        q_sum, go_both = sum_chips(info, q_terms, go_pair, (), (dq,))
+        both = sum_chips(info, q_terms, go_pair, (), (dq,))[0]
         own, sums = own_rows(kv_parts)
         a_turned = a_turned[:2]
         p_cut = P_ROWS // 2
         p_l, p_r = p_sum[0, :, :p_cut], p_sum[0, :, p_cut:]
-    q_mine = lax.psum_scatter(q_sum, "fsdp", scatter_dimension=0, tiled=True)[0]
-    for b in bits_from(8):
-        q_mine = q_mine + c_swap(q_mine, b)
-    go_sum = lax.psum_scatter(go_both, "fsdp", scatter_dimension=0, tiled=True)
+    both = lax.psum_scatter(both, "fsdp", scatter_dimension=0, tiled=True)
     gq_keep, gq_send, part = post_q_call(info, attn_in, dq, w_q, own)
     p_pairs = ((p_l, c_swap(p_l, 2)), (p_r, c_swap(p_r, 4)))
     if n_ctx == 8:
-        to_x, to_y, p_l, p_r, gq_send, q_mine = join_near(
+        to_x, to_y, p_l, p_r, gq_send = join_near(
             info,
             to_x,
             to_y,
             c_swap(far_lo, 2),
             c_swap(far_hi, 4),
             p_pairs,
-            (gq_send, q_mine),
+            (gq_send,),
         )
         totals = (own, to_x, to_y)
         sums = (own, c_swap(to_x, 2), c_swap(to_y, 4))
@@ -1567,9 +1581,11 @@
         totals = (own,)
     gkv_keep, gkv_send = kv_weights_back(info, cos_turn, sin_turn, a_turned, totals, p_l)
     p_pairs = ((p_l, c_swap(p_l, 4)), (p_r, c_swap(p_r, 2)))
-    g_both = join_projections(
-        info, (gq_keep, c_swap(gq_send, 1)), (gkv_keep, c_swap(gkv_send, 1)), p_l
-    )
+    g_both, q_mine = join_projections(
+        info, (gq_keep, c_swap(gq_send, 1)), (gkv_keep, c_swap(gkv_send, 1)), both, p_l
+    )
+    for b in bits_from(8):
+        q_mine = q_mine + c_swap(q_mine, b)
     output = join_output(info, h1, acc_o, got_o, g_both)
     g_sum = lax.psum_scatter(g_both, "fsdp", scatter_dimension=0, tiled=True)
     q_near = stack_two(info, q_mine, c_swap(q_mine, 2), (output,))
@@ -1579,7 +1595,7 @@
     )
     for b in bits_from(8):
         p_pairs = tuple((a + c_swap(a, b), g + c_swap(g, b)) for a, g in p_pairs)
-    g_l, g_r = halve_rows(info, go_sum, g_sum, (input_grad,))
+    g_l, g_r = halve_rows(info, both, g_sum, (input_grad,))
     ffn_sum = join_ffn(info, p_pairs, q_near, q_far, g_l)
     g_l, g_r, ffn_sum = add_pairs(
         info, ((g_l, c_swap(g_l, 2)), (g_r, c_swap(g_r, 4))), (ffn_sum,)

time: 437 us -> 434 us (level)
    reduce_scatter x2 -> x1, waiting for transfers between devices: 7.26 us -> 0.01 us  [on_device(): both = lax.psum_scatter(both, 'fsdp', scatter_dimension=0, tiled=True)]
    ppermute x53, waiting for transfers between devices: 90.3 us -> 96.4 us  [c_swap(): return lax.ppermute(x, 'ctx', [(i, i ^ bit) for i in range(n)])]
  transfers between devices with their start and end apart: 64 -> 63, of which waited for: 22 -> 20; matrix products, arithmetic and copies ran while one was open for 2% -> 2% of each run, Pallas kernels for 49% -> 48%
where the time goes in v6:
time: 434 us; the launch traced here: 428 us
  Pallas kernels  233 us (54%)
  waiting for transfers between devices  102 us (24%)
  starting transfers between devices  48.5 us (11%)
  local copies, waits for them, and re-layouts  24.4 us (6%)
  between operations  14.6 us (3%)
  other arithmetic  4.82 us (1%)
    ppermute x53, waiting for transfers between devices, c_swap(): return lax.ppermute(x, 'ctx', [(i, i ^ bit) for i in range(n)])  96.4 us
    pallas_call x19, Pallas kernels, step_call(): pl.pallas_call(kernel, grid=(1,), out_shape=tuple((jax.ShapeDtypeStruct(s...  67.6 us
    pallas_call x1, Pallas kernels, ffn_call(): pl.pallas_call(ffn_kernel, out_shape=(jax.ShapeDtypeStruct((t, D), F32),...  50.6 us
    ppermute x53, starting transfers between devices, c_swap(): return lax.ppermute(x, 'ctx', [(i, i ^ bit) for i in range(n)])  39 us
    pallas_call x1, Pallas kernels, bwd_call(): pl.pallas_call(lambda *refs: bwd_kernel(n_kv, len(deps), first, prev, out...  38.3 us
    pallas_call x1, Pallas kernels, fwd_call(): pl.pallas_call(lambda *refs: fwd_kernel(n_kv, *refs), grid=(blocks,), out...  30.4 us
    unnamed x93, local copies, waits for them, and re-layouts  16.4 us
    pallas_call x1, Pallas kernels, epi_call(): pl.pallas_call(epi_kernel, grid=(t // ROWS,), out_shape=(jax.ShapeDtypeSt...  12 us
  transfers between devices with their start and end apart: 63, of which 20 were waited for; matrix products, arithmetic and copies ran while one was open for 2% of the time, Pallas kernels for 48%

profile of v6, /device:TPU:0, one launch (start us, length us, event | category | flops | bytes accessed | tf_op | source)
XLA Modules:
  0.0 427.9 jit_solution(2300354382317261953)
XLA Ops:
  13.0 5.1 %collective-permute-start = (bf16[32,1664]{1,0:T(8,128)(2,1)S(1)}, bf16[32,1664]{1,0:T(8,128)(2,1)S(1)}, u32[]{:S(2)}, u32[]{:S(2)}) collective-permute-start(bf16[32,1664]{1,0:T(8,128)(2,1)S(1)} %concatenate.16), channel_id=1, source_target_pairs={{0,3},{1,0},{2,1},{3,2},{4,7},{5,4},{6,5},{7,6},{8,11},{9,8},{10,9... | collective-permute-start | bytes 319496 | tf_op jit(solution)/shard_map/ppermute | solution.py:1352
  22.5 5.4 %prep_weights.1 = (bf16[3,320,960]{2,1,0:T(8,128)(2,1)}, bf16[480,960]{1,0:T(8,128)(2,1)}, bf16[128,960]{1,0:T(8,128)(2,1)}) custom-call(s32[5]{0:T(128)} %stack.35.info_ref.info.refs_0_, bf16[960,640]{1,0:T(8,128)(2,1)} %refs_0_.1, bf16[960,640]{1,0:T(8,128)(2,1)} %refs_1_.1, bf16[960,640]{1,0:T(8,128)(2,1)} %bitcast.53, bf16[240,960]{1,0:T(8,128)(2,1)} %own.1), custom_call_target="tpu_custom_call" | custom-call | flops 1750000000 | bytes 1 | tf_op jit(solution)/shard_map/prep_weights/pallas_call | solution.py:156
  34.1 7.2 %collective-permute-done.4.refs_3_ = bf16[3,32,1664]{2,1,0:T(8,128)(2,1)S(1)} collective-permute-done((bf16[3,32,1664]{2,1,0:T(8,128)(2,1)}, bf16[3,32,1664]{2,1,0:T(8,128)(2,1)S(1)}, u32[]{:S(2)}, u32[]{:S(2)}) %collective-permute-start.4) | collective-permute-done | bytes 319520 | tf_op jit(solution)/shard_map/ppermute | solution.py:1357
  41.3 6.0 %collective-permute-done.6.refs_5_ = bf16[3,32,1664]{2,1,0:T(8,128)(2,1)S(1)} collective-permute-done((bf16[3,32,1664]{2,1,0:T(8,128)(2,1)}, bf16[3,32,1664]{2,1,0:T(8,128)(2,1)S(1)}, u32[]{:S(2)}, u32[]{:S(2)}) %collective-permute-start.6) | collective-permute-done | bytes 319520 | tf_op jit(solution)/shard_map/ppermute | solution.py:1357
  49.7 9.3 %pre.1 = (bf16[768,960]{1,0:T(8,128)(2,1)}, bf16[480,768]{1,0:T(8,128)(2,1)}, bf16[480,768]{1,0:T(8,128)(2,1)}, bf16[768,960]{1,0:T(8,128)(2,1)}, bf16[768,640]{...) custom-call(s32[5]{0:T(128)} %stack.35.info_ref.info.refs_0_, ...), custom_call_target="tpu_custom_call" | custom-call | flops 4200000000 | bytes 1 | tf_op jit(solution)/shard_map/pre/pallas_call | solution.py:321
  61.2 21.9 %collective-permute-done.10.refs_4_.refs_2_.refs_10_ = bf16[768,640]{1,0:T(8,128)(2,1)S(1)} collective-permute-done((bf16[768,640]{1,0:T(8,128)(2,1)}, bf16[768,640]{1,0:T(8,128)(2,1)S(1)}, u32[]{:S(2)}, u32[]{:S(2)}) %collective-permute-start.10) | collective-permute-done | bytes 983072 | tf_op jit(solution)/shard_map/ppermute | solution.py:1357
  87.7 9.1 %collective-permute-done.12.refs_6_.refs_4_.refs_12_ = bf16[384,640]{1,0:T(8,128)(2,1)} collective-permute-done((bf16[384,640]{1,0:T(8,128)(2,1)}, bf16[384,640]{1,0:T(8,128)(2,1)}, u32[]{:S(2)}, u32[]{:S(2)}) %collective-permute-start.12) | collective-permute-done | bytes 491552 | tf_op jit(solution)/shard_map/ppermute | solution.py:1357
  101.8 5.7 %all-gather.3.cloned.1.call-done = bf16[1920,960]{1,0:T(8,128)(2,1)} async-done(((bf16[480,960]{1,0:T(8,128)(2,1)}), bf16[1920,960]{1,0:T(8,128)(2,1)}) %all-gather.3.cloned.1.call-update) | async-done | bytes 3686416 | tf_op jit(solution)/shard_map/all_gather | solution.py:1483
  107.5 4.1 split_quarters.1
  119.6 30.4 %attend.1 = (bf16[768,960]{1,0:T(8,128)(2,1)}, f32[6,16,128]{2,1,0:T(8,128)}, bf16[6,1152,1920]{2,1,0:T(8,128)(2,1)}) custom-call(s32[6,9]{1,0:T(8,128)} %get-tuple-element.190.refs_0_, s32[6,1,128]{2,1,0:T(1,128)} %maximum_subtract_fusion.refs_1_, bf16[768,960]{1,0:T(8,128)(2,1)} %get-tuple-element.100.refs_2_, ...), custom_call_target="tpu_custom_call" | custom-call | flops 11200000000 | bytes 1 | tf_op jit(solution)/shard_map/attend/pallas_call | solution.py:459
  155.8 7.8 %out_projection.1 = (f32[768,960]{1,0:T(8,128)}, bf16[768,1024]{1,0:T(8,128)(2,1)}, bf16[960,960]{1,0:T(8,128)(2,1)}, bf16[480,768]{1,0:T(8,128)(2,1)}, bf16[480,768]{1,0:T(8,128)(2,1)}) custom-call(s32[5]{0:T(128)} %stack.35.info_ref.info.refs_0_, ...), custom_call_target="tpu_custom_call", output_to_operand_aliasing={{3}: (12, {}), {4}: (13, {})} | custom-call | flops 2449999872 | bytes 1 | tf_op jit(solution)/shard_map/out_projection/pallas_call | solution.py:688
  167.9 50.6 %feed_forward.1 = (f32[768,960]{1,0:T(8,128)}, f32[768,960]{1,0:T(8,128)}, bf16[768,1024]{1,0:T(8,128)(2,1)}, bf16[768,512]{1,0:T(8,128)(2,1)}, bf16[768,512]{1,...) custom-call(s32[5]{0:T(128)} %stack.35.info_ref.info.refs_0_, ...), custom_call_target="tpu_custom_call" | custom-call | flops 17500000256 | bytes 1 | tf_op jit(solution)/shard_map/feed_forward/pallas_call | solution.py:855
  226.1 12.0 %feed_forward_norm_back.1 = (f32[768,960]{1,0:T(8,128)}, bf16[768,960]{1,0:T(8,128)(2,1)}, bf16[4,256,512]{2,1,0:T(8,128)(2,1)}, bf16[4,256,512]{2,1,0:T(8,128)(2,1)}) custom-call(s32[5]{0:T(128)} %stack.35.info_ref.info.refs_0_, f32[768,960]{1,0:T(8,128)} %get-tuple-element.114.h1_ref.refs_0_, f32[768,960]{1,0:T(8,128)} %get-tuple-element.122.acc_g, ...), custom_call_target="tpu_custom_call" | custom-call | flops 4200000000 | bytes 1 | tf_op jit(solution)/shard_map/feed_forward_norm_back/pallas_call | solution.py:954
  238.2 38.3 %attend_back_0.1 = (bf16[768,960]{1,0:T(8,128)(2,1)}, bf16[3072,640]{1,0:T(8,128)(2,1)}, bf16[3072,640]{1,0:T(8,128)(2,1)}) custom-call(s32[6,9]{1,0:T(8,128)} %get-tuple-element.190.refs_0_, s32[6,9]{1,0:T(8,128)} %get-tuple-element.189.refs_1_, bf16[768,960]{1,0:T(8,128)(2,1)} %get-tuple-element.100.refs_2_, bf16[768,960]{1,0:T(8,128)(2,1)} %get-tuple-element.130.refs_3_, ...), custom_call_target="tpu_custom_call" | custom-call | flops 3499999887360 | bytes 1 | tf_op jit(solution)/shard_map/attend_back_0/pallas_call | solution.py:612
  276.6 5.1 %sum_chips.1 = (bf16[4,272,1024]{2,1,0:T(8,128)(2,1)}, bf16[3072,640]{1,0:T(8,128)(2,1)}) custom-call(s32[5]{0:T(128)} %stack.35.info_ref.info.refs_0_, bf16[4,3,48,960]{3,2,1,0:T(8,128)(2,1)} %get-tuple-element.136.refs_0_, bf16[4,3,48,960]{3,2,1,0:T(8,128)(2,1)} %collective-permute-done.36.refs_1_, ...), custom_call_target="tpu_custom_call", output_to_operand_aliasing={{1}: (8, {})} | custom-call | flops 1400000000 | bytes 1 | tf_op jit(solution)/shard_map/sum_chips/pallas_call | solution.py:156
  282.6 6.7 %collective-permute-done.40.refs_1_ = bf16[3072,640]{1,0:T(8,128)(2,1)} collective-permute-done((bf16[3072,640]{1,0:T(8,128)(2,1)}, bf16[3072,640]{1,0:T(8,128)(2,1)}, u32[]{:S(2)}, u32[]{:S(2)}) %collective-permute-start.40) | collective-permute-done | bytes 3932192 | tf_op jit(solution)/shard_map/ppermute | solution.py:1357
  289.3 6.1 %join_cores.1 = (bf16[768,640]{1,0:T(8,128)(2,1)}, bf16[768,640]{1,0:T(8,128)(2,1)}, bf16[768,640]{1,0:T(8,128)(2,1)}, bf16[384,640]{1,0:T(8,128)(2,1)}, bf16[38...) custom-call(s32[5]{0:T(128)} %stack.35.info_ref.info.refs_0_, ...), custom_call_target="tpu_custom_call" | custom-call | flops 1750000000 | bytes 1 | tf_op jit(solution)/shard_map/join_cores/pallas_call | solution.py:156
  299.5 8.6 %query_back.1 = (bf16[4,256,512]{2,1,0:T(8,128)(2,1)}, bf16[4,256,512]{2,1,0:T(8,128)(2,1)}, f32[768,960]{1,0:T(8,128)}) custom-call(s32[5]{0:T(128)} %stack.35.info_ref.info.refs_0_, bf16[768,960]{1,0:T(8,128)(2,1)} %get-tuple-element.121.a_ref, bf16[768,960]{1,0:T(8,128)(2,1)} %get-tuple-element.133.refs_6_.g_ref, ...), custom_call_target="tpu_custom_call" | custom-call | flops 2800000000 | bytes 1 | tf_op jit(solution)/shard_map/query_back/pallas_call | solution.py:1001
  308.1 9.4 %collective-permute-done.43.refs_5_ = bf16[3,64,960]{2,1,0:T(8,128)(2,1)S(1)} collective-permute-done((bf16[3,64,960]{2,1,0:T(8,128)(2,1)}, bf16[3,64,960]{2,1,0:T(8,128)(2,1)S(1)}, u32[]{:S(2)}, u32[]{:S(2)}) %collective-permute-start.43) | collective-permute-done | bytes 368672 | tf_op jit(solution)/shard_map/ppermute | solution.py:1357
  322.7 9.0 %key_value_weights_back.1 = (bf16[4,256,384]{2,1,0:T(8,128)(2,1)}, bf16[4,256,384]{2,1,0:T(8,128)(2,1)}) custom-call(s32[5]{0:T(128)} %stack.35.info_ref.info.refs_0_, f32[32,2304]{1,0:T(8,128)} %get-tuple-element.188.refs_3_.cos_ref.refs_7_.refs_0_.refs_4_, f32[32,2304]{1,0:T(8,128)} %get-tuple-element.187.refs_4_.sin_ref.refs_8_.refs_1_.refs_5_, ...), custom_call_target="tpu_custom_call" | custom-call | flops 3849999872 | bytes 1 | tf_op jit(solution)/shard_map/key_value_weights_back/pallas_call | solution.py:156
  345.6 4.9 %join_output.1.refs_2_ = bf16[960,768]{1,0:T(8,128)(2,1)} custom-call(s32[5]{0:T(128)} %stack.35.info_ref.info.refs_0_, f32[768,960]{1,0:T(8,128)} %get-tuple-element.114.h1_ref.refs_0_, f32[768,960]{1,0:T(8,128)} %get-tuple-element.119.refs_1_, bf16[768,1024]{1,0:T(8,128)(2,1)} %copy-done.2, bf16[4,256,896]{2,1,0:T(8,128)(2,1)} %get-tuple-element.165.refs_3_), custom_call_target="tpu_custom_call" | custom-call | flops 1750000000 | bytes 1 | tf_op jit(solution)/shard_map/join_output/pallas_call | solution.py:156
  350.5 20.5 %collective-permute-done.49.refs_1_ = bf16[3,48,960]{2,1,0:T(8,128)(2,1)S(1)} collective-permute-done((bf16[3,48,960]{2,1,0:T(8,128)(2,1)}, bf16[3,48,960]{2,1,0:T(8,128)(2,1)S(1)}, u32[]{:S(2)}, u32[]{:S(2)}) %collective-permute-start.49) | collective-permute-done | bytes 276512 | tf_op jit(solution)/shard_map/ppermute | solution.py:1357
  374.7 8.7 %key_value_back.1.refs_2_ = bf16[960,768]{1,0:T(8,128)(2,1)} custom-call(s32[5]{0:T(128)} %stack.35.info_ref.info.refs_0_, bf16[768,640]{1,0:T(8,128)(2,1)} %get-tuple-element.145._.refs_8_.refs_1_, bf16[768,640]{1,0:T(8,128)(2,1)} %copy-done.8, bf16[768,640]{1,0:T(8,128)(2,1)} %collective-permute-done.48.refs_3_, ...), custom_call_target="tpu_custom_call" | custom-call | flops 2800000000 | bytes 1 | tf_op jit(solution)/shard_map/key_value_back/pallas_call | solution.py:1113
  404.2 6.2 %finish_feed_forward.1 = (f32[960,640]{1,0:T(8,128)}, f32[960,640]{1,0:T(8,128)}, f32[960,640]{1,0:T(8,128)}) custom-call(s32[5]{0:T(128)} %stack.35.info_ref.info.refs_0_, bf16[3,320,960]{2,1,0:T(8,128)(2,1)} %get-tuple-element.175.refs_0_, bf16[3,320,960]{2,1,0:T(8,128)(2,1)} %copy-done.30, bf16[128,1408]{1,0:T(8,128)(2,1)} %get-tuple-element.173.refs_2_.refs_0_), custom_call_target="tpu_custom_call" | custom-call | flops 2100000000 | bytes 1 | tf_op jit(solution)/shard_map/finish_feed_forward/pallas_call | solution.py:156
  (263 shorter events, 115.1 us)
Async XLA Ops:
  7.2 100.3 %all-gather.3.cloned.1.call-start = ((), (), s32[]{:S(2)}) async-start(), calls=%async_computation.6 | async-start | bytes 4915200 | tf_op jit(solution)/shard_map/all_gather | solution.py:1483
  30.5 258.8 %reduce-scatter.4.cloned.1.call-start = ((), (), s32[]{:S(2)}) async-start(), calls=%async_computation.3 | async-start | bytes 3932160 | tf_op jit(solution)/shard_map/reduce_scatter | solution.py:1509
  47.8 39.1 %collective-permute-start.19 = (bf16[960,768]{1,0:T(8,128)(2,1)}, bf16[960,768]{1,0:T(8,128)(2,1)S(1)}, u32[]{:S(2)}, u32[]{:S(2)}) collective-permute-start(bf16[960,768]{1,0:T(8,128)(2,1)} %bitcast.50), channel_id=1, source_target_pairs={{0,4},{4,0},{8,12},{12,8},{16,20},{20,16},{24,28},{28,24},{1,5},{5... | collective-permute-start | bytes 4423688 | tf_op jit(solution)/shard_map/ppermute | solution.py:1357
  61.2 38.5 %collective-permute-start.14 = (bf16[768,640]{1,0:T(8,128)(2,1)}, bf16[768,640]{1,0:T(8,128)(2,1)}, u32[]{:S(2)}, u32[]{:S(2)}) collective-permute-start(bf16[768,640]{1,0:T(8,128)(2,1)} %get-tuple-element.101.refs_3_.refs_1_.refs_9_), channel_id=1, source_target_pairs={{0,4},{4,0},{8,12},{12,8},{16,20},{20,16},{24,28},{28,24},{1,5},{5... | collective-permute-start | bytes 2949128 | tf_op jit(solution)/shard_map/ppermute | solution.py:1357
  111.7 38.5 %collective-permute-start.23 = (bf16[720,960]{1,0:T(8,128)(2,1)}, bf16[720,960]{1,0:T(8,128)(2,1)S(1)}, u32[]{:S(2)}, u32[]{:S(2)}) collective-permute-start(bf16[720,960]{1,0:T(8,128)(2,1)} %get-tuple-element.106.refs_0_), channel_id=1, source_target_pairs={{0,8},{4,12},{8,0},{12,4},{16,24},{20,28},{24,16},{28,20},{1,9},{5... | collective-permute-start | bytes 4147208 | tf_op jit(solution)/shard_map/ppermute | solution.py:1357
  113.2 36.9 %collective-permute-start.24 = (bf16[720,960]{1,0:T(8,128)(2,1)}, bf16[720,960]{1,0:T(8,128)(2,1)S(1)}, u32[]{:S(2)}, u32[]{:S(2)}) collective-permute-start(bf16[720,960]{1,0:T(8,128)(2,1)} %get-tuple-element.108.refs_1_), channel_id=1, source_target_pairs={{0,16},{4,20},{8,24},{12,28},{16,0},{20,4},{24,8},{28,12},{1,17},{... | collective-permute-start | bytes 4147208 | tf_op jit(solution)/shard_map/ppermute | solution.py:1357
  116.4 33.6 %collective-permute-start.20 = (bf16[128,960]{1,0:T(8,128)(2,1)}, bf16[128,960]{1,0:T(8,128)(2,1)S(1)}, u32[]{:S(2)}, u32[]{:S(2)}) collective-permute-start(bf16[128,960]{1,0:T(8,128)(2,1)} %meet.3), channel_id=1, source_target_pairs={{0,3},{1,0},{2,1},{3,2},{4,7},{5,4},{6,5},{7,6},{8,11},{9,8},{10,9... | collective-permute-start | bytes 737288 | tf_op jit(solution)/shard_map/ppermute | solution.py:1352
  117.3 32.8 %collective-permute-start.21 = (bf16[128,960]{1,0:T(8,128)(2,1)}, bf16[128,960]{1,0:T(8,128)(2,1)S(1)}, u32[]{:S(2)}, u32[]{:S(2)}) collective-permute-start(bf16[128,960]{1,0:T(8,128)(2,1)} %meet.3), channel_id=1, source_target_pairs={{0,2},{1,3},{2,0},{3,1},{4,6},{5,7},{6,4},{7,5},{8,10},{9,11},{10,... | collective-permute-start | bytes 737288 | tf_op jit(solution)/shard_map/ppermute | solution.py:1352
  117.5 32.6 %collective-permute-start.22 = (bf16[128,960]{1,0:T(8,128)(2,1)}, bf16[128,960]{1,0:T(8,128)(2,1)S(1)}, u32[]{:S(2)}, u32[]{:S(2)}) collective-permute-start(bf16[128,960]{1,0:T(8,128)(2,1)} %meet.3), channel_id=1, source_target_pairs={{0,1},{1,2},{2,3},{3,0},{4,5},{5,6},{6,7},{7,4},{8,9},{9,10},{10,1... | collective-permute-start | bytes 737288 | tf_op jit(solution)/shard_map/ppermute | solution.py:1352
  163.8 54.7 %collective-permute-start.30 = (bf16[480,768]{1,0:T(8,128)(2,1)}, bf16[480,768]{1,0:T(8,128)(2,1)S(1)}, u32[]{:S(2)}, u32[]{:S(2)}) collective-permute-start(bf16[480,768]{1,0:T(8,128)(2,1)} %get-tuple-element.125.refs_2_), channel_id=1, source_target_pairs={{0,8},{4,12},{8,0},{12,4},{16,24},{20,28},{24,16},{28,20},{1,9},{5... | collective-permute-start | bytes 2211848 | tf_op jit(solution)/shard_map/ppermute | solution.py:1357
  164.4 54.2 %collective-permute-start.32 = (bf16[480,768]{1,0:T(8,128)(2,1)}, bf16[480,768]{1,0:T(8,128)(2,1)S(1)}, u32[]{:S(2)}, u32[]{:S(2)}) collective-permute-start(bf16[480,768]{1,0:T(8,128)(2,1)} %get-tuple-element.125.refs_2_), channel_id=1, source_target_pairs={{0,16},{4,20},{8,24},{12,28},{16,0},{20,4},{24,8},{28,12},{1,17},{... | collective-permute-start | bytes 2211848 | tf_op jit(solution)/shard_map/ppermute | solution.py:1357
  165.0 53.6 %collective-permute-start.31 = (bf16[480,768]{1,0:T(8,128)(2,1)}, bf16[480,768]{1,0:T(8,128)(2,1)S(1)}, u32[]{:S(2)}, u32[]{:S(2)}) collective-permute-start(bf16[480,768]{1,0:T(8,128)(2,1)} %get-tuple-element.126.refs_3_), channel_id=1, source_target_pairs={{0,8},{4,12},{8,0},{12,4},{16,24},{20,28},{24,16},{28,20},{1,9},{5... | collective-permute-start | bytes 2211848 | tf_op jit(solution)/shard_map/ppermute | solution.py:1357
  166.5 52.2 %collective-permute-start.33 = (bf16[480,768]{1,0:T(8,128)(2,1)}, bf16[480,768]{1,0:T(8,128)(2,1)S(1)}, u32[]{:S(2)}, u32[]{:S(2)}) collective-permute-start(bf16[480,768]{1,0:T(8,128)(2,1)} %get-tuple-element.126.refs_3_), channel_id=1, source_target_pairs={{0,16},{4,20},{8,24},{12,28},{16,0},{20,4},{24,8},{28,12},{1,17},{... | collective-permute-start | bytes 2211848 | tf_op jit(solution)/shard_map/ppermute | solution.py:1357
  221.4 55.1 %collective-permute-start.36 = (bf16[4,3,48,960]{3,2,1,0:T(8,128)(2,1)}, bf16[4,3,48,960]{3,2,1,0:T(8,128)(2,1)}, u32[]{:S(2)}, u32[]{:S(2)}) collective-permute-start(bf16[4,3,48,960]{3,2,1,0:T(8,128)(2,1)} %get-tuple-element.137), channel_id=1, source_target_pairs={{0,8},{4,12},{8,0},{12,4},{16,24},{20,28},{24,16},{28,20},{1,9},{5... | collective-permute-start | bytes 3317768 | tf_op jit(solution)/shard_map/ppermute | solution.py:1357
  221.9 54.6 %collective-permute-start.37 = (bf16[4,3,48,960]{3,2,1,0:T(8,128)(2,1)}, bf16[4,3,48,960]{3,2,1,0:T(8,128)(2,1)}, u32[]{:S(2)}, u32[]{:S(2)}) collective-permute-start(bf16[4,3,48,960]{3,2,1,0:T(8,128)(2,1)} %get-tuple-element.138), channel_id=1, source_target_pairs={{0,16},{4,20},{8,24},{12,28},{16,0},{20,4},{24,8},{28,12},{1,17},{... | collective-permute-start | bytes 3317768 | tf_op jit(solution)/shard_map/ppermute | solution.py:1357
  222.5 54.0 %collective-permute-start.38 = (bf16[4,3,48,960]{3,2,1,0:T(8,128)(2,1)}, bf16[4,3,48,960]{3,2,1,0:T(8,128)(2,1)}, u32[]{:S(2)}, u32[]{:S(2)}) collective-permute-start(bf16[4,3,48,960]{3,2,1,0:T(8,128)(2,1)} %get-tuple-element.139), channel_id=1, source_target_pairs={{0,24},{4,28},{8,16},{12,20},{16,8},{20,12},{24,0},{28,4},{1,25},{... | collective-permute-start | bytes 3317768 | tf_op jit(solution)/shard_map/ppermute | solution.py:1357
  224.9 107.4 %reduce-scatter.6.cloned.1.call-start = ((), (), s32[]{:S(2)}) async-start(), calls=%async_computation.4 | async-start | bytes 2785280 | tf_op jit(solution)/shard_map/reduce_scatter | solution.py:1564
  238.1 38.4 %collective-permute-start.39 = (bf16[4,256,512]{2,1,0:T(8,128)(2,1)}, bf16[4,256,512]{2,1,0:T(8,128)(2,1)}, u32[]{:S(2)}, u32[]{:S(2)}) collective-permute-start(bf16[4,256,512]{2,1,0:T(8,128)(2,1)} %get-tuple-element.141), channel_id=1, source_target_pairs={{0,4},{4,0},{8,12},{12,8},{16,20},{20,16},{24,28},{28,24},{1,5},{5... | collective-permute-start | bytes 3145736 | tf_op jit(solution)/shard_map/ppermute | solution.py:1357
  282.6 100.8 %reduce-scatter.8.cloned.1.call-start = ((), (), s32[]{:S(2)}) async-start(), calls=%async_computation.5 | async-start | bytes 2293760 | tf_op jit(solution)/shard_map/reduce_scatter | solution.py:1590
  339.8 33.9 %collective-permute-start.47 = (bf16[768,640]{1,0:T(8,128)(2,1)}, bf16[768,640]{1,0:T(8,128)(2,1)S(1)}, u32[]{:S(2)}, u32[]{:S(2)}) collective-permute-start(bf16[768,640]{1,0:T(8,128)(2,1)} %get-tuple-element.159.refs_9_), channel_id=1, source_target_pairs={{0,8},{4,12},{8,0},{12,4},{16,24},{20,28},{24,16},{28,20},{1,9},{5... | collective-permute-start | bytes 2949128 | tf_op jit(solution)/shard_map/ppermute | solution.py:1357
  341.4 32.3 %collective-permute-start.48 = (bf16[768,640]{1,0:T(8,128)(2,1)}, bf16[768,640]{1,0:T(8,128)(2,1)}, u32[]{:S(2)}, u32[]{:S(2)}) collective-permute-start(bf16[768,640]{1,0:T(8,128)(2,1)} %get-tuple-element.160.refs_10_), channel_id=1, source_target_pairs={{0,16},{4,20},{8,24},{12,28},{16,0},{20,4},{24,8},{28,12},{1,17},{... | collective-permute-start | bytes 2949128 | tf_op jit(solution)/shard_map/ppermute | solution.py:1357
  341.7 29.2 %collective-permute-start.49 = (bf16[3,48,960]{2,1,0:T(8,128)(2,1)}, bf16[3,48,960]{2,1,0:T(8,128)(2,1)S(1)}, u32[]{:S(2)}, u32[]{:S(2)}) collective-permute-start(bf16[3,48,960]{2,1,0:T(8,128)(2,1)} %get-tuple-element.169.refs_0_), channel_id=1, source_target_pairs={{0,8},{4,12},{8,0},{12,4},{16,24},{20,28},{24,16},{28,20},{1,9},{5... | collective-permute-start | bytes 829448 | tf_op jit(solution)/shard_map/ppermute | solution.py:1357
  342.0 47.0 %collective-permute-start.52 = (bf16[3,64,960]{2,1,0:T(8,128)(2,1)S(1)}, bf16[3,64,960]{2,1,0:T(8,128)(2,1)}, u32[]{:S(2)}, u32[]{:S(2)}) collective-permute-start(bf16[3,64,960]{2,1,0:T(8,128)(2,1)S(1)} %copy-done.3), channel_id=1, source_target_pairs={{0,16},{4,20},{8,24},{12,28},{16,0},{20,4},{24,8},{28,12},{1,17},{... | collective-permute-start | bytes 1105928 | tf_op jit(solution)/shard_map/ppermute | solution.py:1357
  343.9 45.1 %collective-permute-start.53 = (bf16[3,64,960]{2,1,0:T(8,128)(2,1)S(1)}, bf16[3,64,960]{2,1,0:T(8,128)(2,1)}, u32[]{:S(2)}, u32[]{:S(2)}) collective-permute-start(bf16[3,64,960]{2,1,0:T(8,128)(2,1)S(1)} %copy-done.22), channel_id=1, source_target_pairs={{0,8},{4,12},{8,0},{12,4},{16,24},{20,28},{24,16},{28,20},{1,9},{5... | collective-permute-start | bytes 1105928 | tf_op jit(solution)/shard_map/ppermute | solution.py:1357
  (84 other events, 566.7 us)
Sparse Core Ops, SparseCore 0:
  30.6 76.8 all-gather.2
  225.0 57.9 reduce-scatter.3
  285.9 46.0 reduce-scatter.5
  339.5 37.5 reduce-scatter.7
